TPU v7x, 32 devices: a whole 2x2x4 slice. The times are simulated.
32 devices in a mesh: grp: 2 (over core), ep: 16 (over z, y, x).
Axes of the slice: x: 2, y: 2, z: 4, core: 2. Of those that a mesh axis runs over, the one named last changes fastest.
Arguments:
- hidden: bfloat16 [2, 4096, 2048], P('grp', 'ep'), may hold values from -6 to 6
- norm_gain: float32 [2, 2048], P('grp'), may hold values from 0.1 to 1.9
- final_gain: float32 [2, 2048], P('grp'), may hold values from 0.1 to 1.9
- router: bfloat16 [2, 2048, 128], P('grp'), may hold values from -0.125 to 0.125
- w_in: bfloat16 [2, 2048, 16384], P('grp', None, 'ep'), may hold values from -0.125 to 0.125
- w_out: bfloat16 [2, 16384, 2048], P('grp', 'ep'), may hold values from -0.125 to 0.125
- expert_ids: int32 [2, 4096, 2], P('grp', 'ep'), may hold values from 0 to 127, as said below
- slot_ids: int32 [2, 4096, 2], P('grp', 'ep'), may hold values from -1 to 5, as said below
- src_len: int32 [16, 4], P('ep'), may hold values from 1 to 128, 256 in all within a row
- tgt_len: int32 [16, 4], P('ep'), may hold values from 1 to 85, 171 in all within a row
- wq: bfloat16 [2048, 1024], P('ep'), may hold values from -1 to 1
- wk: bfloat16 [2048, 1024], P('ep'), may hold values from -1 to 1
- wv: bfloat16 [2048, 1024], P('ep'), may hold values from -0.125 to 0.125
- wo: bfloat16 [2048, 1024], P('ep'), may hold values from -0.5 to 0.5
Outputs:
- layer_out: bfloat16 [2, 4096, 2048], P('grp', 'ep')
Inputs may be any that keep to these rules, and one draw needn't show every extreme that they name: `expert_ids`: each row names two different experts; at most one of them is below 2. `slot_ids`: -1 where the expert is 2 or more; otherwise a slot that no other route of the same device block to the same expert takes. In each group one expert gets all 6 slots from every device block.
All inputs are finite; a program needn't handle non-finite values.
Results may differ from a plain program's by a relative error of at most 0.02.
The roundings to bfloat16 on the way count: a program that leaves them out, or rounds other values in their place, can miss the bound.
Values may be sent and summed in bfloat16 or wider, within the bound.
No kernel may reach another device: no remote copies, remote signals or barrier semaphores. Data moves between devices by JAX's collectives and lax.ppermute only.
A program may use at most 128 MiB of HBM per device.

v0:
```python
import jax
import jax.numpy as jnp
from jax import lax
from jax.sharding import PartitionSpec as P

HD = 128
SPLIT = 8
C = 6
SENT = 4


def shifted(value, axis, steps):
    count = lax.axis_size(axis)
    first, last = (max(0, -steps), min(count, count - steps))
    return lax.ppermute(value, axis, [(source, source + steps) for source in range(first, last)])


def normalize(values, gain):
    mean = jnp.mean(values, -1, keepdims=True)
    centred = values - mean
    spread = jnp.mean(centred * centred, -1, keepdims=True)
    return centred * lax.rsqrt(spread + 1e-05) * gain


def positions(lengths, count):
    ends = jnp.cumsum(lengths)
    above = (jnp.arange(count, dtype=jnp.int32)[:, None] >= ends[None, :]).astype(jnp.int32)
    return jnp.sum(above, axis=1)


def body(
    hidden,
    norm_gain,
    final_gain,
    router,
    w_in,
    w_out,
    expert_ids,
    slot_ids,
    src_len,
    tgt_len,
    wq,
    wk,
    wv,
    wo,
):
    devices = lax.axis_size("ep")
    experts_here = devices // SPLIT
    rows_here = hidden.shape[1]
    width = hidden.shape[2]
    resid = hidden[0].astype(jnp.float32)
    normed = normalize(resid, norm_gain[0]).astype(jnp.bfloat16)
    logits = jnp.dot(normed, router[0], preferred_element_type=jnp.float32)
    routes = expert_ids[0]
    slots = slot_ids[0]
    picked = jnp.take_along_axis(logits, routes, axis=1)
    gate = jax.nn.sigmoid(picked - picked[:, ::-1])
    live = slots >= 0
    place = jnp.max(jnp.where(live, routes * C + slots, -1), axis=1)
    weight = jnp.sum(jnp.where(live, gate, 0.0), axis=1)
    table = (jnp.arange(experts_here * C)[:, None] == place[None, :]).astype(jnp.bfloat16)
    packed = jnp.dot(table, normed, preferred_element_type=jnp.float32).astype(jnp.bfloat16)
    outgoing = jnp.broadcast_to(
        packed.reshape(experts_here, 1, C, width), (experts_here, SPLIT, C, width)
    )
    outgoing = outgoing.reshape(devices, C, width)
    arrived = lax.all_to_all(outgoing, "ep", split_axis=0, concat_axis=0, tiled=True)
    flat = arrived.reshape(-1, width)
    inner = jax.nn.relu(jnp.dot(flat, w_in[0], preferred_element_type=jnp.float32)).astype(
        jnp.bfloat16
    )
    partial_out = jnp.dot(inner, w_out[0], preferred_element_type=jnp.float32).astype(jnp.bfloat16)
    back = lax.all_to_all(
        partial_out.reshape(arrived.shape), "ep", split_axis=0, concat_axis=0, tiled=True
    )
    summed = jnp.sum(back.reshape(experts_here, SPLIT, C, width).astype(jnp.float32), axis=1)
    summed = summed.reshape(experts_here * C, width)
    moe_term = jnp.take(summed, jnp.maximum(place, 0), axis=0) * weight[:, None]
    mixed = resid + moe_term
    normed_out = normalize(mixed, final_gain[0]).astype(jnp.bfloat16)
    group = lax.axis_index("grp")
    heads_width = wq.shape[1]
    memory = shifted(normed_out, "grp", 1)
    q_total = jnp.dot(
        normed_out, lax.all_gather(wq, "ep", axis=0, tiled=True), preferred_element_type=jnp.float32
    )
    k_total = jnp.dot(
        memory, lax.all_gather(wk, "ep", axis=0, tiled=True), preferred_element_type=jnp.float32
    )
    v_total = jnp.dot(
        memory, lax.all_gather(wv, "ep", axis=0, tiled=True), preferred_element_type=jnp.float32
    )
    query = q_total.astype(jnp.bfloat16)
    keys = k_total.astype(jnp.bfloat16)
    values = v_total.astype(jnp.bfloat16)
    seg_q = positions(tgt_len[0], rows_here)
    seg_k = positions(src_len[0], rows_here)
    valid = seg_q < SENT
    allowed = (seg_q[:, None] == seg_k[None, :]) & valid[:, None]
    heads = heads_width // HD
    scores = jnp.einsum(
        "qhd,khd->hqk",
        query.reshape(rows_here, heads, HD),
        keys.reshape(rows_here, heads, HD),
        preferred_element_type=jnp.float32,
    ) * HD ** (-0.5)
    scores = jnp.where(allowed[None], scores, -1e30)
    top = jnp.max(scores, axis=-1, keepdims=True)
    expd = jnp.exp(scores - top)
    prob = (expd / jnp.sum(expd, axis=-1, keepdims=True)).astype(jnp.bfloat16)
    context = jnp.einsum(
        "hqk,khd->qhd",
        prob,
        values.reshape(rows_here, heads, HD),
        preferred_element_type=jnp.float32,
    )
    context = context.astype(jnp.bfloat16).reshape(rows_here, heads_width)
    attended = lax.dot_general(
        context,
        lax.all_gather(wo, "ep", axis=0, tiled=True),
        (((1,), (1,)), ((), ())),
        preferred_element_type=jnp.float32,
    )
    attended = jnp.where(valid[:, None], attended, 0.0)
    decoded = (mixed + attended).astype(jnp.bfloat16)
    return jnp.where(group == 0, normed_out, decoded)[None]


def solution(mesh):
    in_specs = (
        P("grp", "ep", None),
        P("grp", None),
        P("grp", None),
        P("grp", None, None),
        P("grp", None, "ep"),
        P("grp", "ep", None),
        P("grp", "ep", None),
        P("grp", "ep", None),
        P("ep", None),
        P("ep", None),
        P("ep", None),
        P("ep", None),
        P("ep", None),
        P("ep", None),
    )
    out_specs = P("grp", "ep", None)
    return jax.shard_map(body, mesh=mesh, in_specs=in_specs, out_specs=out_specs, check_vma=False)
```

profile of v0, /device:TPU:1, one launch (start us, length us, event | category | flops | bytes accessed | tf_op | source)
XLA Modules:
  0.0 342.4 jit_solution(14036189753341375583)
XLA Ops:
  6.6 0.7 all-gather.5.cloned.1.call-update
  7.3 0.7 all-gather.9.cloned.1.call-update
  8.1 0.7 all-gather.7.cloned.1.call-update
  8.8 0.5 all-gather.11.cloned.1.call-update
  9.3 0.8 copy.26
  10.2 1.4 convert_reduce_fusion
  11.6 0.1 copy.27
  11.7 0.1 fusion.55
  11.9 0.4 fusion.16
  12.3 0.5 convolution_convert_fusion
  12.9 0.8 broadcast_in_dim.77
  13.7 7.4 %all-to-all-start = ((bf16[16,6,2048]{2,1,0:T(8,128)(2,1)}), bf16[16,6,2048]{2,1,0:T(8,128)(2,1)S(1)}, u32[]{:S(2)}, u32[]{:S(2)}) async-start(bf16[16,6,2048]{2,1,0:T(8,128)(2,1)} %bitcast.4), calls=%async_computation | async-start | bytes 1048576 | tf_op jit(solution)/shard_map/all_to_all | solution.py:67
  21.1 0.1 copy.28
  21.3 0.1 reshape.241
  21.4 0.6 fusion.32
  22.0 3.6 %gather_fusion.1 = f32[512]{0:T(512)S(1)} fusion(f32[256,128]{1,0:T(8,128)S(1)} %fusion.32, s32[512]{0:T(512)S(1)} %reshape.241), kind=kCustom, calls=%fused_computation.1 | custom fusion | bytes 8192 | tf_op jit(solution)/shard_map/jit(take_along_axis)/gather | solution.py:56
  25.6 0.1 reshape.244
  25.8 14.6 %all-to-all-done = bf16[16,6,2048]{2,1,0:T(8,128)(2,1)S(1)} async-done(((bf16[16,6,2048]{2,1,0:T(8,128)(2,1)}), bf16[16,6,2048]{2,1,0:T(8,128)(2,1)S(1)}, u32[]{:S(2)}, u32[]{:S(2)}) %all-to-all-start) | async-done | bytes 393248 | tf_op jit(solution)/shard_map/all_to_all | solution.py:67
  40.4 0.1 reshape.221
  40.6 4.9 %fusion.11 = bf16[96,2048]{1,0:T(8,128)(2,1)S(1)} fusion(bf16[1,1024,2048]{2,1,0:T(8,128)(2,1)} %param.19, bf16[96,2048]{1,0:T(8,128)(2,1)S(1)} %reshape.221, bf16[1,2048,1024]{2,1,0:T(8,128)(2,1)} %param.18), kind=kOutput, calls=%fused_computation.17 | convolution fusion | flops 805699584 | bytes 9175040 | tf_op jit(solution)/shard_map/dot_general | solution.py:72
  45.5 0.9 reshape.222
  46.4 5.4 %all-to-all-start.1 = ((bf16[16,6,2048]{2,1,0:T(8,128)(2,1)}), bf16[16,6,2048]{2,1,0:T(8,128)(2,1)S(1)}, u32[]{:S(2)}, u32[]{:S(2)}) async-start(bf16[16,6,2048]{2,1,0:T(8,128)(2,1)} %reshape.222), calls=%async_computation.1 | async-start | bytes 1048576 | tf_op jit(solution)/shard_map/all_to_all | solution.py:73
  51.9 0.2 rev.3
  52.1 0.1 fusion.57
  52.2 17.4 %all-to-all-done.1 = bf16[16,6,2048]{2,1,0:T(8,128)(2,1)S(1)} async-done(((bf16[16,6,2048]{2,1,0:T(8,128)(2,1)}), bf16[16,6,2048]{2,1,0:T(8,128)(2,1)S(1)}, u32[]{:S(2)}, u32[]{:S(2)}) %all-to-all-start.1) | async-done | bytes 393248 | tf_op jit(solution)/shard_map/all_to_all | solution.py:73
  69.6 0.1 convert_reduce_fusion.1
  69.8 2.7 gather_fusion
  72.5 2.3 fusion.77
  74.8 0.3 multiply_reduce_fusion
  75.2 0.3 copy-done.2
  75.5 1.3 multiply_convert_fusion
  76.8 1.5 collective-permute-start
  78.3 0.2 reduce-window.16
  78.5 0.2 reduce-window.17
  78.7 0.1 convert_reduce_fusion.3
  78.9 0.1 compare_and_fusion
  79.0 3.1 collective-permute-done
  82.1 16.7 %all-gather.5.cloned.1.call-done = bf16[2048,1024]{1,0:T(8,128)(2,1)} async-done(((bf16[128,1024]{1,0:T(8,128)(2,1)}), bf16[2048,1024]{1,0:T(8,128)(2,1)}) %all-gather.5.cloned.1.call-update) | async-done | bytes 4194320 | tf_op jit(solution)/shard_map/all_gather | solution.py:91
  98.9 3.8 %convolution_convert_fusion.4 = bf16[256,1024]{1,0:T(8,128)(2,1)S(1)} fusion(bf16[256,2048]{1,0:T(8,128)(2,1)} %collective-permute-done, bf16[2048,1024]{1,0:T(8,128)(2,1)} %all-gather.5.cloned.1.call-done), kind=kOutput, calls=%fused_computation.36 | convolution fusion | flops 1074003968 | bytes 5767168 | tf_op jit(solution)/shard_map/dot_general | solution.py:90
  102.6 1.0 copy.34
  103.7 72.7 %all-gather.9.cloned.1.call-done = bf16[2048,1024]{1,0:T(8,128)(2,1)} async-done(((bf16[128,1024]{1,0:T(8,128)(2,1)}), bf16[2048,1024]{1,0:T(8,128)(2,1)}) %all-gather.9.cloned.1.call-update) | async-done | bytes 4194320 | tf_op jit(solution)/shard_map/all_gather | solution.py:88
  176.4 3.8 %fusion.24 = bf16[32,8,8,128]{3,2,1,0:T(8,128)(2,1)S(1)} fusion(bf16[256,2048]{1,0:T(8,128)(2,1)} %collective-permute-done, bf16[2048,1024]{1,0:T(8,128)(2,1)} %all-gather.9.cloned.1.call-done), kind=kOutput, calls=%fused_computation.38 | convolution fusion | flops 1074003968 | bytes 5767168 | tf_op jit(solution)/shard_map/dot_general | solution.py:87
  180.1 73.7 %all-gather.7.cloned.1.call-done = bf16[2048,1024]{1,0:T(8,128)(2,1)} async-done(((bf16[128,1024]{1,0:T(8,128)(2,1)}), bf16[2048,1024]{1,0:T(8,128)(2,1)}) %all-gather.7.cloned.1.call-update) | async-done | bytes 4194320 | tf_op jit(solution)/shard_map/all_gather | solution.py:85
  253.9 4.6 %fusion.23 = bf16[32,8,8,128]{3,2,1,0:T(8,128)(2,1)} fusion(bf16[256,2048]{1,0:T(8,128)(2,1)} %multiply_convert_fusion, bf16[2048,1024]{1,0:T(8,128)(2,1)} %all-gather.7.cloned.1.call-done), kind=kOutput, calls=%fused_computation.37 | convolution fusion | flops 1074003968 | bytes 5767168 | tf_op jit(solution)/shard_map/dot_general | solution.py:84
  258.5 3.2 fusion.79
  261.6 2.1 convolution_convert_fusion.1
  263.7 67.4 %all-gather.11.cloned.1.call-done = bf16[2048,1024]{1,0:T(8,128)(2,1)} async-done(((bf16[128,1024]{1,0:T(8,128)(2,1)}), bf16[2048,1024]{1,0:T(8,128)(2,1)}) %all-gather.11.cloned.1.call-update) | async-done | bytes 4194320 | tf_op jit(solution)/shard_map/all_gather | solution.py:120
  331.2 4.7 %fusion.15 = bf16[1,256,2048]{2,1,0:T(8,128)(2,1)} fusion(bf16[256,2048]{1,0:T(8,128)(2,1)} %multiply_convert_fusion, f32[256,2048]{1,0:T(8,128)S(1)} %get-tuple-element.6, bf16[256,1024]{0,1:T(8,128)(2,1)S(1)} %bitcast.114, bf16[2048,1024]{1,0:T(8,128)(2,1)} %all-gather.11.cloned.1.call-done, pred[256]{0:T(512)(128)(4,1)S(1)} %broadcast_compare_fusion, ...), kind=kOutput, calls=%fused_computation.19 | convolution fusion | flops 1075838976 | bytes 8913153 | tf_op jit(solution)/shard_map/dot_general | solution.py:118
  (30 shorter events, 0.4 us)
Async XLA Ops:
  6.5 14.9 %copy-start = (bf16[1,2048,128]{2,1,0:T(8,128)(2,1)S(1)}, bf16[1,2048,128]{2,1,0:T(8,128)(2,1)}, u32[]{:S(2)}) copy-start(bf16[1,2048,128]{2,1,0:T(8,128)(2,1)} %param.17) | copy-start | bytes 1572868
  6.5 5.3 %copy-start.1 = (bf16[1,256,2048]{2,1,0:T(8,128)(2,1)S(1)}, bf16[1,256,2048]{2,1,0:T(8,128)(2,1)}, u32[]{:S(2)}) copy-start(bf16[1,256,2048]{2,1,0:T(8,128)(2,1)} %param.14) | copy-start | bytes 3145732
  6.5 5.1 %copy-start.3 = (s32[1,256,2]{1,2,0:T(2,128)S(1)}, s32[1,256,2]{1,2,0:T(2,128)}, u32[]{:S(2)}) copy-start(s32[1,256,2]{1,2,0:T(2,128)} %param.20) | copy-start | bytes 6148
  6.5 5.8 %copy-start.4 = (f32[1,2048]{1,0:T(1,128)S(1)}, f32[1,2048]{1,0:T(1,128)}, u32[]{:S(2)}) copy-start(f32[1,2048]{1,0:T(1,128)} %param.15) | copy-start | bytes 24580
  6.5 92.3 %all-gather.5.cloned.1.call-start = ((), (), s32[]{:S(2)}) async-start(), calls=%async_computation.2 | async-start | bytes 4456448 | tf_op jit(solution)/shard_map/all_gather | solution.py:91
  7.3 169.1 %all-gather.9.cloned.1.call-start = ((), (), s32[]{:S(2)}) async-start(), calls=%async_computation.4 | async-start | bytes 4456448 | tf_op jit(solution)/shard_map/all_gather | solution.py:88
  8.0 245.8 %all-gather.7.cloned.1.call-start = ((), (), s32[]{:S(2)}) async-start(), calls=%async_computation.3 | async-start | bytes 4456448 | tf_op jit(solution)/shard_map/all_gather | solution.py:85
  8.8 322.4 %all-gather.11.cloned.1.call-start = ((), (), s32[]{:S(2)}) async-start(), calls=%async_computation.5 | async-start | bytes 4456448 | tf_op jit(solution)/shard_map/all_gather | solution.py:120
  13.7 26.7 %all-to-all-start = ((bf16[16,6,2048]{2,1,0:T(8,128)(2,1)}), bf16[16,6,2048]{2,1,0:T(8,128)(2,1)S(1)}, u32[]{:S(2)}, u32[]{:S(2)}) async-start(bf16[16,6,2048]{2,1,0:T(8,128)(2,1)} %bitcast.4), calls=%async_computation | async-start | bytes 1048576 | tf_op jit(solution)/shard_map/all_to_all | solution.py:67
  46.4 23.2 %all-to-all-start.1 = ((bf16[16,6,2048]{2,1,0:T(8,128)(2,1)}), bf16[16,6,2048]{2,1,0:T(8,128)(2,1)S(1)}, u32[]{:S(2)}, u32[]{:S(2)}) async-start(bf16[16,6,2048]{2,1,0:T(8,128)(2,1)} %reshape.222), calls=%async_computation.1 | async-start | bytes 1048576 | tf_op jit(solution)/shard_map/all_to_all | solution.py:73
  74.8 0.7 copy-start.2
  75.2 3.1 copy-start.5
  75.2 3.3 copy-start.6
  76.8 5.3 %collective-permute-start = (bf16[256,2048]{1,0:T(8,128)(2,1)}, bf16[256,2048]{1,0:T(8,128)(2,1)}, u32[]{:S(2)}, u32[]{:S(2)}) collective-permute-start(bf16[256,2048]{1,0:T(8,128)(2,1)} %multiply_convert_fusion), channel_id=1, source_target_pairs={{0,16},{1,17},{2,18},{3,19},{4,20},{5,21},{6,22},{7,23},{8,24},{9,... | collective-permute-start | bytes 3145736 | tf_op jit(solution)/shard_map/ppermute | solution.py:15
Sparse Core Ops, SparseCore 0:
  10.1 88.6 all-gather.4
  101.6 74.6 all-gather.8
  179.1 74.6 all-gather.6
  256.5 74.6 all-gather.10
where the time goes:
time: 345 us; the launch traced here: 342 us
  waiting for transfers between devices  268 us (78%)
  matrix products  28.1 us (8%)
  starting transfers between devices  14.4 us (4%)
  between operations  13.4 us (4%)
  local copies, waits for them, and re-layouts  11.2 us (3%)
  other arithmetic  6.97 us (2%)
    all_gather x1, waiting for transfers between devices, body(): lax.all_gather(wq, 'ep', axis=0, tiled=True)  73.7 us
    all_gather x1, waiting for transfers between devices, body(): lax.all_gather(wk, 'ep', axis=0, tiled=True)  72.7 us
    all_gather x1, waiting for transfers between devices, body(): lax.all_gather(wo, 'ep', axis=0, tiled=True)  67.4 us
    all_to_all x1, waiting for transfers between devices, body(): lax.all_to_all(partial_out.reshape(arrived.shape), 'ep', split_axis=0, co...  17.4 us
    all_gather x1, waiting for transfers between devices, body(): lax.all_gather(wv, 'ep', axis=0, tiled=True)  16.7 us
    all_to_all x1, waiting for transfers between devices, body(): lax.all_to_all(outgoing, 'ep', split_axis=0, concat_axis=0, tiled=True)  14.6 us
    all_to_all x1, starting transfers between devices, body(): lax.all_to_all(outgoing, 'ep', split_axis=0, concat_axis=0, tiled=True)  7.41 us
  transfers between devices with their start and end apart: 7, of which 7 were waited for; matrix products, arithmetic and copies ran while one was open for 12% of the time, Pallas kernels for 0%

commit v1 on v0

v1 whole, which is shorter than its diff:
```python
import functools

import jax
import jax.numpy as jnp
from jax import lax
from jax.experimental import pallas as pl
from jax.experimental.pallas import tpu as pltpu
from jax.sharding import PartitionSpec as P

HD = 128
SPLIT = 8
C = 6
PAD = 8
SENT = 4
TGT_TOTAL = 171
MIB = 1 << 20


def normalize(values, gain):
    mean = jnp.mean(values, -1, keepdims=True)
    centred = values - mean
    spread = jnp.mean(centred * centred, -1, keepdims=True)
    return centred * lax.rsqrt(spread + 1e-05) * gain


def positions(lengths, count):
    upto = jnp.arange(SENT)[:, None] <= jnp.arange(SENT)[None, :]
    ends = jnp.sum(jnp.where(upto, lengths[:, None], 0), axis=0)
    above = (jnp.arange(count, dtype=jnp.int32)[:, None] >= ends[None, :]).astype(jnp.int32)
    return jnp.sum(above, axis=1)


def dot(left, right):
    return jnp.dot(left, right, preferred_element_type=jnp.float32)


def dot_rows(left, right):
    return lax.dot_general(
        left, right, (((1,), (1,)), ((), ())), preferred_element_type=jnp.float32
    )


def chips():
    return (4, 2, 2) if lax.axis_size("ep") == 16 else None


def place_of(index):
    depth, high, wide = chips()
    return index // (high * wide), index // wide % high, index % wide


def index_of(z, y, x):
    depth, high, wide = chips()
    return (z % depth * high + y) * wide + x


def moved(value, dz=0, dy=0, dx=0):
    pairs = []
    for source in range(lax.axis_size("ep")):
        z, y, x = place_of(source)
        pairs.append((source, index_of(z + dz, y ^ dy, x ^ dx)))
    return lax.ppermute(value, "ep", pairs)


def specs(smem, vmem, unread=0):
    return (
        [pl.BlockSpec(memory_space=pltpu.SMEM)] * smem
        + [pl.BlockSpec(memory_space=pltpu.VMEM)] * vmem
        + [pl.BlockSpec(memory_space=pl.ANY)] * unread
    )


def local(kernel, name, outs, vmem, after=(), onward=(), order=None):
    scalars = () if order is None else (order,)
    read = len(scalars) + len(vmem)

    def run(*refs):
        kernel(*refs[:read], *refs[read + len(after) + len(onward) :][: len(outs)])

    first = read + len(after)
    return pl.pallas_call(
        run,
        out_shape=[jax.ShapeDtypeStruct(shape, dtype) for shape, dtype in outs]
        + [jax.ShapeDtypeStruct(array.shape, array.dtype) for array in onward],
        in_specs=specs(len(scalars), len(vmem), len(after) + len(onward)),
        out_specs=specs(0, len(outs), len(onward)),
        input_output_aliases={first + i: len(outs) + i for i in range(len(onward))},
        compiler_params=pltpu.CompilerParams(vmem_limit_bytes=16 * MIB),
        name=name,
    )(*scalars, *vmem, *after, *onward)


def pack_kernel(experts, place, both, hidden, gain, router, gate, send):
    count = gate.shape[0]
    slot = lax.broadcasted_iota(jnp.int32, (count, hidden.shape[0]), 0)
    table = slot == place[...]
    rows = dot(table.astype(jnp.bfloat16), hidden[...])
    normed = normalize(rows, gain[...])
    send[...] = jnp.concatenate(
        [normed[e * PAD : (e + 1) * PAD] for e in experts], axis=0
    ).astype(jnp.bfloat16)
    logits = dot(normed.astype(jnp.bfloat16), router[...])
    mine = lax.broadcasted_iota(jnp.int32, (count, 1), 0) // PAD
    others = jnp.sum(jnp.where(table, both[...], 0), axis=1, keepdims=True) - mine
    expert = lax.broadcasted_iota(jnp.int32, logits.shape, 1)
    lead = jnp.where(expert == mine, logits, 0.0) - jnp.where(expert == others, logits, 0.0)
    gate[...] = 1.0 / (1.0 + jnp.exp(-jnp.sum(lead, axis=1, keepdims=True)))


def copies_kernel(rows, out):
    size = rows.shape[0]
    for i in range(out.shape[0] // size):
        out[i * size : (i + 1) * size] = rows[...]


def mlp_kernel(rows, w_in, w_out, pieces):
    inner = jnp.maximum(dot(rows[...], w_in[...]), 0.0).astype(jnp.bfloat16)
    pieces[...] = dot(inner, w_out[...]).astype(jnp.bfloat16)


def sum_kernel(pieces, out):
    size = out.shape[0]
    total = pieces[:size].astype(jnp.float32)
    for low in range(size, pieces.shape[0], size):
        total = total + pieces[low : low + size].astype(jnp.float32)
    out[...] = total


def norm_kernel(experts, place, gate, hidden, gain, parts, mixed, normed):
    count = gate.shape[0]
    summed = [None] * (count // PAD)
    for i, e in enumerate(experts):
        part = parts[i * PAD : (i + 1) * PAD]
        summed[e] = part if summed[e] is None else summed[e] + part
    rows = gate[...] * jnp.concatenate(summed, axis=0)
    high = rows.astype(jnp.bfloat16)
    rest = rows - high.astype(jnp.float32)
    middle = rest.astype(jnp.bfloat16)
    low = (rest - middle.astype(jnp.float32)).astype(jnp.bfloat16)
    slot = lax.broadcasted_iota(jnp.int32, (hidden.shape[0], 3 * count), 1) % count
    picks = (slot == place[...]).astype(jnp.bfloat16)
    total = hidden[...].astype(jnp.float32) + dot(picks, jnp.concatenate([high, middle, low], axis=0))
    mixed[...] = total
    normed[...] = normalize(total, gain[...]).astype(jnp.bfloat16)


def places(routes, slots):
    return jnp.max(jnp.where(slots >= 0, routes * PAD + slots, -1), axis=1)


def expert_rows(hidden, norm_gain, router, w_in, w_out, routes, slots):
    experts = lax.axis_size("ep") // SPLIT
    count = experts * PAD
    width = hidden.shape[1]
    table = jnp.arange(count)[:, None] == places(routes, slots)[None, :]
    rows = dot(table.astype(jnp.bfloat16), hidden)
    normed = normalize(rows, norm_gain).astype(jnp.bfloat16)
    outgoing = jnp.broadcast_to(normed.reshape(experts, 1, PAD, width), (experts, SPLIT, PAD, width))
    arrived = lax.all_to_all(
        outgoing.reshape(experts * SPLIT, PAD, width), "ep", split_axis=0, concat_axis=0, tiled=True
    ).reshape(-1, width)
    inner = jax.nn.relu(dot(arrived, w_in)).astype(jnp.bfloat16)
    piece = dot(inner, w_out).astype(jnp.bfloat16)
    back = lax.all_to_all(
        piece.reshape(-1, PAD, width), "ep", split_axis=0, concat_axis=0, tiled=True
    )
    summed = jnp.sum(back.reshape(experts, SPLIT, PAD, width).astype(jnp.float32), axis=1)
    logits = dot(normed, router)
    mine = jnp.arange(count) // PAD
    both = jnp.sum(routes, axis=1)
    others = jnp.sum(jnp.where(table, both[None, :], 0), axis=1) - mine
    ids = jnp.arange(router.shape[1])[None, :]
    sign = (ids == mine[:, None]).astype(jnp.float32) - (ids == others[:, None]).astype(jnp.float32)
    gate = jax.nn.sigmoid(jnp.sum(logits * sign, axis=1, keepdims=True))
    return gate * summed.reshape(count, width), table


def spread_rows(table, rows):
    high = rows.astype(jnp.bfloat16)
    rest = rows - high.astype(jnp.float32)
    middle = rest.astype(jnp.bfloat16)
    low = (rest - middle.astype(jnp.float32)).astype(jnp.bfloat16)
    picks = jnp.concatenate([table.T.astype(jnp.bfloat16)] * 3, axis=1)
    return dot(picks, jnp.concatenate([high, middle, low], axis=0))


def pairs_of(refs):
    return [tuple(range(low, min(low + 2, len(refs)))) for low in range(0, len(refs), 2)]


def joined(parts, axis):
    return parts[0] if len(parts) == 1 else jnp.concatenate(parts, axis=axis)


def project_kernel(count, order, memory, target, *refs):
    blocks, (kv, q) = refs[:count], refs[-2:]
    add_blocks(order, memory, target, blocks, kv, q, True)


def add_blocks(order, memory, target, blocks, kv, q, fresh):
    rows = blocks[0].shape[0]
    half = q.shape[1]

    def columns(ref, members):
        return joined(
            [ref[:, pl.ds(pl.multiple_of(order[i] * rows, 128), rows)] for i in members], 1
        )

    for step, members in enumerate(pairs_of(blocks)):
        weights = joined([blocks[i][:, : 3 * half] for i in members], 0)
        kv_part = dot(columns(memory, members), weights[:, : 2 * half])
        q_part = dot(columns(target, members), weights[:, 2 * half :])
        if fresh and step == 0:
            kv[...] = kv_part
            q[...] = q_part
        else:
            kv[...] += kv_part
            q[...] += q_part


def attend_kernel(
    early, late, late_order, order, seg_q, seg_k, memory, target, kv_sum, q_sum, *refs
):
    blocks = refs[: early + late]
    own, sent, kv, q, context = refs[early + late :]
    half = q.shape[1]
    rows = blocks[0].shape[0]
    kv[...] = kv_sum[...]
    q[...] = q_sum[...]
    if late:
        add_blocks(late_order, memory, target, blocks[early:], kv, q, False)
    allowed = seg_q[...] == seg_k[...]
    for low in range(0, half, HD):
        query = q[:, low : low + HD].astype(jnp.bfloat16)
        keys = kv[:, low : low + HD].astype(jnp.bfloat16)
        values = kv[:, half + low : half + low + HD].astype(jnp.bfloat16)
        scores = jnp.where(allowed, dot_rows(query, keys) * HD ** (-0.5), -1e30)
        expd = jnp.exp(scores - jnp.max(scores, axis=-1, keepdims=True))
        prob = (expd / jnp.sum(expd, axis=-1, keepdims=True)).astype(jnp.bfloat16)
        context[:, low : low + HD] = dot(prob, values).astype(jnp.bfloat16)
    for members in pairs_of(blocks):
        part = dot_rows(context[...], joined([blocks[i][:, 3 * half :] for i in members], 0))
        for place, i in enumerate(members):
            columns = pl.ds(pl.multiple_of(order[i] * rows, 128), rows)
            value = part[:, place * rows : (place + 1) * rows]
            own[:, columns] = value
            sent[:, columns] = value.astype(jnp.bfloat16)


def project(order, memory, target, blocks):
    half = blocks[0].shape[1] // 4
    return local(
        functools.partial(project_kernel, len(blocks)),
        "project",
        [((memory.shape[0], 2 * half), jnp.float32), ((target.shape[0], half), jnp.float32)],
        (memory, target, *blocks),
        order=order,
    )


def attend(order, seg_q, seg_k, memory, target, sums, early, late):
    half = early[0].shape[1] // 4
    count, width = target.shape
    late_order = order[len(early) :] if late else order
    return pl.pallas_call(
        functools.partial(attend_kernel, len(early), len(late)),
        out_shape=[
            jax.ShapeDtypeStruct((count, width), jnp.float32),
            jax.ShapeDtypeStruct((count, width), jnp.bfloat16),
        ],
        in_specs=specs(2, 6 + len(early) + len(late)),
        out_specs=[pl.BlockSpec(memory_space=pltpu.VMEM)] * 2,
        scratch_shapes=[
            pltpu.VMEM((memory.shape[0], 2 * half), jnp.float32),
            pltpu.VMEM((count, half), jnp.float32),
            pltpu.VMEM((count, half), jnp.bfloat16),
        ],
        compiler_params=pltpu.CompilerParams(vmem_limit_bytes=16 * MIB),
        name="attend",
    )(late_order, order, seg_q[:, None], seg_k[None, :], memory, target, *sums, *early, *late)


def exchanged(rows, groups):
    parts = rows.reshape(len(groups[0]), -1, rows.shape[1])
    return lax.all_to_all(
        parts, "ep", split_axis=0, concat_axis=0, tiled=True, axis_index_groups=groups
    ).reshape(rows.shape)


def by_hand(part, hidden, norm_gain, final_gain, router, w_in, w_out, routes, slots):
    depth, high, wide = chips()
    across = high * wide
    experts = lax.axis_size("ep") // SPLIT
    rows, width = hidden.shape
    z, y, x = place_of(lax.axis_index("ep"))
    place = places(routes, slots)
    held = [level // (depth // experts) for level in range(depth)]
    columns = [[level * across + i for level in range(depth)] for i in range(across)]
    planes = [[level * across + i for i in range(across)] for level in range(depth)]
    line = (depth * PAD, width)
    sheet = (across * depth * PAD, width)

    z1, x0, y0 = moved(part, dz=1), moved(part, dx=1), moved(part, dy=1)
    gate, send = local(
        functools.partial(pack_kernel, held),
        "pack",
        [((experts * PAD, 1), jnp.float32), (line, jnp.bfloat16)],
        (place[None, :], jnp.sum(routes, axis=1)[None, :], hidden, norm_gain[None, :], router),
    )
    column = exchanged(send, columns)

    column, z1, y0 = local(
        copies_kernel, "copies", [(sheet, jnp.bfloat16)], (column,), (x0,), (z1, y0)
    )
    z2, far0, y1 = moved(z1, dz=1), moved(y0, dx=1), moved(z1, dy=1)
    plane = exchanged(column, planes)

    pieces, z1, z2, far0 = local(
        mlp_kernel, "mlp", [(sheet, jnp.bfloat16)], (plane, w_in, w_out), (y1,), (z1, z2, far0)
    )
    z3, x1, y2 = moved(z2, dz=1), moved(z1, dx=1), moved(z2, dy=1)
    back = exchanged(pieces, planes)

    parts, z2, z3, far0 = local(
        sum_kernel, "sum", [(line, jnp.float32)], (back,), (x1, y2), (z2, z3, far0)
    )
    far1, x2, y3 = moved(far0, dz=1), moved(z2, dx=1), moved(z3, dy=1)
    parts = exchanged(parts, columns)

    mixed, normed, z3, far0, x2 = local(
        functools.partial(norm_kernel, held),
        "norm",
        [((rows, width), jnp.float32), ((rows, width), jnp.bfloat16)],
        (place[:, None], gate, hidden, final_gain[None, :], parts),
        (far1, y3),
        (z3, far0, x2),
    )
    far3, x3, far2 = moved(far0, dz=-1), moved(z3, dx=1), moved(x2, dy=1)
    early = {
        (0, 0, 0): part, (1, 0, 0): z1, (2, 0, 0): z2, (3, 0, 0): z3,
        (0, 0, 1): x0, (1, 0, 1): x1, (0, 1, 0): y0, (1, 1, 0): y1,
        (2, 1, 0): y2, (3, 1, 0): y3, (0, 1, 1): far0, (1, 1, 1): far1, (2, 0, 1): x2,
    }
    late = {(3, 0, 1): x3, (3, 1, 1): far3, (2, 1, 1): far2}
    order = jnp.stack([index_of(z - dz, y ^ dy, x ^ dx) for dz, dy, dx in (*early, *late)])
    return mixed, normed, order, list(early.values()), list(late.values())


def body(
    hidden,
    norm_gain,
    final_gain,
    router,
    w_in,
    w_out,
    expert_ids,
    slot_ids,
    src_len,
    tgt_len,
    wq,
    wk,
    wv,
    wo,
):
    group = lax.axis_index("grp")
    encoder = group == 0
    rows_here, width = hidden.shape[1:]
    half = wq.shape[1] // lax.axis_size("grp")
    targets = min(rows_here, -(-TGT_TOTAL // 16) * 16)

    part = jnp.concatenate(
        [lax.dynamic_slice_in_dim(weight, group * half, half, 1) for weight in (wk, wv, wq, wo)], axis=1
    )
    if chips() is None:
        early = [lax.all_gather(part, "ep", axis=0, tiled=True)]
        late = []
        order = jnp.zeros((1,), jnp.int32)
        added, table = expert_rows(
            hidden[0], norm_gain[0], router[0], w_in[0], w_out[0], expert_ids[0], slot_ids[0]
        )
        mixed = hidden[0].astype(jnp.float32) + spread_rows(table, added)
        normed_out = normalize(mixed, final_gain[0]).astype(jnp.bfloat16)
    else:
        mixed, normed_out, order, early, late = by_hand(
            part, hidden[0], norm_gain[0], final_gain[0], router[0], w_in[0], w_out[0],
            expert_ids[0], slot_ids[0],
        )
    other = lax.ppermute(normed_out, "grp", [(0, 1), (1, 0)])
    memory = jnp.where(encoder, normed_out, other)
    target = jnp.where(encoder, other[:targets], normed_out[:targets])

    seg_q = positions(tgt_len[0], targets)
    seg_k = positions(src_len[0], rows_here)
    valid = (seg_q < SENT)[:, None]
    sums = project(order, memory, target, early)
    own, sent = attend(order, seg_q, seg_k, memory, target, sums, early, late)
    total = own + lax.ppermute(sent, "grp", [(0, 1)]).astype(jnp.float32)
    attended = jnp.pad(jnp.where(valid, total, 0.0), ((0, rows_here - targets), (0, 0)))
    decoded = (mixed + attended).astype(jnp.bfloat16)
    return jnp.where(encoder, normed_out, decoded)[None]


def solution(mesh):
    in_specs = (
        P("grp", "ep", None),
        P("grp", None),
        P("grp", None),
        P("grp", None, None),
        P("grp", None, "ep"),
        P("grp", "ep", None),
        P("grp", "ep", None),
        P("grp", "ep", None),
        P("ep", None),
        P("ep", None),
        P("ep", None),
        P("ep", None),
        P("ep", None),
        P("ep", None),
    )
    out_specs = P("grp", "ep", None)
    return jax.shard_map(body, mesh=mesh, in_specs=in_specs, out_specs=out_specs, check_vma=False)
```

time: 345 us -> 123 us (0.36)
  waiting for transfers between devices: 268 us -> 23.1 us
  blocking collectives: 0 us -> 47.8 us
  matrix products: 28.1 us -> 0 us
  between operations: 13.4 us -> 0.41 us
  Pallas kernels: 0 us -> 8.69 us
  starting transfers between devices: 14.4 us -> 21.9 us
  local copies, waits for them, and re-layouts: 11.2 us -> 15.4 us
    all_gather x4 -> x0, waiting for transfers between devices: 231 us -> none  [the longest x1 73.7 us: body(): lax.all_gather(wq, 'ep', axis=0, tiled=True)]
    all_to_all x0 -> x3, blocking collectives: none -> 47.8 us  [exchanged(): lax.all_to_all(parts, 'ep', split_axis=0, concat_axis=0, tiled=True, axis...]
    dot_general x8 -> x0, matrix products: 24.9 us -> none  [the longest x1 4.94 us: body(): jnp.dot(inner, w_out[0], preferred_element_type=jnp.float32)]
    all_to_all x2 -> x1, waiting for transfers between devices: 32.1 us -> 13.2 us  [exchanged(): lax.all_to_all(parts, 'ep', split_axis=0, concat_axis=0, tiled=True, axis...]
    ppermute x1 -> x17, starting transfers between devices: 1.46 us -> 17.3 us  [the longest x15 14.5 us: moved(): return lax.ppermute(value, 'ep', pairs)]
    unnamed x16 -> x68, local copies, waits for them, and re-layouts: 1.27 us -> 12.9 us
    pallas_call x0 -> x7, Pallas kernels: none -> 8.69 us  [the longest x6 5.61 us: local(): pl.pallas_call(run, out_shape=[jax.ShapeDtypeStruct(shape, dtype) for sha...]
    all_to_all x2 -> x1, starting transfers between devices: 12.8 us -> 4.67 us  [exchanged(): lax.all_to_all(parts, 'ep', split_axis=0, concat_axis=0, tiled=True, axis...]
  transfers between devices with their start and end apart: 7 -> 18, of which waited for: 7 -> 5; matrix products, arithmetic and copies ran while one was open for 12% -> 3% of each run, Pallas kernels for 0% -> 3%
where the time goes in v1:
time: 123 us; the launch traced here: 122 us
  blocking collectives  47.8 us (39%)
  waiting for transfers between devices  23.1 us (19%)
  starting transfers between devices  21.9 us (18%)
  local copies, waits for them, and re-layouts  15.4 us (13%)
  Pallas kernels  8.69 us (7%)
  other arithmetic  4.87 us (4%)
    all_to_all x3, blocking collectives, exchanged(): lax.all_to_all(parts, 'ep', split_axis=0, concat_axis=0, tiled=True, axis...  47.8 us
    ppermute x15, starting transfers between devices, moved(): return lax.ppermute(value, 'ep', pairs)  14.5 us
    all_to_all x1, waiting for transfers between devices, exchanged(): lax.all_to_all(parts, 'ep', split_axis=0, concat_axis=0, tiled=True, axis...  13.2 us
    unnamed x68, local copies, waits for them, and re-layouts  12.9 us
    ppermute x15, waiting for transfers between devices, moved(): return lax.ppermute(value, 'ep', pairs)  6.85 us
    pallas_call x6, Pallas kernels, local(): pl.pallas_call(run, out_shape=[jax.ShapeDtypeStruct(shape, dtype) for sha...  5.61 us
    all_to_all x1, starting transfers between devices, exchanged(): lax.all_to_all(parts, 'ep', split_axis=0, concat_axis=0, tiled=True, axis...  4.67 us
    pallas_call x1, Pallas kernels, attend(): pl.pallas_call(functools.partial(attend_kernel, len(early), len(late)), o...  3.08 us
  transfers between devices with their start and end apart: 18, of which 5 were waited for; matrix products, arithmetic and copies ran while one was open for 3% of the time, Pallas kernels for 3%

profile of v1, /device:TPU:1, one launch (start us, length us, event | category | flops | bytes accessed | tf_op | source)
XLA Modules:
  0.0 122.2 jit_solution(16495810742866443140)
XLA Ops:
  0.0 1.1 constant_dynamic-slice_fusion
  1.1 1.0 constant_dynamic-slice_fusion.2
  2.2 2.1 %collective-permute-start.2 = (bf16[128,2048]{1,0:T(8,128)(2,1)S(1)}, bf16[128,2048]{1,0:T(8,128)(2,1)S(1)}, u32[]{:S(2)}, u32[]{:S(2)}) collective-permute-start(bf16[128,2048]{1,0:T(8,128)(2,1)S(1)} %pad_maximum_fusion.refs_3_.refs_0_), channel_id=1, source_target_pairs={{0,2},{1,3},{2,0},{3,1},{4,6},{5,7},{6,4},{7,5},{8,10},{9,11},{10,... | collective-permute-start | bytes 1572872 | tf_op jit(solution)/shard_map/ppermute | solution.py:62
  4.3 1.3 %collective-permute-start.1 = (bf16[128,2048]{1,0:T(8,128)(2,1)S(1)}, bf16[128,2048]{1,0:T(8,128)(2,1)S(1)}, u32[]{:S(2)}, u32[]{:S(2)}) collective-permute-start(bf16[128,2048]{1,0:T(8,128)(2,1)S(1)} %pad_maximum_fusion.refs_3_.refs_0_), channel_id=1, source_target_pairs={{0,4},{1,5},{2,6},{3,7},{4,8},{5,9},{6,10},{7,11},{8,12},{9,13},{1... | collective-permute-start | bytes 1572872 | tf_op jit(solution)/shard_map/ppermute | solution.py:62
  5.6 1.2 collective-permute-start
  6.9 0.7 pack.1
  7.6 15.2 %all_to_all.20 = bf16[4,8,2048]{2,1,0:T(8,128)(2,1)S(1)} all-to-all(bf16[4,8,2048]{2,1,0:T(8,128)(2,1)S(1)} %bitcast.49), channel_id=1, replica_groups={{0,4,8,12},{1,5,9,13},{2,6,10,14},{3,7,11,15},{16,20,24,28},{17,21,25,2..., dimensions={0} | all-to-all | bytes 262144 | tf_op jit(solution)/shard_map/all_to_all | solution.py:285
  23.0 0.3 collective-permute-start.3
  23.3 1.2 collective-permute-start.5
  24.5 17.1 %all_to_all.21 = bf16[4,32,2048]{2,1,0:T(8,128)(2,1)S(1)} all-to-all(bf16[4,32,2048]{2,1,0:T(8,128)(2,1)S(1)} %bitcast.46), channel_id=1, replica_groups={{0,1,2,3},{4,5,6,7},{8,9,10,11},{12,13,14,15},{16,17,18,19},{20,21,22,2..., dimensions={0} | all-to-all | bytes 1048576 | tf_op jit(solution)/shard_map/all_to_all | solution.py:285
  41.7 2.4 %copy-done.19 = bf16[1,1024,2048]{2,1,0:T(8,128)(2,1)S(1)} copy-done((bf16[1,1024,2048]{2,1,0:T(8,128)(2,1)S(1)}, bf16[1,1024,2048]{2,1,0:T(8,128)(2,1)}, u32[]{:S(2)}) %copy-start.19) | copy-done | bytes 4194328
  44.0 1.3 %mlp.1 = (bf16[128,2048]{1,0:T(8,128)(2,1)S(1)}, bf16[128,2048]{1,0:T(8,128)(2,1)S(1)}, bf16[128,2048]{1,0:T(8,128)(2,1)S(1)}, bf16[128,2048]{1,0:T(8,128)(2,1)S(1)}) custom-call(bf16[128,2048]{1,0:T(8,128)(2,1)S(1)} %bitcast.42, bf16[2048,1024]{1,0:T(8,128)(2,1)S(1)} %bitcast.37, ...), custom_call_target="tpu_custom_call", output_to_operand_aliasing={{1}: (4, {}), {2}: (5, {}), {3}: (6, {})} | custom-call | tf_op jit(solution)/shard_map/mlp/pallas_call | solution.py:81
  45.3 2.0 %collective-permute-start.6 = (bf16[128,2048]{1,0:T(8,128)(2,1)S(1)}, bf16[128,2048]{1,0:T(8,128)(2,1)S(1)}, u32[]{:S(2)}, u32[]{:S(2)}) collective-permute-start(bf16[128,2048]{1,0:T(8,128)(2,1)S(1)} %get-tuple-element.33.refs_4_.refs_1_), channel_id=1, source_target_pairs={{0,1},{1,0},{2,3},{3,2},{4,5},{5,4},{6,7},{7,6},{8,9},{9,8},{10,11... | collective-permute-start | bytes 1572872 | tf_op jit(solution)/shard_map/ppermute | solution.py:62
  47.3 0.2 collective-permute-start.7
  47.5 15.5 %all_to_all.22 = bf16[4,32,2048]{2,1,0:T(8,128)(2,1)S(1)} all-to-all(bf16[4,32,2048]{2,1,0:T(8,128)(2,1)S(1)} %bitcast.45), channel_id=1, replica_groups={{0,1,2,3},{4,5,6,7},{8,9,10,11},{12,13,14,15},{16,17,18,19},{20,21,22,2..., dimensions={0} | all-to-all | bytes 1048576 | tf_op jit(solution)/shard_map/all_to_all | solution.py:285
  63.1 0.7 copy-done.6
  63.9 0.2 copy-done.8
  64.0 0.7 copy-done.25
  64.7 1.0 collective-permute-start.10
  65.7 1.3 %collective-permute-start.11 = (bf16[128,2048]{1,0:T(8,128)(2,1)S(1)}, bf16[128,2048]{1,0:T(8,128)(2,1)}, u32[]{:S(2)}, u32[]{:S(2)}) collective-permute-start(bf16[128,2048]{1,0:T(8,128)(2,1)S(1)} %get-tuple-element.39.refs_5_.refs_2_), channel_id=1, source_target_pairs={{0,1},{1,0},{2,3},{3,2},{4,5},{5,4},{6,7},{7,6},{8,9},{9,8},{10,11... | collective-permute-start | bytes 1572872 | tf_op jit(solution)/shard_map/ppermute | solution.py:62
  67.0 4.7 %all-to-all-start.3 = ((f32[4,8,2048]{2,1,0:T(8,128)}), f32[4,8,2048]{2,1,0:T(8,128)S(1)}, u32[]{:S(2)}, u32[]{:S(2)}) async-start(f32[4,8,2048]{2,1,0:T(8,128)} %bitcast.48), calls=%async_computation.3 | async-start | bytes 524288 | tf_op jit(solution)/shard_map/all_to_all | solution.py:285
  71.8 13.2 %all-to-all-done.3 = f32[4,8,2048]{2,1,0:T(8,128)S(1)} async-done(((f32[4,8,2048]{2,1,0:T(8,128)}), f32[4,8,2048]{2,1,0:T(8,128)S(1)}, u32[]{:S(2)}, u32[]{:S(2)}) %all-to-all-start.3) | async-done | bytes 262176 | tf_op jit(solution)/shard_map/all_to_all | solution.py:285
  85.0 0.8 copy-done.10
  85.8 0.8 copy-done.13
  86.6 1.0 copy-done.11
  87.6 1.0 copy-done.14
  88.7 1.2 %copy-done.21 = bf16[1,256,2048]{2,1,0:T(8,128)(2,1)S(1)} copy-done((bf16[1,256,2048]{2,1,0:T(8,128)(2,1)S(1)}, bf16[1,256,2048]{2,1,0:T(8,128)(2,1)}, u32[]{:S(2)}) %copy-start.21) | copy-done | bytes 1048600
  89.9 0.7 copy-done.29
  90.6 1.0 norm.1
  91.6 1.3 %copy-done.22 = f32[256,2048]{1,0:T(8,128)} copy-done((f32[256,2048]{1,0:T(8,128)}, f32[256,2048]{1,0:T(8,128)S(1)}, u32[]{:S(2)}) %copy-start.22) | copy-done | bytes 2097176
  92.9 1.5 %collective-permute-start.12 = (bf16[256,2048]{1,0:T(8,128)(2,1)S(1)}, bf16[256,2048]{1,0:T(8,128)(2,1)}, u32[]{:S(2)}, u32[]{:S(2)}) collective-permute-start(bf16[256,2048]{1,0:T(8,128)(2,1)S(1)} %get-tuple-element.40), channel_id=1, source_target_pairs={{0,16},{16,0},{1,17},{17,1},{2,18},{18,2},{3,19},{19,3},{4,20},{20... | collective-permute-start | bytes 3145736 | tf_op jit(solution)/shard_map/ppermute | solution.py:388
  95.1 1.0 collective-permute-start.13
  96.1 2.5 %collective-permute-start.14 = (bf16[128,2048]{1,0:T(8,128)(2,1)S(1)}, bf16[128,2048]{1,0:T(8,128)(2,1)S(1)}, u32[]{:S(2)}, u32[]{:S(2)}) collective-permute-start(bf16[128,2048]{1,0:T(8,128)(2,1)S(1)} %get-tuple-element.43.refs_13_.refs_10_), channel_id=1, source_target_pairs={{0,12},{1,13},{2,14},{3,15},{4,0},{5,1},{6,2},{7,3},{8,4},{9,5},{1... | collective-permute-start | bytes 1572872 | tf_op jit(solution)/shard_map/ppermute | solution.py:62
  98.6 0.3 collective-permute-start.15
  98.9 1.3 %slice_select_fusion.refs_2_.target = bf16[176,2048]{1,0:T(8,128)(2,1)S(1)} fusion(bf16[256,2048]{1,0:T(8,128)(2,1)} %collective-permute-done.12, bf16[256,2048]{1,0:T(8,128)(2,1)S(1)} %get-tuple-element.40, pred[]{:T(512)S(6)} %eq.22), kind=kLoop, calls=%fused_computation.5 | loop fusion | flops 360448 | bytes 2162689 | tf_op jit(solution)/shard_map/jit(_where)/select_n | solution.py:390
  100.3 1.5 %broadcast_select_fusion.refs_1_.memory = bf16[256,2048]{1,0:T(8,128)(2,1)S(1)} fusion(bf16[256,2048]{1,0:T(8,128)(2,1)S(1)} %get-tuple-element.40, bf16[256,2048]{1,0:T(8,128)(2,1)} %collective-permute-done.12, pred[]{:T(512)S(6)} %eq.22), kind=kLoop, calls=%fused_computation.4 | loop fusion | flops 524288 | bytes 3145729 | tf_op jit(solution)/shard_map/jit(_where)/select_n | solution.py:389
  102.1 0.2 copy-done.9
  102.2 0.2 copy-done.12
  102.4 2.5 %project.1 = (f32[256,1024]{1,0:T(8,128)S(1)}, f32[176,512]{1,0:T(8,128)S(1)}) custom-call(s32[16]{0:T(128)S(1)} %stack.70.refs_0_.order, bf16[256,2048]{1,0:T(8,128)(2,1)S(1)} %broadcast_select_fusion.refs_1_.memory, bf16[176,2048]{1,0:T(8,128)(2,1)S(1)} %slice_select_fusion.refs_2_.target, bf16[128,2048]{1,0:T(8,128)(2,1)S(1)} %copy-done.1, ...), custom_call_target="tpu_custom_call" | custom-call | tf_op jit(solution)/shard_map/project/pallas_call | solution.py:81
  104.9 3.7 %collective-permute-done.13.refs_13_ = bf16[128,2048]{1,0:T(8,128)(2,1)S(1)} collective-permute-done((bf16[128,2048]{1,0:T(8,128)(2,1)S(1)}, bf16[128,2048]{1,0:T(8,128)(2,1)S(1)}, u32[]{:S(2)}, u32[]{:S(2)}) %collective-permute-start.13) | collective-permute-done | bytes 524320 | tf_op jit(solution)/shard_map/ppermute | solution.py:62
  108.7 1.0 collective-permute-done.14.refs_14_
  109.7 2.1 %collective-permute-done.15.refs_15_ = bf16[128,2048]{1,0:T(8,128)(2,1)S(1)} collective-permute-done((bf16[128,2048]{1,0:T(8,128)(2,1)}, bf16[128,2048]{1,0:T(8,128)(2,1)S(1)}, u32[]{:S(2)}, u32[]{:S(2)}) %collective-permute-start.15) | collective-permute-done | bytes 524320 | tf_op jit(solution)/shard_map/ppermute | solution.py:62
  111.8 3.1 %attend.1 = (f32[176,2048]{1,0:T(8,128)S(1)}, bf16[176,2048]{1,0:T(8,128)(2,1)S(1)}) custom-call(s32[3]{0:T(128)S(1)} %pad_add_fusion.late_order, s32[16]{0:T(128)S(1)} %stack.70.refs_0_.order, s32[176,1]{1,0:T(8,128)S(1)} %copy.29.seg_q, s32[1,256]{1,0:T(1,128)S(1)} %bitcast.53, bf16[256,2048]{1,0:T(8,128)(2,1)S(1)} %broadcast_select_fusion.refs_1_.memory, ...), custom_call_target="tpu_custom_call" | custom-call | tf_op jit(solution)/shard_map/attend/pallas_call | solution.py:265
  114.8 1.3 %collective-permute-start.16 = (bf16[176,2048]{1,0:T(8,128)(2,1)S(1)}, bf16[176,2048]{1,0:T(8,128)(2,1)S(1)}, u32[]{:S(2)}, u32[]{:S(2)}) collective-permute-start(bf16[176,2048]{1,0:T(8,128)(2,1)S(1)} %get-tuple-element.48), channel_id=1, source_target_pairs={{0,16},{1,17},{2,18},{3,19},{4,20},{5,21},{6,22},{7,23},{8,24},{9,... | collective-permute-start | bytes 2162696 | tf_op jit(solution)/shard_map/ppermute | solution.py:397
  116.2 3.1 %collective-permute-done.16 = bf16[176,2048]{1,0:T(8,128)(2,1)S(1)} collective-permute-done((bf16[176,2048]{1,0:T(8,128)(2,1)S(1)}, bf16[176,2048]{1,0:T(8,128)(2,1)S(1)}, u32[]{:S(2)}, u32[]{:S(2)}) %collective-permute-start.16) | collective-permute-done | bytes 720928 | tf_op jit(solution)/shard_map/ppermute | solution.py:397
  119.2 0.2 add_select_fusion
  119.4 1.4 %copy-done.23 = f32[256,2048]{1,0:T(8,128)S(1)} copy-done((f32[256,2048]{1,0:T(8,128)S(1)}, f32[256,2048]{1,0:T(8,128)}, u32[]{:S(2)}) %copy-start.23) | copy-done | bytes 2097176
  120.8 1.4 %fusion.1 = bf16[1,256,2048]{2,1,0:T(8,128)(2,1)} fusion(bf16[256,2048]{1,0:T(8,128)(2,1)S(1)} %get-tuple-element.40, f32[256,2048]{1,0:T(8,128)S(1)} %copy-done.23, f32[176,2048]{1,0:T(8,128)S(1)} %add_select_fusion, pred[]{:T(512)S(6)} %eq.22), kind=kLoop, calls=%fused_computation.3 | loop fusion | flops 1572864 | bytes 5636097 | tf_op jit(solution)/shard_map/broadcast_in_dim | solution.py:400
  (83 shorter events, 1.4 us)
Async XLA Ops:
  0.0 6.9 %copy-start.31 = (s32[1,256,2]{1,2,0:T(2,128)S(1)}, s32[1,256,2]{1,2,0:T(2,128)}, u32[]{:S(2)}) copy-start(s32[1,256,2]{1,2,0:T(2,128)} %param.21) | copy-start | bytes 6148
  0.0 6.9 %copy-start.30 = (s32[1,256,2]{1,2,0:T(2,128)S(1)}, s32[1,256,2]{1,2,0:T(2,128)}, u32[]{:S(2)}) copy-start(s32[1,256,2]{1,2,0:T(2,128)} %param.20) | copy-start | bytes 6148
  0.0 6.9 %copy-start.24 = (bf16[1,2048,128]{2,1,0:T(8,128)(2,1)S(1)}, bf16[1,2048,128]{2,1,0:T(8,128)(2,1)}, u32[]{:S(2)}) copy-start(bf16[1,2048,128]{2,1,0:T(8,128)(2,1)} %param.17) | copy-start | bytes 1572868
  0.0 6.9 %copy-start.26 = (f32[1,2048]{1,0:T(1,128)S(1)}, f32[1,2048]{1,0:T(1,128)}, u32[]{:S(2)}) copy-start(f32[1,2048]{1,0:T(1,128)} %refs_3_.2) | copy-start | bytes 24580
  0.0 6.9 %copy-start.20 = (bf16[1,256,2048]{2,1,0:T(8,128)(2,1)S(1)}, bf16[1,256,2048]{2,1,0:T(8,128)(2,1)}, u32[]{:S(2)}) copy-start(bf16[1,256,2048]{2,1,0:T(8,128)(2,1)} %param.14) | copy-start | bytes 3145732
  2.2 20.7 %copy-start = (bf16[128,2048]{1,0:T(8,128)(2,1)}, bf16[128,2048]{1,0:T(8,128)(2,1)S(1)}, u32[]{:S(2)}) copy-start(bf16[128,2048]{1,0:T(8,128)(2,1)S(1)} %pad_maximum_fusion.refs_3_.refs_0_) | copy-start | bytes 1572868
  2.2 20.7 %collective-permute-start.2 = (bf16[128,2048]{1,0:T(8,128)(2,1)S(1)}, bf16[128,2048]{1,0:T(8,128)(2,1)S(1)}, u32[]{:S(2)}, u32[]{:S(2)}) collective-permute-start(bf16[128,2048]{1,0:T(8,128)(2,1)S(1)} %pad_maximum_fusion.refs_3_.refs_0_), channel_id=1, source_target_pairs={{0,2},{1,3},{2,0},{3,1},{4,6},{5,7},{6,4},{7,5},{8,10},{9,11},{10,... | collective-permute-start | bytes 1572872 | tf_op jit(solution)/shard_map/ppermute | solution.py:62
  4.3 18.5 %collective-permute-start.1 = (bf16[128,2048]{1,0:T(8,128)(2,1)S(1)}, bf16[128,2048]{1,0:T(8,128)(2,1)S(1)}, u32[]{:S(2)}, u32[]{:S(2)}) collective-permute-start(bf16[128,2048]{1,0:T(8,128)(2,1)S(1)} %pad_maximum_fusion.refs_3_.refs_0_), channel_id=1, source_target_pairs={{0,4},{1,5},{2,6},{3,7},{4,8},{5,9},{6,10},{7,11},{8,12},{9,13},{1... | collective-permute-start | bytes 1572872 | tf_op jit(solution)/shard_map/ppermute | solution.py:62
  5.6 17.2 %collective-permute-start = (bf16[128,2048]{1,0:T(8,128)(2,1)S(1)}, bf16[128,2048]{1,0:T(8,128)(2,1)S(1)}, u32[]{:S(2)}, u32[]{:S(2)}) collective-permute-start(bf16[128,2048]{1,0:T(8,128)(2,1)S(1)} %pad_maximum_fusion.refs_3_.refs_0_), channel_id=1, source_target_pairs={{0,1},{1,0},{2,3},{3,2},{4,5},{5,4},{6,7},{7,6},{8,9},{9,8},{10,11... | collective-permute-start | bytes 1572872 | tf_op jit(solution)/shard_map/ppermute | solution.py:62
  6.9 34.7 %copy-start.18 = (bf16[1,2048,1024]{2,1,0:T(8,128)(2,1)S(1)}, bf16[1,2048,1024]{2,1,0:T(8,128)(2,1)}, u32[]{:S(2)}) copy-start(bf16[1,2048,1024]{2,1,0:T(8,128)(2,1)} %param.18) | copy-start | bytes 12582916
  7.6 16.9 %copy-start.28 = (f32[16,1]{1,0:T(8,128)}, f32[16,1]{1,0:T(8,128)S(1)}, u32[]{:S(2)}) copy-start(f32[16,1]{1,0:T(8,128)S(1)} %get-tuple-element.27.refs_1_) | copy-start | bytes 196
  22.9 18.7 %copy-start.2 = (bf16[128,2048]{1,0:T(8,128)(2,1)}, bf16[128,2048]{1,0:T(8,128)(2,1)S(1)}, u32[]{:S(2)}) copy-start(bf16[128,2048]{1,0:T(8,128)(2,1)S(1)} %collective-permute-done.refs_1_.refs_7_.refs_4_) | copy-start | bytes 1572868
  22.9 22.4 %copy-start.4 = (bf16[128,2048]{1,0:T(8,128)(2,1)}, bf16[128,2048]{1,0:T(8,128)(2,1)S(1)}, u32[]{:S(2)}) copy-start(bf16[128,2048]{1,0:T(8,128)(2,1)S(1)} %get-tuple-element.31.refs_9_.refs_6_) | copy-start | bytes 1572868
  22.9 18.7 %collective-permute-start.4 = (bf16[128,2048]{1,0:T(8,128)(2,1)S(1)}, bf16[128,2048]{1,0:T(8,128)(2,1)S(1)}, u32[]{:S(2)}, u32[]{:S(2)}) collective-permute-start(bf16[128,2048]{1,0:T(8,128)(2,1)S(1)} %get-tuple-element.30.refs_4_), channel_id=1, source_target_pairs={{0,4},{1,5},{2,6},{3,7},{4,8},{5,9},{6,10},{7,11},{8,12},{9,13},{1... | collective-permute-start | bytes 1572872 | tf_op jit(solution)/shard_map/ppermute | solution.py:62
  23.0 18.6 %collective-permute-start.3 = (bf16[128,2048]{1,0:T(8,128)(2,1)S(1)}, bf16[128,2048]{1,0:T(8,128)(2,1)S(1)}, u32[]{:S(2)}, u32[]{:S(2)}) collective-permute-start(bf16[128,2048]{1,0:T(8,128)(2,1)S(1)} %get-tuple-element.30.refs_4_), channel_id=1, source_target_pairs={{0,2},{1,3},{2,0},{3,1},{4,6},{5,7},{6,4},{7,5},{8,10},{9,11},{10,... | collective-permute-start | bytes 1572872 | tf_op jit(solution)/shard_map/ppermute | solution.py:62
  23.3 18.3 %collective-permute-start.5 = (bf16[128,2048]{1,0:T(8,128)(2,1)S(1)}, bf16[128,2048]{1,0:T(8,128)(2,1)S(1)}, u32[]{:S(2)}, u32[]{:S(2)}) collective-permute-start(bf16[128,2048]{1,0:T(8,128)(2,1)S(1)} %get-tuple-element.31.refs_9_.refs_6_), channel_id=1, source_target_pairs={{0,1},{1,0},{2,3},{3,2},{4,5},{5,4},{6,7},{7,6},{8,9},{9,8},{10,11... | collective-permute-start | bytes 1572872 | tf_op jit(solution)/shard_map/ppermute | solution.py:62
  41.6 3.7 %copy-start.16 = (bf16[128,2048]{1,0:T(8,128)(2,1)}, bf16[128,2048]{1,0:T(8,128)(2,1)S(1)}, u32[]{:S(2)}) copy-start(bf16[128,2048]{1,0:T(8,128)(2,1)S(1)} %collective-permute-done.3.refs_3_.refs_10_.refs_7_) | copy-start | bytes 1572868
  41.6 2.4 %copy-start.19 = (bf16[1,1024,2048]{2,1,0:T(8,128)(2,1)S(1)}, bf16[1,1024,2048]{2,1,0:T(8,128)(2,1)}, u32[]{:S(2)}) copy-start(bf16[1,1024,2048]{2,1,0:T(8,128)(2,1)} %param.19) | copy-start | bytes 12582916
  45.3 17.7 %collective-permute-start.6 = (bf16[128,2048]{1,0:T(8,128)(2,1)S(1)}, bf16[128,2048]{1,0:T(8,128)(2,1)S(1)}, u32[]{:S(2)}, u32[]{:S(2)}) collective-permute-start(bf16[128,2048]{1,0:T(8,128)(2,1)S(1)} %get-tuple-element.33.refs_4_.refs_1_), channel_id=1, source_target_pairs={{0,1},{1,0},{2,3},{3,2},{4,5},{5,4},{6,7},{7,6},{8,9},{9,8},{10,11... | collective-permute-start | bytes 1572872 | tf_op jit(solution)/shard_map/ppermute | solution.py:62
  47.3 15.7 %collective-permute-start.8 = (bf16[128,2048]{1,0:T(8,128)(2,1)S(1)}, bf16[128,2048]{1,0:T(8,128)(2,1)S(1)}, u32[]{:S(2)}, u32[]{:S(2)}) collective-permute-start(bf16[128,2048]{1,0:T(8,128)(2,1)S(1)} %get-tuple-element.34.refs_3_), channel_id=1, source_target_pairs={{0,4},{1,5},{2,6},{3,7},{4,8},{5,9},{6,10},{7,11},{8,12},{9,13},{1... | collective-permute-start | bytes 1572872 | tf_op jit(solution)/shard_map/ppermute | solution.py:62
  47.3 15.7 %collective-permute-start.7 = (bf16[128,2048]{1,0:T(8,128)(2,1)S(1)}, bf16[128,2048]{1,0:T(8,128)(2,1)S(1)}, u32[]{:S(2)}, u32[]{:S(2)}) collective-permute-start(bf16[128,2048]{1,0:T(8,128)(2,1)S(1)} %get-tuple-element.34.refs_3_), channel_id=1, source_target_pairs={{0,2},{1,3},{2,0},{3,1},{4,6},{5,7},{6,4},{7,5},{8,10},{9,11},{10,... | collective-permute-start | bytes 1572872 | tf_op jit(solution)/shard_map/ppermute | solution.py:62
  63.0 0.8 copy-start.6
  63.1 1.0 copy-start.8
  63.1 23.5 %copy-start.27 = (f32[1,2048]{1,0:T(1,128)S(1)}, f32[1,2048]{1,0:T(1,128)}, u32[]{:S(2)}) copy-start(f32[1,2048]{1,0:T(1,128)} %refs_3_.3) | copy-start | bytes 24580
  64.7 20.3 %collective-permute-start.9 = (bf16[128,2048]{1,0:T(8,128)(2,1)S(1)}, bf16[128,2048]{1,0:T(8,128)(2,1)S(1)}, u32[]{:S(2)}, u32[]{:S(2)}) collective-permute-start(bf16[128,2048]{1,0:T(8,128)(2,1)S(1)} %get-tuple-element.37.refs_8_), channel_id=1, source_target_pairs={{0,4},{1,5},{2,6},{3,7},{4,8},{5,9},{6,10},{7,11},{8,12},{9,13},{1... | collective-permute-start | bytes 1572872 | tf_op jit(solution)/shard_map/ppermute | solution.py:62
  64.7 21.1 %collective-permute-start.10 = (bf16[128,2048]{1,0:T(8,128)(2,1)S(1)}, bf16[128,2048]{1,0:T(8,128)(2,1)S(1)}, u32[]{:S(2)}, u32[]{:S(2)}) collective-permute-start(bf16[128,2048]{1,0:T(8,128)(2,1)S(1)} %get-tuple-element.38.refs_7_), channel_id=1, source_target_pairs={{0,2},{1,3},{2,0},{3,1},{4,6},{5,7},{6,4},{7,5},{8,10},{9,11},{10,... | collective-permute-start | bytes 1572872 | tf_op jit(solution)/shard_map/ppermute | solution.py:62
  65.7 20.9 %collective-permute-start.11 = (bf16[128,2048]{1,0:T(8,128)(2,1)S(1)}, bf16[128,2048]{1,0:T(8,128)(2,1)}, u32[]{:S(2)}, u32[]{:S(2)}) collective-permute-start(bf16[128,2048]{1,0:T(8,128)(2,1)S(1)} %get-tuple-element.39.refs_5_.refs_2_), channel_id=1, source_target_pairs={{0,1},{1,0},{2,3},{3,2},{4,5},{5,4},{6,7},{7,6},{8,9},{9,8},{10,11... | collective-permute-start | bytes 1572872 | tf_op jit(solution)/shard_map/ppermute | solution.py:62
  67.0 18.0 %all-to-all-start.3 = ((f32[4,8,2048]{2,1,0:T(8,128)}), f32[4,8,2048]{2,1,0:T(8,128)S(1)}, u32[]{:S(2)}, u32[]{:S(2)}) async-start(f32[4,8,2048]{2,1,0:T(8,128)} %bitcast.48), calls=%async_computation.3 | async-start | bytes 524288 | tf_op jit(solution)/shard_map/all_to_all | solution.py:285
  86.6 1.0 copy-start.11
  87.6 1.0 copy-start.14
  88.7 1.2 %copy-start.21 = (bf16[1,256,2048]{2,1,0:T(8,128)(2,1)S(1)}, bf16[1,256,2048]{2,1,0:T(8,128)(2,1)}, u32[]{:S(2)}) copy-start(bf16[1,256,2048]{2,1,0:T(8,128)(2,1)} %param.14) | copy-start | bytes 3145732
  90.6 3.8 %copy-start.32 = (s32[1,4]{1,0:T(1,128)S(1)}, s32[1,4]{1,0:T(1,128)}, u32[]{:S(2)}) copy-start(s32[1,4]{1,0:T(1,128)} %param.23) | copy-start | bytes 52
  90.6 4.3 %copy-start.33 = (s32[1,4]{1,0:T(1,128)S(1)}, s32[1,4]{1,0:T(1,128)}, u32[]{:S(2)}) copy-start(s32[1,4]{1,0:T(1,128)} %param.22) | copy-start | bytes 52
  91.6 1.4 %copy-start.22 = (f32[256,2048]{1,0:T(8,128)}, f32[256,2048]{1,0:T(8,128)S(1)}, u32[]{:S(2)}) copy-start(f32[256,2048]{1,0:T(8,128)S(1)} %get-tuple-element.41) | copy-start | bytes 6291460
  92.9 6.0 %collective-permute-start.12 = (bf16[256,2048]{1,0:T(8,128)(2,1)S(1)}, bf16[256,2048]{1,0:T(8,128)(2,1)}, u32[]{:S(2)}, u32[]{:S(2)}) collective-permute-start(bf16[256,2048]{1,0:T(8,128)(2,1)S(1)} %get-tuple-element.40), channel_id=1, source_target_pairs={{0,16},{16,0},{1,17},{17,1},{2,18},{18,2},{3,19},{19,3},{4,20},{20... | collective-permute-start | bytes 3145736 | tf_op jit(solution)/shard_map/ppermute | solution.py:388
  95.1 13.6 %collective-permute-start.13 = (bf16[128,2048]{1,0:T(8,128)(2,1)S(1)}, bf16[128,2048]{1,0:T(8,128)(2,1)S(1)}, u32[]{:S(2)}, u32[]{:S(2)}) collective-permute-start(bf16[128,2048]{1,0:T(8,128)(2,1)S(1)} %get-tuple-element.42.refs_6_.refs_3_), channel_id=1, source_target_pairs={{0,1},{1,0},{2,3},{3,2},{4,5},{5,4},{6,7},{7,6},{8,9},{9,8},{10,11... | collective-permute-start | bytes 1572872 | tf_op jit(solution)/shard_map/ppermute | solution.py:62
  96.1 13.6 %collective-permute-start.14 = (bf16[128,2048]{1,0:T(8,128)(2,1)S(1)}, bf16[128,2048]{1,0:T(8,128)(2,1)S(1)}, u32[]{:S(2)}, u32[]{:S(2)}) collective-permute-start(bf16[128,2048]{1,0:T(8,128)(2,1)S(1)} %get-tuple-element.43.refs_13_.refs_10_), channel_id=1, source_target_pairs={{0,12},{1,13},{2,14},{3,15},{4,0},{5,1},{6,2},{7,3},{8,4},{9,5},{1... | collective-permute-start | bytes 1572872 | tf_op jit(solution)/shard_map/ppermute | solution.py:62
  98.6 13.1 %collective-permute-start.15 = (bf16[128,2048]{1,0:T(8,128)(2,1)}, bf16[128,2048]{1,0:T(8,128)(2,1)S(1)}, u32[]{:S(2)}, u32[]{:S(2)}) collective-permute-start(bf16[128,2048]{1,0:T(8,128)(2,1)} %get-tuple-element.44.refs_15_.refs_12_), channel_id=1, source_target_pairs={{0,2},{1,3},{2,0},{3,1},{4,6},{5,7},{6,4},{7,5},{8,10},{9,11},{10,... | collective-permute-start | bytes 1572872 | tf_op jit(solution)/shard_map/ppermute | solution.py:62
  98.9 2.8 %copy-start.15 = (bf16[128,2048]{1,0:T(8,128)(2,1)S(1)}, bf16[128,2048]{1,0:T(8,128)(2,1)}, u32[]{:S(2)}) copy-start(bf16[128,2048]{1,0:T(8,128)(2,1)} %copy-done.13) | copy-start | bytes 1572868
  98.9 2.9 %copy-start.17 = (bf16[128,2048]{1,0:T(8,128)(2,1)S(1)}, bf16[128,2048]{1,0:T(8,128)(2,1)}, u32[]{:S(2)}) copy-start(bf16[128,2048]{1,0:T(8,128)(2,1)} %copy-done.16) | copy-start | bytes 1572868
  100.2 1.6 %copy-start.1 = (bf16[128,2048]{1,0:T(8,128)(2,1)S(1)}, bf16[128,2048]{1,0:T(8,128)(2,1)}, u32[]{:S(2)}) copy-start(bf16[128,2048]{1,0:T(8,128)(2,1)} %copy-done) | copy-start | bytes 1572868
  100.2 1.6 %copy-start.3 = (bf16[128,2048]{1,0:T(8,128)(2,1)S(1)}, bf16[128,2048]{1,0:T(8,128)(2,1)}, u32[]{:S(2)}) copy-start(bf16[128,2048]{1,0:T(8,128)(2,1)} %copy-done.2) | copy-start | bytes 1572868
  100.2 1.7 %copy-start.5 = (bf16[128,2048]{1,0:T(8,128)(2,1)S(1)}, bf16[128,2048]{1,0:T(8,128)(2,1)}, u32[]{:S(2)}) copy-start(bf16[128,2048]{1,0:T(8,128)(2,1)} %copy-done.4) | copy-start | bytes 1572868
  100.3 1.8 %copy-start.7 = (bf16[128,2048]{1,0:T(8,128)(2,1)S(1)}, bf16[128,2048]{1,0:T(8,128)(2,1)}, u32[]{:S(2)}) copy-start(bf16[128,2048]{1,0:T(8,128)(2,1)} %copy-done.6) | copy-start | bytes 1572868
  100.3 2.0 %copy-start.9 = (bf16[128,2048]{1,0:T(8,128)(2,1)S(1)}, bf16[128,2048]{1,0:T(8,128)(2,1)}, u32[]{:S(2)}) copy-start(bf16[128,2048]{1,0:T(8,128)(2,1)} %copy-done.8) | copy-start | bytes 1572868
  100.3 2.1 %copy-start.12 = (bf16[128,2048]{1,0:T(8,128)(2,1)S(1)}, bf16[128,2048]{1,0:T(8,128)(2,1)}, u32[]{:S(2)}) copy-start(bf16[128,2048]{1,0:T(8,128)(2,1)} %copy-done.10) | copy-start | bytes 1572868
  114.8 4.4 %collective-permute-start.16 = (bf16[176,2048]{1,0:T(8,128)(2,1)S(1)}, bf16[176,2048]{1,0:T(8,128)(2,1)S(1)}, u32[]{:S(2)}, u32[]{:S(2)}) collective-permute-start(bf16[176,2048]{1,0:T(8,128)(2,1)S(1)} %get-tuple-element.48), channel_id=1, source_target_pairs={{0,16},{1,17},{2,18},{3,19},{4,20},{5,21},{6,22},{7,23},{8,24},{9,... | collective-permute-start | bytes 2162696 | tf_op jit(solution)/shard_map/ppermute | solution.py:397
  119.2 1.6 %copy-start.23 = (f32[256,2048]{1,0:T(8,128)S(1)}, f32[256,2048]{1,0:T(8,128)}, u32[]{:S(2)}) copy-start(f32[256,2048]{1,0:T(8,128)} %copy-done.22) | copy-start | bytes 6291460
  (4 other events, 3.0 us)

commit v2 on v1

v2 whole, which is shorter than its diff:
```python
import functools

import jax
import jax.numpy as jnp
from jax import lax
from jax.experimental import pallas as pl
from jax.experimental.pallas import tpu as pltpu
from jax.sharding import PartitionSpec as P

HD = 128
SPLIT = 8
C = 6
PAD = 8
SENT = 4
TGT_TOTAL = 171
MIB = 1 << 20


def normalize(values, gain):
    mean = jnp.mean(values, -1, keepdims=True)
    centred = values - mean
    spread = jnp.mean(centred * centred, -1, keepdims=True)
    return centred * lax.rsqrt(spread + 1e-05) * gain


def positions(lengths, count):
    upto = jnp.arange(SENT)[:, None] <= jnp.arange(SENT)[None, :]
    ends = jnp.sum(jnp.where(upto, lengths[:, None], 0), axis=0)
    above = (jnp.arange(count, dtype=jnp.int32)[:, None] >= ends[None, :]).astype(jnp.int32)
    return jnp.sum(above, axis=1)


def dot(left, right):
    return jnp.dot(left, right, preferred_element_type=jnp.float32)


def dot_rows(left, right):
    return lax.dot_general(
        left, right, (((1,), (1,)), ((), ())), preferred_element_type=jnp.float32
    )


def chips():
    return (4, 2, 2) if lax.axis_size("ep") == 16 else None


def place_of(index):
    depth, high, wide = chips()
    return index // (high * wide), index // wide % high, index % wide


def index_of(z, y, x):
    depth, high, wide = chips()
    return (z % depth * high + y) * wide + x


def moved(value, dz=0, dy=0, dx=0):
    pairs = []
    for source in range(lax.axis_size("ep")):
        z, y, x = place_of(source)
        pairs.append((source, index_of(z + dz, y ^ dy, x ^ dx)))
    return lax.ppermute(value, "ep", pairs)


def specs(smem, vmem, unread=0):
    return (
        [pl.BlockSpec(memory_space=pltpu.SMEM)] * smem
        + [pl.BlockSpec(memory_space=pltpu.VMEM)] * vmem
        + [pl.BlockSpec(memory_space=pl.ANY)] * unread
    )


def local(kernel, name, outs, vmem, after=(), onward=(), order=None, far=(), scratch=(), mib=6):
    scalars = () if order is None else (order,)
    read = len(scalars) + len(vmem) + len(far)
    unread = len(after) + len(onward)

    def run(*refs):
        results = refs[read + unread :]
        kernel(*refs[:read], *results[: len(outs)], *results[len(outs) + len(onward) :])

    first = read + len(after)
    return pl.pallas_call(
        run,
        out_shape=[jax.ShapeDtypeStruct(shape, dtype) for shape, dtype in outs]
        + [jax.ShapeDtypeStruct(array.shape, array.dtype) for array in onward],
        in_specs=specs(len(scalars), len(vmem), len(far) + unread),
        out_specs=specs(0, len(outs), len(onward)),
        scratch_shapes=list(scratch),
        input_output_aliases={first + i: len(outs) + i for i in range(len(onward))},
        compiler_params=pltpu.CompilerParams(vmem_limit_bytes=mib * MIB),
        name=name,
    )(*scalars, *vmem, *far, *after, *onward)


def pack_kernel(experts, place, both, hidden, gain, router, gate, send):
    count = gate.shape[0]
    slot = lax.broadcasted_iota(jnp.int32, (count, hidden.shape[0]), 0)
    table = slot == place[...]
    rows = dot(table.astype(jnp.bfloat16), hidden[...])
    normed = normalize(rows, gain[...])
    send[...] = jnp.concatenate(
        [normed[e * PAD : (e + 1) * PAD] for e in experts], axis=0
    ).astype(jnp.bfloat16)
    logits = dot(normed.astype(jnp.bfloat16), router[...])
    mine = lax.broadcasted_iota(jnp.int32, (count, 1), 0) // PAD
    others = jnp.sum(jnp.where(table, both[...], 0), axis=1, keepdims=True) - mine
    expert = lax.broadcasted_iota(jnp.int32, logits.shape, 1)
    lead = jnp.where(expert == mine, logits, 0.0) - jnp.where(expert == others, logits, 0.0)
    gate[...] = 1.0 / (1.0 + jnp.exp(-jnp.sum(lead, axis=1, keepdims=True)))


def gate_kernel():
    pass


def mlp_kernel(rows, w_in, w_out, pieces):
    inner = jnp.maximum(dot(rows[...], w_in[...]), 0.0).astype(jnp.bfloat16)
    pieces[...] = dot(inner, w_out[...]).astype(jnp.bfloat16)


def rows_kernel(experts, gate, parts, rows):
    count = gate.shape[0]
    summed = [None] * (count // PAD)
    for i, e in enumerate(experts):
        part = parts[i * PAD : (i + 1) * PAD].astype(jnp.float32)
        summed[e] = part if summed[e] is None else summed[e] + part
    rows[...] = gate[...] * jnp.concatenate(summed, axis=0)


def mixed_rows(hidden, place, rows_ref):
    rows = rows_ref[...]
    count, size = rows.shape[0], hidden.shape[0]
    high = rows.astype(jnp.bfloat16)
    rest = rows - high.astype(jnp.float32)
    middle = rest.astype(jnp.bfloat16)
    low = (rest - middle.astype(jnp.float32)).astype(jnp.bfloat16)
    slot = lax.broadcasted_iota(jnp.int32, (size, 3 * count), 1) % count
    picks = (slot.astype(jnp.float32) == place[...]).astype(jnp.bfloat16)
    added = dot(picks, jnp.concatenate([high, middle, low], axis=0))
    return hidden[...].astype(jnp.float32) + added


def norm_kernel(group, *refs):
    own, other, (memory, target, mixed) = refs[:4], refs[4:8], refs[8:]

    def run(source, wanted):
        hidden, place, rows, gain = source
        values = mixed_rows(hidden, place, rows)
        memory[...] = normalize(values, gain[...]).astype(jnp.bfloat16)
        hidden, place, rows, gain = wanted
        mixed[...] = mixed_rows(hidden, place, rows)
        target[...] = normalize(mixed[: target.shape[0]], gain[...]).astype(jnp.bfloat16)

    pl.when(group[0] == 0)(lambda: run(own, other))
    pl.when(group[0] != 0)(lambda: run(other, own))


def places(routes, slots):
    return jnp.max(jnp.where(slots >= 0, routes * PAD + slots, -1), axis=1)


def expert_rows(hidden, norm_gain, router, w_in, w_out, routes, slots):
    experts = lax.axis_size("ep") // SPLIT
    count = experts * PAD
    width = hidden.shape[1]
    table = jnp.arange(count)[:, None] == places(routes, slots)[None, :]
    rows = dot(table.astype(jnp.bfloat16), hidden)
    normed = normalize(rows, norm_gain).astype(jnp.bfloat16)
    outgoing = jnp.broadcast_to(normed.reshape(experts, 1, PAD, width), (experts, SPLIT, PAD, width))
    arrived = lax.all_to_all(
        outgoing.reshape(experts * SPLIT, PAD, width), "ep", split_axis=0, concat_axis=0, tiled=True
    ).reshape(-1, width)
    inner = jax.nn.relu(dot(arrived, w_in)).astype(jnp.bfloat16)
    piece = dot(inner, w_out).astype(jnp.bfloat16)
    back = lax.all_to_all(
        piece.reshape(-1, PAD, width), "ep", split_axis=0, concat_axis=0, tiled=True
    )
    summed = jnp.sum(back.reshape(experts, SPLIT, PAD, width).astype(jnp.float32), axis=1)
    logits = dot(normed, router)
    mine = jnp.arange(count) // PAD
    both = jnp.sum(routes, axis=1)
    others = jnp.sum(jnp.where(table, both[None, :], 0), axis=1) - mine
    ids = jnp.arange(router.shape[1])[None, :]
    sign = (ids == mine[:, None]).astype(jnp.float32) - (ids == others[:, None]).astype(jnp.float32)
    gate = jax.nn.sigmoid(jnp.sum(logits * sign, axis=1, keepdims=True))
    return gate * summed.reshape(count, width)


def expert_layer(marks, hidden, norm_gain, router, w_in, w_out, routes, slots):
    devices = lax.axis_size("ep")
    experts = devices // SPLIT
    width = hidden.shape[1]
    place = places(routes, slots)
    held = [device // SPLIT for device in range(devices)]
    blocks = (devices * PAD, width)

    def exchanged(values):
        parts = values.reshape(devices, PAD, width)
        parts = lax.all_to_all(parts, "ep", split_axis=0, concat_axis=0, tiled=True)
        return parts.reshape(values.shape)

    gate, send = local(
        functools.partial(pack_kernel, held),
        "pack",
        [((experts * PAD, 1), jnp.float32), (blocks, jnp.bfloat16)],
        (place[None, :], jnp.sum(routes, axis=1)[None, :], hidden, norm_gain[None, :], router),
    )
    (pieces,) = local(
        mlp_kernel,
        "mlp",
        [(blocks, jnp.bfloat16)],
        (exchanged(send), w_in, w_out),
        marks[0],
    )
    (rows,) = local(
        functools.partial(rows_kernel, held),
        "rows",
        [((experts * PAD, width), jnp.float32)],
        (gate, exchanged(pieces)),
        marks[1],
    )
    return rows


def both_norms(hidden, other_hidden, final_gain, place, rows, targets):
    swap = [(0, 1), (1, 0)]
    place = place[:, None].astype(jnp.float32)
    gain = final_gain[None, :]
    small = jnp.concatenate([gain, jnp.pad(place.T, ((0, 0), (0, gain.shape[1] - place.shape[0])))])
    small = lax.ppermute(small, "grp", swap)
    other_rows = lax.ppermute(rows, "grp", swap)
    own = (hidden, place, rows, gain)
    other = (other_hidden, small[1, : place.shape[0]][:, None], other_rows, small[:1])
    size, width = hidden.shape
    return local(
        norm_kernel,
        "norm",
        [
            ((size, width), jnp.bfloat16),
            ((targets, width), jnp.bfloat16),
            ((size, width), jnp.float32),
        ],
        (*own[:4], *other[:4]),
        order=lax.axis_index("grp")[None],
        mib=12,
    )


EARLY = [
    (0, 0, 0), (1, 0, 0), (2, 0, 0), (3, 0, 0), (0, 0, 1), (1, 0, 1), (0, 1, 0), (1, 1, 0),
    (2, 1, 0), (3, 1, 0), (0, 1, 1), (1, 1, 1), (2, 0, 1),
]
LATE = [(3, 0, 1), (3, 1, 1), (2, 1, 1)]


def gather(part):
    def once(there, *blocks):
        return local(gate_kernel, "gate", [], (), there, blocks)

    z1, x0, y0 = moved(part, dz=1), moved(part, dx=1), moved(part, dy=1)
    z1, y0 = once([x0], z1, y0)
    z2, far0, y1 = moved(z1, dz=1), moved(y0, dx=1), moved(z1, dy=1)
    z1, z2, far0 = once([y1], z1, z2, far0)
    second = [z2]
    z3, x1, y2 = moved(z2, dz=1), moved(z1, dx=1), moved(z2, dy=1)
    z2, z3, far0 = once([x1, y2], z2, z3, far0)
    far1, x2, y3 = moved(far0, dz=1), moved(z2, dx=1), moved(z3, dy=1)
    z3, far0, x2 = once([far1, y3], z3, far0, x2)
    fourth = [x2]
    far3, x3, far2 = moved(far0, dz=-1), moved(z3, dx=1), moved(x2, dy=1)
    early = [part, z1, z2, z3, x0, x1, y0, y1, y2, y3, far0, far1, x2]
    return early, [x3, far3, far2], (second, fourth)


def pairs_of(refs):
    return [tuple(range(low, min(low + 2, len(refs)))) for low in range(0, len(refs), 2)]


def joined(parts, axis):
    return parts[0] if len(parts) == 1 else jnp.concatenate(parts, axis=axis)


def fetched(blocks, columns, near, sems):
    rows = blocks[0].shape[0]
    copies = [
        pltpu.make_async_copy(
            block.at[:, columns], near.at[pl.ds(i * rows, rows)], sems.at[i]
        )
        for i, block in enumerate(blocks)
    ]
    for copy in copies:
        copy.start()
    return copies


def add_blocks(order, memory, target, near, copies, kv, q, fresh):
    rows = near.shape[0] // len(copies)
    half = q.shape[1]

    def columns(ref, members):
        return joined(
            [ref[:, pl.ds(pl.multiple_of(order[i] * rows, 128), rows)] for i in members], 1
        )

    for step, members in enumerate(pairs_of(copies)):
        for i in members:
            copies[i].wait()
        weights = near[members[0] * rows : (members[-1] + 1) * rows]
        kv_part = dot(columns(memory, members), weights[:, : 2 * half])
        q_part = dot(columns(target, members), weights[:, 2 * half :])
        if fresh and step == 0:
            kv[...] = kv_part
            q[...] = q_part
        else:
            kv[...] += kv_part
            q[...] += q_part


def project_kernel(count, order, memory, target, *refs):
    blocks, (kv, q, near, sems) = refs[:count], refs[count:]
    copies = fetched(blocks, pl.ds(0, near.shape[1]), near, sems)
    add_blocks(order, memory, target, near, copies, kv, q, True)


def attend_kernel(early, late, order, seg_q, seg_k, memory, target, kv_sum, q_sum, *refs):
    blocks = refs[: early + late]
    own, sent, kv, q, context, near, near_out, sems, sems_out = refs[early + late :]
    half = q.shape[1]
    rows = blocks[0].shape[0]
    kv[...] = kv_sum[...]
    q[...] = q_sum[...]
    if late:
        copies = fetched(blocks[early:], pl.ds(0, 3 * half), near, sems)
    copies_out = fetched(blocks, pl.ds(3 * half, half), near_out, sems_out)
    if late:
        late_order = [order[early + i] for i in range(late)]
        add_blocks(late_order, memory, target, near, copies, kv, q, False)
    allowed = seg_q[...] == seg_k[...]
    for low in range(0, half, HD):
        query = q[:, low : low + HD].astype(jnp.bfloat16)
        keys = kv[:, low : low + HD].astype(jnp.bfloat16)
        values = kv[:, half + low : half + low + HD].astype(jnp.bfloat16)
        scores = jnp.where(allowed, dot_rows(query, keys) * HD ** (-0.5), -1e30)
        expd = jnp.exp(scores - jnp.max(scores, axis=-1, keepdims=True))
        prob = (expd / jnp.sum(expd, axis=-1, keepdims=True)).astype(jnp.bfloat16)
        context[:, low : low + HD] = dot(prob, values).astype(jnp.bfloat16)
    for copy in copies_out:
        copy.wait()
    for members in pairs_of(blocks):
        part = dot_rows(context[...], near_out[members[0] * rows : (members[-1] + 1) * rows])
        for place, i in enumerate(members):
            columns = pl.ds(pl.multiple_of(order[i] * rows, 128), rows)
            value = part[:, place * rows : (place + 1) * rows]
            own[:, columns] = value
            sent[:, columns] = value.astype(jnp.bfloat16)


def project(order, memory, target, blocks):
    rows, half = blocks[0].shape[0], blocks[0].shape[1] // 4
    return local(
        functools.partial(project_kernel, len(blocks)),
        "project",
        [((memory.shape[0], 2 * half), jnp.float32), ((target.shape[0], half), jnp.float32)],
        (memory, target),
        order=order,
        far=blocks,
        scratch=[
            pltpu.VMEM((len(blocks) * rows, 3 * half), jnp.bfloat16),
            pltpu.SemaphoreType.DMA((len(blocks),)),
        ],
        mib=14,
    )


def attend(order, seg_q, seg_k, memory, target, sums, early, late):
    rows, half = early[0].shape[0], early[0].shape[1] // 4
    count, width = target.shape
    blocks = len(early) + len(late)
    return local(
        functools.partial(attend_kernel, len(early), len(late)),
        "attend",
        [((count, width), jnp.float32), ((count, width), jnp.bfloat16)],
        (seg_q[:, None], seg_k[None, :], memory, target, *sums),
        order=order,
        far=(*early, *late),
        scratch=[
            pltpu.VMEM((memory.shape[0], 2 * half), jnp.float32),
            pltpu.VMEM((count, half), jnp.float32),
            pltpu.VMEM((count, half), jnp.bfloat16),
            pltpu.VMEM((max(len(late), 1) * rows, 3 * half), jnp.bfloat16),
            pltpu.VMEM((blocks * rows, half), jnp.bfloat16),
            pltpu.SemaphoreType.DMA((max(len(late), 1),)),
            pltpu.SemaphoreType.DMA((blocks,)),
        ],
        mib=14,
    )


def body(
    hidden,
    norm_gain,
    final_gain,
    router,
    w_in,
    w_out,
    expert_ids,
    slot_ids,
    src_len,
    tgt_len,
    wq,
    wk,
    wv,
    wo,
):
    group = lax.axis_index("grp")
    encoder = group == 0
    rows_here, width = hidden.shape[1:]
    half = wq.shape[1] // lax.axis_size("grp")
    targets = min(rows_here, -(-TGT_TOTAL // 16) * 16)

    def mine(*weights):
        return jnp.concatenate(
            [lax.dynamic_slice_in_dim(weight, group * half, half, 1) for weight in weights], axis=1
        )

    part = mine(wk, wv, wq, wo)
    other_hidden = lax.ppermute(hidden[0], "grp", [(0, 1), (1, 0)])
    layer = (norm_gain[0], router[0], w_in[0], w_out[0], expert_ids[0], slot_ids[0])
    if chips() is None:
        early, late = [lax.all_gather(part, "ep", axis=0, tiled=True)], []
        order = jnp.zeros((1,), jnp.int32)
        rows = expert_rows(hidden[0], *layer)
    else:
        early, late, marks = gather(part)
        z, y, x = place_of(lax.axis_index("ep"))
        order = jnp.stack([index_of(z - dz, y ^ dy, x ^ dx) for dz, dy, dx in EARLY + LATE])
        rows = expert_layer(marks, hidden[0], *layer)
    memory, target, mixed = both_norms(
        hidden[0], other_hidden, final_gain[0], places(expert_ids[0], slot_ids[0]), rows, targets
    )

    seg_q = positions(tgt_len[0], targets)
    seg_k = positions(src_len[0], rows_here)
    valid = (seg_q < SENT)[:, None]
    sums = project(order, memory, target, early)
    own, sent = attend(order, seg_q, seg_k, memory, target, sums, early, late)
    total = own + lax.ppermute(sent, "grp", [(0, 1)]).astype(jnp.float32)
    attended = jnp.pad(jnp.where(valid, total, 0.0), ((0, rows_here - targets), (0, 0)))
    decoded = (mixed + attended).astype(jnp.bfloat16)
    return jnp.where(encoder, memory, decoded)[None]


def solution(mesh):
    in_specs = (
        P("grp", "ep", None),
        P("grp", None),
        P("grp", None),
        P("grp", None, None),
        P("grp", None, "ep"),
        P("grp", "ep", None),
        P("grp", "ep", None),
        P("grp", "ep", None),
        P("ep", None),
        P("ep", None),
        P("ep", None),
        P("ep", None),
        P("ep", None),
        P("ep", None),
    )
    out_specs = P("grp", "ep", None)
    return jax.shard_map(body, mesh=mesh, in_specs=in_specs, out_specs=out_specs, check_vma=False)
```

time: 123 us -> 120 us (0.976)
  blocking collectives: 47.8 us -> 0 us
  waiting for transfers between devices: 23.1 us -> 38.9 us
  starting transfers between devices: 21.9 us -> 34 us
  local copies, waits for them, and re-layouts: 15.4 us -> 24.3 us
  Pallas kernels: 8.69 us -> 17.1 us
  other arithmetic: 4.87 us -> 3.57 us
    all_to_all x3 -> x0, blocking collectives: 47.8 us -> none  [exchanged(): lax.all_to_all(parts, 'ep', split_axis=0, concat_axis=0, tiled=True, axis...]
    ppermute x15, waiting for transfers between devices: 6.85 us -> 35.7 us  [moved(): return lax.ppermute(value, 'ep', pairs)]
    all_to_all x1 -> x2, waiting for transfers between devices: 13.2 us -> 0.27 us  [exchanged(): parts = lax.all_to_all(parts, 'ep', split_axis=0, concat_axis=0, tiled=True)]
    pallas_call x6 -> x10, Pallas kernels: 5.61 us -> 17.1 us  [local(): pl.pallas_call(run, out_shape=[jax.ShapeDtypeStruct(shape, dtype) for sha...]
    unnamed x68 -> x72, local copies, waits for them, and re-layouts: 12.9 us -> 19.7 us
    ppermute x1 -> x3, starting transfers between devices: 1.5 us -> 6.97 us  [the longest x1 3.8 us: body(): other_hidden = lax.ppermute(hidden[0], 'grp', [(0, 1), (1, 0)])]
    all_to_all x1 -> x2, starting transfers between devices: 4.67 us -> 9.01 us  [exchanged(): parts = lax.all_to_all(parts, 'ep', split_axis=0, concat_axis=0, tiled=True)]
    pallas_call x1 -> x0, Pallas kernels: 3.08 us -> none  [attend(): pl.pallas_call(functools.partial(attend_kernel, len(early), len(late)), o...]
  transfers between devices with their start and end apart: 18 -> 21, of which waited for: 5 -> 6; matrix products, arithmetic and copies ran while one was open for 3% -> 2% of each run, Pallas kernels for 3% -> 10%
where the time goes in v2:
time: 120 us; the launch traced here: 118 us
  waiting for transfers between devices  38.9 us (32%)
  starting transfers between devices  34 us (28%)
  local copies, waits for them, and re-layouts  24.3 us (20%)
  Pallas kernels  17.1 us (14%)
  other arithmetic  3.57 us (3%)
    ppermute x15, waiting for transfers between devices, moved(): return lax.ppermute(value, 'ep', pairs)  35.7 us
    unnamed x72, local copies, waits for them, and re-layouts  19.7 us
    pallas_call x10, Pallas kernels, local(): pl.pallas_call(run, out_shape=[jax.ShapeDtypeStruct(shape, dtype) for sha...  17.1 us
    ppermute x15, starting transfers between devices, moved(): return lax.ppermute(value, 'ep', pairs)  16.8 us
    all_to_all x2, starting transfers between devices, exchanged(): parts = lax.all_to_all(parts, 'ep', split_axis=0, concat_axis=0, tiled=True)  9.01 us
    ppermute x1, starting transfers between devices, body(): other_hidden = lax.ppermute(hidden[0], 'grp', [(0, 1), (1, 0)])  3.8 us
    ppermute x1, starting transfers between devices, both_norms(): other_rows = lax.ppermute(rows, 'grp', swap)  3.1 us
    ppermute x1, waiting for transfers between devices, body(): total = own + lax.ppermute(sent, 'grp', [(0, 1)]).astype(jnp.float32)  2.97 us
  transfers between devices with their start and end apart: 21, of which 6 were waited for; matrix products, arithmetic and copies ran while one was open for 2% of the time, Pallas kernels for 10%

profile of v2, /device:TPU:1, one launch (start us, length us, event | category | flops | bytes accessed | tf_op | source)
XLA Modules:
  0.0 118.5 jit_solution(1855442939434648818)
XLA Ops:
  0.0 1.0 constant_dynamic-slice_fusion
  1.1 1.0 constant_dynamic-slice_fusion.2
  2.1 2.1 %collective-permute-start.2 = (bf16[128,2048]{1,0:T(8,128)(2,1)S(1)}, bf16[128,2048]{1,0:T(8,128)(2,1)S(1)}, u32[]{:S(2)}, u32[]{:S(2)}) collective-permute-start(bf16[128,2048]{1,0:T(8,128)(2,1)S(1)} %pad_maximum_fusion.refs_3_.refs_7_), channel_id=1, source_target_pairs={{0,2},{1,3},{2,0},{3,1},{4,6},{5,7},{6,4},{7,5},{8,10},{9,11},{10,... | collective-permute-start | bytes 1572872 | tf_op jit(solution)/shard_map/ppermute | solution.py:62
  4.3 1.3 %collective-permute-start.1 = (bf16[128,2048]{1,0:T(8,128)(2,1)S(1)}, bf16[128,2048]{1,0:T(8,128)(2,1)S(1)}, u32[]{:S(2)}, u32[]{:S(2)}) collective-permute-start(bf16[128,2048]{1,0:T(8,128)(2,1)S(1)} %pad_maximum_fusion.refs_3_.refs_7_), channel_id=1, source_target_pairs={{0,4},{1,5},{2,6},{3,7},{4,8},{5,9},{6,10},{7,11},{8,12},{9,13},{1... | collective-permute-start | bytes 1572872 | tf_op jit(solution)/shard_map/ppermute | solution.py:62
  5.6 1.2 %collective-permute-start = (bf16[128,2048]{1,0:T(8,128)(2,1)S(1)}, bf16[128,2048]{1,0:T(8,128)(2,1)S(1)}, u32[]{:S(2)}, u32[]{:S(2)}) collective-permute-start(bf16[128,2048]{1,0:T(8,128)(2,1)S(1)} %pad_maximum_fusion.refs_3_.refs_7_), channel_id=1, source_target_pairs={{0,1},{1,0},{2,3},{3,2},{4,5},{5,4},{6,7},{7,6},{8,9},{9,8},{10,11... | collective-permute-start | bytes 1572872 | tf_op jit(solution)/shard_map/ppermute | solution.py:62
  6.8 2.5 %pack.1 = (f32[16,1]{1,0:T(8,128)S(1)}, bf16[128,2048]{1,0:T(8,128)(2,1)}) custom-call(s32[1,256]{1,0:T(1,128)S(1)} %bitcast.40, s32[1,256]{1,0:T(1,128)S(1)} %bitcast.42, bf16[256,2048]{1,0:T(8,128)(2,1)} %bitcast.1.refs_2_.refs_1_, f32[1,2048]{1,0:T(1,128)S(1)} %copy-done.29, bf16[2048,128]{1,0:T(8,128)(2,1)S(1)} %bitcast.39), custom_call_target="tpu_custom_call" | custom-call | tf_op jit(solution)/shard_map/pack/pallas_call | solution.py:83
  9.3 4.2 %all-to-all-start = ((bf16[16,8,2048]{2,1,0:T(8,128)(2,1)}), bf16[16,8,2048]{2,1,0:T(8,128)(2,1)}, u32[]{:S(2)}, u32[]{:S(2)}) async-start(bf16[16,8,2048]{2,1,0:T(8,128)(2,1)} %bitcast.6), calls=%async_computation | async-start | bytes 1048576 | tf_op jit(solution)/shard_map/all_to_all | solution.py:200
  13.6 2.3 %collective-permute-done.2.refs_2_ = bf16[128,2048]{1,0:T(8,128)(2,1)S(1)} collective-permute-done((bf16[128,2048]{1,0:T(8,128)(2,1)S(1)}, bf16[128,2048]{1,0:T(8,128)(2,1)S(1)}, u32[]{:S(2)}, u32[]{:S(2)}) %collective-permute-start.2) | collective-permute-done | bytes 524320 | tf_op jit(solution)/shard_map/ppermute | solution.py:62
  15.9 2.8 %collective-permute-done.1.refs_1_ = bf16[128,2048]{1,0:T(8,128)(2,1)S(1)} collective-permute-done((bf16[128,2048]{1,0:T(8,128)(2,1)S(1)}, bf16[128,2048]{1,0:T(8,128)(2,1)S(1)}, u32[]{:S(2)}, u32[]{:S(2)}) %collective-permute-start.1) | collective-permute-done | bytes 524320 | tf_op jit(solution)/shard_map/ppermute | solution.py:62
  18.7 0.8 copy-done.2
  20.1 1.2 %collective-permute-start.5 = (bf16[128,2048]{1,0:T(8,128)(2,1)S(1)}, bf16[128,2048]{1,0:T(8,128)(2,1)S(1)}, u32[]{:S(2)}, u32[]{:S(2)}) collective-permute-start(bf16[128,2048]{1,0:T(8,128)(2,1)S(1)} %get-tuple-element.28.refs_9_.refs_13_), channel_id=1, source_target_pairs={{0,1},{1,0},{2,3},{3,2},{4,5},{5,4},{6,7},{7,6},{8,9},{9,8},{10,11... | collective-permute-start | bytes 1572872 | tf_op jit(solution)/shard_map/ppermute | solution.py:62
  21.3 17.1 %collective-permute-done.4.refs_2_ = bf16[128,2048]{1,0:T(8,128)(2,1)S(1)} collective-permute-done((bf16[128,2048]{1,0:T(8,128)(2,1)S(1)}, bf16[128,2048]{1,0:T(8,128)(2,1)S(1)}, u32[]{:S(2)}, u32[]{:S(2)}) %collective-permute-start.4) | collective-permute-done | bytes 524320 | tf_op jit(solution)/shard_map/ppermute | solution.py:62
  38.5 1.3 %collective-permute-start.6 = (bf16[128,2048]{1,0:T(8,128)(2,1)S(1)}, bf16[128,2048]{1,0:T(8,128)(2,1)S(1)}, u32[]{:S(2)}, u32[]{:S(2)}) collective-permute-start(bf16[128,2048]{1,0:T(8,128)(2,1)S(1)} %get-tuple-element.30.refs_4_.refs_8_), channel_id=1, source_target_pairs={{0,1},{1,0},{2,3},{3,2},{4,5},{5,4},{6,7},{7,6},{8,9},{9,8},{10,11... | collective-permute-start | bytes 1572872 | tf_op jit(solution)/shard_map/ppermute | solution.py:62
  39.7 1.2 collective-permute-start.8
  41.4 2.2 %copy-done.18 = bf16[1,2048,1024]{2,1,0:T(8,128)(2,1)S(1)} copy-done((bf16[1,2048,1024]{2,1,0:T(8,128)(2,1)S(1)}, bf16[1,2048,1024]{2,1,0:T(8,128)(2,1)}, u32[]{:S(2)}) %copy-start.18) | copy-done | bytes 4194328
  43.6 2.2 %copy-done.19 = bf16[1,1024,2048]{2,1,0:T(8,128)(2,1)S(1)} copy-done((bf16[1,1024,2048]{2,1,0:T(8,128)(2,1)S(1)}, bf16[1,1024,2048]{2,1,0:T(8,128)(2,1)}, u32[]{:S(2)}) %copy-start.19) | copy-done | bytes 4194328
  45.8 2.3 %mlp.1 = bf16[128,2048]{1,0:T(8,128)(2,1)S(1)} custom-call(bf16[128,2048]{1,0:T(8,128)(2,1)} %bitcast.7.refs_0_, bf16[2048,1024]{1,0:T(8,128)(2,1)S(1)} %bitcast.36, bf16[1024,2048]{1,0:T(8,128)(2,1)S(1)} %bitcast.37, bf16[128,2048]{1,0:T(8,128)(2,1)S(1)} %get-tuple-element.29.refs_3_.refs_2_), custom_call_target="tpu_custom_call" | custom-call | tf_op jit(solution)/shard_map/mlp/pallas_call | solution.py:83
  48.2 0.8 copy-done.22
  49.0 4.8 %all-to-all-start.1 = ((bf16[16,8,2048]{2,1,0:T(8,128)(2,1)}), bf16[16,8,2048]{2,1,0:T(8,128)(2,1)}, u32[]{:S(2)}, u32[]{:S(2)}) async-start(bf16[16,8,2048]{2,1,0:T(8,128)(2,1)} %bitcast.38), calls=%async_computation.1 | async-start | bytes 1048576 | tf_op jit(solution)/shard_map/all_to_all | solution.py:200
  53.8 1.4 %collective-permute-start.9 = (bf16[128,2048]{1,0:T(8,128)(2,1)S(1)}, bf16[128,2048]{1,0:T(8,128)(2,1)S(1)}, u32[]{:S(2)}, u32[]{:S(2)}) collective-permute-start(bf16[128,2048]{1,0:T(8,128)(2,1)S(1)} %get-tuple-element.32.refs_3_), channel_id=1, source_target_pairs={{0,4},{1,5},{2,6},{3,7},{4,8},{5,9},{6,10},{7,11},{8,12},{9,13},{1... | collective-permute-start | bytes 1572872 | tf_op jit(solution)/shard_map/ppermute | solution.py:62
  55.2 1.7 %collective-permute-start.10 = (bf16[128,2048]{1,0:T(8,128)(2,1)S(1)}, bf16[128,2048]{1,0:T(8,128)(2,1)S(1)}, u32[]{:S(2)}, u32[]{:S(2)}) collective-permute-start(bf16[128,2048]{1,0:T(8,128)(2,1)S(1)} %get-tuple-element.33.refs_2_), channel_id=1, source_target_pairs={{0,2},{1,3},{2,0},{3,1},{4,6},{5,7},{6,4},{7,5},{8,10},{9,11},{10,... | collective-permute-start | bytes 1572872 | tf_op jit(solution)/shard_map/ppermute | solution.py:62
  57.6 3.8 %collective-permute-start.12 = (bf16[256,2048]{1,0:T(8,128)(2,1)}, bf16[256,2048]{1,0:T(8,128)(2,1)}, u32[]{:S(2)}, u32[]{:S(2)}) collective-permute-start(bf16[256,2048]{1,0:T(8,128)(2,1)} %bitcast.1.refs_2_.refs_1_), channel_id=1, source_target_pairs={{0,16},{16,0},{1,17},{17,1},{2,18},{18,2},{3,19},{19,3},{4,20},{20... | collective-permute-start | bytes 3145736 | tf_op jit(solution)/shard_map/ppermute | solution.py:428
  61.6 13.4 %collective-permute-done.9.refs_0_.refs_14_.refs_18_ = bf16[128,2048]{1,0:T(8,128)(2,1)S(1)} collective-permute-done((bf16[128,2048]{1,0:T(8,128)(2,1)S(1)}, bf16[128,2048]{1,0:T(8,128)(2,1)S(1)}, u32[]{:S(2)}, u32[]{:S(2)}) %collective-permute-start.9) | collective-permute-done | bytes 524320 | tf_op jit(solution)/shard_map/ppermute | solution.py:62
  75.0 1.2 %collective-permute-start.15 = (bf16[128,2048]{1,0:T(8,128)(2,1)S(1)}, bf16[128,2048]{1,0:T(8,128)(2,1)}, u32[]{:S(2)}, u32[]{:S(2)}) collective-permute-start(bf16[128,2048]{1,0:T(8,128)(2,1)S(1)} %get-tuple-element.39.refs_6_.refs_10_), channel_id=1, source_target_pairs={{0,1},{1,0},{2,3},{3,2},{4,5},{5,4},{6,7},{7,6},{8,9},{9,8},{10,11... | collective-permute-start | bytes 1572872 | tf_op jit(solution)/shard_map/ppermute | solution.py:62
  76.2 1.5 %collective-permute-start.16 = (bf16[128,2048]{1,0:T(8,128)(2,1)S(1)}, bf16[128,2048]{1,0:T(8,128)(2,1)}, u32[]{:S(2)}, u32[]{:S(2)}) collective-permute-start(bf16[128,2048]{1,0:T(8,128)(2,1)S(1)} %get-tuple-element.40.refs_13_.refs_17_), channel_id=1, source_target_pairs={{0,12},{1,13},{2,14},{3,15},{4,0},{5,1},{6,2},{7,3},{8,4},{9,5},{1... | collective-permute-start | bytes 1572872 | tf_op jit(solution)/shard_map/ppermute | solution.py:62
  77.7 1.2 collective-permute-start.17
  79.3 0.8 copy.31.refs_1_
  80.3 1.1 rows.1.refs_3_
  81.5 3.1 %collective-permute-start.14 = (f32[16,2048]{1,0:T(8,128)S(1)}, f32[16,2048]{1,0:T(8,128)S(1)}, u32[]{:S(2)}, u32[]{:S(2)}) collective-permute-start(f32[16,2048]{1,0:T(8,128)S(1)} %rows.1.refs_3_), channel_id=1, source_target_pairs={{0,16},{16,0},{1,17},{17,1},{2,18},{18,2},{3,19},{19,3},{4,20},{20... | collective-permute-start | bytes 393224 | tf_op jit(solution)/shard_map/ppermute | solution.py:232
  86.8 0.9 copy-done.27
  87.7 3.2 %norm.1 = (bf16[256,2048]{1,0:T(8,128)(2,1)S(1)}, bf16[176,2048]{1,0:T(8,128)(2,1)S(1)}, f32[256,2048]{1,0:T(8,128)S(1)}) custom-call(s32[1]{0:T(128)} %bitcast.refs_0_, bf16[256,2048]{1,0:T(8,128)(2,1)} %bitcast.1.refs_2_.refs_1_, f32[256,1]{1,0:T(8,128)S(1)} %copy.29.refs_2_, f32[16,2048]{1,0:T(8,128)S(1)} %rows.1.refs_3_, f32[1,2048]{1,0:T(1,128)S(1)} %copy-done.28, ...), custom_call_target="tpu_custom_call" | custom-call | tf_op jit(solution)/shard_map/norm/pallas_call | solution.py:83
  90.9 1.3 %copy-done.20 = f32[256,2048]{1,0:T(8,128)} copy-done((f32[256,2048]{1,0:T(8,128)}, f32[256,2048]{1,0:T(8,128)S(1)}, u32[]{:S(2)}) %copy-start.20) | copy-done | bytes 2097176
  92.2 1.0 copy-done.1
  93.3 1.0 copy-done.3
  94.3 1.0 copy-done.5
  95.4 1.0 copy-done.7
  96.4 1.0 copy-done.9
  97.5 1.0 copy-done.11
  98.5 1.0 copy-done.13
  99.5 1.0 copy-done.15
  100.6 1.0 copy-done.17
  101.6 2.9 %project.1 = (f32[256,1024]{1,0:T(8,128)S(1)}, f32[176,512]{1,0:T(8,128)S(1)}) custom-call(s32[16]{0:T(128)S(1)} %stack.67.refs_0_, bf16[256,2048]{1,0:T(8,128)(2,1)S(1)} %get-tuple-element.36.refs_1_.refs_3_, bf16[176,2048]{1,0:T(8,128)(2,1)S(1)} %get-tuple-element.38.refs_2_.refs_4_, bf16[128,2048]{1,0:T(8,128)(2,1)S(1)} %copy-done.15, ...), custom_call_target="tpu_custom_call" | custom-call | tf_op jit(solution)/shard_map/project/pallas_call | solution.py:83
  104.6 5.0 %attend.1 = (f32[176,2048]{1,0:T(8,128)S(1)}, bf16[176,2048]{1,0:T(8,128)(2,1)}) custom-call(s32[16]{0:T(128)S(1)} %stack.67.refs_0_, s32[176,1]{1,0:T(8,128)S(1)} %copy-done.25, s32[1,256]{1,0:T(1,128)S(1)} %bitcast.43, bf16[256,2048]{1,0:T(8,128)(2,1)S(1)} %get-tuple-element.36.refs_1_.refs_3_, bf16[176,2048]{1,0:T(8,128)(2,1)S(1)} %get-tuple-element.38.refs_2_.refs_4_, ...), custom_call_target="tpu_custom_call" | custom-call | tf_op jit(solution)/shard_map/attend/pallas_call | solution.py:83
  109.6 1.1 copy-done.23
  110.7 1.3 %collective-permute-start.18 = (bf16[176,2048]{1,0:T(8,128)(2,1)}, bf16[176,2048]{1,0:T(8,128)(2,1)S(1)}, u32[]{:S(2)}, u32[]{:S(2)}) collective-permute-start(bf16[176,2048]{1,0:T(8,128)(2,1)} %get-tuple-element.44), channel_id=1, source_target_pairs={{0,16},{1,17},{2,18},{3,19},{4,20},{5,21},{6,22},{7,23},{8,24},{9,... | collective-permute-start | bytes 2162696 | tf_op jit(solution)/shard_map/ppermute | solution.py:448
  112.0 3.0 %collective-permute-done.18 = bf16[176,2048]{1,0:T(8,128)(2,1)S(1)} collective-permute-done((bf16[176,2048]{1,0:T(8,128)(2,1)}, bf16[176,2048]{1,0:T(8,128)(2,1)S(1)}, u32[]{:S(2)}, u32[]{:S(2)}) %collective-permute-start.18) | collective-permute-done | bytes 720928 | tf_op jit(solution)/shard_map/ppermute | solution.py:448
  115.0 1.7 %add_select_fusion = f32[176,2048]{1,0:T(8,128)S(1)} fusion(f32[176,2048]{1,0:T(8,128)} %copy-done.23, bf16[176,2048]{1,0:T(8,128)(2,1)S(1)} %collective-permute-done.18, pred[176]{0:T(512)(128)(4,1)S(1)} %broadcast_compare_fusion), kind=kLoop, calls=%fused_computation.1 | loop fusion | flops 1081344 | bytes 3604656 | tf_op jit(solution)/shard_map/jit(_where)/select_n | solution.py:449
  117.0 1.4 %fusion.1 = bf16[1,256,2048]{2,1,0:T(8,128)(2,1)} fusion(bf16[256,2048]{1,0:T(8,128)(2,1)S(1)} %get-tuple-element.36.refs_1_.refs_3_, f32[256,2048]{1,0:T(8,128)S(1)} %copy-done.21, f32[176,2048]{1,0:T(8,128)S(1)} %add_select_fusion, pred[]{:T(512)S(6)} %eq.22), kind=kLoop, calls=%fused_computation.3 | loop fusion | flops 1572864 | bytes 5636097 | tf_op jit(solution)/shard_map/broadcast_in_dim | solution.py:451
  (96 shorter events, 5.2 us)
Async XLA Ops:
  0.0 6.8 %copy-start.31 = (s32[1,256,2]{1,2,0:T(2,128)S(1)}, s32[1,256,2]{1,2,0:T(2,128)}, u32[]{:S(2)}) copy-start(s32[1,256,2]{1,2,0:T(2,128)} %param.21) | copy-start | bytes 6148
  0.0 6.8 %copy-start.30 = (s32[1,256,2]{1,2,0:T(2,128)S(1)}, s32[1,256,2]{1,2,0:T(2,128)}, u32[]{:S(2)}) copy-start(s32[1,256,2]{1,2,0:T(2,128)} %param.20) | copy-start | bytes 6148
  0.0 6.8 %copy-start.24 = (bf16[1,2048,128]{2,1,0:T(8,128)(2,1)S(1)}, bf16[1,2048,128]{2,1,0:T(8,128)(2,1)}, u32[]{:S(2)}) copy-start(bf16[1,2048,128]{2,1,0:T(8,128)(2,1)} %param.17) | copy-start | bytes 1572868
  0.0 6.8 %copy-start.29 = (f32[1,2048]{1,0:T(1,128)S(1)}, f32[1,2048]{1,0:T(1,128)}, u32[]{:S(2)}) copy-start(f32[1,2048]{1,0:T(1,128)} %refs_3_.1) | copy-start | bytes 24580
  2.1 16.6 %copy-start.14 = (bf16[128,2048]{1,0:T(8,128)(2,1)}, bf16[128,2048]{1,0:T(8,128)(2,1)S(1)}, u32[]{:S(2)}) copy-start(bf16[128,2048]{1,0:T(8,128)(2,1)S(1)} %pad_maximum_fusion.refs_3_.refs_7_) | copy-start | bytes 1572868
  2.1 13.8 %collective-permute-start.2 = (bf16[128,2048]{1,0:T(8,128)(2,1)S(1)}, bf16[128,2048]{1,0:T(8,128)(2,1)S(1)}, u32[]{:S(2)}, u32[]{:S(2)}) collective-permute-start(bf16[128,2048]{1,0:T(8,128)(2,1)S(1)} %pad_maximum_fusion.refs_3_.refs_7_), channel_id=1, source_target_pairs={{0,2},{1,3},{2,0},{3,1},{4,6},{5,7},{6,4},{7,5},{8,10},{9,11},{10,... | collective-permute-start | bytes 1572872 | tf_op jit(solution)/shard_map/ppermute | solution.py:62
  4.3 14.4 %collective-permute-start.1 = (bf16[128,2048]{1,0:T(8,128)(2,1)S(1)}, bf16[128,2048]{1,0:T(8,128)(2,1)S(1)}, u32[]{:S(2)}, u32[]{:S(2)}) collective-permute-start(bf16[128,2048]{1,0:T(8,128)(2,1)S(1)} %pad_maximum_fusion.refs_3_.refs_7_), channel_id=1, source_target_pairs={{0,4},{1,5},{2,6},{3,7},{4,8},{5,9},{6,10},{7,11},{8,12},{9,13},{1... | collective-permute-start | bytes 1572872 | tf_op jit(solution)/shard_map/ppermute | solution.py:62
  5.6 13.1 %collective-permute-start = (bf16[128,2048]{1,0:T(8,128)(2,1)S(1)}, bf16[128,2048]{1,0:T(8,128)(2,1)S(1)}, u32[]{:S(2)}, u32[]{:S(2)}) collective-permute-start(bf16[128,2048]{1,0:T(8,128)(2,1)S(1)} %pad_maximum_fusion.refs_3_.refs_7_), channel_id=1, source_target_pairs={{0,1},{1,0},{2,3},{3,2},{4,5},{5,4},{6,7},{7,6},{8,9},{9,8},{10,11... | collective-permute-start | bytes 1572872 | tf_op jit(solution)/shard_map/ppermute | solution.py:62
  9.3 32.1 %all-to-all-start = ((bf16[16,8,2048]{2,1,0:T(8,128)(2,1)}), bf16[16,8,2048]{2,1,0:T(8,128)(2,1)}, u32[]{:S(2)}, u32[]{:S(2)}) async-start(bf16[16,8,2048]{2,1,0:T(8,128)(2,1)} %bitcast.6), calls=%async_computation | async-start | bytes 1048576 | tf_op jit(solution)/shard_map/all_to_all | solution.py:200
  19.5 19.0 %copy-start.12 = (bf16[128,2048]{1,0:T(8,128)(2,1)}, bf16[128,2048]{1,0:T(8,128)(2,1)S(1)}, u32[]{:S(2)}) copy-start(bf16[128,2048]{1,0:T(8,128)(2,1)S(1)} %get-tuple-element.28.refs_9_.refs_13_) | copy-start | bytes 1572868
  19.5 18.9 %collective-permute-start.4 = (bf16[128,2048]{1,0:T(8,128)(2,1)S(1)}, bf16[128,2048]{1,0:T(8,128)(2,1)S(1)}, u32[]{:S(2)}, u32[]{:S(2)}) collective-permute-start(bf16[128,2048]{1,0:T(8,128)(2,1)S(1)} %get-tuple-element.27.refs_1_), channel_id=1, source_target_pairs={{0,4},{1,5},{2,6},{3,7},{4,8},{5,9},{6,10},{7,11},{8,12},{9,13},{1... | collective-permute-start | bytes 1572872 | tf_op jit(solution)/shard_map/ppermute | solution.py:62
  19.9 18.6 %collective-permute-start.3 = (bf16[128,2048]{1,0:T(8,128)(2,1)S(1)}, bf16[128,2048]{1,0:T(8,128)(2,1)S(1)}, u32[]{:S(2)}, u32[]{:S(2)}) collective-permute-start(bf16[128,2048]{1,0:T(8,128)(2,1)S(1)} %get-tuple-element.27.refs_1_), channel_id=1, source_target_pairs={{0,2},{1,3},{2,0},{3,1},{4,6},{5,7},{6,4},{7,5},{8,10},{9,11},{10,... | collective-permute-start | bytes 1572872 | tf_op jit(solution)/shard_map/ppermute | solution.py:62
  20.1 18.4 %collective-permute-start.5 = (bf16[128,2048]{1,0:T(8,128)(2,1)S(1)}, bf16[128,2048]{1,0:T(8,128)(2,1)S(1)}, u32[]{:S(2)}, u32[]{:S(2)}) collective-permute-start(bf16[128,2048]{1,0:T(8,128)(2,1)S(1)} %get-tuple-element.28.refs_9_.refs_13_), channel_id=1, source_target_pairs={{0,1},{1,0},{2,3},{3,2},{4,5},{5,4},{6,7},{7,6},{8,9},{9,8},{10,11... | collective-permute-start | bytes 1572872 | tf_op jit(solution)/shard_map/ppermute | solution.py:62
  38.4 1.3 %copy-start.16 = (bf16[128,2048]{1,0:T(8,128)(2,1)}, bf16[128,2048]{1,0:T(8,128)(2,1)S(1)}, u32[]{:S(2)}) copy-start(bf16[128,2048]{1,0:T(8,128)(2,1)S(1)} %collective-permute-done.3.refs_0_.refs_10_.refs_14_) | copy-start | bytes 1572868
  38.5 9.7 %copy-start = (bf16[128,2048]{1,0:T(8,128)(2,1)}, bf16[128,2048]{1,0:T(8,128)(2,1)S(1)}, u32[]{:S(2)}) copy-start(bf16[128,2048]{1,0:T(8,128)(2,1)S(1)} %get-tuple-element.30.refs_4_.refs_8_) | copy-start | bytes 1572868
  38.5 15.3 %collective-permute-start.6 = (bf16[128,2048]{1,0:T(8,128)(2,1)S(1)}, bf16[128,2048]{1,0:T(8,128)(2,1)S(1)}, u32[]{:S(2)}, u32[]{:S(2)}) collective-permute-start(bf16[128,2048]{1,0:T(8,128)(2,1)S(1)} %get-tuple-element.30.refs_4_.refs_8_), channel_id=1, source_target_pairs={{0,1},{1,0},{2,3},{3,2},{4,5},{5,4},{6,7},{7,6},{8,9},{9,8},{10,11... | collective-permute-start | bytes 1572872 | tf_op jit(solution)/shard_map/ppermute | solution.py:62
  39.7 14.0 %collective-permute-start.8 = (bf16[128,2048]{1,0:T(8,128)(2,1)S(1)}, bf16[128,2048]{1,0:T(8,128)(2,1)S(1)}, u32[]{:S(2)}, u32[]{:S(2)}) collective-permute-start(bf16[128,2048]{1,0:T(8,128)(2,1)S(1)} %get-tuple-element.29.refs_3_.refs_2_), channel_id=1, source_target_pairs={{0,4},{1,5},{2,6},{3,7},{4,8},{5,9},{6,10},{7,11},{8,12},{9,13},{1... | collective-permute-start | bytes 1572872 | tf_op jit(solution)/shard_map/ppermute | solution.py:62
  40.9 12.9 %collective-permute-start.7 = (bf16[128,2048]{1,0:T(8,128)(2,1)S(1)}, bf16[128,2048]{1,0:T(8,128)(2,1)S(1)}, u32[]{:S(2)}, u32[]{:S(2)}) collective-permute-start(bf16[128,2048]{1,0:T(8,128)(2,1)S(1)} %get-tuple-element.29.refs_3_.refs_2_), channel_id=1, source_target_pairs={{0,2},{1,3},{2,0},{3,1},{4,6},{5,7},{6,4},{7,5},{8,10},{9,11},{10,... | collective-permute-start | bytes 1572872 | tf_op jit(solution)/shard_map/ppermute | solution.py:62
  41.4 2.2 %copy-start.18 = (bf16[1,2048,1024]{2,1,0:T(8,128)(2,1)S(1)}, bf16[1,2048,1024]{2,1,0:T(8,128)(2,1)}, u32[]{:S(2)}) copy-start(bf16[1,2048,1024]{2,1,0:T(8,128)(2,1)} %param.18) | copy-start | bytes 12582916
  43.6 2.2 %copy-start.19 = (bf16[1,1024,2048]{2,1,0:T(8,128)(2,1)S(1)}, bf16[1,1024,2048]{2,1,0:T(8,128)(2,1)}, u32[]{:S(2)}) copy-start(bf16[1,1024,2048]{2,1,0:T(8,128)(2,1)} %param.19) | copy-start | bytes 12582916
  49.0 31.4 %all-to-all-start.1 = ((bf16[16,8,2048]{2,1,0:T(8,128)(2,1)}), bf16[16,8,2048]{2,1,0:T(8,128)(2,1)}, u32[]{:S(2)}, u32[]{:S(2)}) async-start(bf16[16,8,2048]{2,1,0:T(8,128)(2,1)} %bitcast.38), calls=%async_computation.1 | async-start | bytes 1048576 | tf_op jit(solution)/shard_map/all_to_all | solution.py:200
  53.7 7.6 %copy-start.28 = (f32[1,2048]{1,0:T(1,128)S(1)}, f32[1,2048]{1,0:T(1,128)}, u32[]{:S(2)}) copy-start(f32[1,2048]{1,0:T(1,128)} %refs_4_.1) | copy-start | bytes 24580
  53.7 7.7 %copy-start.34 = (s32[1,4]{1,0:T(1,128)S(1)}, s32[1,4]{1,0:T(1,128)}, u32[]{:S(2)}) copy-start(s32[1,4]{1,0:T(1,128)} %param.22) | copy-start | bytes 52
  53.8 21.2 %copy-start.4 = (bf16[128,2048]{1,0:T(8,128)(2,1)}, bf16[128,2048]{1,0:T(8,128)(2,1)S(1)}, u32[]{:S(2)}) copy-start(bf16[128,2048]{1,0:T(8,128)(2,1)S(1)} %collective-permute-done.6.refs_0_.refs_8_.refs_12_) | copy-start | bytes 1572868
  53.8 3.1 %copy-start.6 = (bf16[128,2048]{1,0:T(8,128)(2,1)}, bf16[128,2048]{1,0:T(8,128)(2,1)S(1)}, u32[]{:S(2)}) copy-start(bf16[128,2048]{1,0:T(8,128)(2,1)S(1)} %collective-permute-done.7.refs_1_.refs_11_.refs_15_) | copy-start | bytes 1572868
  53.8 25.2 %copy-start.35 = (s32[1,4]{1,0:T(1,128)S(1)}, s32[1,4]{1,0:T(1,128)}, u32[]{:S(2)}) copy-start(s32[1,4]{1,0:T(1,128)} %param.23) | copy-start | bytes 52
  53.8 21.1 %collective-permute-start.9 = (bf16[128,2048]{1,0:T(8,128)(2,1)S(1)}, bf16[128,2048]{1,0:T(8,128)(2,1)S(1)}, u32[]{:S(2)}, u32[]{:S(2)}) collective-permute-start(bf16[128,2048]{1,0:T(8,128)(2,1)S(1)} %get-tuple-element.32.refs_3_), channel_id=1, source_target_pairs={{0,4},{1,5},{2,6},{3,7},{4,8},{5,9},{6,10},{7,11},{8,12},{9,13},{1... | collective-permute-start | bytes 1572872 | tf_op jit(solution)/shard_map/ppermute | solution.py:62
  55.2 19.7 %collective-permute-start.10 = (bf16[128,2048]{1,0:T(8,128)(2,1)S(1)}, bf16[128,2048]{1,0:T(8,128)(2,1)S(1)}, u32[]{:S(2)}, u32[]{:S(2)}) collective-permute-start(bf16[128,2048]{1,0:T(8,128)(2,1)S(1)} %get-tuple-element.33.refs_2_), channel_id=1, source_target_pairs={{0,2},{1,3},{2,0},{3,1},{4,6},{5,7},{6,4},{7,5},{8,10},{9,11},{10,... | collective-permute-start | bytes 1572872 | tf_op jit(solution)/shard_map/ppermute | solution.py:62
  56.9 18.1 %collective-permute-start.11 = (bf16[128,2048]{1,0:T(8,128)(2,1)S(1)}, bf16[128,2048]{1,0:T(8,128)(2,1)S(1)}, u32[]{:S(2)}, u32[]{:S(2)}) collective-permute-start(bf16[128,2048]{1,0:T(8,128)(2,1)S(1)} %get-tuple-element.34.refs_5_.refs_9_), channel_id=1, source_target_pairs={{0,1},{1,0},{2,3},{3,2},{4,5},{5,4},{6,7},{7,6},{8,9},{9,8},{10,11... | collective-permute-start | bytes 1572872 | tf_op jit(solution)/shard_map/ppermute | solution.py:62
  57.6 28.6 %collective-permute-start.12 = (bf16[256,2048]{1,0:T(8,128)(2,1)}, bf16[256,2048]{1,0:T(8,128)(2,1)}, u32[]{:S(2)}, u32[]{:S(2)}) collective-permute-start(bf16[256,2048]{1,0:T(8,128)(2,1)} %bitcast.1.refs_2_.refs_1_), channel_id=1, source_target_pairs={{0,16},{16,0},{1,17},{17,1},{2,18},{18,2},{3,19},{19,3},{4,20},{20... | collective-permute-start | bytes 3145736 | tf_op jit(solution)/shard_map/ppermute | solution.py:428
  61.4 20.1 %collective-permute-start.13 = (f32[2,2048]{1,0:T(2,128)S(1)}, f32[2,2048]{1,0:T(2,128)}, u32[]{:S(2)}, u32[]{:S(2)}) collective-permute-start(f32[2,2048]{1,0:T(2,128)S(1)} %fusion.2), channel_id=1, source_target_pairs={{0,16},{16,0},{1,17},{17,1},{2,18},{18,2},{3,19},{19,3},{4,20},{20... | collective-permute-start | bytes 49160 | tf_op jit(solution)/shard_map/ppermute | solution.py:231
  75.0 4.4 %copy-start.8 = (bf16[128,2048]{1,0:T(8,128)(2,1)}, bf16[128,2048]{1,0:T(8,128)(2,1)S(1)}, u32[]{:S(2)}) copy-start(bf16[128,2048]{1,0:T(8,128)(2,1)S(1)} %collective-permute-done.9.refs_0_.refs_14_.refs_18_) | copy-start | bytes 1572868
  75.0 2.8 %copy-start.10 = (bf16[128,2048]{1,0:T(8,128)(2,1)}, bf16[128,2048]{1,0:T(8,128)(2,1)S(1)}, u32[]{:S(2)}) copy-start(bf16[128,2048]{1,0:T(8,128)(2,1)S(1)} %collective-permute-done.10.refs_1_.refs_12_.refs_16_) | copy-start | bytes 1572868
  75.0 29.5 %collective-permute-start.15 = (bf16[128,2048]{1,0:T(8,128)(2,1)S(1)}, bf16[128,2048]{1,0:T(8,128)(2,1)}, u32[]{:S(2)}, u32[]{:S(2)}) collective-permute-start(bf16[128,2048]{1,0:T(8,128)(2,1)S(1)} %get-tuple-element.39.refs_6_.refs_10_), channel_id=1, source_target_pairs={{0,1},{1,0},{2,3},{3,2},{4,5},{5,4},{6,7},{7,6},{8,9},{9,8},{10,11... | collective-permute-start | bytes 1572872 | tf_op jit(solution)/shard_map/ppermute | solution.py:62
  76.2 28.3 %collective-permute-start.16 = (bf16[128,2048]{1,0:T(8,128)(2,1)S(1)}, bf16[128,2048]{1,0:T(8,128)(2,1)}, u32[]{:S(2)}, u32[]{:S(2)}) collective-permute-start(bf16[128,2048]{1,0:T(8,128)(2,1)S(1)} %get-tuple-element.40.refs_13_.refs_17_), channel_id=1, source_target_pairs={{0,12},{1,13},{2,14},{3,15},{4,0},{5,1},{6,2},{7,3},{8,4},{9,5},{1... | collective-permute-start | bytes 1572872 | tf_op jit(solution)/shard_map/ppermute | solution.py:62
  77.7 26.8 %collective-permute-start.17 = (bf16[128,2048]{1,0:T(8,128)(2,1)S(1)}, bf16[128,2048]{1,0:T(8,128)(2,1)}, u32[]{:S(2)}, u32[]{:S(2)}) collective-permute-start(bf16[128,2048]{1,0:T(8,128)(2,1)S(1)} %get-tuple-element.35.refs_2_.refs_15_.refs_19_), channel_id=1, source_target_pairs={{0,2},{1,3},{2,0},{3,1},{4,6},{5,7},{6,4},{7,5},{8,10},{9,11},{10,... | collective-permute-start | bytes 1572872 | tf_op jit(solution)/shard_map/ppermute | solution.py:62
  79.2 5.4 %copy-start.32 = (s32[176]{0:T(256)}, s32[176]{0:T(256)S(1)}, u32[]{:S(2)}) copy-start(s32[176]{0:T(256)S(1)} %convert_reduce_fusion.1) | copy-start | bytes 2116
  81.5 4.7 %collective-permute-start.14 = (f32[16,2048]{1,0:T(8,128)S(1)}, f32[16,2048]{1,0:T(8,128)S(1)}, u32[]{:S(2)}, u32[]{:S(2)}) collective-permute-start(f32[16,2048]{1,0:T(8,128)S(1)} %rows.1.refs_3_), channel_id=1, source_target_pairs={{0,16},{16,0},{1,17},{17,1},{2,18},{18,2},{3,19},{19,3},{4,20},{20... | collective-permute-start | bytes 393224 | tf_op jit(solution)/shard_map/ppermute | solution.py:232
  90.9 1.3 %copy-start.20 = (f32[256,2048]{1,0:T(8,128)}, f32[256,2048]{1,0:T(8,128)S(1)}, u32[]{:S(2)}) copy-start(f32[256,2048]{1,0:T(8,128)S(1)} %get-tuple-element.37) | copy-start | bytes 6291460
  92.2 1.0 copy-start.1
  93.3 1.0 copy-start.3
  94.3 1.0 copy-start.5
  95.4 1.0 copy-start.7
  101.6 2.9 %copy-start.25 = (s32[176,1]{1,0:T(8,128)S(1)}, s32[176,1]{1,0:T(8,128)}, u32[]{:S(2)}) copy-start(s32[176,1]{1,0:T(8,128)} %copy.31.refs_1_) | copy-start | bytes 2116
  104.6 7.4 %copy-start.33 = (s32[176]{0:T(256)S(1)}, s32[176]{0:T(256)}, u32[]{:S(2)}) copy-start(s32[176]{0:T(256)} %copy-done.32) | copy-start | bytes 2116
  109.6 1.1 copy-start.23
  110.7 4.3 %collective-permute-start.18 = (bf16[176,2048]{1,0:T(8,128)(2,1)}, bf16[176,2048]{1,0:T(8,128)(2,1)S(1)}, u32[]{:S(2)}, u32[]{:S(2)}) collective-permute-start(bf16[176,2048]{1,0:T(8,128)(2,1)} %get-tuple-element.44), channel_id=1, source_target_pairs={{0,16},{1,17},{2,18},{3,19},{4,20},{5,21},{6,22},{7,23},{8,24},{9,... | collective-permute-start | bytes 2162696 | tf_op jit(solution)/shard_map/ppermute | solution.py:448
  115.0 2.0 %copy-start.21 = (f32[256,2048]{1,0:T(8,128)S(1)}, f32[256,2048]{1,0:T(8,128)}, u32[]{:S(2)}) copy-start(f32[256,2048]{1,0:T(8,128)} %copy-done.20) | copy-start | bytes 6291460
  (9 other events, 8.4 us)

commit v3 on v2

--- a/solution.py
+++ b/solution.py
@@ -66,7 +66,7 @@
     return (
         [pl.BlockSpec(memory_space=pltpu.SMEM)] * smem
         + [pl.BlockSpec(memory_space=pltpu.VMEM)] * vmem
-        + [pl.BlockSpec(memory_space=pl.ANY)] * unread
+        + [pl.BlockSpec(memory_space=pltpu.HBM)] * unread
     )
 
 
@@ -356,6 +356,21 @@
             sent[:, columns] = value.astype(jnp.bfloat16)
 
 
+def finish_kernel(group, memory, mixed, own, received, valid, out):
+    count = own.shape[0]
+
+    @pl.when(group[0] == 0)
+    def _():
+        out[...] = memory[...]
+
+    @pl.when(group[0] != 0)
+    def _():
+        total = own[...] + received[...].astype(jnp.float32)
+        attended = jnp.where(valid[...] > 0.0, total, 0.0)
+        out[:count] = (mixed[:count] + attended).astype(jnp.bfloat16)
+        out[count:] = mixed[count:].astype(jnp.bfloat16)
+
+
 def project(order, memory, target, blocks):
     rows, half = blocks[0].shape[0], blocks[0].shape[1] // 4
     return local(
@@ -369,7 +384,7 @@
             pltpu.VMEM((len(blocks) * rows, 3 * half), jnp.bfloat16),
             pltpu.SemaphoreType.DMA((len(blocks),)),
         ],
-        mib=14,
+        mib=52,
     )
 
 
@@ -393,7 +408,7 @@
             pltpu.SemaphoreType.DMA((max(len(late), 1),)),
             pltpu.SemaphoreType.DMA((blocks,)),
         ],
-        mib=14,
+        mib=52,
     )
 
 
@@ -414,7 +429,6 @@
     wo,
 ):
     group = lax.axis_index("grp")
-    encoder = group == 0
     rows_here, width = hidden.shape[1:]
     half = wq.shape[1] // lax.axis_size("grp")
     targets = min(rows_here, -(-TGT_TOTAL // 16) * 16)
@@ -442,13 +456,18 @@
 
     seg_q = positions(tgt_len[0], targets)
     seg_k = positions(src_len[0], rows_here)
-    valid = (seg_q < SENT)[:, None]
     sums = project(order, memory, target, early)
     own, sent = attend(order, seg_q, seg_k, memory, target, sums, early, late)
-    total = own + lax.ppermute(sent, "grp", [(0, 1)]).astype(jnp.float32)
-    attended = jnp.pad(jnp.where(valid, total, 0.0), ((0, rows_here - targets), (0, 0)))
-    decoded = (mixed + attended).astype(jnp.bfloat16)
-    return jnp.where(encoder, memory, decoded)[None]
+    received = lax.ppermute(sent, "grp", [(0, 1)])
+    (out,) = local(
+        finish_kernel,
+        "finish",
+        [((rows_here, width), jnp.bfloat16)],
+        (memory, mixed, own, received, (seg_q < SENT).astype(jnp.float32)[:, None]),
+        order=group[None],
+        mib=8,
+    )
+    return out[None]
 
 
 def solution(mesh):

time: 120 us -> 123 us (1.025)
  the two profiles are of different devices: /device:TPU:1 before, /device:TPU:29 now
where the time goes in v3:
time: 123 us; the launch traced here: 122 us
  starting transfers between devices  45.6 us (37%)
  waiting for transfers between devices  35.8 us (29%)
  Pallas kernels  20.6 us (17%)
  local copies, waits for them, and re-layouts  18.8 us (15%)
    ppermute x15, waiting for transfers between devices, moved(): return lax.ppermute(value, 'ep', pairs)  32.5 us
    pallas_call x11, Pallas kernels, local(): pl.pallas_call(run, out_shape=[jax.ShapeDtypeStruct(shape, dtype) for sha...  20.6 us
    unnamed x54, local copies, waits for them, and re-layouts  15.6 us
    ppermute x15, starting transfers between devices, moved(): return lax.ppermute(value, 'ep', pairs)  14.1 us
    ppermute x1, starting transfers between devices, both_norms(): other_rows = lax.ppermute(rows, 'grp', swap)  13.8 us
    all_to_all x2, starting transfers between devices, exchanged(): parts = lax.all_to_all(parts, 'ep', split_axis=0, concat_axis=0, tiled=True)  12.9 us
    ppermute x1, starting transfers between devices, body(): other_hidden = lax.ppermute(hidden[0], 'grp', [(0, 1), (1, 0)])  3.43 us
    ppermute x1, waiting for transfers between devices, body(): received = lax.ppermute(sent, 'grp', [(0, 1)])  2.98 us
  transfers between devices with their start and end apart: 21, of which 6 were waited for; matrix products, arithmetic and copies ran while one was open for 2% of the time, Pallas kernels for 10%

profile of v3, /device:TPU:29, one launch (start us, length us, event | category | flops | bytes accessed | tf_op | source)
XLA Modules:
  0.0 122.3 jit_solution(7754599248171470684)
XLA Ops:
  0.0 1.0 constant_dynamic-slice_fusion
  1.0 1.0 constant_dynamic-slice_fusion.2
  2.1 1.3 %collective-permute-start = (bf16[128,2048]{1,0:T(8,128)(2,1)S(1)}, bf16[128,2048]{1,0:T(8,128)(2,1)S(1)}, u32[]{:S(2)}, u32[]{:S(2)}) collective-permute-start(bf16[128,2048]{1,0:T(8,128)(2,1)S(1)} %pad_maximum_fusion.refs_3_.refs_7_), channel_id=1, source_target_pairs={{0,1},{1,0},{2,3},{3,2},{4,5},{5,4},{6,7},{7,6},{8,9},{9,8},{10,11... | collective-permute-start | bytes 1572872 | tf_op jit(solution)/shard_map/ppermute | solution.py:62
  3.3 0.2 collective-permute-start.2
  3.6 0.7 fusion.2
  4.3 1.2 copy-done.15
  5.5 1.0 copy-done.21
  6.5 0.7 copy-done.24
  7.2 0.7 pack.1
  8.0 0.8 copy-done.22
  8.7 6.2 %all-to-all-start = ((bf16[16,8,2048]{2,1,0:T(8,128)(2,1)}), bf16[16,8,2048]{2,1,0:T(8,128)(2,1)}, u32[]{:S(2)}, u32[]{:S(2)}) async-start(bf16[16,8,2048]{2,1,0:T(8,128)(2,1)} %bitcast.42), calls=%async_computation | async-start | bytes 1048576 | tf_op jit(solution)/shard_map/all_to_all | solution.py:200
  15.0 0.8 collective-permute-done.1.refs_1_
  15.8 0.2 collective-permute-start.3
  16.0 1.9 %collective-permute-start.4 = (bf16[128,2048]{1,0:T(8,128)(2,1)S(1)}, bf16[128,2048]{1,0:T(8,128)(2,1)S(1)}, u32[]{:S(2)}, u32[]{:S(2)}) collective-permute-start(bf16[128,2048]{1,0:T(8,128)(2,1)S(1)} %get-tuple-element.27.refs_1_), channel_id=1, source_target_pairs={{0,4},{1,5},{2,6},{3,7},{4,8},{5,9},{6,10},{7,11},{8,12},{9,13},{1... | collective-permute-start | bytes 1572872 | tf_op jit(solution)/shard_map/ppermute | solution.py:62
  17.9 0.5 collective-permute-start.5
  18.4 15.0 %collective-permute-done.3.refs_0_.refs_10_.refs_14_ = bf16[128,2048]{1,0:T(8,128)(2,1)S(1)} collective-permute-done((bf16[128,2048]{1,0:T(8,128)(2,1)S(1)}, bf16[128,2048]{1,0:T(8,128)(2,1)S(1)}, u32[]{:S(2)}, u32[]{:S(2)}) %collective-permute-start.3) | collective-permute-done | bytes 524320 | tf_op jit(solution)/shard_map/ppermute | solution.py:62
  33.5 2.4 %collective-permute-done.4.refs_2_ = bf16[128,2048]{1,0:T(8,128)(2,1)S(1)} collective-permute-done((bf16[128,2048]{1,0:T(8,128)(2,1)S(1)}, bf16[128,2048]{1,0:T(8,128)(2,1)S(1)}, u32[]{:S(2)}, u32[]{:S(2)}) %collective-permute-start.4) | collective-permute-done | bytes 524320 | tf_op jit(solution)/shard_map/ppermute | solution.py:62
  35.9 0.5 collective-permute-start.6
  36.5 2.5 %collective-permute-start.8 = (bf16[128,2048]{1,0:T(8,128)(2,1)S(1)}, bf16[128,2048]{1,0:T(8,128)(2,1)S(1)}, u32[]{:S(2)}, u32[]{:S(2)}) collective-permute-start(bf16[128,2048]{1,0:T(8,128)(2,1)S(1)} %get-tuple-element.29.refs_3_.refs_2_), channel_id=1, source_target_pairs={{0,4},{1,5},{2,6},{3,7},{4,8},{5,9},{6,10},{7,11},{8,12},{9,13},{1... | collective-permute-start | bytes 1572872 | tf_op jit(solution)/shard_map/ppermute | solution.py:62
  39.0 2.2 %copy-done.13 = bf16[1,2048,1024]{2,1,0:T(8,128)(2,1)S(1)} copy-done((bf16[1,2048,1024]{2,1,0:T(8,128)(2,1)S(1)}, bf16[1,2048,1024]{2,1,0:T(8,128)(2,1)}, u32[]{:S(2)}) %copy-start.13) | copy-done | bytes 4194328
  41.2 2.2 %copy-done.14 = bf16[1,1024,2048]{2,1,0:T(8,128)(2,1)S(1)} copy-done((bf16[1,1024,2048]{2,1,0:T(8,128)(2,1)S(1)}, bf16[1,1024,2048]{2,1,0:T(8,128)(2,1)}, u32[]{:S(2)}) %copy-start.14) | copy-done | bytes 4194328
  43.4 2.4 %mlp.1 = bf16[128,2048]{1,0:T(8,128)(2,1)S(1)} custom-call(bf16[128,2048]{1,0:T(8,128)(2,1)} %bitcast.7.refs_0_, bf16[2048,1024]{1,0:T(8,128)(2,1)S(1)} %bitcast.35, bf16[1024,2048]{1,0:T(8,128)(2,1)S(1)} %bitcast.36, bf16[128,2048]{1,0:T(8,128)(2,1)S(1)} %get-tuple-element.29.refs_3_.refs_2_), custom_call_target="tpu_custom_call" | custom-call | tf_op jit(solution)/shard_map/mlp/pallas_call | solution.py:83
  45.8 0.8 copy-done.18
  46.6 6.7 %all-to-all-start.1 = ((bf16[16,8,2048]{2,1,0:T(8,128)(2,1)}), bf16[16,8,2048]{2,1,0:T(8,128)(2,1)}, u32[]{:S(2)}, u32[]{:S(2)}) async-start(bf16[16,8,2048]{2,1,0:T(8,128)(2,1)} %bitcast.40), calls=%async_computation.1 | async-start | bytes 1048576 | tf_op jit(solution)/shard_map/all_to_all | solution.py:200
  53.3 0.3 collective-permute-start.9
  53.8 0.3 copy-done.6
  54.0 1.2 collective-permute-start.11
  55.2 3.4 %collective-permute-start.12 = (bf16[256,2048]{1,0:T(8,128)(2,1)}, bf16[256,2048]{1,0:T(8,128)(2,1)}, u32[]{:S(2)}, u32[]{:S(2)}) collective-permute-start(bf16[256,2048]{1,0:T(8,128)(2,1)} %bitcast.37), channel_id=1, source_target_pairs={{0,16},{16,0},{1,17},{17,1},{2,18},{18,2},{3,19},{19,3},{4,20},{20... | collective-permute-start | bytes 3145736 | tf_op jit(solution)/shard_map/ppermute | solution.py:442
  58.8 14.2 %collective-permute-done.9.refs_0_.refs_14_.refs_18_ = bf16[128,2048]{1,0:T(8,128)(2,1)S(1)} collective-permute-done((bf16[128,2048]{1,0:T(8,128)(2,1)S(1)}, bf16[128,2048]{1,0:T(8,128)(2,1)S(1)}, u32[]{:S(2)}, u32[]{:S(2)}) %collective-permute-start.9) | collective-permute-done | bytes 524320 | tf_op jit(solution)/shard_map/ppermute | solution.py:62
  73.1 1.2 %collective-permute-start.15 = (bf16[128,2048]{1,0:T(8,128)(2,1)S(1)}, bf16[128,2048]{1,0:T(8,128)(2,1)}, u32[]{:S(2)}, u32[]{:S(2)}) collective-permute-start(bf16[128,2048]{1,0:T(8,128)(2,1)S(1)} %get-tuple-element.39.refs_6_.refs_10_), channel_id=1, source_target_pairs={{0,1},{1,0},{2,3},{3,2},{4,5},{5,4},{6,7},{7,6},{8,9},{9,8},{10,11... | collective-permute-start | bytes 1572872 | tf_op jit(solution)/shard_map/ppermute | solution.py:62
  74.3 3.5 %collective-permute-start.16 = (bf16[128,2048]{1,0:T(8,128)(2,1)S(1)}, bf16[128,2048]{1,0:T(8,128)(2,1)}, u32[]{:S(2)}, u32[]{:S(2)}) collective-permute-start(bf16[128,2048]{1,0:T(8,128)(2,1)S(1)} %get-tuple-element.40.refs_13_.refs_17_), channel_id=1, source_target_pairs={{0,12},{1,13},{2,14},{3,15},{4,0},{5,1},{6,2},{7,3},{8,4},{9,5},{1... | collective-permute-start | bytes 1572872 | tf_op jit(solution)/shard_map/ppermute | solution.py:62
  77.8 0.5 collective-permute-start.17
  79.1 1.1 rows.1.refs_3_
  80.3 13.8 %collective-permute-start.14 = (f32[16,2048]{1,0:T(8,128)S(1)}, f32[16,2048]{1,0:T(8,128)}, u32[]{:S(2)}, u32[]{:S(2)}) collective-permute-start(f32[16,2048]{1,0:T(8,128)S(1)} %rows.1.refs_3_), channel_id=1, source_target_pairs={{0,16},{16,0},{1,17},{17,1},{2,18},{18,2},{3,19},{19,3},{4,20},{20... | collective-permute-start | bytes 393224 | tf_op jit(solution)/shard_map/ppermute | solution.py:232
  94.1 0.8 copy.35.refs_6_
  94.9 0.3 collective-permute-done.14.refs_7_
  95.2 1.2 copy-done.16
  96.4 0.9 copy-done.20
  97.3 2.9 %norm.1 = (bf16[256,2048]{1,0:T(8,128)(2,1)S(1)}, bf16[176,2048]{1,0:T(8,128)(2,1)S(1)}, f32[256,2048]{1,0:T(8,128)S(1)}) custom-call(s32[1]{0:T(128)} %bitcast.refs_0_, bf16[256,2048]{1,0:T(8,128)(2,1)S(1)} %bitcast.39, f32[256,1]{1,0:T(8,128)S(1)} %copy.34.refs_2_, f32[16,2048]{1,0:T(8,128)S(1)} %rows.1.refs_3_, f32[1,2048]{1,0:T(1,128)S(1)} %copy-done.23, ...), custom_call_target="tpu_custom_call" | custom-call | tf_op jit(solution)/shard_map/norm/pallas_call | solution.py:83
  100.2 1.0 copy-done.1
  101.2 0.9 copy-done.17
  102.0 1.0 copy-done.11
  103.1 5.2 %project.1 = (f32[256,1024]{1,0:T(8,128)}, f32[176,512]{1,0:T(8,128)S(1)}) custom-call(s32[16]{0:T(128)S(1)} %stack.67.refs_0_, bf16[256,2048]{1,0:T(8,128)(2,1)} %copy-done.1, bf16[176,2048]{1,0:T(8,128)(2,1)} %copy-done.17, bf16[128,2048]{1,0:T(8,128)(2,1)S(1)} %copy-done.11, bf16[128,2048]{1,0:T(8,128)(2,1)S(1)} %get-tuple-element.30.refs_4_.refs_8_, ...), custom_call_target="tpu_custom_call" | custom-call | tf_op jit(solution)/shard_map/project/pallas_call | solution.py:83
  108.3 6.8 %attend.1 = (f32[176,2048]{1,0:T(8,128)}, bf16[176,2048]{1,0:T(8,128)(2,1)}) custom-call(s32[16]{0:T(128)S(1)} %stack.67.refs_0_, s32[176,1]{1,0:T(8,128)S(1)} %copy.36.refs_1_, s32[1,256]{1,0:T(1,128)S(1)} %bitcast.46, bf16[256,2048]{1,0:T(8,128)(2,1)} %copy-done.1, bf16[176,2048]{1,0:T(8,128)(2,1)} %copy-done.17, f32[256,1024]{1,0:T(8,128)} %get-tuple-element.41.refs_5_, ...), custom_call_target="tpu_custom_call" | custom-call | tf_op jit(solution)/shard_map/attend/pallas_call | solution.py:83
  115.1 1.3 %collective-permute-start.18 = (bf16[176,2048]{1,0:T(8,128)(2,1)}, bf16[176,2048]{1,0:T(8,128)(2,1)S(1)}, u32[]{:S(2)}, u32[]{:S(2)}) collective-permute-start(bf16[176,2048]{1,0:T(8,128)(2,1)} %get-tuple-element.44), channel_id=1, source_target_pairs={{0,16},{1,17},{2,18},{3,19},{4,20},{5,21},{6,22},{7,23},{8,24},{9,... | collective-permute-start | bytes 2162696 | tf_op jit(solution)/shard_map/ppermute | solution.py:461
  116.4 3.0 %collective-permute-done.18.refs_4_ = bf16[176,2048]{1,0:T(8,128)(2,1)S(1)} collective-permute-done((bf16[176,2048]{1,0:T(8,128)(2,1)}, bf16[176,2048]{1,0:T(8,128)(2,1)S(1)}, u32[]{:S(2)}, u32[]{:S(2)}) %collective-permute-start.18) | collective-permute-done | bytes 720928 | tf_op jit(solution)/shard_map/ppermute | solution.py:461
  119.4 1.4 %copy-done.19 = f32[176,2048]{1,0:T(8,128)S(1)} copy-done((f32[176,2048]{1,0:T(8,128)S(1)}, f32[176,2048]{1,0:T(8,128)}, u32[]{:S(2)}) %copy-start.19) | copy-done | bytes 1441816
  120.8 1.5 %finish.1 = bf16[256,2048]{1,0:T(8,128)(2,1)} custom-call(s32[1]{0:T(128)} %bitcast.refs_0_, bf16[256,2048]{1,0:T(8,128)(2,1)S(1)} %copy-done.2, f32[256,2048]{1,0:T(8,128)S(1)} %get-tuple-element.37.refs_2_, f32[176,2048]{1,0:T(8,128)S(1)} %copy-done.19, bf16[176,2048]{1,0:T(8,128)(2,1)S(1)} %collective-permute-done.18.refs_4_, ...), custom_call_target="tpu_custom_call" | custom-call | tf_op jit(solution)/shard_map/finish/pallas_call | solution.py:83
  (77 shorter events, 1.2 us)
Async XLA Ops:
  2.0 33.8 %copy-start.10 = (bf16[128,2048]{1,0:T(8,128)(2,1)}, bf16[128,2048]{1,0:T(8,128)(2,1)S(1)}, u32[]{:S(2)}) copy-start(bf16[128,2048]{1,0:T(8,128)(2,1)S(1)} %pad_maximum_fusion.refs_3_.refs_7_) | copy-start | bytes 1572868
  2.1 12.9 %collective-permute-start = (bf16[128,2048]{1,0:T(8,128)(2,1)S(1)}, bf16[128,2048]{1,0:T(8,128)(2,1)S(1)}, u32[]{:S(2)}, u32[]{:S(2)}) collective-permute-start(bf16[128,2048]{1,0:T(8,128)(2,1)S(1)} %pad_maximum_fusion.refs_3_.refs_7_), channel_id=1, source_target_pairs={{0,1},{1,0},{2,3},{3,2},{4,5},{5,4},{6,7},{7,6},{8,9},{9,8},{10,11... | collective-permute-start | bytes 1572872 | tf_op jit(solution)/shard_map/ppermute | solution.py:62
  3.3 12.5 %collective-permute-start.1 = (bf16[128,2048]{1,0:T(8,128)(2,1)S(1)}, bf16[128,2048]{1,0:T(8,128)(2,1)S(1)}, u32[]{:S(2)}, u32[]{:S(2)}) collective-permute-start(bf16[128,2048]{1,0:T(8,128)(2,1)S(1)} %pad_maximum_fusion.refs_3_.refs_7_), channel_id=1, source_target_pairs={{0,4},{1,5},{2,6},{3,7},{4,8},{5,9},{6,10},{7,11},{8,12},{9,13},{1... | collective-permute-start | bytes 1572872 | tf_op jit(solution)/shard_map/ppermute | solution.py:62
  3.3 12.5 %collective-permute-start.2 = (bf16[128,2048]{1,0:T(8,128)(2,1)S(1)}, bf16[128,2048]{1,0:T(8,128)(2,1)S(1)}, u32[]{:S(2)}, u32[]{:S(2)}) collective-permute-start(bf16[128,2048]{1,0:T(8,128)(2,1)S(1)} %pad_maximum_fusion.refs_3_.refs_7_), channel_id=1, source_target_pairs={{0,2},{1,3},{2,0},{3,1},{4,6},{5,7},{6,4},{7,5},{8,10},{9,11},{10,... | collective-permute-start | bytes 1572872 | tf_op jit(solution)/shard_map/ppermute | solution.py:62
  4.3 1.2 %copy-start.15 = (bf16[1,256,2048]{2,1,0:T(8,128)(2,1)S(1)}, bf16[1,256,2048]{2,1,0:T(8,128)(2,1)}, u32[]{:S(2)}) copy-start(bf16[1,256,2048]{2,1,0:T(8,128)(2,1)} %param.14) | copy-start | bytes 3145732
  5.5 1.0 copy-start.21
  6.5 0.7 copy-start.24
  7.9 0.8 copy-start.22
  8.7 30.2 %all-to-all-start = ((bf16[16,8,2048]{2,1,0:T(8,128)(2,1)}), bf16[16,8,2048]{2,1,0:T(8,128)(2,1)}, u32[]{:S(2)}, u32[]{:S(2)}) async-start(bf16[16,8,2048]{2,1,0:T(8,128)(2,1)} %bitcast.42), calls=%async_computation | async-start | bytes 1048576 | tf_op jit(solution)/shard_map/all_to_all | solution.py:200
  15.0 30.8 %copy-start.5 = (bf16[128,2048]{1,0:T(8,128)(2,1)}, bf16[128,2048]{1,0:T(8,128)(2,1)S(1)}, u32[]{:S(2)}) copy-start(bf16[128,2048]{1,0:T(8,128)(2,1)S(1)} %collective-permute-done.refs_0_.refs_7_.refs_11_) | copy-start | bytes 1572868
  15.8 20.6 %copy-start.9 = (bf16[128,2048]{1,0:T(8,128)(2,1)}, bf16[128,2048]{1,0:T(8,128)(2,1)S(1)}, u32[]{:S(2)}) copy-start(bf16[128,2048]{1,0:T(8,128)(2,1)S(1)} %get-tuple-element.28.refs_9_.refs_13_) | copy-start | bytes 1572868
  15.8 17.6 %collective-permute-start.3 = (bf16[128,2048]{1,0:T(8,128)(2,1)S(1)}, bf16[128,2048]{1,0:T(8,128)(2,1)S(1)}, u32[]{:S(2)}, u32[]{:S(2)}) collective-permute-start(bf16[128,2048]{1,0:T(8,128)(2,1)S(1)} %get-tuple-element.27.refs_1_), channel_id=1, source_target_pairs={{0,2},{1,3},{2,0},{3,1},{4,6},{5,7},{6,4},{7,5},{8,10},{9,11},{10,... | collective-permute-start | bytes 1572872 | tf_op jit(solution)/shard_map/ppermute | solution.py:62
  16.0 19.8 %collective-permute-start.4 = (bf16[128,2048]{1,0:T(8,128)(2,1)S(1)}, bf16[128,2048]{1,0:T(8,128)(2,1)S(1)}, u32[]{:S(2)}, u32[]{:S(2)}) collective-permute-start(bf16[128,2048]{1,0:T(8,128)(2,1)S(1)} %get-tuple-element.27.refs_1_), channel_id=1, source_target_pairs={{0,4},{1,5},{2,6},{3,7},{4,8},{5,9},{6,10},{7,11},{8,12},{9,13},{1... | collective-permute-start | bytes 1572872 | tf_op jit(solution)/shard_map/ppermute | solution.py:62
  17.9 18.0 %collective-permute-start.5 = (bf16[128,2048]{1,0:T(8,128)(2,1)S(1)}, bf16[128,2048]{1,0:T(8,128)(2,1)S(1)}, u32[]{:S(2)}, u32[]{:S(2)}) collective-permute-start(bf16[128,2048]{1,0:T(8,128)(2,1)S(1)} %get-tuple-element.28.refs_9_.refs_13_), channel_id=1, source_target_pairs={{0,1},{1,0},{2,3},{3,2},{4,5},{5,4},{6,7},{7,6},{8,9},{9,8},{10,11... | collective-permute-start | bytes 1572872 | tf_op jit(solution)/shard_map/ppermute | solution.py:62
  33.5 3.0 %copy-start.12 = (bf16[128,2048]{1,0:T(8,128)(2,1)}, bf16[128,2048]{1,0:T(8,128)(2,1)S(1)}, u32[]{:S(2)}) copy-start(bf16[128,2048]{1,0:T(8,128)(2,1)S(1)} %collective-permute-done.3.refs_0_.refs_10_.refs_14_) | copy-start | bytes 1572868
  35.9 17.4 %collective-permute-start.6 = (bf16[128,2048]{1,0:T(8,128)(2,1)S(1)}, bf16[128,2048]{1,0:T(8,128)(2,1)S(1)}, u32[]{:S(2)}, u32[]{:S(2)}) collective-permute-start(bf16[128,2048]{1,0:T(8,128)(2,1)S(1)} %get-tuple-element.30.refs_4_.refs_8_), channel_id=1, source_target_pairs={{0,1},{1,0},{2,3},{3,2},{4,5},{5,4},{6,7},{7,6},{8,9},{9,8},{10,11... | collective-permute-start | bytes 1572872 | tf_op jit(solution)/shard_map/ppermute | solution.py:62
  36.4 16.9 %collective-permute-start.7 = (bf16[128,2048]{1,0:T(8,128)(2,1)S(1)}, bf16[128,2048]{1,0:T(8,128)(2,1)}, u32[]{:S(2)}, u32[]{:S(2)}) collective-permute-start(bf16[128,2048]{1,0:T(8,128)(2,1)S(1)} %get-tuple-element.29.refs_3_.refs_2_), channel_id=1, source_target_pairs={{0,2},{1,3},{2,0},{3,1},{4,6},{5,7},{6,4},{7,5},{8,10},{9,11},{10,... | collective-permute-start | bytes 1572872 | tf_op jit(solution)/shard_map/ppermute | solution.py:62
  36.5 16.8 %collective-permute-start.8 = (bf16[128,2048]{1,0:T(8,128)(2,1)S(1)}, bf16[128,2048]{1,0:T(8,128)(2,1)S(1)}, u32[]{:S(2)}, u32[]{:S(2)}) collective-permute-start(bf16[128,2048]{1,0:T(8,128)(2,1)S(1)} %get-tuple-element.29.refs_3_.refs_2_), channel_id=1, source_target_pairs={{0,4},{1,5},{2,6},{3,7},{4,8},{5,9},{6,10},{7,11},{8,12},{9,13},{1... | collective-permute-start | bytes 1572872 | tf_op jit(solution)/shard_map/ppermute | solution.py:62
  39.0 2.2 %copy-start.13 = (bf16[1,2048,1024]{2,1,0:T(8,128)(2,1)S(1)}, bf16[1,2048,1024]{2,1,0:T(8,128)(2,1)}, u32[]{:S(2)}) copy-start(bf16[1,2048,1024]{2,1,0:T(8,128)(2,1)} %param.18) | copy-start | bytes 12582916
  41.2 2.2 %copy-start.14 = (bf16[1,1024,2048]{2,1,0:T(8,128)(2,1)S(1)}, bf16[1,1024,2048]{2,1,0:T(8,128)(2,1)}, u32[]{:S(2)}) copy-start(bf16[1,1024,2048]{2,1,0:T(8,128)(2,1)} %param.19) | copy-start | bytes 12582916
  43.4 15.3 %copy-start.23 = (f32[1,2048]{1,0:T(1,128)S(1)}, f32[1,2048]{1,0:T(1,128)}, u32[]{:S(2)}) copy-start(f32[1,2048]{1,0:T(1,128)} %refs_4_.1) | copy-start | bytes 24580
  43.4 15.4 %copy-start.25 = (s32[1,4]{1,0:T(1,128)S(1)}, s32[1,4]{1,0:T(1,128)}, u32[]{:S(2)}) copy-start(s32[1,4]{1,0:T(1,128)} %param.23) | copy-start | bytes 52
  45.8 0.8 copy-start.18
  46.6 31.9 %copy-start.26 = (s32[1,4]{1,0:T(1,128)S(1)}, s32[1,4]{1,0:T(1,128)}, u32[]{:S(2)}) copy-start(s32[1,4]{1,0:T(1,128)} %param.22) | copy-start | bytes 52
  46.6 32.6 %all-to-all-start.1 = ((bf16[16,8,2048]{2,1,0:T(8,128)(2,1)}), bf16[16,8,2048]{2,1,0:T(8,128)(2,1)}, u32[]{:S(2)}, u32[]{:S(2)}) async-start(bf16[16,8,2048]{2,1,0:T(8,128)(2,1)} %bitcast.40), calls=%async_computation.1 | async-start | bytes 1048576 | tf_op jit(solution)/shard_map/all_to_all | solution.py:200
  53.2 0.8 copy-start.6
  53.3 19.8 %collective-permute-start.9 = (bf16[128,2048]{1,0:T(8,128)(2,1)S(1)}, bf16[128,2048]{1,0:T(8,128)(2,1)S(1)}, u32[]{:S(2)}, u32[]{:S(2)}) collective-permute-start(bf16[128,2048]{1,0:T(8,128)(2,1)S(1)} %get-tuple-element.32.refs_3_), channel_id=1, source_target_pairs={{0,4},{1,5},{2,6},{3,7},{4,8},{5,9},{6,10},{7,11},{8,12},{9,13},{1... | collective-permute-start | bytes 1572872 | tf_op jit(solution)/shard_map/ppermute | solution.py:62
  53.6 19.4 %collective-permute-start.10 = (bf16[128,2048]{1,0:T(8,128)(2,1)S(1)}, bf16[128,2048]{1,0:T(8,128)(2,1)S(1)}, u32[]{:S(2)}, u32[]{:S(2)}) collective-permute-start(bf16[128,2048]{1,0:T(8,128)(2,1)S(1)} %get-tuple-element.33.refs_2_), channel_id=1, source_target_pairs={{0,2},{1,3},{2,0},{3,1},{4,6},{5,7},{6,4},{7,5},{8,10},{9,11},{10,... | collective-permute-start | bytes 1572872 | tf_op jit(solution)/shard_map/ppermute | solution.py:62
  54.0 19.0 %collective-permute-start.11 = (bf16[128,2048]{1,0:T(8,128)(2,1)S(1)}, bf16[128,2048]{1,0:T(8,128)(2,1)S(1)}, u32[]{:S(2)}, u32[]{:S(2)}) collective-permute-start(bf16[128,2048]{1,0:T(8,128)(2,1)S(1)} %get-tuple-element.34.refs_5_.refs_9_), channel_id=1, source_target_pairs={{0,1},{1,0},{2,3},{3,2},{4,5},{5,4},{6,7},{7,6},{8,9},{9,8},{10,11... | collective-permute-start | bytes 1572872 | tf_op jit(solution)/shard_map/ppermute | solution.py:62
  55.2 39.6 %collective-permute-start.12 = (bf16[256,2048]{1,0:T(8,128)(2,1)}, bf16[256,2048]{1,0:T(8,128)(2,1)}, u32[]{:S(2)}, u32[]{:S(2)}) collective-permute-start(bf16[256,2048]{1,0:T(8,128)(2,1)} %bitcast.37), channel_id=1, source_target_pairs={{0,16},{16,0},{1,17},{17,1},{2,18},{18,2},{3,19},{19,3},{4,20},{20... | collective-permute-start | bytes 3145736 | tf_op jit(solution)/shard_map/ppermute | solution.py:442
  58.7 21.6 %collective-permute-start.13 = (f32[2,2048]{1,0:T(2,128)S(1)}, f32[2,2048]{1,0:T(2,128)S(1)}, u32[]{:S(2)}, u32[]{:S(2)}) collective-permute-start(f32[2,2048]{1,0:T(2,128)S(1)} %fusion), channel_id=1, source_target_pairs={{0,16},{16,0},{1,17},{17,1},{2,18},{18,2},{3,19},{19,3},{4,20},{20... | collective-permute-start | bytes 49160 | tf_op jit(solution)/shard_map/ppermute | solution.py:231
  73.0 29.0 %copy-start.7 = (bf16[128,2048]{1,0:T(8,128)(2,1)}, bf16[128,2048]{1,0:T(8,128)(2,1)S(1)}, u32[]{:S(2)}) copy-start(bf16[128,2048]{1,0:T(8,128)(2,1)S(1)} %collective-permute-done.9.refs_0_.refs_14_.refs_18_) | copy-start | bytes 1572868
  73.0 4.8 %copy-start.8 = (bf16[128,2048]{1,0:T(8,128)(2,1)}, bf16[128,2048]{1,0:T(8,128)(2,1)S(1)}, u32[]{:S(2)}) copy-start(bf16[128,2048]{1,0:T(8,128)(2,1)S(1)} %collective-permute-done.10.refs_1_.refs_12_.refs_16_) | copy-start | bytes 1572868
  73.1 29.0 %copy-start = (bf16[128,2048]{1,0:T(8,128)(2,1)}, bf16[128,2048]{1,0:T(8,128)(2,1)S(1)}, u32[]{:S(2)}) copy-start(bf16[128,2048]{1,0:T(8,128)(2,1)S(1)} %get-tuple-element.40.refs_13_.refs_17_) | copy-start | bytes 1572868
  73.1 29.0 %copy-start.3 = (bf16[128,2048]{1,0:T(8,128)(2,1)}, bf16[128,2048]{1,0:T(8,128)(2,1)S(1)}, u32[]{:S(2)}) copy-start(bf16[128,2048]{1,0:T(8,128)(2,1)S(1)} %get-tuple-element.39.refs_6_.refs_10_) | copy-start | bytes 1572868
  73.1 28.9 %copy-start.4 = (bf16[128,2048]{1,0:T(8,128)(2,1)}, bf16[128,2048]{1,0:T(8,128)(2,1)S(1)}, u32[]{:S(2)}) copy-start(bf16[128,2048]{1,0:T(8,128)(2,1)S(1)} %get-tuple-element.35.refs_2_.refs_15_.refs_19_) | copy-start | bytes 1572868
  73.1 35.1 %collective-permute-start.15 = (bf16[128,2048]{1,0:T(8,128)(2,1)S(1)}, bf16[128,2048]{1,0:T(8,128)(2,1)}, u32[]{:S(2)}, u32[]{:S(2)}) collective-permute-start(bf16[128,2048]{1,0:T(8,128)(2,1)S(1)} %get-tuple-element.39.refs_6_.refs_10_), channel_id=1, source_target_pairs={{0,1},{1,0},{2,3},{3,2},{4,5},{5,4},{6,7},{7,6},{8,9},{9,8},{10,11... | collective-permute-start | bytes 1572872 | tf_op jit(solution)/shard_map/ppermute | solution.py:62
  74.3 33.9 %collective-permute-start.16 = (bf16[128,2048]{1,0:T(8,128)(2,1)S(1)}, bf16[128,2048]{1,0:T(8,128)(2,1)}, u32[]{:S(2)}, u32[]{:S(2)}) collective-permute-start(bf16[128,2048]{1,0:T(8,128)(2,1)S(1)} %get-tuple-element.40.refs_13_.refs_17_), channel_id=1, source_target_pairs={{0,12},{1,13},{2,14},{3,15},{4,0},{5,1},{6,2},{7,3},{8,4},{9,5},{1... | collective-permute-start | bytes 1572872 | tf_op jit(solution)/shard_map/ppermute | solution.py:62
  77.8 30.4 %collective-permute-start.17 = (bf16[128,2048]{1,0:T(8,128)(2,1)S(1)}, bf16[128,2048]{1,0:T(8,128)(2,1)}, u32[]{:S(2)}, u32[]{:S(2)}) collective-permute-start(bf16[128,2048]{1,0:T(8,128)(2,1)S(1)} %get-tuple-element.35.refs_2_.refs_15_.refs_19_), channel_id=1, source_target_pairs={{0,2},{1,3},{2,0},{3,1},{4,6},{5,7},{6,4},{7,5},{8,10},{9,11},{10,... | collective-permute-start | bytes 1572872 | tf_op jit(solution)/shard_map/ppermute | solution.py:62
  80.3 14.9 %collective-permute-start.14 = (f32[16,2048]{1,0:T(8,128)S(1)}, f32[16,2048]{1,0:T(8,128)}, u32[]{:S(2)}, u32[]{:S(2)}) collective-permute-start(f32[16,2048]{1,0:T(8,128)S(1)} %rows.1.refs_3_), channel_id=1, source_target_pairs={{0,16},{16,0},{1,17},{17,1},{2,18},{18,2},{3,19},{19,3},{4,20},{20... | collective-permute-start | bytes 393224 | tf_op jit(solution)/shard_map/ppermute | solution.py:232
  95.2 1.2 %copy-start.16 = (bf16[1,256,2048]{2,1,0:T(8,128)(2,1)S(1)}, bf16[1,256,2048]{2,1,0:T(8,128)(2,1)}, u32[]{:S(2)}) copy-start(bf16[1,256,2048]{2,1,0:T(8,128)(2,1)} %param.14) | copy-start | bytes 3145732
  96.4 0.9 copy-start.20
  100.2 1.0 copy-start.1
  101.2 0.9 copy-start.17
  102.0 1.0 copy-start.11
  108.3 11.1 %copy-start.2 = (bf16[256,2048]{1,0:T(8,128)(2,1)S(1)}, bf16[256,2048]{1,0:T(8,128)(2,1)}, u32[]{:S(2)}) copy-start(bf16[256,2048]{1,0:T(8,128)(2,1)} %copy-done.1) | copy-start | bytes 3145732
  115.1 4.3 %collective-permute-start.18 = (bf16[176,2048]{1,0:T(8,128)(2,1)}, bf16[176,2048]{1,0:T(8,128)(2,1)S(1)}, u32[]{:S(2)}, u32[]{:S(2)}) collective-permute-start(bf16[176,2048]{1,0:T(8,128)(2,1)} %get-tuple-element.44), channel_id=1, source_target_pairs={{0,16},{1,17},{2,18},{3,19},{4,20},{5,21},{6,22},{7,23},{8,24},{9,... | collective-permute-start | bytes 2162696 | tf_op jit(solution)/shard_map/ppermute | solution.py:461
  119.4 1.4 %copy-start.19 = (f32[176,2048]{1,0:T(8,128)S(1)}, f32[176,2048]{1,0:T(8,128)}, u32[]{:S(2)}) copy-start(f32[176,2048]{1,0:T(8,128)} %get-tuple-element.43.refs_3_) | copy-start | bytes 4325380

commit v4 on v3

v4 whole, which is shorter than its diff:
```python
import functools

import jax
import jax.numpy as jnp
from jax import lax
from jax.experimental import pallas as pl
from jax.experimental.pallas import tpu as pltpu
from jax.sharding import PartitionSpec as P

HD = 128
SPLIT = 8
C = 6
PAD = 8
SENT = 4
TGT_TOTAL = 171
MIB = 1 << 20


def normalize(values, gain):
    mean = jnp.mean(values, -1, keepdims=True)
    centred = values - mean
    spread = jnp.mean(centred * centred, -1, keepdims=True)
    return centred * lax.rsqrt(spread + 1e-05) * gain


def positions(lengths, count):
    upto = jnp.arange(SENT)[:, None] <= jnp.arange(SENT)[None, :]
    ends = jnp.sum(jnp.where(upto, lengths[:, None], 0), axis=0)
    above = (jnp.arange(count, dtype=jnp.int32)[:, None] >= ends[None, :]).astype(jnp.int32)
    return jnp.sum(above, axis=1)


def dot(left, right):
    return jnp.dot(left, right, preferred_element_type=jnp.float32)


def dot_rows(left, right):
    return lax.dot_general(
        left, right, (((1,), (1,)), ((), ())), preferred_element_type=jnp.float32
    )


def chips():
    return (4, 2, 2) if lax.axis_size("ep") == 16 else None


def place_of(index):
    depth, high, wide = chips()
    return index // (high * wide), index // wide % high, index % wide


def index_of(z, y, x):
    depth, high, wide = chips()
    return (z % depth * high + y) * wide + x


def moved(value, dz=0, dy=0, dx=0):
    pairs = []
    for source in range(lax.axis_size("ep")):
        z, y, x = place_of(source)
        pairs.append((source, index_of(z + dz, y ^ dy, x ^ dx)))
    return lax.ppermute(value, "ep", pairs)


def local(kernel, name, outs, vmem, order=None, updated=(), after=(), onward=(), scratch=(), mib=6):
    scalars = () if order is None else (order,)
    read = len(scalars) + len(vmem)
    kept = (*updated, *onward)
    first = read + len(after)

    def run(*refs):
        results = refs[first + len(kept) :]
        changed = len(outs) + len(updated)
        kernel(*refs[:read], *results[:changed], *results[len(outs) + len(kept) :])

    def specs(vmem, anywhere):
        return [pl.BlockSpec(memory_space=pltpu.VMEM)] * vmem + [
            pl.BlockSpec(memory_space=pl.ANY)
        ] * anywhere

    inward = specs(len(vmem), len(after)) + specs(len(updated), len(onward))
    return pl.pallas_call(
        run,
        out_shape=[jax.ShapeDtypeStruct(shape, dtype) for shape, dtype in outs]
        + [jax.ShapeDtypeStruct(array.shape, array.dtype) for array in kept],
        in_specs=[pl.BlockSpec(memory_space=pltpu.SMEM)] * len(scalars) + inward,
        out_specs=specs(len(outs) + len(updated), len(onward)),
        scratch_shapes=list(scratch),
        input_output_aliases={first + i: len(outs) + i for i in range(len(kept))},
        compiler_params=pltpu.CompilerParams(vmem_limit_bytes=mib * MIB),
        name=name,
    )(*scalars, *vmem, *after, *kept)


def pack_kernel(experts, place, both, hidden, gain, router, gate, send):
    count = gate.shape[0]
    slot = lax.broadcasted_iota(jnp.int32, (count, hidden.shape[0]), 0)
    table = slot == place[...]
    rows = dot(table.astype(jnp.bfloat16), hidden[...])
    normed = normalize(rows, gain[...])
    send[...] = jnp.concatenate(
        [normed[e * PAD : (e + 1) * PAD] for e in experts], axis=0
    ).astype(jnp.bfloat16)
    logits = dot(normed.astype(jnp.bfloat16), router[...])
    mine = lax.broadcasted_iota(jnp.int32, (count, 1), 0) // PAD
    others = jnp.sum(jnp.where(table, both[...], 0), axis=1, keepdims=True) - mine
    expert = lax.broadcasted_iota(jnp.int32, logits.shape, 1)
    lead = jnp.where(expert == mine, logits, 0.0) - jnp.where(expert == others, logits, 0.0)
    gate[...] = 1.0 / (1.0 + jnp.exp(-jnp.sum(lead, axis=1, keepdims=True)))


def gate_kernel(*refs):
    pass


def mlp_kernel(rows, w_in, w_out, pieces):
    inner = jnp.maximum(dot(rows[...], w_in[...]), 0.0).astype(jnp.bfloat16)
    pieces[...] = dot(inner, w_out[...]).astype(jnp.bfloat16)


def rows_kernel(experts, gate, parts, rows):
    count = gate.shape[0]
    summed = [None] * (count // PAD)
    for i, e in enumerate(experts):
        part = parts[i * PAD : (i + 1) * PAD].astype(jnp.float32)
        summed[e] = part if summed[e] is None else summed[e] + part
    rows[...] = gate[...] * jnp.concatenate(summed, axis=0)


def mixed_rows(hidden, place, rows_ref):
    rows = rows_ref[...]
    count, size = rows.shape[0], hidden.shape[0]
    high = rows.astype(jnp.bfloat16)
    rest = rows - high.astype(jnp.float32)
    middle = rest.astype(jnp.bfloat16)
    low = (rest - middle.astype(jnp.float32)).astype(jnp.bfloat16)
    slot = lax.broadcasted_iota(jnp.int32, (size, 3 * count), 1) % count
    picks = (slot.astype(jnp.float32) == place[...]).astype(jnp.bfloat16)
    added = dot(picks, jnp.concatenate([high, middle, low], axis=0))
    return hidden[...].astype(jnp.float32) + added


def norm_kernel(group, *refs):
    own, other, (memory, target, mixed) = refs[:4], refs[4:8], refs[8:]

    def run(source, wanted):
        hidden, place, rows, gain = source
        values = mixed_rows(hidden, place, rows)
        memory[...] = normalize(values, gain[...]).astype(jnp.bfloat16)
        hidden, place, rows, gain = wanted
        mixed[...] = mixed_rows(hidden, place, rows)
        target[...] = normalize(mixed[: target.shape[0]], gain[...]).astype(jnp.bfloat16)

    pl.when(group[0] == 0)(lambda: run(own, other))
    pl.when(group[0] != 0)(lambda: run(other, own))


def places(routes, slots):
    return jnp.max(jnp.where(slots >= 0, routes * PAD + slots, -1), axis=1)


def expert_rows(hidden, norm_gain, router, w_in, w_out, routes, slots):
    experts = lax.axis_size("ep") // SPLIT
    count = experts * PAD
    width = hidden.shape[1]
    table = jnp.arange(count)[:, None] == places(routes, slots)[None, :]
    rows = dot(table.astype(jnp.bfloat16), hidden)
    normed = normalize(rows, norm_gain).astype(jnp.bfloat16)
    outgoing = jnp.broadcast_to(normed.reshape(experts, 1, PAD, width), (experts, SPLIT, PAD, width))
    arrived = lax.all_to_all(
        outgoing.reshape(experts * SPLIT, PAD, width), "ep", split_axis=0, concat_axis=0, tiled=True
    ).reshape(-1, width)
    inner = jax.nn.relu(dot(arrived, w_in)).astype(jnp.bfloat16)
    piece = dot(inner, w_out).astype(jnp.bfloat16)
    back = lax.all_to_all(
        piece.reshape(-1, PAD, width), "ep", split_axis=0, concat_axis=0, tiled=True
    )
    summed = jnp.sum(back.reshape(experts, SPLIT, PAD, width).astype(jnp.float32), axis=1)
    logits = dot(normed, router)
    mine = jnp.arange(count) // PAD
    both = jnp.sum(routes, axis=1)
    others = jnp.sum(jnp.where(table, both[None, :], 0), axis=1) - mine
    ids = jnp.arange(router.shape[1])[None, :]
    sign = (ids == mine[:, None]).astype(jnp.float32) - (ids == others[:, None]).astype(jnp.float32)
    gate = jax.nn.sigmoid(jnp.sum(logits * sign, axis=1, keepdims=True))
    return gate * summed.reshape(count, width)


def expert_layer(marks, hidden, norm_gain, router, w_in, w_out, routes, slots):
    devices = lax.axis_size("ep")
    held = [device // SPLIT for device in range(devices)]
    width = hidden.shape[1]

    def exchanged(values):
        parts = values.reshape(devices, PAD, width)
        parts = lax.all_to_all(parts, "ep", split_axis=0, concat_axis=0, tiled=True)
        return parts.reshape(values.shape)

    gate, send = local(
        functools.partial(pack_kernel, held),
        "pack",
        [((devices // SPLIT * PAD, 1), jnp.float32), ((devices * PAD, width), jnp.bfloat16)],
        (
            places(routes, slots)[None, :],
            jnp.sum(routes, axis=1)[None, :],
            hidden,
            norm_gain[None, :],
            router,
        ),
    )
    (pieces,) = local(
        mlp_kernel,
        "mlp",
        [(send.shape, jnp.bfloat16)],
        (exchanged(send), w_in, w_out),
        after=[marks[0]],
    )
    (rows,) = local(
        functools.partial(rows_kernel, held),
        "rows",
        [((gate.shape[0], width), jnp.float32)],
        (gate, exchanged(pieces)),
        after=[marks[1]],
    )
    return rows


def both_norms(hidden, others, small, final_gain, rows, targets):
    other_hidden, other_small = others
    other_rows = lax.ppermute(rows, "grp", [(0, 1), (1, 0)])
    size, width = hidden.shape
    own = (hidden, small[1, :size][:, None], rows, small[:1])
    other = (other_hidden, other_small[1, :size][:, None], other_rows, other_small[:1])
    return local(
        norm_kernel,
        "norm",
        [
            ((size, width), jnp.bfloat16),
            ((targets, width), jnp.bfloat16),
            ((size, width), jnp.float32),
        ],
        (*own, *other),
        order=lax.axis_index("grp")[None],
        mib=12,
    )


def collect_kernel(order, *refs):
    blocks, gathered = refs[:-1], refs[-1]
    rows = blocks[0].shape[0]
    for i, block in enumerate(blocks):
        gathered[pl.ds(pl.multiple_of(order[i] * rows, rows), rows)] = block[...]


def first_kernel(count, order, *refs):
    collect_kernel(order, *refs)
    gathered, rows = refs[-1], refs[0].shape[0]
    for i in range(count, order.shape[0]):
        empty = jnp.zeros((rows, gathered.shape[1]), gathered.dtype)
        gathered[pl.ds(pl.multiple_of(order[i] * rows, rows), rows)] = empty


def gather(part):
    z, y, x = place_of(lax.axis_index("ep"))

    def order(*steps):
        return jnp.stack([index_of(z - dz, y ^ dy, x ^ dx) for dz, dy, dx in steps])

    def once(there, *blocks, near=()):
        return local(gate_kernel, "gate", [], near, after=there, onward=blocks)

    def collected(gathered, blocks, *steps):
        return local(
            collect_kernel, "collect", [], blocks, order=order(*steps), updated=[gathered]
        )[0]

    last = ((3, 0, 1), (3, 1, 1), (2, 1, 1))
    z1, x0, y0 = moved(part, dz=1), moved(part, dx=1), moved(part, dy=1)
    z1, y0 = once([x0], z1, y0)
    z2, far0, y1 = moved(z1, dz=1), moved(y0, dx=1), moved(z1, dy=1)
    (gathered,) = local(
        functools.partial(first_kernel, 4),
        "first",
        [((part.shape[0] * lax.axis_size("ep"), part.shape[1]), part.dtype)],
        (part, z1, x0, y0),
        order=order((0, 0, 0), (1, 0, 0), (0, 0, 1), (0, 1, 0), *last),
    )
    z1, z2, far0 = once([y1], z1, z2, far0, near=[gathered])
    z3, x1, y2 = moved(z2, dz=1), moved(z1, dx=1), moved(z2, dy=1)
    marks = [z2]
    gathered = collected(gathered, (z2, far0, y1), (2, 0, 0), (0, 1, 1), (1, 1, 0))
    z2, z3, far0 = once([x1, y2], z2, z3, far0, near=[gathered])
    far1, x2, y3 = moved(far0, dz=1), moved(z2, dx=1), moved(z3, dy=1)
    gathered = collected(gathered, (z3, x1, y2), (3, 0, 0), (1, 0, 1), (2, 1, 0))
    z3, far0, x2 = once([far1, y3], z3, far0, x2, near=[gathered])
    marks.append(x2)
    far3, x3, far2 = moved(far0, dz=-1), moved(z3, dx=1), moved(x2, dy=1)
    gathered = collected(gathered, (far1, x2, y3), (1, 1, 1), (2, 0, 1), (3, 1, 0))
    return gathered, (x3, far3, far2), order(*last), marks


def project_kernel(memory, target, gathered, kv, q):
    half = q.shape[1]
    for low in range(0, gathered.shape[0], 256):
        rows = slice(low, low + 256)
        kv_part = dot(memory[:, rows], gathered[rows, : 2 * half])
        q_part = dot(target[:, rows], gathered[rows, 2 * half : 3 * half])
        if low == 0:
            kv[...] = kv_part
            q[...] = q_part
        else:
            kv[...] += kv_part
            q[...] += q_part


def attend_kernel(count, order, seg_q, seg_k, memory, target, gathered, *refs):
    blocks, (sent, kv, q, mixed, context) = refs[:count], refs[count:]
    half = q.shape[1]
    rows = blocks[0].shape[0] if blocks else 0
    targets = target.shape[0]
    places = [pl.ds(pl.multiple_of(order[i] * rows, 128), rows) for i in range(count)]
    for block, columns in zip(blocks, places):
        kv[...] += dot(memory[:, columns], block[:, : 2 * half])
        q[...] += dot(target[:, columns], block[:, 2 * half : 3 * half])
    allowed = seg_q[...] == seg_k[...]
    for low in range(0, half, HD):
        query = q[:, low : low + HD].astype(jnp.bfloat16)
        keys = kv[:, low : low + HD].astype(jnp.bfloat16)
        values = kv[:, half + low : half + low + HD].astype(jnp.bfloat16)
        scores = jnp.where(allowed, dot_rows(query, keys) * HD ** (-0.5), -1e30)
        expd = jnp.exp(scores - jnp.max(scores, axis=-1, keepdims=True))
        prob = (expd / jnp.sum(expd, axis=-1, keepdims=True)).astype(jnp.bfloat16)
        context[:, low : low + HD] = dot(prob, values).astype(jnp.bfloat16)
    valid = (seg_q[...] < SENT).astype(jnp.float32)
    for low in range(0, gathered.shape[0], 256):
        part = dot_rows(context[...], gathered[low : low + 256, 3 * half :]) * valid
        sent[:, low : low + 256] = part.astype(jnp.bfloat16)
        mixed[:targets, low : low + 256] += part
    for block, columns in zip(blocks, places):
        part = dot_rows(context[...], block[:, 3 * half :]) * valid
        sent[:, columns] = part.astype(jnp.bfloat16)
        mixed[:targets, columns] += part


def attended(order, seg_q, seg_k, memory, target, gathered, late, kv, q, mixed):
    return local(
        functools.partial(attend_kernel, len(late)),
        "attend",
        [(target.shape, jnp.bfloat16)],
        (seg_q[:, None], seg_k[None, :], memory, target, gathered, *late),
        order=order,
        updated=[kv, q, mixed],
        scratch=[pltpu.VMEM(q.shape, jnp.bfloat16)],
    )


def finish_kernel(group, memory, mixed, received, out):
    count = received.shape[0]

    @pl.when(group[0] == 0)
    def _():
        out[...] = memory[...]

    @pl.when(group[0] != 0)
    def _():
        out[:count] = (mixed[:count] + received[...].astype(jnp.float32)).astype(jnp.bfloat16)
        out[count:] = mixed[count:].astype(jnp.bfloat16)


def body(
    hidden,
    norm_gain,
    final_gain,
    router,
    w_in,
    w_out,
    expert_ids,
    slot_ids,
    src_len,
    tgt_len,
    wq,
    wk,
    wv,
    wo,
):
    group = lax.axis_index("grp")
    rows_here, width = hidden.shape[1:]
    half = wq.shape[1] // lax.axis_size("grp")
    targets = min(rows_here, -(-TGT_TOTAL // 16) * 16)

    def mine(*weights):
        return jnp.concatenate(
            [lax.dynamic_slice_in_dim(weight, group * half, half, 1) for weight in weights], axis=1
        )

    tokens, routes, slots = hidden[0], expert_ids[0], slot_ids[0]
    place = places(routes, slots).astype(jnp.float32)
    small = jnp.stack([final_gain[0], jnp.pad(place, (0, width - rows_here))])
    part = mine(wk, wv, wq, wo)
    if chips() is None:
        gathered, late = lax.all_gather(part, "ep", axis=0, tiled=True), ()
        late_order = jnp.zeros((1,), jnp.int32)
        rows = expert_rows(tokens, norm_gain[0], router[0], w_in[0], w_out[0], routes, slots)
    else:
        gathered, late, late_order, marks = gather(part)
        rows = expert_layer(
            marks, tokens, norm_gain[0], router[0], w_in[0], w_out[0], routes, slots
        )
    others = [lax.ppermute(value, "grp", [(0, 1), (1, 0)]) for value in (tokens, small)]
    memory, target, mixed = both_norms(tokens, others, small, final_gain[0], rows, targets)

    seg_q = positions(tgt_len[0], targets)
    seg_k = positions(src_len[0], rows_here)
    kv, q = local(
        project_kernel,
        "project",
        [((rows_here, 2 * half), jnp.float32), ((targets, half), jnp.float32)],
        (memory, target, gathered),
    )
    sent, _, _, mixed = attended(
        late_order, seg_q, seg_k, memory, target, gathered, late, kv, q, mixed
    )
    received = lax.ppermute(sent, "grp", [(0, 1)])
    (out,) = local(
        finish_kernel,
        "finish",
        [((rows_here, width), jnp.bfloat16)],
        (memory, mixed, received),
        order=group[None],
    )
    return out[None]


def solution(mesh):
    in_specs = (
        P("grp", "ep", None),
        P("grp", None),
        P("grp", None),
        P("grp", None, None),
        P("grp", None, "ep"),
        P("grp", "ep", None),
        P("grp", "ep", None),
        P("grp", "ep", None),
        P("ep", None),
        P("ep", None),
        P("ep", None),
        P("ep", None),
        P("ep", None),
        P("ep", None),
    )
    out_specs = P("grp", "ep", None)
    return jax.shard_map(body, mesh=mesh, in_specs=in_specs, out_specs=out_specs, check_vma=False)
```

time: 123 us -> 121 us (0.984)
  the two profiles are of different devices: /device:TPU:29 before, /device:TPU:1 now
where the time goes in v4:
time: 121 us; the launch traced here: 120 us
  local copies, waits for them, and re-layouts  38.9 us (32%)
  starting transfers between devices  32.5 us (27%)
  waiting for transfers between devices  27.4 us (23%)
  Pallas kernels  19.2 us (16%)
  other arithmetic  1.97 us (2%)
    unnamed x44, local copies, waits for them, and re-layouts  35.8 us
    ppermute x15, waiting for transfers between devices, moved(): return lax.ppermute(value, 'ep', pairs)  24.6 us
    pallas_call x15, Pallas kernels, local(): pl.pallas_call(run, out_shape=[jax.ShapeDtypeStruct(shape, dtype) for sha...  19.2 us
    ppermute x15, starting transfers between devices, moved(): return lax.ppermute(value, 'ep', pairs)  18.2 us
    all_to_all x2, starting transfers between devices, exchanged(): parts = lax.all_to_all(parts, 'ep', split_axis=0, concat_axis=0, tiled=True)  8.83 us
    ppermute x1, waiting for transfers between devices, body(): received = lax.ppermute(sent, 'grp', [(0, 1)])  2.79 us
  transfers between devices with their start and end apart: 21, of which 7 were waited for; matrix products, arithmetic and copies ran while one was open for 3% of the time, Pallas kernels for 12%

profile of v4, /device:TPU:1, one launch (start us, length us, event | category | flops | bytes accessed | tf_op | source)
XLA Modules:
  0.0 120.3 jit_solution(8221061744070819411)
XLA Ops:
  0.0 1.0 constant_dynamic-slice_fusion
  1.0 1.0 constant_dynamic-slice_fusion.2
  2.1 2.1 %collective-permute-start = (bf16[128,2048]{1,0:T(8,128)(2,1)S(1)}, bf16[128,2048]{1,0:T(8,128)(2,1)S(1)}, u32[]{:S(2)}, u32[]{:S(2)}) collective-permute-start(bf16[128,2048]{1,0:T(8,128)(2,1)S(1)} %pad_maximum_fusion.refs_1_), channel_id=1, source_target_pairs={{0,1},{1,0},{2,3},{3,2},{4,5},{5,4},{6,7},{7,6},{8,9},{9,8},{10,11... | collective-permute-start | bytes 1572872 | tf_op jit(solution)/shard_map/ppermute | solution.py:62
  4.2 1.3 %collective-permute-start.1 = (bf16[128,2048]{1,0:T(8,128)(2,1)S(1)}, bf16[128,2048]{1,0:T(8,128)(2,1)S(1)}, u32[]{:S(2)}, u32[]{:S(2)}) collective-permute-start(bf16[128,2048]{1,0:T(8,128)(2,1)S(1)} %pad_maximum_fusion.refs_1_), channel_id=1, source_target_pairs={{0,4},{1,5},{2,6},{3,7},{4,8},{5,9},{6,10},{7,11},{8,12},{9,13},{1... | collective-permute-start | bytes 1572872 | tf_op jit(solution)/shard_map/ppermute | solution.py:62
  5.5 1.2 %collective-permute-start.2 = (bf16[128,2048]{1,0:T(8,128)(2,1)S(1)}, bf16[128,2048]{1,0:T(8,128)(2,1)}, u32[]{:S(2)}, u32[]{:S(2)}) collective-permute-start(bf16[128,2048]{1,0:T(8,128)(2,1)S(1)} %pad_maximum_fusion.refs_1_), channel_id=1, source_target_pairs={{0,2},{1,3},{2,0},{3,1},{4,6},{5,7},{6,4},{7,5},{8,10},{9,11},{10,... | collective-permute-start | bytes 1572872 | tf_op jit(solution)/shard_map/ppermute | solution.py:62
  7.4 1.2 %copy-done.10 = bf16[1,256,2048]{2,1,0:T(8,128)(2,1)S(1)} copy-done((bf16[1,256,2048]{2,1,0:T(8,128)(2,1)S(1)}, bf16[1,256,2048]{2,1,0:T(8,128)(2,1)}, u32[]{:S(2)}) %copy-start.10) | copy-done | bytes 1048600
  8.6 1.0 copy-done.15
  10.4 1.3 %pack.1 = (f32[16,1]{1,0:T(8,128)S(1)}, bf16[128,2048]{1,0:T(8,128)(2,1)}) custom-call(s32[1,256]{1,0:T(1,128)S(1)} %bitcast.44, s32[1,256]{1,0:T(1,128)S(1)} %bitcast.45, bf16[256,2048]{1,0:T(8,128)(2,1)S(1)} %bitcast.39, f32[1,2048]{1,0:T(1,128)S(1)} %copy-done.18, bf16[2048,128]{1,0:T(8,128)(2,1)S(1)} %bitcast.43), custom_call_target="tpu_custom_call" | custom-call | tf_op jit(solution)/shard_map/pack/pallas_call | solution.py:82
  11.7 4.2 %all-to-all-start = ((bf16[16,8,2048]{2,1,0:T(8,128)(2,1)}), bf16[16,8,2048]{2,1,0:T(8,128)(2,1)}, u32[]{:S(2)}, u32[]{:S(2)}) async-start(bf16[16,8,2048]{2,1,0:T(8,128)(2,1)} %bitcast.7), calls=%async_computation | async-start | bytes 1048576 | tf_op jit(solution)/shard_map/all_to_all | solution.py:196
  15.9 2.6 %collective-permute-done.1.refs_1_ = bf16[128,2048]{1,0:T(8,128)(2,1)S(1)} collective-permute-done((bf16[128,2048]{1,0:T(8,128)(2,1)S(1)}, bf16[128,2048]{1,0:T(8,128)(2,1)S(1)}, u32[]{:S(2)}, u32[]{:S(2)}) %collective-permute-start.1) | collective-permute-done | bytes 524320 | tf_op jit(solution)/shard_map/ppermute | solution.py:62
  18.6 1.2 %collective-permute-start.3 = (bf16[128,2048]{1,0:T(8,128)(2,1)S(1)}, bf16[128,2048]{1,0:T(8,128)(2,1)}, u32[]{:S(2)}, u32[]{:S(2)}) collective-permute-start(bf16[128,2048]{1,0:T(8,128)(2,1)S(1)} %get-tuple-element.27.refs_2_), channel_id=1, source_target_pairs={{0,2},{1,3},{2,0},{3,1},{4,6},{5,7},{6,4},{7,5},{8,10},{9,11},{10,... | collective-permute-start | bytes 1572872 | tf_op jit(solution)/shard_map/ppermute | solution.py:62
  20.6 1.0 copy-done.14
  21.7 1.4 %first.1.refs_0_.refs_4_ = bf16[2048,2048]{1,0:T(8,128)(2,1)S(1)} custom-call(s32[7]{0:T(128)S(1)} %stack.80.refs_0_, bf16[128,2048]{1,0:T(8,128)(2,1)S(1)} %copy-done.14, bf16[128,2048]{1,0:T(8,128)(2,1)S(1)} %get-tuple-element.27.refs_2_, bf16[128,2048]{1,0:T(8,128)(2,1)S(1)} %collective-permute-done.refs_0_.refs_3_, ...), custom_call_target="tpu_custom_call" | custom-call | tf_op jit(solution)/shard_map/first/pallas_call | solution.py:82
  23.1 12.5 %collective-permute-done.3.refs_1_.refs_3_ = bf16[128,2048]{1,0:T(8,128)(2,1)} collective-permute-done((bf16[128,2048]{1,0:T(8,128)(2,1)S(1)}, bf16[128,2048]{1,0:T(8,128)(2,1)}, u32[]{:S(2)}, u32[]{:S(2)}) %collective-permute-start.3) | collective-permute-done | bytes 524320 | tf_op jit(solution)/shard_map/ppermute | solution.py:62
  35.6 2.5 %collective-permute-done.4.refs_3_ = bf16[128,2048]{1,0:T(8,128)(2,1)S(1)} collective-permute-done((bf16[128,2048]{1,0:T(8,128)(2,1)S(1)}, bf16[128,2048]{1,0:T(8,128)(2,1)S(1)}, u32[]{:S(2)}, u32[]{:S(2)}) %collective-permute-start.4) | collective-permute-done | bytes 524320 | tf_op jit(solution)/shard_map/ppermute | solution.py:62
  38.1 3.3 %copy-done = bf16[2048,2048]{1,0:T(8,128)(2,1)} copy-done((bf16[2048,2048]{1,0:T(8,128)(2,1)}, bf16[2048,2048]{1,0:T(8,128)(2,1)S(1)}, u32[]{:S(2)}) %copy-start) | copy-done | bytes 8388632
  41.4 1.4 %collective-permute-start.6 = (bf16[128,2048]{1,0:T(8,128)(2,1)S(1)}, bf16[128,2048]{1,0:T(8,128)(2,1)}, u32[]{:S(2)}, u32[]{:S(2)}) collective-permute-start(bf16[128,2048]{1,0:T(8,128)(2,1)S(1)} %get-tuple-element.31), channel_id=1, source_target_pairs={{0,1},{1,0},{2,3},{3,2},{4,5},{5,4},{6,7},{7,6},{8,9},{9,8},{10,11... | collective-permute-start | bytes 1572872 | tf_op jit(solution)/shard_map/ppermute | solution.py:62
  42.8 1.1 collective-permute-start.7
  43.9 1.5 %collective-permute-start.8 = (bf16[128,2048]{1,0:T(8,128)(2,1)S(1)}, bf16[128,2048]{1,0:T(8,128)(2,1)S(1)}, u32[]{:S(2)}, u32[]{:S(2)}) collective-permute-start(bf16[128,2048]{1,0:T(8,128)(2,1)S(1)} %get-tuple-element.29.refs_3_.refs_1_), channel_id=1, source_target_pairs={{0,4},{1,5},{2,6},{3,7},{4,8},{5,9},{6,10},{7,11},{8,12},{9,13},{1... | collective-permute-start | bytes 1572872 | tf_op jit(solution)/shard_map/ppermute | solution.py:62
  45.4 1.9 %collective-permute-start.12 = (bf16[256,2048]{1,0:T(8,128)(2,1)S(1)}, bf16[256,2048]{1,0:T(8,128)(2,1)}, u32[]{:S(2)}, u32[]{:S(2)}) collective-permute-start(bf16[256,2048]{1,0:T(8,128)(2,1)S(1)} %bitcast.40), channel_id=1, source_target_pairs={{0,16},{16,0},{1,17},{17,1},{2,18},{18,2},{3,19},{19,3},{4,20},{20... | collective-permute-start | bytes 3145736 | tf_op jit(solution)/shard_map/ppermute | solution.py:409
  47.5 2.2 %copy-done.8 = bf16[1,2048,1024]{2,1,0:T(8,128)(2,1)S(1)} copy-done((bf16[1,2048,1024]{2,1,0:T(8,128)(2,1)S(1)}, bf16[1,2048,1024]{2,1,0:T(8,128)(2,1)}, u32[]{:S(2)}) %copy-start.8) | copy-done | bytes 4194328
  49.7 2.2 %copy-done.9 = bf16[1,1024,2048]{2,1,0:T(8,128)(2,1)S(1)} copy-done((bf16[1,1024,2048]{2,1,0:T(8,128)(2,1)S(1)}, bf16[1,1024,2048]{2,1,0:T(8,128)(2,1)}, u32[]{:S(2)}) %copy-start.9) | copy-done | bytes 4194328
  51.8 2.4 %mlp.1 = bf16[128,2048]{1,0:T(8,128)(2,1)S(1)} custom-call(bf16[128,2048]{1,0:T(8,128)(2,1)} %bitcast.8.refs_0_, bf16[2048,1024]{1,0:T(8,128)(2,1)S(1)} %bitcast.37, bf16[1024,2048]{1,0:T(8,128)(2,1)S(1)} %bitcast.38, bf16[128,2048]{1,0:T(8,128)(2,1)S(1)} %get-tuple-element.29.refs_3_.refs_1_), custom_call_target="tpu_custom_call" | custom-call | tf_op jit(solution)/shard_map/mlp/pallas_call | solution.py:82
  55.0 4.6 %all-to-all-start.1 = ((bf16[16,8,2048]{2,1,0:T(8,128)(2,1)}), bf16[16,8,2048]{2,1,0:T(8,128)(2,1)}, u32[]{:S(2)}, u32[]{:S(2)}) async-start(bf16[16,8,2048]{2,1,0:T(8,128)(2,1)} %bitcast.42), calls=%async_computation.1 | async-start | bytes 1048576 | tf_op jit(solution)/shard_map/all_to_all | solution.py:196
  59.7 3.4 %copy-done.1 = bf16[2048,2048]{1,0:T(8,128)(2,1)S(1)} copy-done((bf16[2048,2048]{1,0:T(8,128)(2,1)S(1)}, bf16[2048,2048]{1,0:T(8,128)(2,1)}, u32[]{:S(2)}) %copy-start.1) | copy-done | bytes 8388632
  63.1 1.2 collect.3.refs_0_.refs_4_
  64.3 3.3 %copy-done.2 = bf16[2048,2048]{1,0:T(8,128)(2,1)} copy-done((bf16[2048,2048]{1,0:T(8,128)(2,1)}, bf16[2048,2048]{1,0:T(8,128)(2,1)S(1)}, u32[]{:S(2)}) %copy-start.2) | copy-done | bytes 8388632
  67.6 1.3 %collective-permute-start.10 = (bf16[128,2048]{1,0:T(8,128)(2,1)S(1)}, bf16[128,2048]{1,0:T(8,128)(2,1)}, u32[]{:S(2)}, u32[]{:S(2)}) collective-permute-start(bf16[128,2048]{1,0:T(8,128)(2,1)S(1)} %get-tuple-element.32.refs_1_.refs_3_), channel_id=1, source_target_pairs={{0,2},{1,3},{2,0},{3,1},{4,6},{5,7},{6,4},{7,5},{8,10},{9,11},{10,... | collective-permute-start | bytes 1572872 | tf_op jit(solution)/shard_map/ppermute | solution.py:62
  68.9 1.2 collective-permute-start.11
  70.1 1.2 collective-permute-start.9
  72.2 3.4 %copy-done.3 = bf16[2048,2048]{1,0:T(8,128)(2,1)S(1)} copy-done((bf16[2048,2048]{1,0:T(8,128)(2,1)S(1)}, bf16[2048,2048]{1,0:T(8,128)(2,1)}, u32[]{:S(2)}) %copy-start.3) | copy-done | bytes 8388632
  75.6 1.3 %collect.4.refs_0_.refs_4_ = bf16[2048,2048]{1,0:T(8,128)(2,1)S(1)} custom-call(s32[3]{0:T(128)S(1)} %pad_add_fusion.refs_0_, bf16[128,2048]{1,0:T(8,128)(2,1)S(1)} %get-tuple-element.32.refs_1_.refs_3_, bf16[128,2048]{1,0:T(8,128)(2,1)} %collective-permute-done.6.refs_1_.refs_2_, ...), custom_call_target="tpu_custom_call", output_to_operand_aliasing={{}: (4, {})} | custom-call | tf_op jit(solution)/shard_map/collect/pallas_call | solution.py:82
  77.0 5.2 %collective-permute-done.10.refs_2_.refs_3_ = bf16[128,2048]{1,0:T(8,128)(2,1)} collective-permute-done((bf16[128,2048]{1,0:T(8,128)(2,1)S(1)}, bf16[128,2048]{1,0:T(8,128)(2,1)}, u32[]{:S(2)}, u32[]{:S(2)}) %collective-permute-start.10) | collective-permute-done | bytes 524320 | tf_op jit(solution)/shard_map/ppermute | solution.py:62
  82.6 1.2 collective-permute-done.9.refs_1_
  83.8 3.3 %copy-done.4 = bf16[2048,2048]{1,0:T(8,128)(2,1)} copy-done((bf16[2048,2048]{1,0:T(8,128)(2,1)}, bf16[2048,2048]{1,0:T(8,128)(2,1)S(1)}, u32[]{:S(2)}) %copy-start.4) | copy-done | bytes 8388632
  87.5 3.5 %collective-permute-start.16 = (bf16[128,2048]{1,0:T(8,128)(2,1)S(1)}, bf16[128,2048]{1,0:T(8,128)(2,1)}, u32[]{:S(2)}, u32[]{:S(2)}) collective-permute-start(bf16[128,2048]{1,0:T(8,128)(2,1)S(1)} %get-tuple-element.39), channel_id=1, source_target_pairs={{0,12},{1,13},{2,14},{3,15},{4,0},{5,1},{6,2},{7,3},{8,4},{9,5},{1... | collective-permute-start | bytes 1572872 | tf_op jit(solution)/shard_map/ppermute | solution.py:62
  92.1 1.1 rows.1.refs_3_
  93.2 2.2 %collective-permute-start.14 = (f32[16,2048]{1,0:T(8,128)S(1)}, f32[16,2048]{1,0:T(8,128)}, u32[]{:S(2)}, u32[]{:S(2)}) collective-permute-start(f32[16,2048]{1,0:T(8,128)S(1)} %rows.1.refs_3_), channel_id=1, source_target_pairs={{0,16},{16,0},{1,17},{17,1},{2,18},{18,2},{3,19},{19,3},{4,20},{20... | collective-permute-start | bytes 393224 | tf_op jit(solution)/shard_map/ppermute | solution.py:230
  95.5 3.4 %copy-done.5 = bf16[2048,2048]{1,0:T(8,128)(2,1)S(1)} copy-done((bf16[2048,2048]{1,0:T(8,128)(2,1)S(1)}, bf16[2048,2048]{1,0:T(8,128)(2,1)}, u32[]{:S(2)}) %copy-start.5) | copy-done | bytes 8388632
  98.9 1.3 %collect.5.refs_2_.refs_5_ = bf16[2048,2048]{1,0:T(8,128)(2,1)S(1)} custom-call(s32[3]{0:T(128)S(1)} %pad_add_fusion.3.refs_0_, bf16[128,2048]{1,0:T(8,128)(2,1)} %collective-permute-done.9.refs_1_, bf16[128,2048]{1,0:T(8,128)(2,1)S(1)} %get-tuple-element.35.refs_2_, ...), custom_call_target="tpu_custom_call", output_to_operand_aliasing={{}: (4, {})} | custom-call | tf_op jit(solution)/shard_map/collect/pallas_call | solution.py:82
  100.2 3.3 %copy-done.6 = bf16[2048,2048]{1,0:T(8,128)(2,1)} copy-done((bf16[2048,2048]{1,0:T(8,128)(2,1)}, bf16[2048,2048]{1,0:T(8,128)(2,1)S(1)}, u32[]{:S(2)}) %copy-start.6) | copy-done | bytes 8388632
  103.5 2.9 %norm.1 = (bf16[256,2048]{1,0:T(8,128)(2,1)S(1)}, bf16[176,2048]{1,0:T(8,128)(2,1)S(1)}, f32[256,2048]{1,0:T(8,128)S(1)}) custom-call(s32[1]{0:T(128)} %bitcast.refs_0_, bf16[256,2048]{1,0:T(8,128)(2,1)S(1)} %bitcast.41, f32[256,1]{1,0:T(8,128)S(1)} %copy.35.refs_2_, f32[16,2048]{1,0:T(8,128)S(1)} %rows.1.refs_3_, f32[1,2048]{1,0:T(1,128)S(1)} %copy-done.17, ...), custom_call_target="tpu_custom_call" | custom-call | tf_op jit(solution)/shard_map/norm/pallas_call | solution.py:82
  106.5 3.4 %copy-done.7 = bf16[2048,2048]{1,0:T(8,128)(2,1)S(1)} copy-done((bf16[2048,2048]{1,0:T(8,128)(2,1)S(1)}, bf16[2048,2048]{1,0:T(8,128)(2,1)}, u32[]{:S(2)}) %copy-start.7) | copy-done | bytes 8388632
  109.9 1.6 %project.1 = (f32[256,1024]{1,0:T(8,128)S(1)}, f32[176,512]{1,0:T(8,128)S(1)}) custom-call(bf16[256,2048]{1,0:T(8,128)(2,1)S(1)} %get-tuple-element.36.refs_0_.refs_3_.refs_1_, bf16[176,2048]{1,0:T(8,128)(2,1)S(1)} %get-tuple-element.37.refs_1_.refs_4_, bf16[2048,2048]{1,0:T(8,128)(2,1)S(1)} %copy-done.7), custom_call_target="tpu_custom_call" | custom-call | tf_op jit(solution)/shard_map/project/pallas_call | solution.py:82
  111.5 3.5 %attend.1 = (bf16[176,2048]{1,0:T(8,128)(2,1)S(1)}, f32[256,1024]{1,0:T(8,128)S(1)}, f32[176,512]{1,0:T(8,128)S(1)}, f32[256,2048]{1,0:T(8,128)S(1)}) custom-call(s32[3]{0:T(128)S(1)} %pad_add_fusion.2.refs_0_, s32[176,1]{1,0:T(8,128)S(1)} %copy-done.16, s32[1,256]{1,0:T(1,128)S(1)} %bitcast.46, ...), custom_call_target="tpu_custom_call", output_to_operand_aliasing={{1}: (9, {}), {2}: (10, {}), {3}: (11, {})} | custom-call | tf_op jit(solution)/shard_map/attend/pallas_call | solution.py:82
  115.1 1.3 %collective-permute-start.18 = (bf16[176,2048]{1,0:T(8,128)(2,1)S(1)}, bf16[176,2048]{1,0:T(8,128)(2,1)S(1)}, u32[]{:S(2)}, u32[]{:S(2)}) collective-permute-start(bf16[176,2048]{1,0:T(8,128)(2,1)S(1)} %get-tuple-element.44), channel_id=1, source_target_pairs={{0,16},{1,17},{2,18},{3,19},{4,20},{5,21},{6,22},{7,23},{8,24},{9,... | collective-permute-start | bytes 2162696 | tf_op jit(solution)/shard_map/ppermute | solution.py:423
  116.4 2.8 %collective-permute-done.18.refs_3_ = bf16[176,2048]{1,0:T(8,128)(2,1)S(1)} collective-permute-done((bf16[176,2048]{1,0:T(8,128)(2,1)S(1)}, bf16[176,2048]{1,0:T(8,128)(2,1)S(1)}, u32[]{:S(2)}, u32[]{:S(2)}) %collective-permute-start.18) | collective-permute-done | bytes 720928 | tf_op jit(solution)/shard_map/ppermute | solution.py:423
  119.1 1.2 finish.1
  (75 shorter events, 6.5 us)
Async XLA Ops:
  2.0 18.5 %copy-start.13 = (bf16[128,2048]{1,0:T(8,128)(2,1)}, bf16[128,2048]{1,0:T(8,128)(2,1)S(1)}, u32[]{:S(2)}) copy-start(bf16[128,2048]{1,0:T(8,128)(2,1)S(1)} %pad_maximum_fusion.refs_1_) | copy-start | bytes 1572868
  2.1 13.9 %collective-permute-start = (bf16[128,2048]{1,0:T(8,128)(2,1)S(1)}, bf16[128,2048]{1,0:T(8,128)(2,1)S(1)}, u32[]{:S(2)}, u32[]{:S(2)}) collective-permute-start(bf16[128,2048]{1,0:T(8,128)(2,1)S(1)} %pad_maximum_fusion.refs_1_), channel_id=1, source_target_pairs={{0,1},{1,0},{2,3},{3,2},{4,5},{5,4},{6,7},{7,6},{8,9},{9,8},{10,11... | collective-permute-start | bytes 1572872 | tf_op jit(solution)/shard_map/ppermute | solution.py:62
  4.2 14.4 %collective-permute-start.1 = (bf16[128,2048]{1,0:T(8,128)(2,1)S(1)}, bf16[128,2048]{1,0:T(8,128)(2,1)S(1)}, u32[]{:S(2)}, u32[]{:S(2)}) collective-permute-start(bf16[128,2048]{1,0:T(8,128)(2,1)S(1)} %pad_maximum_fusion.refs_1_), channel_id=1, source_target_pairs={{0,4},{1,5},{2,6},{3,7},{4,8},{5,9},{6,10},{7,11},{8,12},{9,13},{1... | collective-permute-start | bytes 1572872 | tf_op jit(solution)/shard_map/ppermute | solution.py:62
  5.5 13.1 %collective-permute-start.2 = (bf16[128,2048]{1,0:T(8,128)(2,1)S(1)}, bf16[128,2048]{1,0:T(8,128)(2,1)}, u32[]{:S(2)}, u32[]{:S(2)}) collective-permute-start(bf16[128,2048]{1,0:T(8,128)(2,1)S(1)} %pad_maximum_fusion.refs_1_), channel_id=1, source_target_pairs={{0,2},{1,3},{2,0},{3,1},{4,6},{5,7},{6,4},{7,5},{8,10},{9,11},{10,... | collective-permute-start | bytes 1572872 | tf_op jit(solution)/shard_map/ppermute | solution.py:62
  7.4 1.2 %copy-start.10 = (bf16[1,256,2048]{2,1,0:T(8,128)(2,1)S(1)}, bf16[1,256,2048]{2,1,0:T(8,128)(2,1)}, u32[]{:S(2)}) copy-start(bf16[1,256,2048]{2,1,0:T(8,128)(2,1)} %param.14) | copy-start | bytes 3145732
  8.6 1.0 copy-start.15
  9.7 0.7 copy-start.18
  11.7 35.8 %all-to-all-start = ((bf16[16,8,2048]{2,1,0:T(8,128)(2,1)}), bf16[16,8,2048]{2,1,0:T(8,128)(2,1)}, u32[]{:S(2)}, u32[]{:S(2)}) async-start(bf16[16,8,2048]{2,1,0:T(8,128)(2,1)} %bitcast.7), calls=%async_computation | async-start | bytes 1048576 | tf_op jit(solution)/shard_map/all_to_all | solution.py:196
  18.6 17.0 %collective-permute-start.3 = (bf16[128,2048]{1,0:T(8,128)(2,1)S(1)}, bf16[128,2048]{1,0:T(8,128)(2,1)}, u32[]{:S(2)}, u32[]{:S(2)}) collective-permute-start(bf16[128,2048]{1,0:T(8,128)(2,1)S(1)} %get-tuple-element.27.refs_2_), channel_id=1, source_target_pairs={{0,2},{1,3},{2,0},{3,1},{4,6},{5,7},{6,4},{7,5},{8,10},{9,11},{10,... | collective-permute-start | bytes 1572872 | tf_op jit(solution)/shard_map/ppermute | solution.py:62
  19.8 18.3 %collective-permute-start.4 = (bf16[128,2048]{1,0:T(8,128)(2,1)S(1)}, bf16[128,2048]{1,0:T(8,128)(2,1)S(1)}, u32[]{:S(2)}, u32[]{:S(2)}) collective-permute-start(bf16[128,2048]{1,0:T(8,128)(2,1)S(1)} %get-tuple-element.27.refs_2_), channel_id=1, source_target_pairs={{0,4},{1,5},{2,6},{3,7},{4,8},{5,9},{6,10},{7,11},{8,12},{9,13},{1... | collective-permute-start | bytes 1572872 | tf_op jit(solution)/shard_map/ppermute | solution.py:62
  20.3 17.8 %collective-permute-start.5 = (bf16[128,2048]{1,0:T(8,128)(2,1)}, bf16[128,2048]{1,0:T(8,128)(2,1)S(1)}, u32[]{:S(2)}, u32[]{:S(2)}) collective-permute-start(bf16[128,2048]{1,0:T(8,128)(2,1)} %get-tuple-element.28.refs_4_), channel_id=1, source_target_pairs={{0,1},{1,0},{2,3},{3,2},{4,5},{5,4},{6,7},{7,6},{8,9},{9,8},{10,11... | collective-permute-start | bytes 1572872 | tf_op jit(solution)/shard_map/ppermute | solution.py:62
  20.6 1.0 copy-start.14
  21.7 23.7 %copy-start.11 = (bf16[1,256,2048]{2,1,0:T(8,128)(2,1)S(1)}, bf16[1,256,2048]{2,1,0:T(8,128)(2,1)}, u32[]{:S(2)}) copy-start(bf16[1,256,2048]{2,1,0:T(8,128)(2,1)} %param.14) | copy-start | bytes 3145732
  21.7 25.6 %copy-start.17 = (f32[1,2048]{1,0:T(1,128)S(1)}, f32[1,2048]{1,0:T(1,128)}, u32[]{:S(2)}) copy-start(f32[1,2048]{1,0:T(1,128)} %refs_4_.1) | copy-start | bytes 24580
  38.1 3.3 %copy-start = (bf16[2048,2048]{1,0:T(8,128)(2,1)}, bf16[2048,2048]{1,0:T(8,128)(2,1)S(1)}, u32[]{:S(2)}) copy-start(bf16[2048,2048]{1,0:T(8,128)(2,1)S(1)} %first.1.refs_0_.refs_4_) | copy-start | bytes 25165828
  41.4 22.9 %collective-permute-start.6 = (bf16[128,2048]{1,0:T(8,128)(2,1)S(1)}, bf16[128,2048]{1,0:T(8,128)(2,1)}, u32[]{:S(2)}, u32[]{:S(2)}) collective-permute-start(bf16[128,2048]{1,0:T(8,128)(2,1)S(1)} %get-tuple-element.31), channel_id=1, source_target_pairs={{0,1},{1,0},{2,3},{3,2},{4,5},{5,4},{6,7},{7,6},{8,9},{9,8},{10,11... | collective-permute-start | bytes 1572872 | tf_op jit(solution)/shard_map/ppermute | solution.py:62
  42.8 21.5 %collective-permute-start.7 = (bf16[128,2048]{1,0:T(8,128)(2,1)S(1)}, bf16[128,2048]{1,0:T(8,128)(2,1)}, u32[]{:S(2)}, u32[]{:S(2)}) collective-permute-start(bf16[128,2048]{1,0:T(8,128)(2,1)S(1)} %get-tuple-element.29.refs_3_.refs_1_), channel_id=1, source_target_pairs={{0,2},{1,3},{2,0},{3,1},{4,6},{5,7},{6,4},{7,5},{8,10},{9,11},{10,... | collective-permute-start | bytes 1572872 | tf_op jit(solution)/shard_map/ppermute | solution.py:62
  43.9 20.4 %collective-permute-start.8 = (bf16[128,2048]{1,0:T(8,128)(2,1)S(1)}, bf16[128,2048]{1,0:T(8,128)(2,1)S(1)}, u32[]{:S(2)}, u32[]{:S(2)}) collective-permute-start(bf16[128,2048]{1,0:T(8,128)(2,1)S(1)} %get-tuple-element.29.refs_3_.refs_1_), channel_id=1, source_target_pairs={{0,4},{1,5},{2,6},{3,7},{4,8},{5,9},{6,10},{7,11},{8,12},{9,13},{1... | collective-permute-start | bytes 1572872 | tf_op jit(solution)/shard_map/ppermute | solution.py:62
  45.4 58.2 %collective-permute-start.12 = (bf16[256,2048]{1,0:T(8,128)(2,1)S(1)}, bf16[256,2048]{1,0:T(8,128)(2,1)}, u32[]{:S(2)}, u32[]{:S(2)}) collective-permute-start(bf16[256,2048]{1,0:T(8,128)(2,1)S(1)} %bitcast.40), channel_id=1, source_target_pairs={{0,16},{16,0},{1,17},{17,1},{2,18},{18,2},{3,19},{19,3},{4,20},{20... | collective-permute-start | bytes 3145736 | tf_op jit(solution)/shard_map/ppermute | solution.py:409
  47.3 45.9 %collective-permute-start.13 = (f32[2,2048]{1,0:T(2,128)S(1)}, f32[2,2048]{1,0:T(2,128)S(1)}, u32[]{:S(2)}, u32[]{:S(2)}) collective-permute-start(f32[2,2048]{1,0:T(2,128)S(1)} %pad_maximum_fusion.1), channel_id=1, source_target_pairs={{0,16},{16,0},{1,17},{17,1},{2,18},{18,2},{3,19},{19,3},{4,20},{20... | collective-permute-start | bytes 49160 | tf_op jit(solution)/shard_map/ppermute | solution.py:409
  47.5 2.2 %copy-start.8 = (bf16[1,2048,1024]{2,1,0:T(8,128)(2,1)S(1)}, bf16[1,2048,1024]{2,1,0:T(8,128)(2,1)}, u32[]{:S(2)}) copy-start(bf16[1,2048,1024]{2,1,0:T(8,128)(2,1)} %param.18) | copy-start | bytes 12582916
  49.7 2.2 %copy-start.9 = (bf16[1,1024,2048]{2,1,0:T(8,128)(2,1)S(1)}, bf16[1,1024,2048]{2,1,0:T(8,128)(2,1)}, u32[]{:S(2)}) copy-start(bf16[1,1024,2048]{2,1,0:T(8,128)(2,1)} %param.19) | copy-start | bytes 12582916
  54.2 0.8 copy-start.12
  55.0 37.0 %all-to-all-start.1 = ((bf16[16,8,2048]{2,1,0:T(8,128)(2,1)}), bf16[16,8,2048]{2,1,0:T(8,128)(2,1)}, u32[]{:S(2)}, u32[]{:S(2)}) async-start(bf16[16,8,2048]{2,1,0:T(8,128)(2,1)} %bitcast.42), calls=%async_computation.1 | async-start | bytes 1048576 | tf_op jit(solution)/shard_map/all_to_all | solution.py:196
  59.7 3.4 %copy-start.1 = (bf16[2048,2048]{1,0:T(8,128)(2,1)S(1)}, bf16[2048,2048]{1,0:T(8,128)(2,1)}, u32[]{:S(2)}) copy-start(bf16[2048,2048]{1,0:T(8,128)(2,1)} %copy-done) | copy-start | bytes 25165828
  64.3 7.1 %copy-start.20 = (s32[1,4]{1,0:T(1,128)S(1)}, s32[1,4]{1,0:T(1,128)}, u32[]{:S(2)}) copy-start(s32[1,4]{1,0:T(1,128)} %param.23) | copy-start | bytes 52
  64.3 7.3 %copy-start.21 = (s32[1,4]{1,0:T(1,128)S(1)}, s32[1,4]{1,0:T(1,128)}, u32[]{:S(2)}) copy-start(s32[1,4]{1,0:T(1,128)} %param.22) | copy-start | bytes 52
  64.3 3.3 %copy-start.2 = (bf16[2048,2048]{1,0:T(8,128)(2,1)}, bf16[2048,2048]{1,0:T(8,128)(2,1)S(1)}, u32[]{:S(2)}) copy-start(bf16[2048,2048]{1,0:T(8,128)(2,1)S(1)} %collect.3.refs_0_.refs_4_) | copy-start | bytes 25165828
  67.6 14.6 %collective-permute-start.10 = (bf16[128,2048]{1,0:T(8,128)(2,1)S(1)}, bf16[128,2048]{1,0:T(8,128)(2,1)}, u32[]{:S(2)}, u32[]{:S(2)}) collective-permute-start(bf16[128,2048]{1,0:T(8,128)(2,1)S(1)} %get-tuple-element.32.refs_1_.refs_3_), channel_id=1, source_target_pairs={{0,2},{1,3},{2,0},{3,1},{4,6},{5,7},{6,4},{7,5},{8,10},{9,11},{10,... | collective-permute-start | bytes 1572872 | tf_op jit(solution)/shard_map/ppermute | solution.py:62
  68.9 13.7 %collective-permute-start.11 = (bf16[128,2048]{1,0:T(8,128)(2,1)S(1)}, bf16[128,2048]{1,0:T(8,128)(2,1)S(1)}, u32[]{:S(2)}, u32[]{:S(2)}) collective-permute-start(bf16[128,2048]{1,0:T(8,128)(2,1)S(1)} %get-tuple-element.34), channel_id=1, source_target_pairs={{0,1},{1,0},{2,3},{3,2},{4,5},{5,4},{6,7},{7,6},{8,9},{9,8},{10,11... | collective-permute-start | bytes 1572872 | tf_op jit(solution)/shard_map/ppermute | solution.py:62
  70.1 13.7 %collective-permute-start.9 = (bf16[128,2048]{1,0:T(8,128)(2,1)S(1)}, bf16[128,2048]{1,0:T(8,128)(2,1)}, u32[]{:S(2)}, u32[]{:S(2)}) collective-permute-start(bf16[128,2048]{1,0:T(8,128)(2,1)S(1)} %get-tuple-element.33.refs_4_), channel_id=1, source_target_pairs={{0,4},{1,5},{2,6},{3,7},{4,8},{5,9},{6,10},{7,11},{8,12},{9,13},{1... | collective-permute-start | bytes 1572872 | tf_op jit(solution)/shard_map/ppermute | solution.py:62
  72.2 3.4 %copy-start.3 = (bf16[2048,2048]{1,0:T(8,128)(2,1)S(1)}, bf16[2048,2048]{1,0:T(8,128)(2,1)}, u32[]{:S(2)}) copy-start(bf16[2048,2048]{1,0:T(8,128)(2,1)} %copy-done.2) | copy-start | bytes 25165828
  83.8 3.3 %copy-start.4 = (bf16[2048,2048]{1,0:T(8,128)(2,1)}, bf16[2048,2048]{1,0:T(8,128)(2,1)S(1)}, u32[]{:S(2)}) copy-start(bf16[2048,2048]{1,0:T(8,128)(2,1)S(1)} %collect.4.refs_0_.refs_4_) | copy-start | bytes 25165828
  87.1 24.4 %collective-permute-start.15 = (bf16[128,2048]{1,0:T(8,128)(2,1)S(1)}, bf16[128,2048]{1,0:T(8,128)(2,1)}, u32[]{:S(2)}, u32[]{:S(2)}) collective-permute-start(bf16[128,2048]{1,0:T(8,128)(2,1)S(1)} %get-tuple-element.38), channel_id=1, source_target_pairs={{0,1},{1,0},{2,3},{3,2},{4,5},{5,4},{6,7},{7,6},{8,9},{9,8},{10,11... | collective-permute-start | bytes 1572872 | tf_op jit(solution)/shard_map/ppermute | solution.py:62
  87.5 24.0 %collective-permute-start.16 = (bf16[128,2048]{1,0:T(8,128)(2,1)S(1)}, bf16[128,2048]{1,0:T(8,128)(2,1)}, u32[]{:S(2)}, u32[]{:S(2)}) collective-permute-start(bf16[128,2048]{1,0:T(8,128)(2,1)S(1)} %get-tuple-element.39), channel_id=1, source_target_pairs={{0,12},{1,13},{2,14},{3,15},{4,0},{5,1},{6,2},{7,3},{8,4},{9,5},{1... | collective-permute-start | bytes 1572872 | tf_op jit(solution)/shard_map/ppermute | solution.py:62
  90.9 20.6 %collective-permute-start.17 = (bf16[128,2048]{1,0:T(8,128)(2,1)S(1)}, bf16[128,2048]{1,0:T(8,128)(2,1)}, u32[]{:S(2)}, u32[]{:S(2)}) collective-permute-start(bf16[128,2048]{1,0:T(8,128)(2,1)S(1)} %get-tuple-element.35.refs_2_), channel_id=1, source_target_pairs={{0,2},{1,3},{2,0},{3,1},{4,6},{5,7},{6,4},{7,5},{8,10},{9,11},{10,... | collective-permute-start | bytes 1572872 | tf_op jit(solution)/shard_map/ppermute | solution.py:62
  93.2 10.3 %collective-permute-start.14 = (f32[16,2048]{1,0:T(8,128)S(1)}, f32[16,2048]{1,0:T(8,128)}, u32[]{:S(2)}, u32[]{:S(2)}) collective-permute-start(f32[16,2048]{1,0:T(8,128)S(1)} %rows.1.refs_3_), channel_id=1, source_target_pairs={{0,16},{16,0},{1,17},{17,1},{2,18},{18,2},{3,19},{19,3},{4,20},{20... | collective-permute-start | bytes 393224 | tf_op jit(solution)/shard_map/ppermute | solution.py:230
  95.5 3.4 %copy-start.5 = (bf16[2048,2048]{1,0:T(8,128)(2,1)S(1)}, bf16[2048,2048]{1,0:T(8,128)(2,1)}, u32[]{:S(2)}) copy-start(bf16[2048,2048]{1,0:T(8,128)(2,1)} %copy-done.4) | copy-start | bytes 25165828
  100.2 3.3 %copy-start.6 = (bf16[2048,2048]{1,0:T(8,128)(2,1)}, bf16[2048,2048]{1,0:T(8,128)(2,1)S(1)}, u32[]{:S(2)}) copy-start(bf16[2048,2048]{1,0:T(8,128)(2,1)S(1)} %collect.5.refs_2_.refs_5_) | copy-start | bytes 25165828
  103.5 8.0 %copy-start.16 = (s32[176,1]{1,0:T(8,128)S(1)}, s32[176,1]{1,0:T(8,128)}, u32[]{:S(2)}) copy-start(s32[176,1]{1,0:T(8,128)} %copy.37.refs_1_) | copy-start | bytes 2116
  103.5 8.0 %copy-start.19 = (s32[256]{0:T(256)S(1)}, s32[256]{0:T(256)}, u32[]{:S(2)}) copy-start(s32[256]{0:T(256)} %convert_reduce_fusion) | copy-start | bytes 3076
  106.5 3.4 %copy-start.7 = (bf16[2048,2048]{1,0:T(8,128)(2,1)S(1)}, bf16[2048,2048]{1,0:T(8,128)(2,1)}, u32[]{:S(2)}) copy-start(bf16[2048,2048]{1,0:T(8,128)(2,1)} %copy-done.6) | copy-start | bytes 25165828
  115.1 4.1 %collective-permute-start.18 = (bf16[176,2048]{1,0:T(8,128)(2,1)S(1)}, bf16[176,2048]{1,0:T(8,128)(2,1)S(1)}, u32[]{:S(2)}, u32[]{:S(2)}) collective-permute-start(bf16[176,2048]{1,0:T(8,128)(2,1)S(1)} %get-tuple-element.44), channel_id=1, source_target_pairs={{0,16},{1,17},{2,18},{3,19},{4,20},{5,21},{6,22},{7,23},{8,24},{9,... | collective-permute-start | bytes 2162696 | tf_op jit(solution)/shard_map/ppermute | solution.py:423

commit v5 on v3

--- a/solution.py
+++ b/solution.py
@@ -93,15 +93,15 @@
     )(*scalars, *vmem, *far, *after, *onward)
 
 
-def pack_kernel(experts, place, both, hidden, gain, router, gate, send):
+def pack_kernel(held, place, both, hidden, gain, router, gate, own, other):
     count = gate.shape[0]
     slot = lax.broadcasted_iota(jnp.int32, (count, hidden.shape[0]), 0)
     table = slot == place[...]
     rows = dot(table.astype(jnp.bfloat16), hidden[...])
     normed = normalize(rows, gain[...])
-    send[...] = jnp.concatenate(
-        [normed[e * PAD : (e + 1) * PAD] for e in experts], axis=0
-    ).astype(jnp.bfloat16)
+    near, far = halves(held, normed)
+    own[...] = near.astype(jnp.bfloat16)
+    other[...] = far.astype(jnp.bfloat16)
     logits = dot(normed.astype(jnp.bfloat16), router[...])
     mine = lax.broadcasted_iota(jnp.int32, (count, 1), 0) // PAD
     others = jnp.sum(jnp.where(table, both[...], 0), axis=1, keepdims=True) - mine
@@ -110,22 +110,54 @@
     gate[...] = 1.0 / (1.0 + jnp.exp(-jnp.sum(lead, axis=1, keepdims=True)))
 
 
+def halves(held, rows):
+    first = held[0] == 0
+    return jnp.where(first, rows[:PAD], rows[PAD:]), jnp.where(first, rows[PAD:], rows[:PAD])
+
+
+def copies_kernel(own, arrived, out):
+    rows = jnp.concatenate([ref[...].astype(jnp.float32) for ref in (own, arrived)], axis=0)
+    rows = rows.astype(jnp.bfloat16)
+    for low in range(0, out.shape[0], 2 * PAD):
+        out[low : low + 2 * PAD] = rows
+
+
+def sum_kernel(pieces, own, other):
+    total = pieces[: 2 * PAD].astype(jnp.float32)
+    for low in range(2 * PAD, pieces.shape[0], 2 * PAD):
+        total = total + pieces[low : low + 2 * PAD].astype(jnp.float32)
+    own[...] = total[:PAD]
+    other[...] = total[PAD:]
+
+
 def gate_kernel():
     pass
 
 
-def mlp_kernel(rows, w_in, w_out, pieces):
-    inner = jnp.maximum(dot(rows[...], w_in[...]), 0.0).astype(jnp.bfloat16)
-    pieces[...] = dot(inner, w_out[...]).astype(jnp.bfloat16)
-
-
-def rows_kernel(experts, gate, parts, rows):
-    count = gate.shape[0]
-    summed = [None] * (count // PAD)
-    for i, e in enumerate(experts):
-        part = parts[i * PAD : (i + 1) * PAD].astype(jnp.float32)
-        summed[e] = part if summed[e] is None else summed[e] + part
-    rows[...] = gate[...] * jnp.concatenate(summed, axis=0)
+def mlp_kernel(rows, w_in, w_out, pieces, near_in, near_out, inner, sems):
+    steps = sems.shape[1]
+    wide = w_in.shape[1] // steps
+    copies = []
+    for i in range(steps):
+        part = pl.ds(i * wide, wide)
+        copies.append(pltpu.make_async_copy(w_in.at[:, part], near_in.at[:, part], sems.at[0, i]))
+    for i in range(steps):
+        part = pl.ds(i * wide, wide)
+        copies.append(pltpu.make_async_copy(w_out.at[part], near_out.at[part], sems.at[1, i]))
+    for copy in copies:
+        copy.start()
+    for i in range(steps):
+        copies[i].wait()
+        part = slice(i * wide, (i + 1) * wide)
+        inner[:, part] = jnp.maximum(dot(rows[...], near_in[:, part]), 0.0).astype(jnp.bfloat16)
+    for i in range(steps):
+        copies[steps + i].wait()
+    pieces[...] = dot(inner[...], near_out[...]).astype(jnp.bfloat16)
+
+
+def rows_kernel(held, gate, own, arrived, rows):
+    both = jnp.concatenate([own[...], arrived[...]], axis=0)
+    rows[...] = gate[...] * jnp.concatenate(halves(held, both), axis=0)
 
 
 def mixed_rows(hidden, place, rows_ref):
@@ -189,36 +221,59 @@
 
 def expert_layer(marks, hidden, norm_gain, router, w_in, w_out, routes, slots):
     devices = lax.axis_size("ep")
-    experts = devices // SPLIT
     width = hidden.shape[1]
-    place = places(routes, slots)
-    held = [device // SPLIT for device in range(devices)]
-    blocks = (devices * PAD, width)
+    depth = chips()[0]
+    held = (place_of(lax.axis_index("ep"))[0] // (depth // 2))[None]
+    groups = [list(range(low, low + SPLIT)) for low in range(0, devices, SPLIT)]
+    small, wide = (PAD, width), (2 * PAD * SPLIT, width)
 
     def exchanged(values):
-        parts = values.reshape(devices, PAD, width)
-        parts = lax.all_to_all(parts, "ep", split_axis=0, concat_axis=0, tiled=True)
+        parts = values.reshape(SPLIT, 2 * PAD, width)
+        parts = lax.all_to_all(
+            parts, "ep", split_axis=0, concat_axis=0, tiled=True, axis_index_groups=groups
+        )
         return parts.reshape(values.shape)
 
-    gate, send = local(
-        functools.partial(pack_kernel, held),
+    gate, own, other = local(
+        pack_kernel,
         "pack",
-        [((experts * PAD, 1), jnp.float32), (blocks, jnp.bfloat16)],
-        (place[None, :], jnp.sum(routes, axis=1)[None, :], hidden, norm_gain[None, :], router),
+        [((2 * PAD, 1), jnp.float32), (small, jnp.bfloat16), (small, jnp.bfloat16)],
+        (
+            places(routes, slots)[None, :],
+            jnp.sum(routes, axis=1)[None, :],
+            hidden,
+            norm_gain[None, :],
+            router,
+        ),
+        order=held,
+    )
+    (send,) = local(
+        copies_kernel, "copies", [(wide, jnp.bfloat16)], (own, moved(other, dz=depth // 2))
     )
     (pieces,) = local(
         mlp_kernel,
         "mlp",
-        [(blocks, jnp.bfloat16)],
-        (exchanged(send), w_in, w_out),
+        [(wide, jnp.bfloat16)],
+        (exchanged(send),),
         marks[0],
+        far=(w_in, w_out),
+        scratch=[
+            pltpu.VMEM(w_in.shape, w_in.dtype),
+            pltpu.VMEM(w_out.shape, w_out.dtype),
+            pltpu.VMEM((wide[0], w_in.shape[1]), jnp.bfloat16),
+            pltpu.SemaphoreType.DMA((2, 4)),
+        ],
+        mib=16,
+    )
+    own, other = local(
+        sum_kernel, "sum", [(small, jnp.float32)] * 2, (exchanged(pieces),), marks[1]
     )
     (rows,) = local(
-        functools.partial(rows_kernel, held),
+        rows_kernel,
         "rows",
-        [((experts * PAD, width), jnp.float32)],
-        (gate, exchanged(pieces)),
-        marks[1],
+        [((2 * PAD, width), jnp.float32)],
+        (gate, own, moved(other, dz=depth // 2)),
+        order=held,
     )
     return rows
 
@@ -384,7 +439,7 @@
             pltpu.VMEM((len(blocks) * rows, 3 * half), jnp.bfloat16),
             pltpu.SemaphoreType.DMA((len(blocks),)),
         ],
-        mib=52,
+        mib=14,
     )
 
 
@@ -408,7 +463,7 @@
             pltpu.SemaphoreType.DMA((max(len(late), 1),)),
             pltpu.SemaphoreType.DMA((blocks,)),
         ],
-        mib=52,
+        mib=14,
     )
 
 

time: 123 us -> 131 us (1.065)
  the two profiles are of different devices: /device:TPU:29 before, /device:TPU:1 now
where the time goes in v5:
time: 131 us; the launch traced here: 130 us
  waiting for transfers between devices  50.4 us (38%)
  starting transfers between devices  36.4 us (28%)
  local copies, waits for them, and re-layouts  22.6 us (17%)
  Pallas kernels  18.7 us (14%)
    ppermute x17, waiting for transfers between devices, moved(): return lax.ppermute(value, 'ep', pairs)  47 us
    ppermute x17, starting transfers between devices, moved(): return lax.ppermute(value, 'ep', pairs)  22.1 us
    unnamed x54, local copies, waits for them, and re-layouts  19.4 us
    pallas_call x13, Pallas kernels, local(): pl.pallas_call(run, out_shape=[jax.ShapeDtypeStruct(shape, dtype) for sha...  18.7 us
    all_to_all x2, starting transfers between devices, exchanged(): lax.all_to_all(parts, 'ep', split_axis=0, concat_axis=0, tiled=True, axis...  8.42 us
    ppermute x1, waiting for transfers between devices, body(): received = lax.ppermute(sent, 'grp', [(0, 1)])  2.77 us
  transfers between devices with their start and end apart: 23, of which 7 were waited for; matrix products, arithmetic and copies ran while one was open for 2% of the time, Pallas kernels for 10%

profile of v5, /device:TPU:1, one launch (start us, length us, event | category | flops | bytes accessed | tf_op | source)
XLA Modules:
  0.0 129.8 jit_solution(2240333111317619691)
XLA Ops:
  0.0 1.0 constant_dynamic-slice_fusion
  1.0 1.0 constant_dynamic-slice_fusion.2
  2.1 2.1 %collective-permute-start.1 = (bf16[128,2048]{1,0:T(8,128)(2,1)S(1)}, bf16[128,2048]{1,0:T(8,128)(2,1)S(1)}, u32[]{:S(2)}, u32[]{:S(2)}) collective-permute-start(bf16[128,2048]{1,0:T(8,128)(2,1)S(1)} %pad_maximum_fusion.refs_3_.refs_7_), channel_id=1, source_target_pairs={{0,1},{1,0},{2,3},{3,2},{4,5},{5,4},{6,7},{7,6},{8,9},{9,8},{10,11... | collective-permute-start | bytes 1572872 | tf_op jit(solution)/shard_map/ppermute | solution.py:62
  4.2 1.3 collective-permute-start.2
  5.5 1.2 collective-permute-start.3
  7.4 1.2 copy-done.14
  8.6 1.0 copy-done.17
  11.1 2.3 %collective-permute-start = (bf16[8,2048]{1,0:T(8,128)(2,1)S(1)}, bf16[8,2048]{1,0:T(8,128)(2,1)S(1)}, u32[]{:S(2)}, u32[]{:S(2)}) collective-permute-start(bf16[8,2048]{1,0:T(8,128)(2,1)S(1)} %get-tuple-element.30), channel_id=1, source_target_pairs={{0,8},{1,9},{2,10},{3,11},{4,12},{5,13},{6,14},{7,15},{8,0},{9,1},... | collective-permute-start | bytes 98312 | tf_op jit(solution)/shard_map/ppermute | solution.py:62
  13.4 7.9 %collective-permute-done.refs_1_ = bf16[8,2048]{1,0:T(8,128)(2,1)S(1)} collective-permute-done((bf16[8,2048]{1,0:T(8,128)(2,1)S(1)}, bf16[8,2048]{1,0:T(8,128)(2,1)S(1)}, u32[]{:S(2)}, u32[]{:S(2)}) %collective-permute-start) | collective-permute-done | bytes 32800 | tf_op jit(solution)/shard_map/ppermute | solution.py:62
  22.1 4.1 %all-to-all-start = ((bf16[8,16,2048]{2,1,0:T(8,128)(2,1)}), bf16[8,16,2048]{2,1,0:T(8,128)(2,1)}, u32[]{:S(2)}, u32[]{:S(2)}) async-start(bf16[8,16,2048]{2,1,0:T(8,128)(2,1)} %bitcast.7), calls=%async_computation | async-start | bytes 1048576 | tf_op jit(solution)/shard_map/all_to_all | solution.py:232
  26.3 1.4 %collective-permute-start.4 = (bf16[128,2048]{1,0:T(8,128)(2,1)S(1)}, bf16[128,2048]{1,0:T(8,128)(2,1)S(1)}, u32[]{:S(2)}, u32[]{:S(2)}) collective-permute-start(bf16[128,2048]{1,0:T(8,128)(2,1)S(1)} %get-tuple-element.31.refs_1_), channel_id=1, source_target_pairs={{0,2},{1,3},{2,0},{3,1},{4,6},{5,7},{6,4},{7,5},{8,10},{9,11},{10,... | collective-permute-start | bytes 1572872 | tf_op jit(solution)/shard_map/ppermute | solution.py:62
  27.7 1.2 collective-permute-start.5
  28.9 1.2 collective-permute-start.6
  30.1 14.7 %collective-permute-done.4.refs_0_.refs_10_.refs_14_ = bf16[128,2048]{1,0:T(8,128)(2,1)S(1)} collective-permute-done((bf16[128,2048]{1,0:T(8,128)(2,1)S(1)}, bf16[128,2048]{1,0:T(8,128)(2,1)S(1)}, u32[]{:S(2)}, u32[]{:S(2)}) %collective-permute-start.4) | collective-permute-done | bytes 524320 | tf_op jit(solution)/shard_map/ppermute | solution.py:62
  44.8 2.2 %collective-permute-start.7 = (bf16[128,2048]{1,0:T(8,128)(2,1)S(1)}, bf16[128,2048]{1,0:T(8,128)(2,1)S(1)}, u32[]{:S(2)}, u32[]{:S(2)}) collective-permute-start(bf16[128,2048]{1,0:T(8,128)(2,1)S(1)} %get-tuple-element.34.refs_4_.refs_8_), channel_id=1, source_target_pairs={{0,1},{1,0},{2,3},{3,2},{4,5},{5,4},{6,7},{7,6},{8,9},{9,8},{10,11... | collective-permute-start | bytes 1572872 | tf_op jit(solution)/shard_map/ppermute | solution.py:62
  47.1 1.3 collective-permute-start.9
  48.4 2.2 %copy-done.12 = bf16[1,2048,1024]{2,1,0:T(8,128)(2,1)S(1)} copy-done((bf16[1,2048,1024]{2,1,0:T(8,128)(2,1)S(1)}, bf16[1,2048,1024]{2,1,0:T(8,128)(2,1)}, u32[]{:S(2)}) %copy-start.12) | copy-done | bytes 4194328
  50.6 2.2 %copy-done.13 = bf16[1,1024,2048]{2,1,0:T(8,128)(2,1)S(1)} copy-done((bf16[1,1024,2048]{2,1,0:T(8,128)(2,1)S(1)}, bf16[1,1024,2048]{2,1,0:T(8,128)(2,1)}, u32[]{:S(2)}) %copy-start.13) | copy-done | bytes 4194328
  52.8 4.4 %mlp.1 = bf16[128,2048]{1,0:T(8,128)(2,1)S(1)} custom-call(bf16[128,2048]{1,0:T(8,128)(2,1)} %bitcast.8.refs_0_, bf16[2048,1024]{1,0:T(8,128)(2,1)S(1)} %bitcast.36, bf16[1024,2048]{1,0:T(8,128)(2,1)S(1)} %bitcast.37, bf16[128,2048]{1,0:T(8,128)(2,1)S(1)} %get-tuple-element.33.refs_3_.refs_2_), custom_call_target="tpu_custom_call" | custom-call | tf_op jit(solution)/shard_map/mlp/pallas_call | solution.py:83
  58.0 4.3 %all-to-all-start.1 = ((bf16[8,16,2048]{2,1,0:T(8,128)(2,1)}), bf16[8,16,2048]{2,1,0:T(8,128)(2,1)}, u32[]{:S(2)}, u32[]{:S(2)}) async-start(bf16[8,16,2048]{2,1,0:T(8,128)(2,1)} %bitcast.41), calls=%async_computation.1 | async-start | bytes 1048576 | tf_op jit(solution)/shard_map/all_to_all | solution.py:232
  62.4 1.4 %collective-permute-start.10 = (bf16[128,2048]{1,0:T(8,128)(2,1)S(1)}, bf16[128,2048]{1,0:T(8,128)(2,1)S(1)}, u32[]{:S(2)}, u32[]{:S(2)}) collective-permute-start(bf16[128,2048]{1,0:T(8,128)(2,1)S(1)} %get-tuple-element.36.refs_3_), channel_id=1, source_target_pairs={{0,4},{1,5},{2,6},{3,7},{4,8},{5,9},{6,10},{7,11},{8,12},{9,13},{1... | collective-permute-start | bytes 1572872 | tf_op jit(solution)/shard_map/ppermute | solution.py:62
  63.7 1.2 collective-permute-start.11
  64.9 1.2 collective-permute-start.12
  66.1 2.6 %collective-permute-start.14 = (bf16[256,2048]{1,0:T(8,128)(2,1)}, bf16[256,2048]{1,0:T(8,128)(2,1)}, u32[]{:S(2)}, u32[]{:S(2)}) collective-permute-start(bf16[256,2048]{1,0:T(8,128)(2,1)} %bitcast.38), channel_id=1, source_target_pairs={{0,16},{16,0},{1,17},{17,1},{2,18},{18,2},{3,19},{19,3},{4,20},{20... | collective-permute-start | bytes 3145736 | tf_op jit(solution)/shard_map/ppermute | solution.py:497
  68.9 11.6 %collective-permute-done.10.refs_0_.refs_14_.refs_18_ = bf16[128,2048]{1,0:T(8,128)(2,1)S(1)} collective-permute-done((bf16[128,2048]{1,0:T(8,128)(2,1)S(1)}, bf16[128,2048]{1,0:T(8,128)(2,1)S(1)}, u32[]{:S(2)}, u32[]{:S(2)}) %collective-permute-start.10) | collective-permute-done | bytes 524320 | tf_op jit(solution)/shard_map/ppermute | solution.py:62
  80.5 1.0 collective-permute-done.11.refs_1_.refs_12_.refs_16_
  81.6 1.1 collective-permute-start.17
  82.7 1.8 %collective-permute-start.18 = (bf16[128,2048]{1,0:T(8,128)(2,1)S(1)}, bf16[128,2048]{1,0:T(8,128)(2,1)}, u32[]{:S(2)}, u32[]{:S(2)}) collective-permute-start(bf16[128,2048]{1,0:T(8,128)(2,1)S(1)} %get-tuple-element.46.refs_13_.refs_17_), channel_id=1, source_target_pairs={{0,12},{1,13},{2,14},{3,15},{4,0},{5,1},{6,2},{7,3},{8,4},{9,5},{1... | collective-permute-start | bytes 1572872 | tf_op jit(solution)/shard_map/ppermute | solution.py:62
  84.6 1.1 sum.1
  86.4 0.9 collective-permute-start.13
  87.4 11.7 %collective-permute-done.13.refs_3_ = f32[8,2048]{1,0:T(8,128)S(1)} collective-permute-done((f32[8,2048]{1,0:T(8,128)S(1)}, f32[8,2048]{1,0:T(8,128)S(1)}, u32[]{:S(2)}, u32[]{:S(2)}) %collective-permute-start.13) | collective-permute-done | bytes 65568 | tf_op jit(solution)/shard_map/ppermute | solution.py:62
  99.7 2.0 %collective-permute-start.15 = (f32[2,2048]{1,0:T(2,128)S(1)}, f32[2,2048]{1,0:T(2,128)S(1)}, u32[]{:S(2)}, u32[]{:S(2)}) collective-permute-start(f32[2,2048]{1,0:T(2,128)S(1)} %fusion), channel_id=1, source_target_pairs={{0,16},{16,0},{1,17},{17,1},{2,18},{18,2},{3,19},{19,3},{4,20},{20... | collective-permute-start | bytes 49160 | tf_op jit(solution)/shard_map/ppermute | solution.py:286
  102.3 0.8 copy-done.20
  103.1 0.8 copy-done.22
  105.6 1.2 copy-done.15
  106.8 0.9 copy-done.18
  107.7 3.1 %norm.1 = (bf16[256,2048]{1,0:T(8,128)(2,1)S(1)}, bf16[176,2048]{1,0:T(8,128)(2,1)S(1)}, f32[256,2048]{1,0:T(8,128)S(1)}) custom-call(s32[1]{0:T(128)} %bitcast.refs_0_, bf16[256,2048]{1,0:T(8,128)(2,1)S(1)} %bitcast.40, f32[256,1]{1,0:T(8,128)S(1)} %copy.34.refs_2_, f32[16,2048]{1,0:T(8,128)S(1)} %rows.1.refs_3_, f32[1,2048]{1,0:T(1,128)S(1)} %copy-done.23, ...), custom_call_target="tpu_custom_call" | custom-call | tf_op jit(solution)/shard_map/norm/pallas_call | solution.py:83
  110.8 1.0 copy-done.1
  111.8 1.0 copy-done.3
  112.9 1.0 copy-done.5
  113.9 1.0 copy-done.7
  115.0 1.0 copy-done.9
  116.0 1.0 copy-done.11
  117.0 2.9 %project.1 = (f32[256,1024]{1,0:T(8,128)S(1)}, f32[176,512]{1,0:T(8,128)S(1)}) custom-call(s32[16]{0:T(128)S(1)} %stack.67.refs_0_, bf16[256,2048]{1,0:T(8,128)(2,1)S(1)} %get-tuple-element.42.refs_1_.refs_3_, bf16[176,2048]{1,0:T(8,128)(2,1)S(1)} %get-tuple-element.44.refs_2_.refs_4_, bf16[128,2048]{1,0:T(8,128)(2,1)S(1)} %copy-done.9, ...), custom_call_target="tpu_custom_call" | custom-call | tf_op jit(solution)/shard_map/project/pallas_call | solution.py:83
  119.9 4.2 %attend.1 = (f32[176,2048]{1,0:T(8,128)S(1)}, bf16[176,2048]{1,0:T(8,128)(2,1)S(1)}) custom-call(s32[16]{0:T(128)S(1)} %stack.67.refs_0_, s32[176,1]{1,0:T(8,128)S(1)} %copy.36.refs_1_, s32[1,256]{1,0:T(1,128)S(1)} %bitcast.46, bf16[256,2048]{1,0:T(8,128)(2,1)S(1)} %get-tuple-element.42.refs_1_.refs_3_, ...), custom_call_target="tpu_custom_call" | custom-call | tf_op jit(solution)/shard_map/attend/pallas_call | solution.py:83
  124.1 1.3 collective-permute-start.20
  125.5 2.8 %collective-permute-done.20.refs_4_ = bf16[176,2048]{1,0:T(8,128)(2,1)S(1)} collective-permute-done((bf16[176,2048]{1,0:T(8,128)(2,1)S(1)}, bf16[176,2048]{1,0:T(8,128)(2,1)S(1)}, u32[]{:S(2)}, u32[]{:S(2)}) %collective-permute-start.20) | collective-permute-done | bytes 720928 | tf_op jit(solution)/shard_map/ppermute | solution.py:516
  128.2 1.5 %finish.1 = bf16[256,2048]{1,0:T(8,128)(2,1)} custom-call(s32[1]{0:T(128)} %bitcast.refs_0_, bf16[256,2048]{1,0:T(8,128)(2,1)S(1)} %get-tuple-element.42.refs_1_.refs_3_, f32[256,2048]{1,0:T(8,128)S(1)} %get-tuple-element.43.refs_2_, f32[176,2048]{1,0:T(8,128)S(1)} %get-tuple-element.49.refs_3_, bf16[176,2048]{1,0:T(8,128)(2,1)S(1)} %collective-permute-done.20.refs_4_, ...), custom_call_target="tpu_custom_call" | custom-call | tf_op jit(solution)/shard_map/finish/pallas_call | solution.py:83
  (83 shorter events, 7.5 us)
Async XLA Ops:
  2.0 42.7 %copy-start.8 = (bf16[128,2048]{1,0:T(8,128)(2,1)}, bf16[128,2048]{1,0:T(8,128)(2,1)S(1)}, u32[]{:S(2)}) copy-start(bf16[128,2048]{1,0:T(8,128)(2,1)S(1)} %pad_maximum_fusion.refs_3_.refs_7_) | copy-start | bytes 1572868
  2.1 24.2 %collective-permute-start.1 = (bf16[128,2048]{1,0:T(8,128)(2,1)S(1)}, bf16[128,2048]{1,0:T(8,128)(2,1)S(1)}, u32[]{:S(2)}, u32[]{:S(2)}) collective-permute-start(bf16[128,2048]{1,0:T(8,128)(2,1)S(1)} %pad_maximum_fusion.refs_3_.refs_7_), channel_id=1, source_target_pairs={{0,1},{1,0},{2,3},{3,2},{4,5},{5,4},{6,7},{7,6},{8,9},{9,8},{10,11... | collective-permute-start | bytes 1572872 | tf_op jit(solution)/shard_map/ppermute | solution.py:62
  4.2 22.1 %collective-permute-start.2 = (bf16[128,2048]{1,0:T(8,128)(2,1)S(1)}, bf16[128,2048]{1,0:T(8,128)(2,1)S(1)}, u32[]{:S(2)}, u32[]{:S(2)}) collective-permute-start(bf16[128,2048]{1,0:T(8,128)(2,1)S(1)} %pad_maximum_fusion.refs_3_.refs_7_), channel_id=1, source_target_pairs={{0,4},{1,5},{2,6},{3,7},{4,8},{5,9},{6,10},{7,11},{8,12},{9,13},{1... | collective-permute-start | bytes 1572872 | tf_op jit(solution)/shard_map/ppermute | solution.py:62
  5.5 20.8 %collective-permute-start.3 = (bf16[128,2048]{1,0:T(8,128)(2,1)S(1)}, bf16[128,2048]{1,0:T(8,128)(2,1)S(1)}, u32[]{:S(2)}, u32[]{:S(2)}) collective-permute-start(bf16[128,2048]{1,0:T(8,128)(2,1)S(1)} %pad_maximum_fusion.refs_3_.refs_7_), channel_id=1, source_target_pairs={{0,2},{1,3},{2,0},{3,1},{4,6},{5,7},{6,4},{7,5},{8,10},{9,11},{10,... | collective-permute-start | bytes 1572872 | tf_op jit(solution)/shard_map/ppermute | solution.py:62
  7.4 1.2 copy-start.14
  8.6 1.0 copy-start.17
  9.7 0.7 copy-start.24
  11.1 10.2 %collective-permute-start = (bf16[8,2048]{1,0:T(8,128)(2,1)S(1)}, bf16[8,2048]{1,0:T(8,128)(2,1)S(1)}, u32[]{:S(2)}, u32[]{:S(2)}) collective-permute-start(bf16[8,2048]{1,0:T(8,128)(2,1)S(1)} %get-tuple-element.30), channel_id=1, source_target_pairs={{0,8},{1,9},{2,10},{3,11},{4,12},{5,13},{6,14},{7,15},{8,0},{9,1},... | collective-permute-start | bytes 98312 | tf_op jit(solution)/shard_map/ppermute | solution.py:62
  22.1 26.4 %all-to-all-start = ((bf16[8,16,2048]{2,1,0:T(8,128)(2,1)}), bf16[8,16,2048]{2,1,0:T(8,128)(2,1)}, u32[]{:S(2)}, u32[]{:S(2)}) async-start(bf16[8,16,2048]{2,1,0:T(8,128)(2,1)} %bitcast.7), calls=%async_computation | async-start | bytes 1048576 | tf_op jit(solution)/shard_map/all_to_all | solution.py:232
  26.3 20.7 %copy-start.6 = (bf16[128,2048]{1,0:T(8,128)(2,1)}, bf16[128,2048]{1,0:T(8,128)(2,1)S(1)}, u32[]{:S(2)}) copy-start(bf16[128,2048]{1,0:T(8,128)(2,1)S(1)} %get-tuple-element.32.refs_9_.refs_13_) | copy-start | bytes 1572868
  26.3 18.5 %collective-permute-start.4 = (bf16[128,2048]{1,0:T(8,128)(2,1)S(1)}, bf16[128,2048]{1,0:T(8,128)(2,1)S(1)}, u32[]{:S(2)}, u32[]{:S(2)}) collective-permute-start(bf16[128,2048]{1,0:T(8,128)(2,1)S(1)} %get-tuple-element.31.refs_1_), channel_id=1, source_target_pairs={{0,2},{1,3},{2,0},{3,1},{4,6},{5,7},{6,4},{7,5},{8,10},{9,11},{10,... | collective-permute-start | bytes 1572872 | tf_op jit(solution)/shard_map/ppermute | solution.py:62
  27.7 17.1 %collective-permute-start.5 = (bf16[128,2048]{1,0:T(8,128)(2,1)S(1)}, bf16[128,2048]{1,0:T(8,128)(2,1)S(1)}, u32[]{:S(2)}, u32[]{:S(2)}) collective-permute-start(bf16[128,2048]{1,0:T(8,128)(2,1)S(1)} %get-tuple-element.31.refs_1_), channel_id=1, source_target_pairs={{0,4},{1,5},{2,6},{3,7},{4,8},{5,9},{6,10},{7,11},{8,12},{9,13},{1... | collective-permute-start | bytes 1572872 | tf_op jit(solution)/shard_map/ppermute | solution.py:62
  28.9 15.9 %collective-permute-start.6 = (bf16[128,2048]{1,0:T(8,128)(2,1)S(1)}, bf16[128,2048]{1,0:T(8,128)(2,1)S(1)}, u32[]{:S(2)}, u32[]{:S(2)}) collective-permute-start(bf16[128,2048]{1,0:T(8,128)(2,1)S(1)} %get-tuple-element.32.refs_9_.refs_13_), channel_id=1, source_target_pairs={{0,1},{1,0},{2,3},{3,2},{4,5},{5,4},{6,7},{7,6},{8,9},{9,8},{10,11... | collective-permute-start | bytes 1572872 | tf_op jit(solution)/shard_map/ppermute | solution.py:62
  44.8 2.4 %copy-start.10 = (bf16[128,2048]{1,0:T(8,128)(2,1)}, bf16[128,2048]{1,0:T(8,128)(2,1)S(1)}, u32[]{:S(2)}) copy-start(bf16[128,2048]{1,0:T(8,128)(2,1)S(1)} %collective-permute-done.4.refs_0_.refs_10_.refs_14_) | copy-start | bytes 1572868
  44.8 17.5 %collective-permute-start.7 = (bf16[128,2048]{1,0:T(8,128)(2,1)S(1)}, bf16[128,2048]{1,0:T(8,128)(2,1)S(1)}, u32[]{:S(2)}, u32[]{:S(2)}) collective-permute-start(bf16[128,2048]{1,0:T(8,128)(2,1)S(1)} %get-tuple-element.34.refs_4_.refs_8_), channel_id=1, source_target_pairs={{0,1},{1,0},{2,3},{3,2},{4,5},{5,4},{6,7},{7,6},{8,9},{9,8},{10,11... | collective-permute-start | bytes 1572872 | tf_op jit(solution)/shard_map/ppermute | solution.py:62
  47.0 15.3 %collective-permute-start.8 = (bf16[128,2048]{1,0:T(8,128)(2,1)S(1)}, bf16[128,2048]{1,0:T(8,128)(2,1)}, u32[]{:S(2)}, u32[]{:S(2)}) collective-permute-start(bf16[128,2048]{1,0:T(8,128)(2,1)S(1)} %get-tuple-element.33.refs_3_.refs_2_), channel_id=1, source_target_pairs={{0,2},{1,3},{2,0},{3,1},{4,6},{5,7},{6,4},{7,5},{8,10},{9,11},{10,... | collective-permute-start | bytes 1572872 | tf_op jit(solution)/shard_map/ppermute | solution.py:62
  47.1 15.2 %collective-permute-start.9 = (bf16[128,2048]{1,0:T(8,128)(2,1)S(1)}, bf16[128,2048]{1,0:T(8,128)(2,1)S(1)}, u32[]{:S(2)}, u32[]{:S(2)}) collective-permute-start(bf16[128,2048]{1,0:T(8,128)(2,1)S(1)} %get-tuple-element.33.refs_3_.refs_2_), channel_id=1, source_target_pairs={{0,4},{1,5},{2,6},{3,7},{4,8},{5,9},{6,10},{7,11},{8,12},{9,13},{1... | collective-permute-start | bytes 1572872 | tf_op jit(solution)/shard_map/ppermute | solution.py:62
  48.4 2.2 %copy-start.12 = (bf16[1,2048,1024]{2,1,0:T(8,128)(2,1)S(1)}, bf16[1,2048,1024]{2,1,0:T(8,128)(2,1)}, u32[]{:S(2)}) copy-start(bf16[1,2048,1024]{2,1,0:T(8,128)(2,1)} %param.18) | copy-start | bytes 12582916
  50.6 2.2 %copy-start.13 = (bf16[1,1024,2048]{2,1,0:T(8,128)(2,1)S(1)}, bf16[1,1024,2048]{2,1,0:T(8,128)(2,1)}, u32[]{:S(2)}) copy-start(bf16[1,1024,2048]{2,1,0:T(8,128)(2,1)} %param.19) | copy-start | bytes 12582916
  52.8 15.9 %copy-start.25 = (s32[1,4]{1,0:T(1,128)S(1)}, s32[1,4]{1,0:T(1,128)}, u32[]{:S(2)}) copy-start(s32[1,4]{1,0:T(1,128)} %param.23) | copy-start | bytes 52
  52.8 16.0 %copy-start.23 = (f32[1,2048]{1,0:T(1,128)S(1)}, f32[1,2048]{1,0:T(1,128)}, u32[]{:S(2)}) copy-start(f32[1,2048]{1,0:T(1,128)} %refs_4_.3) | copy-start | bytes 24580
  57.2 0.8 copy-start.16
  58.0 29.3 %copy-start.26 = (s32[1,4]{1,0:T(1,128)S(1)}, s32[1,4]{1,0:T(1,128)}, u32[]{:S(2)}) copy-start(s32[1,4]{1,0:T(1,128)} %param.22) | copy-start | bytes 52
  58.0 26.6 %all-to-all-start.1 = ((bf16[8,16,2048]{2,1,0:T(8,128)(2,1)}), bf16[8,16,2048]{2,1,0:T(8,128)(2,1)}, u32[]{:S(2)}, u32[]{:S(2)}) async-start(bf16[8,16,2048]{2,1,0:T(8,128)(2,1)} %bitcast.41), calls=%async_computation.1 | async-start | bytes 1048576 | tf_op jit(solution)/shard_map/all_to_all | solution.py:232
  62.3 2.6 %copy-start = (bf16[128,2048]{1,0:T(8,128)(2,1)}, bf16[128,2048]{1,0:T(8,128)(2,1)S(1)}, u32[]{:S(2)}) copy-start(bf16[128,2048]{1,0:T(8,128)(2,1)S(1)} %collective-permute-done.7.refs_0_.refs_8_.refs_12_) | copy-start | bytes 1572868
  62.4 18.2 %collective-permute-start.10 = (bf16[128,2048]{1,0:T(8,128)(2,1)S(1)}, bf16[128,2048]{1,0:T(8,128)(2,1)S(1)}, u32[]{:S(2)}, u32[]{:S(2)}) collective-permute-start(bf16[128,2048]{1,0:T(8,128)(2,1)S(1)} %get-tuple-element.36.refs_3_), channel_id=1, source_target_pairs={{0,4},{1,5},{2,6},{3,7},{4,8},{5,9},{6,10},{7,11},{8,12},{9,13},{1... | collective-permute-start | bytes 1572872 | tf_op jit(solution)/shard_map/ppermute | solution.py:62
  63.7 17.8 %collective-permute-start.11 = (bf16[128,2048]{1,0:T(8,128)(2,1)S(1)}, bf16[128,2048]{1,0:T(8,128)(2,1)S(1)}, u32[]{:S(2)}, u32[]{:S(2)}) collective-permute-start(bf16[128,2048]{1,0:T(8,128)(2,1)S(1)} %get-tuple-element.37.refs_2_), channel_id=1, source_target_pairs={{0,2},{1,3},{2,0},{3,1},{4,6},{5,7},{6,4},{7,5},{8,10},{9,11},{10,... | collective-permute-start | bytes 1572872 | tf_op jit(solution)/shard_map/ppermute | solution.py:62
  64.9 16.6 %collective-permute-start.12 = (bf16[128,2048]{1,0:T(8,128)(2,1)S(1)}, bf16[128,2048]{1,0:T(8,128)(2,1)S(1)}, u32[]{:S(2)}, u32[]{:S(2)}) collective-permute-start(bf16[128,2048]{1,0:T(8,128)(2,1)S(1)} %get-tuple-element.38.refs_5_.refs_9_), channel_id=1, source_target_pairs={{0,1},{1,0},{2,3},{3,2},{4,5},{5,4},{6,7},{7,6},{8,9},{9,8},{10,11... | collective-permute-start | bytes 1572872 | tf_op jit(solution)/shard_map/ppermute | solution.py:62
  66.1 38.8 %collective-permute-start.14 = (bf16[256,2048]{1,0:T(8,128)(2,1)}, bf16[256,2048]{1,0:T(8,128)(2,1)}, u32[]{:S(2)}, u32[]{:S(2)}) collective-permute-start(bf16[256,2048]{1,0:T(8,128)(2,1)} %bitcast.38), channel_id=1, source_target_pairs={{0,16},{16,0},{1,17},{17,1},{2,18},{18,2},{3,19},{19,3},{4,20},{20... | collective-permute-start | bytes 3145736 | tf_op jit(solution)/shard_map/ppermute | solution.py:497
  80.5 4.0 %copy-start.2 = (bf16[128,2048]{1,0:T(8,128)(2,1)}, bf16[128,2048]{1,0:T(8,128)(2,1)S(1)}, u32[]{:S(2)}) copy-start(bf16[128,2048]{1,0:T(8,128)(2,1)S(1)} %collective-permute-done.10.refs_0_.refs_14_.refs_18_) | copy-start | bytes 1572868
  81.6 3.0 %copy-start.4 = (bf16[128,2048]{1,0:T(8,128)(2,1)}, bf16[128,2048]{1,0:T(8,128)(2,1)S(1)}, u32[]{:S(2)}) copy-start(bf16[128,2048]{1,0:T(8,128)(2,1)S(1)} %collective-permute-done.11.refs_1_.refs_12_.refs_16_) | copy-start | bytes 1572868
  81.6 38.4 %collective-permute-start.17 = (bf16[128,2048]{1,0:T(8,128)(2,1)S(1)}, bf16[128,2048]{1,0:T(8,128)(2,1)}, u32[]{:S(2)}, u32[]{:S(2)}) collective-permute-start(bf16[128,2048]{1,0:T(8,128)(2,1)S(1)} %get-tuple-element.45.refs_6_.refs_10_), channel_id=1, source_target_pairs={{0,1},{1,0},{2,3},{3,2},{4,5},{5,4},{6,7},{7,6},{8,9},{9,8},{10,11... | collective-permute-start | bytes 1572872 | tf_op jit(solution)/shard_map/ppermute | solution.py:62
  82.7 37.2 %collective-permute-start.18 = (bf16[128,2048]{1,0:T(8,128)(2,1)S(1)}, bf16[128,2048]{1,0:T(8,128)(2,1)}, u32[]{:S(2)}, u32[]{:S(2)}) collective-permute-start(bf16[128,2048]{1,0:T(8,128)(2,1)S(1)} %get-tuple-element.46.refs_13_.refs_17_), channel_id=1, source_target_pairs={{0,12},{1,13},{2,14},{3,15},{4,0},{5,1},{6,2},{7,3},{8,4},{9,5},{1... | collective-permute-start | bytes 1572872 | tf_op jit(solution)/shard_map/ppermute | solution.py:62
  84.5 35.4 %collective-permute-start.19 = (bf16[128,2048]{1,0:T(8,128)(2,1)S(1)}, bf16[128,2048]{1,0:T(8,128)(2,1)}, u32[]{:S(2)}, u32[]{:S(2)}) collective-permute-start(bf16[128,2048]{1,0:T(8,128)(2,1)S(1)} %get-tuple-element.39.refs_1_.refs_15_.refs_19_), channel_id=1, source_target_pairs={{0,2},{1,3},{2,0},{3,1},{4,6},{5,7},{6,4},{7,5},{8,10},{9,11},{10,... | collective-permute-start | bytes 1572872 | tf_op jit(solution)/shard_map/ppermute | solution.py:62
  86.4 12.8 %collective-permute-start.13 = (f32[8,2048]{1,0:T(8,128)S(1)}, f32[8,2048]{1,0:T(8,128)S(1)}, u32[]{:S(2)}, u32[]{:S(2)}) collective-permute-start(f32[8,2048]{1,0:T(8,128)S(1)} %get-tuple-element.41), channel_id=1, source_target_pairs={{0,8},{1,9},{2,10},{3,11},{4,12},{5,13},{6,14},{7,15},{8,0},{9,1},... | collective-permute-start | bytes 196616 | tf_op jit(solution)/shard_map/ppermute | solution.py:62
  99.7 4.3 %collective-permute-start.15 = (f32[2,2048]{1,0:T(2,128)S(1)}, f32[2,2048]{1,0:T(2,128)S(1)}, u32[]{:S(2)}, u32[]{:S(2)}) collective-permute-start(f32[2,2048]{1,0:T(2,128)S(1)} %fusion), channel_id=1, source_target_pairs={{0,16},{16,0},{1,17},{17,1},{2,18},{18,2},{3,19},{19,3},{4,20},{20... | collective-permute-start | bytes 49160 | tf_op jit(solution)/shard_map/ppermute | solution.py:286
  102.3 0.8 copy-start.20
  103.1 0.8 copy-start.22
  104.1 1.5 %collective-permute-start.16 = (f32[16,2048]{1,0:T(8,128)S(1)}, f32[16,2048]{1,0:T(8,128)}, u32[]{:S(2)}, u32[]{:S(2)}) collective-permute-start(f32[16,2048]{1,0:T(8,128)S(1)} %rows.1.refs_3_), channel_id=1, source_target_pairs={{0,16},{16,0},{1,17},{17,1},{2,18},{18,2},{3,19},{19,3},{4,20},{20... | collective-permute-start | bytes 393224 | tf_op jit(solution)/shard_map/ppermute | solution.py:287
  105.6 1.2 copy-start.15
  106.8 0.9 copy-start.18
  110.8 1.0 copy-start.1
  111.8 1.0 copy-start.3
  112.9 1.0 copy-start.5
  113.9 1.0 copy-start.7
  115.0 1.0 copy-start.9
  116.0 1.0 copy-start.11
  124.1 4.1 %collective-permute-start.20 = (bf16[176,2048]{1,0:T(8,128)(2,1)S(1)}, bf16[176,2048]{1,0:T(8,128)(2,1)S(1)}, u32[]{:S(2)}, u32[]{:S(2)}) collective-permute-start(bf16[176,2048]{1,0:T(8,128)(2,1)S(1)} %get-tuple-element.50), channel_id=1, source_target_pairs={{0,16},{1,17},{2,18},{3,19},{4,20},{5,21},{6,22},{7,23},{8,24},{9,... | collective-permute-start | bytes 2162696 | tf_op jit(solution)/shard_map/ppermute | solution.py:516
  (2 other events, 1.3 us)

commit v6 on v3

--- a/solution.py
+++ b/solution.py
@@ -281,6 +281,9 @@
     return parts[0] if len(parts) == 1 else jnp.concatenate(parts, axis=axis)
 
 
+AHEAD = 4
+
+
 def fetched(blocks, columns, near, sems):
     rows = blocks[0].shape[0]
     copies = [
@@ -289,9 +292,16 @@
         )
         for i, block in enumerate(blocks)
     ]
-    for copy in copies:
+    for copy in copies[:AHEAD]:
         copy.start()
     return copies
+
+
+def arrived(copies, members):
+    for i in members:
+        copies[i].wait()
+        if i + AHEAD < len(copies):
+            copies[i + AHEAD].start()
 
 
 def add_blocks(order, memory, target, near, copies, kv, q, fresh):
@@ -304,8 +314,7 @@
         )
 
     for step, members in enumerate(pairs_of(copies)):
-        for i in members:
-            copies[i].wait()
+        arrived(copies, members)
         weights = near[members[0] * rows : (members[-1] + 1) * rows]
         kv_part = dot(columns(memory, members), weights[:, : 2 * half])
         q_part = dot(columns(target, members), weights[:, 2 * half :])
@@ -332,10 +341,9 @@
     q[...] = q_sum[...]
     if late:
         copies = fetched(blocks[early:], pl.ds(0, 3 * half), near, sems)
-    copies_out = fetched(blocks, pl.ds(3 * half, half), near_out, sems_out)
-    if late:
         late_order = [order[early + i] for i in range(late)]
         add_blocks(late_order, memory, target, near, copies, kv, q, False)
+    copies_out = fetched(blocks, pl.ds(3 * half, half), near_out, sems_out)
     allowed = seg_q[...] == seg_k[...]
     for low in range(0, half, HD):
         query = q[:, low : low + HD].astype(jnp.bfloat16)
@@ -345,9 +353,8 @@
         expd = jnp.exp(scores - jnp.max(scores, axis=-1, keepdims=True))
         prob = (expd / jnp.sum(expd, axis=-1, keepdims=True)).astype(jnp.bfloat16)
         context[:, low : low + HD] = dot(prob, values).astype(jnp.bfloat16)
-    for copy in copies_out:
-        copy.wait()
     for members in pairs_of(blocks):
+        arrived(copies_out, members)
         part = dot_rows(context[...], near_out[members[0] * rows : (members[-1] + 1) * rows])
         for place, i in enumerate(members):
             columns = pl.ds(pl.multiple_of(order[i] * rows, 128), rows)

time: 123 us -> 127 us (1.033)
  Pallas kernels: 20.6 us -> 24.4 us
    pallas_call x11, Pallas kernels: 20.6 us -> 24.4 us  [local(): pl.pallas_call(run, out_shape=[jax.ShapeDtypeStruct(shape, dtype) for sha...]
  transfers between devices with their start and end apart: 21 -> 21, of which waited for: 6 -> 6; matrix products, arithmetic and copies ran while one was open for 2% -> 2% of each run, Pallas kernels for 10% -> 11%
where the time goes in v6:
time: 127 us; the launch traced here: 126 us
  starting transfers between devices  45.6 us (36%)
  waiting for transfers between devices  35.8 us (28%)
  Pallas kernels  24.4 us (19%)
  local copies, waits for them, and re-layouts  18.8 us (15%)
    ppermute x15, waiting for transfers between devices, moved(): return lax.ppermute(value, 'ep', pairs)  32.5 us
    pallas_call x11, Pallas kernels, local(): pl.pallas_call(run, out_shape=[jax.ShapeDtypeStruct(shape, dtype) for sha...  24.4 us
    unnamed x54, local copies, waits for them, and re-layouts  15.6 us
    ppermute x15, starting transfers between devices, moved(): return lax.ppermute(value, 'ep', pairs)  14.1 us
    ppermute x1, starting transfers between devices, both_norms(): other_rows = lax.ppermute(rows, 'grp', swap)  13.8 us
    all_to_all x2, starting transfers between devices, exchanged(): parts = lax.all_to_all(parts, 'ep', split_axis=0, concat_axis=0, tiled=True)  12.9 us
    ppermute x1, starting transfers between devices, body(): other_hidden = lax.ppermute(hidden[0], 'grp', [(0, 1), (1, 0)])  3.43 us
    ppermute x1, waiting for transfers between devices, body(): received = lax.ppermute(sent, 'grp', [(0, 1)])  2.98 us
  transfers between devices with their start and end apart: 21, of which 6 were waited for; matrix products, arithmetic and copies ran while one was open for 2% of the time, Pallas kernels for 11%

profile of v6, /device:TPU:29, one launch (start us, length us, event | category | flops | bytes accessed | tf_op | source)
XLA Modules:
  0.0 126.2 jit_solution(11180371136793956120)
XLA Ops:
  0.0 1.0 constant_dynamic-slice_fusion
  1.0 1.0 constant_dynamic-slice_fusion.2
  2.1 1.3 %collective-permute-start = (bf16[128,2048]{1,0:T(8,128)(2,1)S(1)}, bf16[128,2048]{1,0:T(8,128)(2,1)S(1)}, u32[]{:S(2)}, u32[]{:S(2)}) collective-permute-start(bf16[128,2048]{1,0:T(8,128)(2,1)S(1)} %pad_maximum_fusion.refs_3_.refs_7_), channel_id=1, source_target_pairs={{0,1},{1,0},{2,3},{3,2},{4,5},{5,4},{6,7},{7,6},{8,9},{9,8},{10,11... | collective-permute-start | bytes 1572872 | tf_op jit(solution)/shard_map/ppermute | solution.py:62
  3.3 0.2 collective-permute-start.2
  3.6 0.7 fusion.2
  4.3 1.2 copy-done.15
  5.5 1.0 copy-done.21
  6.5 0.7 copy-done.24
  7.2 0.7 pack.1
  8.0 0.8 copy-done.22
  8.7 6.2 %all-to-all-start = ((bf16[16,8,2048]{2,1,0:T(8,128)(2,1)}), bf16[16,8,2048]{2,1,0:T(8,128)(2,1)}, u32[]{:S(2)}, u32[]{:S(2)}) async-start(bf16[16,8,2048]{2,1,0:T(8,128)(2,1)} %bitcast.42), calls=%async_computation | async-start | bytes 1048576 | tf_op jit(solution)/shard_map/all_to_all | solution.py:200
  15.0 0.8 collective-permute-done.1.refs_1_
  15.8 0.2 collective-permute-start.3
  16.0 1.9 %collective-permute-start.4 = (bf16[128,2048]{1,0:T(8,128)(2,1)S(1)}, bf16[128,2048]{1,0:T(8,128)(2,1)S(1)}, u32[]{:S(2)}, u32[]{:S(2)}) collective-permute-start(bf16[128,2048]{1,0:T(8,128)(2,1)S(1)} %get-tuple-element.27.refs_1_), channel_id=1, source_target_pairs={{0,4},{1,5},{2,6},{3,7},{4,8},{5,9},{6,10},{7,11},{8,12},{9,13},{1... | collective-permute-start | bytes 1572872 | tf_op jit(solution)/shard_map/ppermute | solution.py:62
  17.9 0.5 collective-permute-start.5
  18.4 15.0 %collective-permute-done.3.refs_0_.refs_10_.refs_14_ = bf16[128,2048]{1,0:T(8,128)(2,1)S(1)} collective-permute-done((bf16[128,2048]{1,0:T(8,128)(2,1)S(1)}, bf16[128,2048]{1,0:T(8,128)(2,1)S(1)}, u32[]{:S(2)}, u32[]{:S(2)}) %collective-permute-start.3) | collective-permute-done | bytes 524320 | tf_op jit(solution)/shard_map/ppermute | solution.py:62
  33.5 2.4 %collective-permute-done.4.refs_2_ = bf16[128,2048]{1,0:T(8,128)(2,1)S(1)} collective-permute-done((bf16[128,2048]{1,0:T(8,128)(2,1)S(1)}, bf16[128,2048]{1,0:T(8,128)(2,1)S(1)}, u32[]{:S(2)}, u32[]{:S(2)}) %collective-permute-start.4) | collective-permute-done | bytes 524320 | tf_op jit(solution)/shard_map/ppermute | solution.py:62
  35.9 0.5 collective-permute-start.6
  36.5 2.5 %collective-permute-start.8 = (bf16[128,2048]{1,0:T(8,128)(2,1)S(1)}, bf16[128,2048]{1,0:T(8,128)(2,1)S(1)}, u32[]{:S(2)}, u32[]{:S(2)}) collective-permute-start(bf16[128,2048]{1,0:T(8,128)(2,1)S(1)} %get-tuple-element.29.refs_3_.refs_2_), channel_id=1, source_target_pairs={{0,4},{1,5},{2,6},{3,7},{4,8},{5,9},{6,10},{7,11},{8,12},{9,13},{1... | collective-permute-start | bytes 1572872 | tf_op jit(solution)/shard_map/ppermute | solution.py:62
  39.0 2.2 %copy-done.13 = bf16[1,2048,1024]{2,1,0:T(8,128)(2,1)S(1)} copy-done((bf16[1,2048,1024]{2,1,0:T(8,128)(2,1)S(1)}, bf16[1,2048,1024]{2,1,0:T(8,128)(2,1)}, u32[]{:S(2)}) %copy-start.13) | copy-done | bytes 4194328
  41.2 2.2 %copy-done.14 = bf16[1,1024,2048]{2,1,0:T(8,128)(2,1)S(1)} copy-done((bf16[1,1024,2048]{2,1,0:T(8,128)(2,1)S(1)}, bf16[1,1024,2048]{2,1,0:T(8,128)(2,1)}, u32[]{:S(2)}) %copy-start.14) | copy-done | bytes 4194328
  43.4 2.4 %mlp.1 = bf16[128,2048]{1,0:T(8,128)(2,1)S(1)} custom-call(bf16[128,2048]{1,0:T(8,128)(2,1)} %bitcast.7.refs_0_, bf16[2048,1024]{1,0:T(8,128)(2,1)S(1)} %bitcast.35, bf16[1024,2048]{1,0:T(8,128)(2,1)S(1)} %bitcast.36, bf16[128,2048]{1,0:T(8,128)(2,1)S(1)} %get-tuple-element.29.refs_3_.refs_2_), custom_call_target="tpu_custom_call" | custom-call | tf_op jit(solution)/shard_map/mlp/pallas_call | solution.py:83
  45.8 0.8 copy-done.18
  46.6 6.7 %all-to-all-start.1 = ((bf16[16,8,2048]{2,1,0:T(8,128)(2,1)}), bf16[16,8,2048]{2,1,0:T(8,128)(2,1)}, u32[]{:S(2)}, u32[]{:S(2)}) async-start(bf16[16,8,2048]{2,1,0:T(8,128)(2,1)} %bitcast.40), calls=%async_computation.1 | async-start | bytes 1048576 | tf_op jit(solution)/shard_map/all_to_all | solution.py:200
  53.3 0.3 collective-permute-start.9
  53.8 0.3 copy-done.6
  54.0 1.2 collective-permute-start.11
  55.2 3.4 %collective-permute-start.12 = (bf16[256,2048]{1,0:T(8,128)(2,1)}, bf16[256,2048]{1,0:T(8,128)(2,1)}, u32[]{:S(2)}, u32[]{:S(2)}) collective-permute-start(bf16[256,2048]{1,0:T(8,128)(2,1)} %bitcast.37), channel_id=1, source_target_pairs={{0,16},{16,0},{1,17},{17,1},{2,18},{18,2},{3,19},{19,3},{4,20},{20... | collective-permute-start | bytes 3145736 | tf_op jit(solution)/shard_map/ppermute | solution.py:449
  58.8 14.2 %collective-permute-done.9.refs_0_.refs_14_.refs_18_ = bf16[128,2048]{1,0:T(8,128)(2,1)S(1)} collective-permute-done((bf16[128,2048]{1,0:T(8,128)(2,1)S(1)}, bf16[128,2048]{1,0:T(8,128)(2,1)S(1)}, u32[]{:S(2)}, u32[]{:S(2)}) %collective-permute-start.9) | collective-permute-done | bytes 524320 | tf_op jit(solution)/shard_map/ppermute | solution.py:62
  73.1 1.2 collective-permute-start.15
  74.3 3.5 %collective-permute-start.16 = (bf16[128,2048]{1,0:T(8,128)(2,1)S(1)}, bf16[128,2048]{1,0:T(8,128)(2,1)}, u32[]{:S(2)}, u32[]{:S(2)}) collective-permute-start(bf16[128,2048]{1,0:T(8,128)(2,1)S(1)} %get-tuple-element.40.refs_13_.refs_17_), channel_id=1, source_target_pairs={{0,12},{1,13},{2,14},{3,15},{4,0},{5,1},{6,2},{7,3},{8,4},{9,5},{1... | collective-permute-start | bytes 1572872 | tf_op jit(solution)/shard_map/ppermute | solution.py:62
  77.8 0.5 collective-permute-start.17
  79.1 1.1 rows.1.refs_3_
  80.3 13.8 %collective-permute-start.14 = (f32[16,2048]{1,0:T(8,128)S(1)}, f32[16,2048]{1,0:T(8,128)}, u32[]{:S(2)}, u32[]{:S(2)}) collective-permute-start(f32[16,2048]{1,0:T(8,128)S(1)} %rows.1.refs_3_), channel_id=1, source_target_pairs={{0,16},{16,0},{1,17},{17,1},{2,18},{18,2},{3,19},{19,3},{4,20},{20... | collective-permute-start | bytes 393224 | tf_op jit(solution)/shard_map/ppermute | solution.py:232
  94.1 0.8 copy.35.refs_6_
  94.9 0.3 collective-permute-done.14.refs_7_
  95.2 1.2 copy-done.16
  96.4 0.9 copy-done.20
  97.3 2.9 %norm.1 = (bf16[256,2048]{1,0:T(8,128)(2,1)S(1)}, bf16[176,2048]{1,0:T(8,128)(2,1)S(1)}, f32[256,2048]{1,0:T(8,128)S(1)}) custom-call(s32[1]{0:T(128)} %bitcast.refs_0_, bf16[256,2048]{1,0:T(8,128)(2,1)S(1)} %bitcast.39, f32[256,1]{1,0:T(8,128)S(1)} %copy.34.refs_2_, f32[16,2048]{1,0:T(8,128)S(1)} %rows.1.refs_3_, f32[1,2048]{1,0:T(1,128)S(1)} %copy-done.23, ...), custom_call_target="tpu_custom_call" | custom-call | tf_op jit(solution)/shard_map/norm/pallas_call | solution.py:83
  100.2 1.0 copy-done.1
  101.2 0.9 copy-done.17
  102.0 1.0 copy-done.11
  103.1 6.4 %project.1 = (f32[256,1024]{1,0:T(8,128)}, f32[176,512]{1,0:T(8,128)S(1)}) custom-call(s32[16]{0:T(128)S(1)} %stack.67.refs_0_, bf16[256,2048]{1,0:T(8,128)(2,1)} %copy-done.1, bf16[176,2048]{1,0:T(8,128)(2,1)} %copy-done.17, bf16[128,2048]{1,0:T(8,128)(2,1)S(1)} %copy-done.11, bf16[128,2048]{1,0:T(8,128)(2,1)S(1)} %get-tuple-element.30.refs_4_.refs_8_, ...), custom_call_target="tpu_custom_call" | custom-call | tf_op jit(solution)/shard_map/project/pallas_call | solution.py:83
  109.5 9.5 %attend.1 = (f32[176,2048]{1,0:T(8,128)}, bf16[176,2048]{1,0:T(8,128)(2,1)}) custom-call(s32[16]{0:T(128)S(1)} %stack.67.refs_0_, s32[176,1]{1,0:T(8,128)S(1)} %copy.36.refs_1_, s32[1,256]{1,0:T(1,128)S(1)} %bitcast.46, bf16[256,2048]{1,0:T(8,128)(2,1)} %copy-done.1, bf16[176,2048]{1,0:T(8,128)(2,1)} %copy-done.17, f32[256,1024]{1,0:T(8,128)} %get-tuple-element.41.refs_5_, ...), custom_call_target="tpu_custom_call" | custom-call | tf_op jit(solution)/shard_map/attend/pallas_call | solution.py:83
  119.0 1.3 %collective-permute-start.18 = (bf16[176,2048]{1,0:T(8,128)(2,1)}, bf16[176,2048]{1,0:T(8,128)(2,1)S(1)}, u32[]{:S(2)}, u32[]{:S(2)}) collective-permute-start(bf16[176,2048]{1,0:T(8,128)(2,1)} %get-tuple-element.44), channel_id=1, source_target_pairs={{0,16},{1,17},{2,18},{3,19},{4,20},{5,21},{6,22},{7,23},{8,24},{9,... | collective-permute-start | bytes 2162696 | tf_op jit(solution)/shard_map/ppermute | solution.py:468
  120.3 3.0 %collective-permute-done.18.refs_4_ = bf16[176,2048]{1,0:T(8,128)(2,1)S(1)} collective-permute-done((bf16[176,2048]{1,0:T(8,128)(2,1)}, bf16[176,2048]{1,0:T(8,128)(2,1)S(1)}, u32[]{:S(2)}, u32[]{:S(2)}) %collective-permute-start.18) | collective-permute-done | bytes 720928 | tf_op jit(solution)/shard_map/ppermute | solution.py:468
  123.3 1.4 %copy-done.19 = f32[176,2048]{1,0:T(8,128)S(1)} copy-done((f32[176,2048]{1,0:T(8,128)S(1)}, f32[176,2048]{1,0:T(8,128)}, u32[]{:S(2)}) %copy-start.19) | copy-done | bytes 1441816
  124.6 1.5 %finish.1 = bf16[256,2048]{1,0:T(8,128)(2,1)} custom-call(s32[1]{0:T(128)} %bitcast.refs_0_, bf16[256,2048]{1,0:T(8,128)(2,1)S(1)} %copy-done.2, f32[256,2048]{1,0:T(8,128)S(1)} %get-tuple-element.37.refs_2_, f32[176,2048]{1,0:T(8,128)S(1)} %copy-done.19, bf16[176,2048]{1,0:T(8,128)(2,1)S(1)} %collective-permute-done.18.refs_4_, ...), custom_call_target="tpu_custom_call" | custom-call | tf_op jit(solution)/shard_map/finish/pallas_call | solution.py:83
  (77 shorter events, 1.2 us)
Async XLA Ops:
  2.0 33.8 %copy-start.10 = (bf16[128,2048]{1,0:T(8,128)(2,1)}, bf16[128,2048]{1,0:T(8,128)(2,1)S(1)}, u32[]{:S(2)}) copy-start(bf16[128,2048]{1,0:T(8,128)(2,1)S(1)} %pad_maximum_fusion.refs_3_.refs_7_) | copy-start | bytes 1572868
  2.1 12.9 %collective-permute-start = (bf16[128,2048]{1,0:T(8,128)(2,1)S(1)}, bf16[128,2048]{1,0:T(8,128)(2,1)S(1)}, u32[]{:S(2)}, u32[]{:S(2)}) collective-permute-start(bf16[128,2048]{1,0:T(8,128)(2,1)S(1)} %pad_maximum_fusion.refs_3_.refs_7_), channel_id=1, source_target_pairs={{0,1},{1,0},{2,3},{3,2},{4,5},{5,4},{6,7},{7,6},{8,9},{9,8},{10,11... | collective-permute-start | bytes 1572872 | tf_op jit(solution)/shard_map/ppermute | solution.py:62
  3.3 12.5 %collective-permute-start.1 = (bf16[128,2048]{1,0:T(8,128)(2,1)S(1)}, bf16[128,2048]{1,0:T(8,128)(2,1)S(1)}, u32[]{:S(2)}, u32[]{:S(2)}) collective-permute-start(bf16[128,2048]{1,0:T(8,128)(2,1)S(1)} %pad_maximum_fusion.refs_3_.refs_7_), channel_id=1, source_target_pairs={{0,4},{1,5},{2,6},{3,7},{4,8},{5,9},{6,10},{7,11},{8,12},{9,13},{1... | collective-permute-start | bytes 1572872 | tf_op jit(solution)/shard_map/ppermute | solution.py:62
  3.3 12.5 %collective-permute-start.2 = (bf16[128,2048]{1,0:T(8,128)(2,1)S(1)}, bf16[128,2048]{1,0:T(8,128)(2,1)S(1)}, u32[]{:S(2)}, u32[]{:S(2)}) collective-permute-start(bf16[128,2048]{1,0:T(8,128)(2,1)S(1)} %pad_maximum_fusion.refs_3_.refs_7_), channel_id=1, source_target_pairs={{0,2},{1,3},{2,0},{3,1},{4,6},{5,7},{6,4},{7,5},{8,10},{9,11},{10,... | collective-permute-start | bytes 1572872 | tf_op jit(solution)/shard_map/ppermute | solution.py:62
  4.3 1.2 copy-start.15
  5.5 1.0 copy-start.21
  6.5 0.7 copy-start.24
  7.9 0.8 copy-start.22
  8.7 30.2 %all-to-all-start = ((bf16[16,8,2048]{2,1,0:T(8,128)(2,1)}), bf16[16,8,2048]{2,1,0:T(8,128)(2,1)}, u32[]{:S(2)}, u32[]{:S(2)}) async-start(bf16[16,8,2048]{2,1,0:T(8,128)(2,1)} %bitcast.42), calls=%async_computation | async-start | bytes 1048576 | tf_op jit(solution)/shard_map/all_to_all | solution.py:200
  15.0 30.8 %copy-start.5 = (bf16[128,2048]{1,0:T(8,128)(2,1)}, bf16[128,2048]{1,0:T(8,128)(2,1)S(1)}, u32[]{:S(2)}) copy-start(bf16[128,2048]{1,0:T(8,128)(2,1)S(1)} %collective-permute-done.refs_0_.refs_7_.refs_11_) | copy-start | bytes 1572868
  15.8 20.6 %copy-start.9 = (bf16[128,2048]{1,0:T(8,128)(2,1)}, bf16[128,2048]{1,0:T(8,128)(2,1)S(1)}, u32[]{:S(2)}) copy-start(bf16[128,2048]{1,0:T(8,128)(2,1)S(1)} %get-tuple-element.28.refs_9_.refs_13_) | copy-start | bytes 1572868
  15.8 17.6 %collective-permute-start.3 = (bf16[128,2048]{1,0:T(8,128)(2,1)S(1)}, bf16[128,2048]{1,0:T(8,128)(2,1)S(1)}, u32[]{:S(2)}, u32[]{:S(2)}) collective-permute-start(bf16[128,2048]{1,0:T(8,128)(2,1)S(1)} %get-tuple-element.27.refs_1_), channel_id=1, source_target_pairs={{0,2},{1,3},{2,0},{3,1},{4,6},{5,7},{6,4},{7,5},{8,10},{9,11},{10,... | collective-permute-start | bytes 1572872 | tf_op jit(solution)/shard_map/ppermute | solution.py:62
  16.0 19.8 %collective-permute-start.4 = (bf16[128,2048]{1,0:T(8,128)(2,1)S(1)}, bf16[128,2048]{1,0:T(8,128)(2,1)S(1)}, u32[]{:S(2)}, u32[]{:S(2)}) collective-permute-start(bf16[128,2048]{1,0:T(8,128)(2,1)S(1)} %get-tuple-element.27.refs_1_), channel_id=1, source_target_pairs={{0,4},{1,5},{2,6},{3,7},{4,8},{5,9},{6,10},{7,11},{8,12},{9,13},{1... | collective-permute-start | bytes 1572872 | tf_op jit(solution)/shard_map/ppermute | solution.py:62
  17.9 18.0 %collective-permute-start.5 = (bf16[128,2048]{1,0:T(8,128)(2,1)S(1)}, bf16[128,2048]{1,0:T(8,128)(2,1)S(1)}, u32[]{:S(2)}, u32[]{:S(2)}) collective-permute-start(bf16[128,2048]{1,0:T(8,128)(2,1)S(1)} %get-tuple-element.28.refs_9_.refs_13_), channel_id=1, source_target_pairs={{0,1},{1,0},{2,3},{3,2},{4,5},{5,4},{6,7},{7,6},{8,9},{9,8},{10,11... | collective-permute-start | bytes 1572872 | tf_op jit(solution)/shard_map/ppermute | solution.py:62
  33.5 3.0 %copy-start.12 = (bf16[128,2048]{1,0:T(8,128)(2,1)}, bf16[128,2048]{1,0:T(8,128)(2,1)S(1)}, u32[]{:S(2)}) copy-start(bf16[128,2048]{1,0:T(8,128)(2,1)S(1)} %collective-permute-done.3.refs_0_.refs_10_.refs_14_) | copy-start | bytes 1572868
  35.9 17.4 %collective-permute-start.6 = (bf16[128,2048]{1,0:T(8,128)(2,1)S(1)}, bf16[128,2048]{1,0:T(8,128)(2,1)S(1)}, u32[]{:S(2)}, u32[]{:S(2)}) collective-permute-start(bf16[128,2048]{1,0:T(8,128)(2,1)S(1)} %get-tuple-element.30.refs_4_.refs_8_), channel_id=1, source_target_pairs={{0,1},{1,0},{2,3},{3,2},{4,5},{5,4},{6,7},{7,6},{8,9},{9,8},{10,11... | collective-permute-start | bytes 1572872 | tf_op jit(solution)/shard_map/ppermute | solution.py:62
  36.4 16.9 %collective-permute-start.7 = (bf16[128,2048]{1,0:T(8,128)(2,1)S(1)}, bf16[128,2048]{1,0:T(8,128)(2,1)}, u32[]{:S(2)}, u32[]{:S(2)}) collective-permute-start(bf16[128,2048]{1,0:T(8,128)(2,1)S(1)} %get-tuple-element.29.refs_3_.refs_2_), channel_id=1, source_target_pairs={{0,2},{1,3},{2,0},{3,1},{4,6},{5,7},{6,4},{7,5},{8,10},{9,11},{10,... | collective-permute-start | bytes 1572872 | tf_op jit(solution)/shard_map/ppermute | solution.py:62
  36.5 16.8 %collective-permute-start.8 = (bf16[128,2048]{1,0:T(8,128)(2,1)S(1)}, bf16[128,2048]{1,0:T(8,128)(2,1)S(1)}, u32[]{:S(2)}, u32[]{:S(2)}) collective-permute-start(bf16[128,2048]{1,0:T(8,128)(2,1)S(1)} %get-tuple-element.29.refs_3_.refs_2_), channel_id=1, source_target_pairs={{0,4},{1,5},{2,6},{3,7},{4,8},{5,9},{6,10},{7,11},{8,12},{9,13},{1... | collective-permute-start | bytes 1572872 | tf_op jit(solution)/shard_map/ppermute | solution.py:62
  39.0 2.2 %copy-start.13 = (bf16[1,2048,1024]{2,1,0:T(8,128)(2,1)S(1)}, bf16[1,2048,1024]{2,1,0:T(8,128)(2,1)}, u32[]{:S(2)}) copy-start(bf16[1,2048,1024]{2,1,0:T(8,128)(2,1)} %param.18) | copy-start | bytes 12582916
  41.2 2.2 %copy-start.14 = (bf16[1,1024,2048]{2,1,0:T(8,128)(2,1)S(1)}, bf16[1,1024,2048]{2,1,0:T(8,128)(2,1)}, u32[]{:S(2)}) copy-start(bf16[1,1024,2048]{2,1,0:T(8,128)(2,1)} %param.19) | copy-start | bytes 12582916
  43.4 15.3 %copy-start.23 = (f32[1,2048]{1,0:T(1,128)S(1)}, f32[1,2048]{1,0:T(1,128)}, u32[]{:S(2)}) copy-start(f32[1,2048]{1,0:T(1,128)} %refs_4_.1) | copy-start | bytes 24580
  43.4 15.4 %copy-start.25 = (s32[1,4]{1,0:T(1,128)S(1)}, s32[1,4]{1,0:T(1,128)}, u32[]{:S(2)}) copy-start(s32[1,4]{1,0:T(1,128)} %param.23) | copy-start | bytes 52
  45.8 0.8 copy-start.18
  46.6 31.9 %copy-start.26 = (s32[1,4]{1,0:T(1,128)S(1)}, s32[1,4]{1,0:T(1,128)}, u32[]{:S(2)}) copy-start(s32[1,4]{1,0:T(1,128)} %param.22) | copy-start | bytes 52
  46.6 32.6 %all-to-all-start.1 = ((bf16[16,8,2048]{2,1,0:T(8,128)(2,1)}), bf16[16,8,2048]{2,1,0:T(8,128)(2,1)}, u32[]{:S(2)}, u32[]{:S(2)}) async-start(bf16[16,8,2048]{2,1,0:T(8,128)(2,1)} %bitcast.40), calls=%async_computation.1 | async-start | bytes 1048576 | tf_op jit(solution)/shard_map/all_to_all | solution.py:200
  53.2 0.8 copy-start.6
  53.3 19.8 %collective-permute-start.9 = (bf16[128,2048]{1,0:T(8,128)(2,1)S(1)}, bf16[128,2048]{1,0:T(8,128)(2,1)S(1)}, u32[]{:S(2)}, u32[]{:S(2)}) collective-permute-start(bf16[128,2048]{1,0:T(8,128)(2,1)S(1)} %get-tuple-element.32.refs_3_), channel_id=1, source_target_pairs={{0,4},{1,5},{2,6},{3,7},{4,8},{5,9},{6,10},{7,11},{8,12},{9,13},{1... | collective-permute-start | bytes 1572872 | tf_op jit(solution)/shard_map/ppermute | solution.py:62
  53.6 19.4 %collective-permute-start.10 = (bf16[128,2048]{1,0:T(8,128)(2,1)S(1)}, bf16[128,2048]{1,0:T(8,128)(2,1)S(1)}, u32[]{:S(2)}, u32[]{:S(2)}) collective-permute-start(bf16[128,2048]{1,0:T(8,128)(2,1)S(1)} %get-tuple-element.33.refs_2_), channel_id=1, source_target_pairs={{0,2},{1,3},{2,0},{3,1},{4,6},{5,7},{6,4},{7,5},{8,10},{9,11},{10,... | collective-permute-start | bytes 1572872 | tf_op jit(solution)/shard_map/ppermute | solution.py:62
  54.0 19.0 %collective-permute-start.11 = (bf16[128,2048]{1,0:T(8,128)(2,1)S(1)}, bf16[128,2048]{1,0:T(8,128)(2,1)S(1)}, u32[]{:S(2)}, u32[]{:S(2)}) collective-permute-start(bf16[128,2048]{1,0:T(8,128)(2,1)S(1)} %get-tuple-element.34.refs_5_.refs_9_), channel_id=1, source_target_pairs={{0,1},{1,0},{2,3},{3,2},{4,5},{5,4},{6,7},{7,6},{8,9},{9,8},{10,11... | collective-permute-start | bytes 1572872 | tf_op jit(solution)/shard_map/ppermute | solution.py:62
  55.2 39.6 %collective-permute-start.12 = (bf16[256,2048]{1,0:T(8,128)(2,1)}, bf16[256,2048]{1,0:T(8,128)(2,1)}, u32[]{:S(2)}, u32[]{:S(2)}) collective-permute-start(bf16[256,2048]{1,0:T(8,128)(2,1)} %bitcast.37), channel_id=1, source_target_pairs={{0,16},{16,0},{1,17},{17,1},{2,18},{18,2},{3,19},{19,3},{4,20},{20... | collective-permute-start | bytes 3145736 | tf_op jit(solution)/shard_map/ppermute | solution.py:449
  58.7 21.6 %collective-permute-start.13 = (f32[2,2048]{1,0:T(2,128)S(1)}, f32[2,2048]{1,0:T(2,128)S(1)}, u32[]{:S(2)}, u32[]{:S(2)}) collective-permute-start(f32[2,2048]{1,0:T(2,128)S(1)} %fusion), channel_id=1, source_target_pairs={{0,16},{16,0},{1,17},{17,1},{2,18},{18,2},{3,19},{19,3},{4,20},{20... | collective-permute-start | bytes 49160 | tf_op jit(solution)/shard_map/ppermute | solution.py:231
  73.0 29.0 %copy-start.7 = (bf16[128,2048]{1,0:T(8,128)(2,1)}, bf16[128,2048]{1,0:T(8,128)(2,1)S(1)}, u32[]{:S(2)}) copy-start(bf16[128,2048]{1,0:T(8,128)(2,1)S(1)} %collective-permute-done.9.refs_0_.refs_14_.refs_18_) | copy-start | bytes 1572868
  73.0 4.8 %copy-start.8 = (bf16[128,2048]{1,0:T(8,128)(2,1)}, bf16[128,2048]{1,0:T(8,128)(2,1)S(1)}, u32[]{:S(2)}) copy-start(bf16[128,2048]{1,0:T(8,128)(2,1)S(1)} %collective-permute-done.10.refs_1_.refs_12_.refs_16_) | copy-start | bytes 1572868
  73.1 29.0 %copy-start = (bf16[128,2048]{1,0:T(8,128)(2,1)}, bf16[128,2048]{1,0:T(8,128)(2,1)S(1)}, u32[]{:S(2)}) copy-start(bf16[128,2048]{1,0:T(8,128)(2,1)S(1)} %get-tuple-element.40.refs_13_.refs_17_) | copy-start | bytes 1572868
  73.1 29.0 %copy-start.3 = (bf16[128,2048]{1,0:T(8,128)(2,1)}, bf16[128,2048]{1,0:T(8,128)(2,1)S(1)}, u32[]{:S(2)}) copy-start(bf16[128,2048]{1,0:T(8,128)(2,1)S(1)} %get-tuple-element.39.refs_6_.refs_10_) | copy-start | bytes 1572868
  73.1 28.9 %copy-start.4 = (bf16[128,2048]{1,0:T(8,128)(2,1)}, bf16[128,2048]{1,0:T(8,128)(2,1)S(1)}, u32[]{:S(2)}) copy-start(bf16[128,2048]{1,0:T(8,128)(2,1)S(1)} %get-tuple-element.35.refs_2_.refs_15_.refs_19_) | copy-start | bytes 1572868
  73.1 36.4 %collective-permute-start.15 = (bf16[128,2048]{1,0:T(8,128)(2,1)S(1)}, bf16[128,2048]{1,0:T(8,128)(2,1)}, u32[]{:S(2)}, u32[]{:S(2)}) collective-permute-start(bf16[128,2048]{1,0:T(8,128)(2,1)S(1)} %get-tuple-element.39.refs_6_.refs_10_), channel_id=1, source_target_pairs={{0,1},{1,0},{2,3},{3,2},{4,5},{5,4},{6,7},{7,6},{8,9},{9,8},{10,11... | collective-permute-start | bytes 1572872 | tf_op jit(solution)/shard_map/ppermute | solution.py:62
  74.3 35.1 %collective-permute-start.16 = (bf16[128,2048]{1,0:T(8,128)(2,1)S(1)}, bf16[128,2048]{1,0:T(8,128)(2,1)}, u32[]{:S(2)}, u32[]{:S(2)}) collective-permute-start(bf16[128,2048]{1,0:T(8,128)(2,1)S(1)} %get-tuple-element.40.refs_13_.refs_17_), channel_id=1, source_target_pairs={{0,12},{1,13},{2,14},{3,15},{4,0},{5,1},{6,2},{7,3},{8,4},{9,5},{1... | collective-permute-start | bytes 1572872 | tf_op jit(solution)/shard_map/ppermute | solution.py:62
  77.8 31.6 %collective-permute-start.17 = (bf16[128,2048]{1,0:T(8,128)(2,1)S(1)}, bf16[128,2048]{1,0:T(8,128)(2,1)}, u32[]{:S(2)}, u32[]{:S(2)}) collective-permute-start(bf16[128,2048]{1,0:T(8,128)(2,1)S(1)} %get-tuple-element.35.refs_2_.refs_15_.refs_19_), channel_id=1, source_target_pairs={{0,2},{1,3},{2,0},{3,1},{4,6},{5,7},{6,4},{7,5},{8,10},{9,11},{10,... | collective-permute-start | bytes 1572872 | tf_op jit(solution)/shard_map/ppermute | solution.py:62
  80.3 14.9 %collective-permute-start.14 = (f32[16,2048]{1,0:T(8,128)S(1)}, f32[16,2048]{1,0:T(8,128)}, u32[]{:S(2)}, u32[]{:S(2)}) collective-permute-start(f32[16,2048]{1,0:T(8,128)S(1)} %rows.1.refs_3_), channel_id=1, source_target_pairs={{0,16},{16,0},{1,17},{17,1},{2,18},{18,2},{3,19},{19,3},{4,20},{20... | collective-permute-start | bytes 393224 | tf_op jit(solution)/shard_map/ppermute | solution.py:232
  95.2 1.2 copy-start.16
  96.4 0.9 copy-start.20
  100.2 1.0 copy-start.1
  101.2 0.9 copy-start.17
  102.0 1.0 copy-start.11
  109.5 13.8 %copy-start.2 = (bf16[256,2048]{1,0:T(8,128)(2,1)S(1)}, bf16[256,2048]{1,0:T(8,128)(2,1)}, u32[]{:S(2)}) copy-start(bf16[256,2048]{1,0:T(8,128)(2,1)} %copy-done.1) | copy-start | bytes 3145732
  119.0 4.3 %collective-permute-start.18 = (bf16[176,2048]{1,0:T(8,128)(2,1)}, bf16[176,2048]{1,0:T(8,128)(2,1)S(1)}, u32[]{:S(2)}, u32[]{:S(2)}) collective-permute-start(bf16[176,2048]{1,0:T(8,128)(2,1)} %get-tuple-element.44), channel_id=1, source_target_pairs={{0,16},{1,17},{2,18},{3,19},{4,20},{5,21},{6,22},{7,23},{8,24},{9,... | collective-permute-start | bytes 2162696 | tf_op jit(solution)/shard_map/ppermute | solution.py:468
  123.3 1.4 %copy-start.19 = (f32[176,2048]{1,0:T(8,128)S(1)}, f32[176,2048]{1,0:T(8,128)}, u32[]{:S(2)}) copy-start(f32[176,2048]{1,0:T(8,128)} %get-tuple-element.43.refs_3_) | copy-start | bytes 4325380

commit v7 on v3

--- a/solution.py
+++ b/solution.py
@@ -408,7 +408,7 @@
             pltpu.SemaphoreType.DMA((max(len(late), 1),)),
             pltpu.SemaphoreType.DMA((blocks,)),
         ],
-        mib=52,
+        mib=14,
     )
 
 

time: 123 us -> 127 us (1.033)
  local copies, waits for them, and re-layouts: 18.8 us -> 24.5 us
  Pallas kernels: 20.6 us -> 18.1 us
    unnamed x54 -> x78, local copies, waits for them, and re-layouts: 15.6 us -> 21.4 us
    pallas_call x11, Pallas kernels: 20.6 us -> 18.1 us  [local(): pl.pallas_call(run, out_shape=[jax.ShapeDtypeStruct(shape, dtype) for sha...]
where the time goes in v7:
time: 127 us; the launch traced here: 126 us
  starting transfers between devices  45.6 us (36%)
  waiting for transfers between devices  35.5 us (28%)
  local copies, waits for them, and re-layouts  24.5 us (19%)
  Pallas kernels  18.1 us (14%)
    ppermute x15, waiting for transfers between devices, moved(): return lax.ppermute(value, 'ep', pairs)  32.5 us
    unnamed x78, local copies, waits for them, and re-layouts  21.4 us
    pallas_call x11, Pallas kernels, local(): pl.pallas_call(run, out_shape=[jax.ShapeDtypeStruct(shape, dtype) for sha...  18.1 us
    ppermute x15, starting transfers between devices, moved(): return lax.ppermute(value, 'ep', pairs)  14.1 us
    ppermute x1, starting transfers between devices, both_norms(): other_rows = lax.ppermute(rows, 'grp', swap)  13.8 us
    all_to_all x2, starting transfers between devices, exchanged(): parts = lax.all_to_all(parts, 'ep', split_axis=0, concat_axis=0, tiled=True)  12.9 us
    ppermute x1, starting transfers between devices, body(): other_hidden = lax.ppermute(hidden[0], 'grp', [(0, 1), (1, 0)])  3.39 us
    ppermute x1, waiting for transfers between devices, body(): received = lax.ppermute(sent, 'grp', [(0, 1)])  2.77 us
  transfers between devices with their start and end apart: 21, of which 6 were waited for; matrix products, arithmetic and copies ran while one was open for 2% of the time, Pallas kernels for 10%

profile of v7, /device:TPU:29, one launch (start us, length us, event | category | flops | bytes accessed | tf_op | source)
XLA Modules:
  0.0 125.5 jit_solution(4873700543905767234)
XLA Ops:
  0.0 1.0 constant_dynamic-slice_fusion
  1.0 1.0 constant_dynamic-slice_fusion.2
  2.1 1.3 %collective-permute-start = (bf16[128,2048]{1,0:T(8,128)(2,1)S(1)}, bf16[128,2048]{1,0:T(8,128)(2,1)S(1)}, u32[]{:S(2)}, u32[]{:S(2)}) collective-permute-start(bf16[128,2048]{1,0:T(8,128)(2,1)S(1)} %pad_maximum_fusion.refs_3_.refs_7_), channel_id=1, source_target_pairs={{0,1},{1,0},{2,3},{3,2},{4,5},{5,4},{6,7},{7,6},{8,9},{9,8},{10,11... | collective-permute-start | bytes 1572872 | tf_op jit(solution)/shard_map/ppermute | solution.py:62
  3.6 0.7 fusion.2
  4.3 1.2 copy-done.24
  5.5 1.0 copy-done.31
  6.5 0.7 copy-done.36
  7.2 0.7 pack.1
  8.0 0.8 copy-done.32
  8.7 6.2 %all-to-all-start = ((bf16[16,8,2048]{2,1,0:T(8,128)(2,1)}), bf16[16,8,2048]{2,1,0:T(8,128)(2,1)}, u32[]{:S(2)}, u32[]{:S(2)}) async-start(bf16[16,8,2048]{2,1,0:T(8,128)(2,1)} %bitcast.42), calls=%async_computation | async-start | bytes 1048576 | tf_op jit(solution)/shard_map/all_to_all | solution.py:200
  15.0 0.8 collective-permute-done.1.refs_1_
  16.0 1.9 %collective-permute-start.4 = (bf16[128,2048]{1,0:T(8,128)(2,1)S(1)}, bf16[128,2048]{1,0:T(8,128)(2,1)S(1)}, u32[]{:S(2)}, u32[]{:S(2)}) collective-permute-start(bf16[128,2048]{1,0:T(8,128)(2,1)S(1)} %get-tuple-element.27.refs_1_), channel_id=1, source_target_pairs={{0,4},{1,5},{2,6},{3,7},{4,8},{5,9},{6,10},{7,11},{8,12},{9,13},{1... | collective-permute-start | bytes 1572872 | tf_op jit(solution)/shard_map/ppermute | solution.py:62
  17.9 0.5 collective-permute-start.5
  18.4 15.0 %collective-permute-done.3.refs_0_.refs_10_.refs_14_ = bf16[128,2048]{1,0:T(8,128)(2,1)S(1)} collective-permute-done((bf16[128,2048]{1,0:T(8,128)(2,1)S(1)}, bf16[128,2048]{1,0:T(8,128)(2,1)S(1)}, u32[]{:S(2)}, u32[]{:S(2)}) %collective-permute-start.3) | collective-permute-done | bytes 524320 | tf_op jit(solution)/shard_map/ppermute | solution.py:62
  33.5 2.4 %collective-permute-done.4.refs_2_ = bf16[128,2048]{1,0:T(8,128)(2,1)S(1)} collective-permute-done((bf16[128,2048]{1,0:T(8,128)(2,1)S(1)}, bf16[128,2048]{1,0:T(8,128)(2,1)S(1)}, u32[]{:S(2)}, u32[]{:S(2)}) %collective-permute-start.4) | collective-permute-done | bytes 524320 | tf_op jit(solution)/shard_map/ppermute | solution.py:62
  36.5 2.5 %collective-permute-start.8 = (bf16[128,2048]{1,0:T(8,128)(2,1)S(1)}, bf16[128,2048]{1,0:T(8,128)(2,1)S(1)}, u32[]{:S(2)}, u32[]{:S(2)}) collective-permute-start(bf16[128,2048]{1,0:T(8,128)(2,1)S(1)} %get-tuple-element.29.refs_3_.refs_2_), channel_id=1, source_target_pairs={{0,4},{1,5},{2,6},{3,7},{4,8},{5,9},{6,10},{7,11},{8,12},{9,13},{1... | collective-permute-start | bytes 1572872 | tf_op jit(solution)/shard_map/ppermute | solution.py:62
  39.0 2.2 %copy-done.22 = bf16[1,2048,1024]{2,1,0:T(8,128)(2,1)S(1)} copy-done((bf16[1,2048,1024]{2,1,0:T(8,128)(2,1)S(1)}, bf16[1,2048,1024]{2,1,0:T(8,128)(2,1)}, u32[]{:S(2)}) %copy-start.22) | copy-done | bytes 4194328
  41.2 2.2 %copy-done.23 = bf16[1,1024,2048]{2,1,0:T(8,128)(2,1)S(1)} copy-done((bf16[1,1024,2048]{2,1,0:T(8,128)(2,1)S(1)}, bf16[1,1024,2048]{2,1,0:T(8,128)(2,1)}, u32[]{:S(2)}) %copy-start.23) | copy-done | bytes 4194328
  43.4 2.4 %mlp.1 = bf16[128,2048]{1,0:T(8,128)(2,1)S(1)} custom-call(bf16[128,2048]{1,0:T(8,128)(2,1)} %bitcast.7.refs_0_, bf16[2048,1024]{1,0:T(8,128)(2,1)S(1)} %bitcast.35, bf16[1024,2048]{1,0:T(8,128)(2,1)S(1)} %bitcast.36, bf16[128,2048]{1,0:T(8,128)(2,1)S(1)} %get-tuple-element.29.refs_3_.refs_2_), custom_call_target="tpu_custom_call" | custom-call | tf_op jit(solution)/shard_map/mlp/pallas_call | solution.py:83
  45.8 0.8 copy-done.28
  46.5 6.7 %all-to-all-start.1 = ((bf16[16,8,2048]{2,1,0:T(8,128)(2,1)}), bf16[16,8,2048]{2,1,0:T(8,128)(2,1)}, u32[]{:S(2)}, u32[]{:S(2)}) async-start(bf16[16,8,2048]{2,1,0:T(8,128)(2,1)} %bitcast.40), calls=%async_computation.1 | async-start | bytes 1048576 | tf_op jit(solution)/shard_map/all_to_all | solution.py:200
  54.1 1.2 collective-permute-start.11
  55.3 3.4 %collective-permute-start.12 = (bf16[256,2048]{1,0:T(8,128)(2,1)}, bf16[256,2048]{1,0:T(8,128)(2,1)}, u32[]{:S(2)}, u32[]{:S(2)}) collective-permute-start(bf16[256,2048]{1,0:T(8,128)(2,1)} %bitcast.37), channel_id=1, source_target_pairs={{0,16},{16,0},{1,17},{17,1},{2,18},{18,2},{3,19},{19,3},{4,20},{20... | collective-permute-start | bytes 3145736 | tf_op jit(solution)/shard_map/ppermute | solution.py:442
  58.9 14.2 %collective-permute-done.9.refs_0_.refs_14_.refs_18_ = bf16[128,2048]{1,0:T(8,128)(2,1)S(1)} collective-permute-done((bf16[128,2048]{1,0:T(8,128)(2,1)S(1)}, bf16[128,2048]{1,0:T(8,128)(2,1)S(1)}, u32[]{:S(2)}, u32[]{:S(2)}) %collective-permute-start.9) | collective-permute-done | bytes 524320 | tf_op jit(solution)/shard_map/ppermute | solution.py:62
  73.1 1.2 collective-permute-start.15
  74.3 3.5 %collective-permute-start.16 = (bf16[128,2048]{1,0:T(8,128)(2,1)S(1)}, bf16[128,2048]{1,0:T(8,128)(2,1)}, u32[]{:S(2)}, u32[]{:S(2)}) collective-permute-start(bf16[128,2048]{1,0:T(8,128)(2,1)S(1)} %get-tuple-element.40.refs_13_.refs_17_), channel_id=1, source_target_pairs={{0,12},{1,13},{2,14},{3,15},{4,0},{5,1},{6,2},{7,3},{8,4},{9,5},{1... | collective-permute-start | bytes 1572872 | tf_op jit(solution)/shard_map/ppermute | solution.py:62
  77.8 0.5 collective-permute-start.17
  79.1 1.1 rows.1.refs_3_
  80.3 13.8 %collective-permute-start.14 = (f32[16,2048]{1,0:T(8,128)S(1)}, f32[16,2048]{1,0:T(8,128)}, u32[]{:S(2)}, u32[]{:S(2)}) collective-permute-start(f32[16,2048]{1,0:T(8,128)S(1)} %rows.1.refs_3_), channel_id=1, source_target_pairs={{0,16},{16,0},{1,17},{17,1},{2,18},{18,2},{3,19},{19,3},{4,20},{20... | collective-permute-start | bytes 393224 | tf_op jit(solution)/shard_map/ppermute | solution.py:232
  94.1 0.8 copy.35.refs_6_
  95.2 1.2 copy-done.25
  96.4 0.9 copy-done.30
  97.3 2.9 %norm.1 = (bf16[256,2048]{1,0:T(8,128)(2,1)S(1)}, bf16[176,2048]{1,0:T(8,128)(2,1)S(1)}, f32[256,2048]{1,0:T(8,128)S(1)}) custom-call(s32[1]{0:T(128)} %bitcast.refs_0_, bf16[256,2048]{1,0:T(8,128)(2,1)S(1)} %bitcast.39, f32[256,1]{1,0:T(8,128)S(1)} %copy.34.refs_2_, f32[16,2048]{1,0:T(8,128)S(1)} %rows.1.refs_3_, f32[1,2048]{1,0:T(1,128)S(1)} %copy-done.35, ...), custom_call_target="tpu_custom_call" | custom-call | tf_op jit(solution)/shard_map/norm/pallas_call | solution.py:83
  100.2 1.0 copy-done.2
  101.2 0.9 copy-done.26
  102.0 1.0 copy-done.19
  103.1 5.4 %project.1 = (f32[256,1024]{1,0:T(8,128)}, f32[176,512]{1,0:T(8,128)S(1)}) custom-call(s32[16]{0:T(128)S(1)} %stack.67.refs_0_, bf16[256,2048]{1,0:T(8,128)(2,1)} %copy-done.2, bf16[176,2048]{1,0:T(8,128)(2,1)} %copy-done.26, bf16[128,2048]{1,0:T(8,128)(2,1)S(1)} %copy-done.19, bf16[128,2048]{1,0:T(8,128)(2,1)S(1)} %get-tuple-element.30.refs_4_.refs_8_, ...), custom_call_target="tpu_custom_call" | custom-call | tf_op jit(solution)/shard_map/project/pallas_call | solution.py:83
  108.5 0.7 copy-done.33
  109.4 1.0 copy-done.1
  110.4 1.0 copy-done.5
  111.4 1.0 copy-done.7
  112.5 1.0 copy-done.13
  113.5 1.2 copy-done.29
  114.7 1.0 copy-done.34
  115.7 4.2 %attend.1 = (f32[176,2048]{1,0:T(8,128)S(1)}, bf16[176,2048]{1,0:T(8,128)(2,1)S(1)}) custom-call(s32[16]{0:T(128)S(1)} %stack.67.refs_0_, s32[176,1]{1,0:T(8,128)S(1)} %copy.36.refs_1_, s32[1,256]{1,0:T(1,128)S(1)} %bitcast.46, bf16[256,2048]{1,0:T(8,128)(2,1)S(1)} %copy-done.3, bf16[176,2048]{1,0:T(8,128)(2,1)S(1)} %copy-done.27, ...), custom_call_target="tpu_custom_call" | custom-call | tf_op jit(solution)/shard_map/attend/pallas_call | solution.py:83
  119.9 1.3 %collective-permute-start.18 = (bf16[176,2048]{1,0:T(8,128)(2,1)S(1)}, bf16[176,2048]{1,0:T(8,128)(2,1)S(1)}, u32[]{:S(2)}, u32[]{:S(2)}) collective-permute-start(bf16[176,2048]{1,0:T(8,128)(2,1)S(1)} %get-tuple-element.44), channel_id=1, source_target_pairs={{0,16},{1,17},{2,18},{3,19},{4,20},{5,21},{6,22},{7,23},{8,24},{9,... | collective-permute-start | bytes 2162696 | tf_op jit(solution)/shard_map/ppermute | solution.py:461
  121.2 2.8 %collective-permute-done.18.refs_4_ = bf16[176,2048]{1,0:T(8,128)(2,1)S(1)} collective-permute-done((bf16[176,2048]{1,0:T(8,128)(2,1)S(1)}, bf16[176,2048]{1,0:T(8,128)(2,1)S(1)}, u32[]{:S(2)}, u32[]{:S(2)}) %collective-permute-start.18) | collective-permute-done | bytes 720928 | tf_op jit(solution)/shard_map/ppermute | solution.py:461
  124.0 1.5 %finish.1 = bf16[256,2048]{1,0:T(8,128)(2,1)} custom-call(s32[1]{0:T(128)} %bitcast.refs_0_, bf16[256,2048]{1,0:T(8,128)(2,1)S(1)} %copy-done.3, f32[256,2048]{1,0:T(8,128)S(1)} %get-tuple-element.37.refs_2_, f32[176,2048]{1,0:T(8,128)S(1)} %get-tuple-element.43.refs_3_, bf16[176,2048]{1,0:T(8,128)(2,1)S(1)} %collective-permute-done.18.refs_4_, ...), custom_call_target="tpu_custom_call" | custom-call | tf_op jit(solution)/shard_map/finish/pallas_call | solution.py:83
  (101 shorter events, 3.1 us)
Async XLA Ops:
  2.0 33.8 %copy-start.18 = (bf16[128,2048]{1,0:T(8,128)(2,1)}, bf16[128,2048]{1,0:T(8,128)(2,1)S(1)}, u32[]{:S(2)}) copy-start(bf16[128,2048]{1,0:T(8,128)(2,1)S(1)} %pad_maximum_fusion.refs_3_.refs_7_) | copy-start | bytes 1572868
  2.1 12.9 %collective-permute-start = (bf16[128,2048]{1,0:T(8,128)(2,1)S(1)}, bf16[128,2048]{1,0:T(8,128)(2,1)S(1)}, u32[]{:S(2)}, u32[]{:S(2)}) collective-permute-start(bf16[128,2048]{1,0:T(8,128)(2,1)S(1)} %pad_maximum_fusion.refs_3_.refs_7_), channel_id=1, source_target_pairs={{0,1},{1,0},{2,3},{3,2},{4,5},{5,4},{6,7},{7,6},{8,9},{9,8},{10,11... | collective-permute-start | bytes 1572872 | tf_op jit(solution)/shard_map/ppermute | solution.py:62
  3.3 12.5 %collective-permute-start.1 = (bf16[128,2048]{1,0:T(8,128)(2,1)S(1)}, bf16[128,2048]{1,0:T(8,128)(2,1)S(1)}, u32[]{:S(2)}, u32[]{:S(2)}) collective-permute-start(bf16[128,2048]{1,0:T(8,128)(2,1)S(1)} %pad_maximum_fusion.refs_3_.refs_7_), channel_id=1, source_target_pairs={{0,4},{1,5},{2,6},{3,7},{4,8},{5,9},{6,10},{7,11},{8,12},{9,13},{1... | collective-permute-start | bytes 1572872 | tf_op jit(solution)/shard_map/ppermute | solution.py:62
  3.3 12.5 %collective-permute-start.2 = (bf16[128,2048]{1,0:T(8,128)(2,1)S(1)}, bf16[128,2048]{1,0:T(8,128)(2,1)S(1)}, u32[]{:S(2)}, u32[]{:S(2)}) collective-permute-start(bf16[128,2048]{1,0:T(8,128)(2,1)S(1)} %pad_maximum_fusion.refs_3_.refs_7_), channel_id=1, source_target_pairs={{0,2},{1,3},{2,0},{3,1},{4,6},{5,7},{6,4},{7,5},{8,10},{9,11},{10,... | collective-permute-start | bytes 1572872 | tf_op jit(solution)/shard_map/ppermute | solution.py:62
  4.3 1.2 copy-start.24
  5.5 1.0 copy-start.31
  8.7 30.2 %all-to-all-start = ((bf16[16,8,2048]{2,1,0:T(8,128)(2,1)}), bf16[16,8,2048]{2,1,0:T(8,128)(2,1)}, u32[]{:S(2)}, u32[]{:S(2)}) async-start(bf16[16,8,2048]{2,1,0:T(8,128)(2,1)} %bitcast.42), calls=%async_computation | async-start | bytes 1048576 | tf_op jit(solution)/shard_map/all_to_all | solution.py:200
  15.0 30.7 %copy-start.8 = (bf16[128,2048]{1,0:T(8,128)(2,1)}, bf16[128,2048]{1,0:T(8,128)(2,1)S(1)}, u32[]{:S(2)}) copy-start(bf16[128,2048]{1,0:T(8,128)(2,1)S(1)} %collective-permute-done.refs_0_.refs_7_.refs_11_) | copy-start | bytes 1572868
  15.8 20.6 %copy-start.16 = (bf16[128,2048]{1,0:T(8,128)(2,1)}, bf16[128,2048]{1,0:T(8,128)(2,1)S(1)}, u32[]{:S(2)}) copy-start(bf16[128,2048]{1,0:T(8,128)(2,1)S(1)} %get-tuple-element.28.refs_9_.refs_13_) | copy-start | bytes 1572868
  15.8 17.6 %collective-permute-start.3 = (bf16[128,2048]{1,0:T(8,128)(2,1)S(1)}, bf16[128,2048]{1,0:T(8,128)(2,1)S(1)}, u32[]{:S(2)}, u32[]{:S(2)}) collective-permute-start(bf16[128,2048]{1,0:T(8,128)(2,1)S(1)} %get-tuple-element.27.refs_1_), channel_id=1, source_target_pairs={{0,2},{1,3},{2,0},{3,1},{4,6},{5,7},{6,4},{7,5},{8,10},{9,11},{10,... | collective-permute-start | bytes 1572872 | tf_op jit(solution)/shard_map/ppermute | solution.py:62
  16.0 19.8 %collective-permute-start.4 = (bf16[128,2048]{1,0:T(8,128)(2,1)S(1)}, bf16[128,2048]{1,0:T(8,128)(2,1)S(1)}, u32[]{:S(2)}, u32[]{:S(2)}) collective-permute-start(bf16[128,2048]{1,0:T(8,128)(2,1)S(1)} %get-tuple-element.27.refs_1_), channel_id=1, source_target_pairs={{0,4},{1,5},{2,6},{3,7},{4,8},{5,9},{6,10},{7,11},{8,12},{9,13},{1... | collective-permute-start | bytes 1572872 | tf_op jit(solution)/shard_map/ppermute | solution.py:62
  17.9 18.0 %collective-permute-start.5 = (bf16[128,2048]{1,0:T(8,128)(2,1)S(1)}, bf16[128,2048]{1,0:T(8,128)(2,1)S(1)}, u32[]{:S(2)}, u32[]{:S(2)}) collective-permute-start(bf16[128,2048]{1,0:T(8,128)(2,1)S(1)} %get-tuple-element.28.refs_9_.refs_13_), channel_id=1, source_target_pairs={{0,1},{1,0},{2,3},{3,2},{4,5},{5,4},{6,7},{7,6},{8,9},{9,8},{10,11... | collective-permute-start | bytes 1572872 | tf_op jit(solution)/shard_map/ppermute | solution.py:62
  33.5 3.0 %copy-start.20 = (bf16[128,2048]{1,0:T(8,128)(2,1)}, bf16[128,2048]{1,0:T(8,128)(2,1)S(1)}, u32[]{:S(2)}) copy-start(bf16[128,2048]{1,0:T(8,128)(2,1)S(1)} %collective-permute-done.3.refs_0_.refs_10_.refs_14_) | copy-start | bytes 1572868
  35.9 17.4 %collective-permute-start.6 = (bf16[128,2048]{1,0:T(8,128)(2,1)S(1)}, bf16[128,2048]{1,0:T(8,128)(2,1)S(1)}, u32[]{:S(2)}, u32[]{:S(2)}) collective-permute-start(bf16[128,2048]{1,0:T(8,128)(2,1)S(1)} %get-tuple-element.30.refs_4_.refs_8_), channel_id=1, source_target_pairs={{0,1},{1,0},{2,3},{3,2},{4,5},{5,4},{6,7},{7,6},{8,9},{9,8},{10,11... | collective-permute-start | bytes 1572872 | tf_op jit(solution)/shard_map/ppermute | solution.py:62
  36.4 16.9 %collective-permute-start.7 = (bf16[128,2048]{1,0:T(8,128)(2,1)S(1)}, bf16[128,2048]{1,0:T(8,128)(2,1)}, u32[]{:S(2)}, u32[]{:S(2)}) collective-permute-start(bf16[128,2048]{1,0:T(8,128)(2,1)S(1)} %get-tuple-element.29.refs_3_.refs_2_), channel_id=1, source_target_pairs={{0,2},{1,3},{2,0},{3,1},{4,6},{5,7},{6,4},{7,5},{8,10},{9,11},{10,... | collective-permute-start | bytes 1572872 | tf_op jit(solution)/shard_map/ppermute | solution.py:62
  36.5 16.8 %collective-permute-start.8 = (bf16[128,2048]{1,0:T(8,128)(2,1)S(1)}, bf16[128,2048]{1,0:T(8,128)(2,1)S(1)}, u32[]{:S(2)}, u32[]{:S(2)}) collective-permute-start(bf16[128,2048]{1,0:T(8,128)(2,1)S(1)} %get-tuple-element.29.refs_3_.refs_2_), channel_id=1, source_target_pairs={{0,4},{1,5},{2,6},{3,7},{4,8},{5,9},{6,10},{7,11},{8,12},{9,13},{1... | collective-permute-start | bytes 1572872 | tf_op jit(solution)/shard_map/ppermute | solution.py:62
  39.0 2.2 %copy-start.22 = (bf16[1,2048,1024]{2,1,0:T(8,128)(2,1)S(1)}, bf16[1,2048,1024]{2,1,0:T(8,128)(2,1)}, u32[]{:S(2)}) copy-start(bf16[1,2048,1024]{2,1,0:T(8,128)(2,1)} %param.18) | copy-start | bytes 12582916
  41.2 2.2 %copy-start.23 = (bf16[1,1024,2048]{2,1,0:T(8,128)(2,1)S(1)}, bf16[1,1024,2048]{2,1,0:T(8,128)(2,1)}, u32[]{:S(2)}) copy-start(bf16[1,1024,2048]{2,1,0:T(8,128)(2,1)} %param.19) | copy-start | bytes 12582916
  43.4 15.3 %copy-start.35 = (f32[1,2048]{1,0:T(1,128)S(1)}, f32[1,2048]{1,0:T(1,128)}, u32[]{:S(2)}) copy-start(f32[1,2048]{1,0:T(1,128)} %refs_4_.1) | copy-start | bytes 24580
  43.4 15.4 %copy-start.37 = (s32[1,4]{1,0:T(1,128)S(1)}, s32[1,4]{1,0:T(1,128)}, u32[]{:S(2)}) copy-start(s32[1,4]{1,0:T(1,128)} %param.23) | copy-start | bytes 52
  46.5 31.9 %copy-start.38 = (s32[1,4]{1,0:T(1,128)S(1)}, s32[1,4]{1,0:T(1,128)}, u32[]{:S(2)}) copy-start(s32[1,4]{1,0:T(1,128)} %param.22) | copy-start | bytes 52
  46.5 32.6 %all-to-all-start.1 = ((bf16[16,8,2048]{2,1,0:T(8,128)(2,1)}), bf16[16,8,2048]{2,1,0:T(8,128)(2,1)}, u32[]{:S(2)}, u32[]{:S(2)}) async-start(bf16[16,8,2048]{2,1,0:T(8,128)(2,1)} %bitcast.40), calls=%async_computation.1 | async-start | bytes 1048576 | tf_op jit(solution)/shard_map/all_to_all | solution.py:200
  53.3 19.8 %collective-permute-start.9 = (bf16[128,2048]{1,0:T(8,128)(2,1)S(1)}, bf16[128,2048]{1,0:T(8,128)(2,1)S(1)}, u32[]{:S(2)}, u32[]{:S(2)}) collective-permute-start(bf16[128,2048]{1,0:T(8,128)(2,1)S(1)} %get-tuple-element.32.refs_3_), channel_id=1, source_target_pairs={{0,4},{1,5},{2,6},{3,7},{4,8},{5,9},{6,10},{7,11},{8,12},{9,13},{1... | collective-permute-start | bytes 1572872 | tf_op jit(solution)/shard_map/ppermute | solution.py:62
  53.6 19.4 %collective-permute-start.10 = (bf16[128,2048]{1,0:T(8,128)(2,1)S(1)}, bf16[128,2048]{1,0:T(8,128)(2,1)S(1)}, u32[]{:S(2)}, u32[]{:S(2)}) collective-permute-start(bf16[128,2048]{1,0:T(8,128)(2,1)S(1)} %get-tuple-element.33.refs_2_), channel_id=1, source_target_pairs={{0,2},{1,3},{2,0},{3,1},{4,6},{5,7},{6,4},{7,5},{8,10},{9,11},{10,... | collective-permute-start | bytes 1572872 | tf_op jit(solution)/shard_map/ppermute | solution.py:62
  54.1 19.0 %collective-permute-start.11 = (bf16[128,2048]{1,0:T(8,128)(2,1)S(1)}, bf16[128,2048]{1,0:T(8,128)(2,1)S(1)}, u32[]{:S(2)}, u32[]{:S(2)}) collective-permute-start(bf16[128,2048]{1,0:T(8,128)(2,1)S(1)} %get-tuple-element.34.refs_5_.refs_9_), channel_id=1, source_target_pairs={{0,1},{1,0},{2,3},{3,2},{4,5},{5,4},{6,7},{7,6},{8,9},{9,8},{10,11... | collective-permute-start | bytes 1572872 | tf_op jit(solution)/shard_map/ppermute | solution.py:62
  55.3 39.6 %collective-permute-start.12 = (bf16[256,2048]{1,0:T(8,128)(2,1)}, bf16[256,2048]{1,0:T(8,128)(2,1)}, u32[]{:S(2)}, u32[]{:S(2)}) collective-permute-start(bf16[256,2048]{1,0:T(8,128)(2,1)} %bitcast.37), channel_id=1, source_target_pairs={{0,16},{16,0},{1,17},{17,1},{2,18},{18,2},{3,19},{19,3},{4,20},{20... | collective-permute-start | bytes 3145736 | tf_op jit(solution)/shard_map/ppermute | solution.py:442
  58.7 21.6 %collective-permute-start.13 = (f32[2,2048]{1,0:T(2,128)S(1)}, f32[2,2048]{1,0:T(2,128)S(1)}, u32[]{:S(2)}, u32[]{:S(2)}) collective-permute-start(f32[2,2048]{1,0:T(2,128)S(1)} %fusion), channel_id=1, source_target_pairs={{0,16},{16,0},{1,17},{17,1},{2,18},{18,2},{3,19},{19,3},{4,20},{20... | collective-permute-start | bytes 49160 | tf_op jit(solution)/shard_map/ppermute | solution.py:231
  73.0 29.0 %copy-start.12 = (bf16[128,2048]{1,0:T(8,128)(2,1)}, bf16[128,2048]{1,0:T(8,128)(2,1)S(1)}, u32[]{:S(2)}) copy-start(bf16[128,2048]{1,0:T(8,128)(2,1)S(1)} %collective-permute-done.9.refs_0_.refs_14_.refs_18_) | copy-start | bytes 1572868
  73.0 4.8 %copy-start.14 = (bf16[128,2048]{1,0:T(8,128)(2,1)}, bf16[128,2048]{1,0:T(8,128)(2,1)S(1)}, u32[]{:S(2)}) copy-start(bf16[128,2048]{1,0:T(8,128)(2,1)S(1)} %collective-permute-done.10.refs_1_.refs_12_.refs_16_) | copy-start | bytes 1572868
  73.1 29.0 %copy-start = (bf16[128,2048]{1,0:T(8,128)(2,1)}, bf16[128,2048]{1,0:T(8,128)(2,1)S(1)}, u32[]{:S(2)}) copy-start(bf16[128,2048]{1,0:T(8,128)(2,1)S(1)} %get-tuple-element.40.refs_13_.refs_17_) | copy-start | bytes 1572868
  73.1 29.0 %copy-start.4 = (bf16[128,2048]{1,0:T(8,128)(2,1)}, bf16[128,2048]{1,0:T(8,128)(2,1)S(1)}, u32[]{:S(2)}) copy-start(bf16[128,2048]{1,0:T(8,128)(2,1)S(1)} %get-tuple-element.39.refs_6_.refs_10_) | copy-start | bytes 1572868
  73.1 29.0 %copy-start.6 = (bf16[128,2048]{1,0:T(8,128)(2,1)}, bf16[128,2048]{1,0:T(8,128)(2,1)S(1)}, u32[]{:S(2)}) copy-start(bf16[128,2048]{1,0:T(8,128)(2,1)S(1)} %get-tuple-element.35.refs_2_.refs_15_.refs_19_) | copy-start | bytes 1572868
  73.1 36.2 %collective-permute-start.15 = (bf16[128,2048]{1,0:T(8,128)(2,1)S(1)}, bf16[128,2048]{1,0:T(8,128)(2,1)}, u32[]{:S(2)}, u32[]{:S(2)}) collective-permute-start(bf16[128,2048]{1,0:T(8,128)(2,1)S(1)} %get-tuple-element.39.refs_6_.refs_10_), channel_id=1, source_target_pairs={{0,1},{1,0},{2,3},{3,2},{4,5},{5,4},{6,7},{7,6},{8,9},{9,8},{10,11... | collective-permute-start | bytes 1572872 | tf_op jit(solution)/shard_map/ppermute | solution.py:62
  74.3 34.9 %collective-permute-start.16 = (bf16[128,2048]{1,0:T(8,128)(2,1)S(1)}, bf16[128,2048]{1,0:T(8,128)(2,1)}, u32[]{:S(2)}, u32[]{:S(2)}) collective-permute-start(bf16[128,2048]{1,0:T(8,128)(2,1)S(1)} %get-tuple-element.40.refs_13_.refs_17_), channel_id=1, source_target_pairs={{0,12},{1,13},{2,14},{3,15},{4,0},{5,1},{6,2},{7,3},{8,4},{9,5},{1... | collective-permute-start | bytes 1572872 | tf_op jit(solution)/shard_map/ppermute | solution.py:62
  77.8 31.4 %collective-permute-start.17 = (bf16[128,2048]{1,0:T(8,128)(2,1)S(1)}, bf16[128,2048]{1,0:T(8,128)(2,1)}, u32[]{:S(2)}, u32[]{:S(2)}) collective-permute-start(bf16[128,2048]{1,0:T(8,128)(2,1)S(1)} %get-tuple-element.35.refs_2_.refs_15_.refs_19_), channel_id=1, source_target_pairs={{0,2},{1,3},{2,0},{3,1},{4,6},{5,7},{6,4},{7,5},{8,10},{9,11},{10,... | collective-permute-start | bytes 1572872 | tf_op jit(solution)/shard_map/ppermute | solution.py:62
  80.3 14.9 %collective-permute-start.14 = (f32[16,2048]{1,0:T(8,128)S(1)}, f32[16,2048]{1,0:T(8,128)}, u32[]{:S(2)}, u32[]{:S(2)}) collective-permute-start(f32[16,2048]{1,0:T(8,128)S(1)} %rows.1.refs_3_), channel_id=1, source_target_pairs={{0,16},{16,0},{1,17},{17,1},{2,18},{18,2},{3,19},{19,3},{4,20},{20... | collective-permute-start | bytes 393224 | tf_op jit(solution)/shard_map/ppermute | solution.py:232
  95.2 1.2 copy-start.25
  102.0 1.0 copy-start.19
  103.1 6.2 %copy-start.3 = (bf16[256,2048]{1,0:T(8,128)(2,1)S(1)}, bf16[256,2048]{1,0:T(8,128)(2,1)}, u32[]{:S(2)}) copy-start(bf16[256,2048]{1,0:T(8,128)(2,1)} %copy-done.2) | copy-start | bytes 3145732
  103.1 6.2 %copy-start.9 = (bf16[128,2048]{1,0:T(8,128)(2,1)S(1)}, bf16[128,2048]{1,0:T(8,128)(2,1)}, u32[]{:S(2)}) copy-start(bf16[128,2048]{1,0:T(8,128)(2,1)} %copy-done.8) | copy-start | bytes 1572868
  103.1 6.2 %copy-start.11 = (bf16[128,2048]{1,0:T(8,128)(2,1)S(1)}, bf16[128,2048]{1,0:T(8,128)(2,1)}, u32[]{:S(2)}) copy-start(bf16[128,2048]{1,0:T(8,128)(2,1)} %copy-done.10) | copy-start | bytes 1572868
  103.1 6.2 %copy-start.15 = (bf16[128,2048]{1,0:T(8,128)(2,1)S(1)}, bf16[128,2048]{1,0:T(8,128)(2,1)}, u32[]{:S(2)}) copy-start(bf16[128,2048]{1,0:T(8,128)(2,1)} %copy-done.14) | copy-start | bytes 1572868
  103.1 6.2 %copy-start.17 = (bf16[128,2048]{1,0:T(8,128)(2,1)S(1)}, bf16[128,2048]{1,0:T(8,128)(2,1)}, u32[]{:S(2)}) copy-start(bf16[128,2048]{1,0:T(8,128)(2,1)} %copy-done.16) | copy-start | bytes 1572868
  103.1 6.2 %copy-start.21 = (bf16[128,2048]{1,0:T(8,128)(2,1)S(1)}, bf16[128,2048]{1,0:T(8,128)(2,1)}, u32[]{:S(2)}) copy-start(bf16[128,2048]{1,0:T(8,128)(2,1)} %copy-done.20) | copy-start | bytes 1572868
  103.1 6.2 %copy-start.27 = (bf16[176,2048]{1,0:T(8,128)(2,1)S(1)}, bf16[176,2048]{1,0:T(8,128)(2,1)}, u32[]{:S(2)}) copy-start(bf16[176,2048]{1,0:T(8,128)(2,1)} %copy-done.26) | copy-start | bytes 2162692
  109.4 1.0 copy-start.1
  113.5 1.2 copy-start.29
  119.9 4.1 %collective-permute-start.18 = (bf16[176,2048]{1,0:T(8,128)(2,1)S(1)}, bf16[176,2048]{1,0:T(8,128)(2,1)S(1)}, u32[]{:S(2)}, u32[]{:S(2)}) collective-permute-start(bf16[176,2048]{1,0:T(8,128)(2,1)S(1)} %get-tuple-element.44), channel_id=1, source_target_pairs={{0,16},{1,17},{2,18},{3,19},{4,20},{5,21},{6,22},{7,23},{8,24},{9,... | collective-permute-start | bytes 2162696 | tf_op jit(solution)/shard_map/ppermute | solution.py:461
  (12 other events, 10.7 us)

commit v8 on v7

--- a/solution.py
+++ b/solution.py
@@ -66,7 +66,7 @@
     return (
         [pl.BlockSpec(memory_space=pltpu.SMEM)] * smem
         + [pl.BlockSpec(memory_space=pltpu.VMEM)] * vmem
-        + [pl.BlockSpec(memory_space=pltpu.HBM)] * unread
+        + [pl.BlockSpec(memory_space=pl.ANY)] * unread
     )
 
 
@@ -187,7 +187,7 @@
     return gate * summed.reshape(count, width)
 
 
-def expert_layer(marks, hidden, norm_gain, router, w_in, w_out, routes, slots):
+def expert_layer(mark, hidden, norm_gain, router, w_in, w_out, routes, slots):
     devices = lax.axis_size("ep")
     experts = devices // SPLIT
     width = hidden.shape[1]
@@ -211,14 +211,13 @@
         "mlp",
         [(blocks, jnp.bfloat16)],
         (exchanged(send), w_in, w_out),
-        marks[0],
+        mark,
     )
     (rows,) = local(
         functools.partial(rows_kernel, held),
         "rows",
         [((experts * PAD, width), jnp.float32)],
         (gate, exchanged(pieces)),
-        marks[1],
     )
     return rows
 
@@ -266,11 +265,14 @@
     z3, x1, y2 = moved(z2, dz=1), moved(z1, dx=1), moved(z2, dy=1)
     z2, z3, far0 = once([x1, y2], z2, z3, far0)
     far1, x2, y3 = moved(far0, dz=1), moved(z2, dx=1), moved(z3, dy=1)
-    z3, far0, x2 = once([far1, y3], z3, far0, x2)
-    fourth = [x2]
+    return [part, z1, z2, z3, x0, x1, y0, y1, y2, y3, far0, far1, x2], second
+
+
+def last_round(early, rows):
+    part, z1, z2, z3, x0, x1, y0, y1, y2, y3, far0, far1, x2 = early
+    z3, far0, x2 = local(gate_kernel, "gate", [], (), [far1, y3, rows], [z3, far0, x2])
     far3, x3, far2 = moved(far0, dz=-1), moved(z3, dx=1), moved(x2, dy=1)
-    early = [part, z1, z2, z3, x0, x1, y0, y1, y2, y3, far0, far1, x2]
-    return early, [x3, far3, far2], (second, fourth)
+    return [part, z1, z2, z3, x0, x1, y0, y1, y2, y3, far0, far1, x2], [x3, far3, far2]
 
 
 def pairs_of(refs):
@@ -384,7 +386,7 @@
             pltpu.VMEM((len(blocks) * rows, 3 * half), jnp.bfloat16),
             pltpu.SemaphoreType.DMA((len(blocks),)),
         ],
-        mib=52,
+        mib=14,
     )
 
 
@@ -446,10 +448,11 @@
         order = jnp.zeros((1,), jnp.int32)
         rows = expert_rows(hidden[0], *layer)
     else:
-        early, late, marks = gather(part)
+        early, mark = gather(part)
         z, y, x = place_of(lax.axis_index("ep"))
         order = jnp.stack([index_of(z - dz, y ^ dy, x ^ dx) for dz, dy, dx in EARLY + LATE])
-        rows = expert_layer(marks, hidden[0], *layer)
+        rows = expert_layer(mark, hidden[0], *layer)
+        early, late = last_round(early, rows)
     memory, target, mixed = both_norms(
         hidden[0], other_hidden, final_gain[0], places(expert_ids[0], slot_ids[0]), rows, targets
     )

time: 127 us -> 110 us (0.87)
  local copies, waits for them, and re-layouts: 24.5 us -> 17.3 us
  starting transfers between devices: 45.6 us -> 40.4 us
  Pallas kernels: 18.1 us -> 15.6 us
    unnamed x78 -> x36, local copies, waits for them, and re-layouts: 21.4 us -> 14.2 us
    ppermute x15, waiting for transfers between devices: 32.5 us -> 25.3 us  [moved(): return lax.ppermute(value, 'ep', pairs)]
    all_to_all x2, waiting for transfers between devices: 0.01 us -> 6.1 us  [exchanged(): parts = lax.all_to_all(parts, 'ep', split_axis=0, concat_axis=0, tiled=True)]
    ppermute x1, starting transfers between devices: 13.8 us -> 8.15 us  [both_norms(): other_rows = lax.ppermute(rows, 'grp', swap)]
    pallas_call x11, Pallas kernels: 18.1 us -> 15.6 us  [local(): pl.pallas_call(run, out_shape=[jax.ShapeDtypeStruct(shape, dtype) for sha...]
  transfers between devices with their start and end apart: 21 -> 21, of which waited for: 6 -> 7; matrix products, arithmetic and copies ran while one was open for 2% -> 2% of each run, Pallas kernels for 10% -> 9%
where the time goes in v8:
time: 110 us; the launch traced here: 109 us
  starting transfers between devices  40.4 us (37%)
  waiting for transfers between devices  34.4 us (31%)
  local copies, waits for them, and re-layouts  17.3 us (16%)
  Pallas kernels  15.6 us (14%)
  other arithmetic  1.13 us (1%)
    ppermute x15, waiting for transfers between devices, moved(): return lax.ppermute(value, 'ep', pairs)  25.3 us
    pallas_call x11, Pallas kernels, local(): pl.pallas_call(run, out_shape=[jax.ShapeDtypeStruct(shape, dtype) for sha...  15.6 us
    ppermute x15, starting transfers between devices, moved(): return lax.ppermute(value, 'ep', pairs)  14.4 us
    unnamed x36, local copies, waits for them, and re-layouts  14.2 us
    all_to_all x2, starting transfers between devices, exchanged(): parts = lax.all_to_all(parts, 'ep', split_axis=0, concat_axis=0, tiled=True)  12.9 us
    ppermute x1, starting transfers between devices, both_norms(): other_rows = lax.ppermute(rows, 'grp', swap)  8.15 us
    all_to_all x2, waiting for transfers between devices, exchanged(): parts = lax.all_to_all(parts, 'ep', split_axis=0, concat_axis=0, tiled=True)  6.1 us
    ppermute x1, starting transfers between devices, body(): other_hidden = lax.ppermute(hidden[0], 'grp', [(0, 1), (1, 0)])  3.58 us
  transfers between devices with their start and end apart: 21, of which 7 were waited for; matrix products, arithmetic and copies ran while one was open for 2% of the time, Pallas kernels for 9%

profile of v8, /device:TPU:29, one launch (start us, length us, event | category | flops | bytes accessed | tf_op | source)
XLA Modules:
  0.0 109.3 jit_solution(10368555119258095380)
XLA Ops:
  0.0 1.0 constant_dynamic-slice_fusion
  1.0 1.0 constant_dynamic-slice_fusion.2
  2.1 1.3 %collective-permute-start = (bf16[128,2048]{1,0:T(8,128)(2,1)S(1)}, bf16[128,2048]{1,0:T(8,128)(2,1)S(1)}, u32[]{:S(2)}, u32[]{:S(2)}) collective-permute-start(bf16[128,2048]{1,0:T(8,128)(2,1)S(1)} %pad_maximum_fusion.refs_3_.refs_7_), channel_id=1, source_target_pairs={{0,1},{1,0},{2,3},{3,2},{4,5},{5,4},{6,7},{7,6},{8,9},{9,8},{10,11... | collective-permute-start | bytes 1572872 | tf_op jit(solution)/shard_map/ppermute | solution.py:62
  3.3 0.2 collective-permute-start.2
  3.6 0.7 fusion.2
  4.3 1.2 %copy-done.8 = bf16[1,256,2048]{2,1,0:T(8,128)(2,1)S(1)} copy-done((bf16[1,256,2048]{2,1,0:T(8,128)(2,1)S(1)}, bf16[1,256,2048]{2,1,0:T(8,128)(2,1)}, u32[]{:S(2)}) %copy-start.8) | copy-done | bytes 1048600
  5.5 1.0 copy-done.12
  6.5 0.7 copy-done.15
  7.2 0.7 pack.1
  7.9 0.8 copy-done.13
  8.7 6.3 %all-to-all-start = ((bf16[16,8,2048]{2,1,0:T(8,128)(2,1)}), bf16[16,8,2048]{2,1,0:T(8,128)(2,1)}, u32[]{:S(2)}, u32[]{:S(2)}) async-start(bf16[16,8,2048]{2,1,0:T(8,128)(2,1)} %bitcast.42), calls=%async_computation | async-start | bytes 1048576 | tf_op jit(solution)/shard_map/all_to_all | solution.py:200
  15.0 0.8 collective-permute-done.1.refs_1_
  15.8 0.3 collective-permute-start.3
  16.1 1.9 %collective-permute-start.4 = (bf16[128,2048]{1,0:T(8,128)(2,1)S(1)}, bf16[128,2048]{1,0:T(8,128)(2,1)S(1)}, u32[]{:S(2)}, u32[]{:S(2)}) collective-permute-start(bf16[128,2048]{1,0:T(8,128)(2,1)S(1)} %get-tuple-element.27.refs_1_), channel_id=1, source_target_pairs={{0,4},{1,5},{2,6},{3,7},{4,8},{5,9},{6,10},{7,11},{8,12},{9,13},{1... | collective-permute-start | bytes 1572872 | tf_op jit(solution)/shard_map/ppermute | solution.py:62
  18.0 0.5 collective-permute-start.5
  18.5 15.1 %collective-permute-done.3.refs_0_.refs_10_.refs_14_ = bf16[128,2048]{1,0:T(8,128)(2,1)S(1)} collective-permute-done((bf16[128,2048]{1,0:T(8,128)(2,1)S(1)}, bf16[128,2048]{1,0:T(8,128)(2,1)S(1)}, u32[]{:S(2)}, u32[]{:S(2)}) %collective-permute-start.3) | collective-permute-done | bytes 524320 | tf_op jit(solution)/shard_map/ppermute | solution.py:62
  33.6 2.3 %collective-permute-done.4.refs_2_ = bf16[128,2048]{1,0:T(8,128)(2,1)S(1)} collective-permute-done((bf16[128,2048]{1,0:T(8,128)(2,1)S(1)}, bf16[128,2048]{1,0:T(8,128)(2,1)S(1)}, u32[]{:S(2)}, u32[]{:S(2)}) %collective-permute-start.4) | collective-permute-done | bytes 524320 | tf_op jit(solution)/shard_map/ppermute | solution.py:62
  35.9 0.5 collective-permute-start.9
  36.5 2.5 %collective-permute-start.11 = (bf16[128,2048]{1,0:T(8,128)(2,1)S(1)}, bf16[128,2048]{1,0:T(8,128)(2,1)S(1)}, u32[]{:S(2)}, u32[]{:S(2)}) collective-permute-start(bf16[128,2048]{1,0:T(8,128)(2,1)S(1)} %get-tuple-element.29.refs_3_.refs_2_), channel_id=1, source_target_pairs={{0,4},{1,5},{2,6},{3,7},{4,8},{5,9},{6,10},{7,11},{8,12},{9,13},{1... | collective-permute-start | bytes 1572872 | tf_op jit(solution)/shard_map/ppermute | solution.py:62
  39.0 2.2 %copy-done.6 = bf16[1,2048,1024]{2,1,0:T(8,128)(2,1)S(1)} copy-done((bf16[1,2048,1024]{2,1,0:T(8,128)(2,1)S(1)}, bf16[1,2048,1024]{2,1,0:T(8,128)(2,1)}, u32[]{:S(2)}) %copy-start.6) | copy-done | bytes 4194328
  41.2 2.2 %copy-done.7 = bf16[1,1024,2048]{2,1,0:T(8,128)(2,1)S(1)} copy-done((bf16[1,1024,2048]{2,1,0:T(8,128)(2,1)S(1)}, bf16[1,1024,2048]{2,1,0:T(8,128)(2,1)}, u32[]{:S(2)}) %copy-start.7) | copy-done | bytes 4194328
  43.4 2.4 %mlp.1 = bf16[128,2048]{1,0:T(8,128)(2,1)S(1)} custom-call(bf16[128,2048]{1,0:T(8,128)(2,1)} %bitcast.7.refs_0_, bf16[2048,1024]{1,0:T(8,128)(2,1)S(1)} %bitcast.35, bf16[1024,2048]{1,0:T(8,128)(2,1)S(1)} %bitcast.36, bf16[128,2048]{1,0:T(8,128)(2,1)S(1)} %get-tuple-element.29.refs_3_.refs_2_), custom_call_target="tpu_custom_call" | custom-call | tf_op jit(solution)/shard_map/mlp/pallas_call | solution.py:83
  45.8 0.8 copy-done.10
  46.6 6.7 %all-to-all-start.1 = ((bf16[16,8,2048]{2,1,0:T(8,128)(2,1)}), bf16[16,8,2048]{2,1,0:T(8,128)(2,1)}, u32[]{:S(2)}, u32[]{:S(2)}) async-start(bf16[16,8,2048]{2,1,0:T(8,128)(2,1)} %bitcast.40), calls=%async_computation.1 | async-start | bytes 1048576 | tf_op jit(solution)/shard_map/all_to_all | solution.py:200
  53.3 0.3 collective-permute-start.12
  53.6 0.2 collective-permute-start.13
  53.8 1.3 %collective-permute-start.14 = (bf16[128,2048]{1,0:T(8,128)(2,1)S(1)}, bf16[128,2048]{1,0:T(8,128)(2,1)}, u32[]{:S(2)}, u32[]{:S(2)}) collective-permute-start(bf16[128,2048]{1,0:T(8,128)(2,1)S(1)} %get-tuple-element.35.refs_5_.refs_9_), channel_id=1, source_target_pairs={{0,1},{1,0},{2,3},{3,2},{4,5},{5,4},{6,7},{7,6},{8,9},{9,8},{10,11... | collective-permute-start | bytes 1572872 | tf_op jit(solution)/shard_map/ppermute | solution.py:62
  55.1 3.6 %collective-permute-start.6 = (bf16[256,2048]{1,0:T(8,128)(2,1)}, bf16[256,2048]{1,0:T(8,128)(2,1)}, u32[]{:S(2)}, u32[]{:S(2)}) collective-permute-start(bf16[256,2048]{1,0:T(8,128)(2,1)} %bitcast.37), channel_id=1, source_target_pairs={{0,16},{16,0},{1,17},{17,1},{2,18},{18,2},{3,19},{19,3},{4,20},{20... | collective-permute-start | bytes 3145736 | tf_op jit(solution)/shard_map/ppermute | solution.py:444
  58.8 6.1 %all-to-all-done.1 = bf16[16,8,2048]{2,1,0:T(8,128)(2,1)} async-done(((bf16[16,8,2048]{2,1,0:T(8,128)(2,1)}), bf16[16,8,2048]{2,1,0:T(8,128)(2,1)}, u32[]{:S(2)}, u32[]{:S(2)}) %all-to-all-start.1) | async-done | bytes 524320 | tf_op jit(solution)/shard_map/all_to_all | solution.py:200
  64.9 1.1 %rows.1.refs_3_.refs_2_ = f32[16,2048]{1,0:T(8,128)S(1)} custom-call(f32[16,1]{1,0:T(8,128)S(1)} %get-tuple-element.25.refs_0_, bf16[128,2048]{1,0:T(8,128)(2,1)} %bitcast.11.refs_1_), custom_call_target="tpu_custom_call" | custom-call | tf_op jit(solution)/shard_map/rows/pallas_call | solution.py:83
  66.1 7.1 %collective-permute-done.12.refs_0_.refs_14_.refs_18_ = bf16[128,2048]{1,0:T(8,128)(2,1)} collective-permute-done((bf16[128,2048]{1,0:T(8,128)(2,1)S(1)}, bf16[128,2048]{1,0:T(8,128)(2,1)}, u32[]{:S(2)}, u32[]{:S(2)}) %collective-permute-start.12) | collective-permute-done | bytes 524320 | tf_op jit(solution)/shard_map/ppermute | solution.py:62
  73.1 1.2 %collective-permute-start.15 = (bf16[128,2048]{1,0:T(8,128)(2,1)S(1)}, bf16[128,2048]{1,0:T(8,128)(2,1)}, u32[]{:S(2)}, u32[]{:S(2)}) collective-permute-start(bf16[128,2048]{1,0:T(8,128)(2,1)S(1)} %get-tuple-element.38.refs_6_.refs_10_), channel_id=1, source_target_pairs={{0,1},{1,0},{2,3},{3,2},{4,5},{5,4},{6,7},{7,6},{8,9},{9,8},{10,11... | collective-permute-start | bytes 1572872 | tf_op jit(solution)/shard_map/ppermute | solution.py:62
  74.4 3.5 %collective-permute-start.16 = (bf16[128,2048]{1,0:T(8,128)(2,1)S(1)}, bf16[128,2048]{1,0:T(8,128)(2,1)}, u32[]{:S(2)}, u32[]{:S(2)}) collective-permute-start(bf16[128,2048]{1,0:T(8,128)(2,1)S(1)} %get-tuple-element.39.refs_13_.refs_17_), channel_id=1, source_target_pairs={{0,12},{1,13},{2,14},{3,15},{4,0},{5,1},{6,2},{7,3},{8,4},{9,5},{1... | collective-permute-start | bytes 1572872 | tf_op jit(solution)/shard_map/ppermute | solution.py:62
  77.9 0.6 collective-permute-start.17
  79.2 8.2 %collective-permute-start.8 = (f32[16,2048]{1,0:T(8,128)S(1)}, f32[16,2048]{1,0:T(8,128)}, u32[]{:S(2)}, u32[]{:S(2)}) collective-permute-start(f32[16,2048]{1,0:T(8,128)S(1)} %rows.1.refs_3_.refs_2_), channel_id=1, source_target_pairs={{0,16},{16,0},{1,17},{17,1},{2,18},{18,2},{3,19},{19,3},{4,20},{20... | collective-permute-start | bytes 393224 | tf_op jit(solution)/shard_map/ppermute | solution.py:231
  87.4 0.8 copy.35.refs_6_
  88.2 0.3 collective-permute-done.8.refs_7_
  88.5 1.2 %copy-done.9 = bf16[1,256,2048]{2,1,0:T(8,128)(2,1)S(1)} copy-done((bf16[1,256,2048]{2,1,0:T(8,128)(2,1)S(1)}, bf16[1,256,2048]{2,1,0:T(8,128)(2,1)}, u32[]{:S(2)}) %copy-start.9) | copy-done | bytes 1048600
  89.7 0.9 copy-done.11
  90.6 2.9 %norm.1 = (bf16[256,2048]{1,0:T(8,128)(2,1)S(1)}, bf16[176,2048]{1,0:T(8,128)(2,1)S(1)}, f32[256,2048]{1,0:T(8,128)S(1)}) custom-call(s32[1]{0:T(128)} %bitcast.refs_0_, bf16[256,2048]{1,0:T(8,128)(2,1)S(1)} %bitcast.39, f32[256,1]{1,0:T(8,128)S(1)} %copy.34.refs_2_, f32[16,2048]{1,0:T(8,128)S(1)} %rows.1.refs_3_.refs_2_, f32[1,2048]{1,0:T(1,128)S(1)} %copy-done.14, ...), custom_call_target="tpu_custom_call" | custom-call | tf_op jit(solution)/shard_map/norm/pallas_call | solution.py:83
  93.5 1.0 copy-done.1
  94.5 1.0 copy-done.3
  95.6 1.0 copy-done.5
  96.6 2.9 %project.1 = (f32[256,1024]{1,0:T(8,128)S(1)}, f32[176,512]{1,0:T(8,128)S(1)}) custom-call(s32[16]{0:T(128)S(1)} %stack.67.refs_0_, bf16[256,2048]{1,0:T(8,128)(2,1)S(1)} %get-tuple-element.30.refs_1_.refs_3_, bf16[176,2048]{1,0:T(8,128)(2,1)S(1)} %get-tuple-element.32.refs_2_.refs_4_, bf16[128,2048]{1,0:T(8,128)(2,1)S(1)} %copy-done.3, ...), custom_call_target="tpu_custom_call" | custom-call | tf_op jit(solution)/shard_map/project/pallas_call | solution.py:83
  99.5 4.2 %attend.1 = (f32[176,2048]{1,0:T(8,128)S(1)}, bf16[176,2048]{1,0:T(8,128)(2,1)S(1)}) custom-call(s32[16]{0:T(128)S(1)} %stack.67.refs_0_, s32[176,1]{1,0:T(8,128)S(1)} %copy.36.refs_1_, s32[1,256]{1,0:T(1,128)S(1)} %bitcast.46, bf16[256,2048]{1,0:T(8,128)(2,1)S(1)} %get-tuple-element.30.refs_1_.refs_3_, ...), custom_call_target="tpu_custom_call" | custom-call | tf_op jit(solution)/shard_map/attend/pallas_call | solution.py:83
  103.7 1.3 %collective-permute-start.18 = (bf16[176,2048]{1,0:T(8,128)(2,1)S(1)}, bf16[176,2048]{1,0:T(8,128)(2,1)S(1)}, u32[]{:S(2)}, u32[]{:S(2)}) collective-permute-start(bf16[176,2048]{1,0:T(8,128)(2,1)S(1)} %get-tuple-element.44), channel_id=1, source_target_pairs={{0,16},{1,17},{2,18},{3,19},{4,20},{5,21},{6,22},{7,23},{8,24},{9,... | collective-permute-start | bytes 2162696 | tf_op jit(solution)/shard_map/ppermute | solution.py:464
  105.0 2.8 %collective-permute-done.18.refs_4_ = bf16[176,2048]{1,0:T(8,128)(2,1)S(1)} collective-permute-done((bf16[176,2048]{1,0:T(8,128)(2,1)S(1)}, bf16[176,2048]{1,0:T(8,128)(2,1)S(1)}, u32[]{:S(2)}, u32[]{:S(2)}) %collective-permute-start.18) | collective-permute-done | bytes 720928 | tf_op jit(solution)/shard_map/ppermute | solution.py:464
  107.8 1.5 %finish.1 = bf16[256,2048]{1,0:T(8,128)(2,1)} custom-call(s32[1]{0:T(128)} %bitcast.refs_0_, bf16[256,2048]{1,0:T(8,128)(2,1)S(1)} %get-tuple-element.30.refs_1_.refs_3_, f32[256,2048]{1,0:T(8,128)S(1)} %get-tuple-element.31.refs_2_, f32[176,2048]{1,0:T(8,128)S(1)} %get-tuple-element.43.refs_3_, bf16[176,2048]{1,0:T(8,128)(2,1)S(1)} %collective-permute-done.18.refs_4_, ...), custom_call_target="tpu_custom_call" | custom-call | tf_op jit(solution)/shard_map/finish/pallas_call | solution.py:83
  (59 shorter events, 1.0 us)
Async XLA Ops:
  2.0 13.8 %copy-start.2 = (bf16[128,2048]{1,0:T(8,128)(2,1)}, bf16[128,2048]{1,0:T(8,128)(2,1)S(1)}, u32[]{:S(2)}) copy-start(bf16[128,2048]{1,0:T(8,128)(2,1)S(1)} %pad_maximum_fusion.refs_3_.refs_7_) | copy-start | bytes 1572868
  2.1 13.0 %collective-permute-start = (bf16[128,2048]{1,0:T(8,128)(2,1)S(1)}, bf16[128,2048]{1,0:T(8,128)(2,1)S(1)}, u32[]{:S(2)}, u32[]{:S(2)}) collective-permute-start(bf16[128,2048]{1,0:T(8,128)(2,1)S(1)} %pad_maximum_fusion.refs_3_.refs_7_), channel_id=1, source_target_pairs={{0,1},{1,0},{2,3},{3,2},{4,5},{5,4},{6,7},{7,6},{8,9},{9,8},{10,11... | collective-permute-start | bytes 1572872 | tf_op jit(solution)/shard_map/ppermute | solution.py:62
  3.3 12.5 %collective-permute-start.1 = (bf16[128,2048]{1,0:T(8,128)(2,1)S(1)}, bf16[128,2048]{1,0:T(8,128)(2,1)S(1)}, u32[]{:S(2)}, u32[]{:S(2)}) collective-permute-start(bf16[128,2048]{1,0:T(8,128)(2,1)S(1)} %pad_maximum_fusion.refs_3_.refs_7_), channel_id=1, source_target_pairs={{0,4},{1,5},{2,6},{3,7},{4,8},{5,9},{6,10},{7,11},{8,12},{9,13},{1... | collective-permute-start | bytes 1572872 | tf_op jit(solution)/shard_map/ppermute | solution.py:62
  3.3 12.5 %collective-permute-start.2 = (bf16[128,2048]{1,0:T(8,128)(2,1)S(1)}, bf16[128,2048]{1,0:T(8,128)(2,1)S(1)}, u32[]{:S(2)}, u32[]{:S(2)}) collective-permute-start(bf16[128,2048]{1,0:T(8,128)(2,1)S(1)} %pad_maximum_fusion.refs_3_.refs_7_), channel_id=1, source_target_pairs={{0,2},{1,3},{2,0},{3,1},{4,6},{5,7},{6,4},{7,5},{8,10},{9,11},{10,... | collective-permute-start | bytes 1572872 | tf_op jit(solution)/shard_map/ppermute | solution.py:62
  4.3 1.2 %copy-start.8 = (bf16[1,256,2048]{2,1,0:T(8,128)(2,1)S(1)}, bf16[1,256,2048]{2,1,0:T(8,128)(2,1)}, u32[]{:S(2)}) copy-start(bf16[1,256,2048]{2,1,0:T(8,128)(2,1)} %param.14) | copy-start | bytes 3145732
  5.5 1.0 copy-start.12
  6.5 0.7 copy-start.15
  7.9 0.8 copy-start.13
  8.7 30.2 %all-to-all-start = ((bf16[16,8,2048]{2,1,0:T(8,128)(2,1)}), bf16[16,8,2048]{2,1,0:T(8,128)(2,1)}, u32[]{:S(2)}, u32[]{:S(2)}) async-start(bf16[16,8,2048]{2,1,0:T(8,128)(2,1)} %bitcast.42), calls=%async_computation | async-start | bytes 1048576 | tf_op jit(solution)/shard_map/all_to_all | solution.py:200
  15.8 20.6 %copy-start = (bf16[128,2048]{1,0:T(8,128)(2,1)}, bf16[128,2048]{1,0:T(8,128)(2,1)S(1)}, u32[]{:S(2)}) copy-start(bf16[128,2048]{1,0:T(8,128)(2,1)S(1)} %get-tuple-element.28.refs_9_.refs_13_) | copy-start | bytes 1572868
  15.8 17.8 %collective-permute-start.3 = (bf16[128,2048]{1,0:T(8,128)(2,1)S(1)}, bf16[128,2048]{1,0:T(8,128)(2,1)S(1)}, u32[]{:S(2)}, u32[]{:S(2)}) collective-permute-start(bf16[128,2048]{1,0:T(8,128)(2,1)S(1)} %get-tuple-element.27.refs_1_), channel_id=1, source_target_pairs={{0,2},{1,3},{2,0},{3,1},{4,6},{5,7},{6,4},{7,5},{8,10},{9,11},{10,... | collective-permute-start | bytes 1572872 | tf_op jit(solution)/shard_map/ppermute | solution.py:62
  16.1 19.8 %collective-permute-start.4 = (bf16[128,2048]{1,0:T(8,128)(2,1)S(1)}, bf16[128,2048]{1,0:T(8,128)(2,1)S(1)}, u32[]{:S(2)}, u32[]{:S(2)}) collective-permute-start(bf16[128,2048]{1,0:T(8,128)(2,1)S(1)} %get-tuple-element.27.refs_1_), channel_id=1, source_target_pairs={{0,4},{1,5},{2,6},{3,7},{4,8},{5,9},{6,10},{7,11},{8,12},{9,13},{1... | collective-permute-start | bytes 1572872 | tf_op jit(solution)/shard_map/ppermute | solution.py:62
  18.0 17.9 %collective-permute-start.5 = (bf16[128,2048]{1,0:T(8,128)(2,1)S(1)}, bf16[128,2048]{1,0:T(8,128)(2,1)S(1)}, u32[]{:S(2)}, u32[]{:S(2)}) collective-permute-start(bf16[128,2048]{1,0:T(8,128)(2,1)S(1)} %get-tuple-element.28.refs_9_.refs_13_), channel_id=1, source_target_pairs={{0,1},{1,0},{2,3},{3,2},{4,5},{5,4},{6,7},{7,6},{8,9},{9,8},{10,11... | collective-permute-start | bytes 1572872 | tf_op jit(solution)/shard_map/ppermute | solution.py:62
  33.6 2.9 %copy-start.4 = (bf16[128,2048]{1,0:T(8,128)(2,1)}, bf16[128,2048]{1,0:T(8,128)(2,1)S(1)}, u32[]{:S(2)}) copy-start(bf16[128,2048]{1,0:T(8,128)(2,1)S(1)} %collective-permute-done.3.refs_0_.refs_10_.refs_14_) | copy-start | bytes 1572868
  35.9 17.4 %collective-permute-start.9 = (bf16[128,2048]{1,0:T(8,128)(2,1)S(1)}, bf16[128,2048]{1,0:T(8,128)(2,1)S(1)}, u32[]{:S(2)}, u32[]{:S(2)}) collective-permute-start(bf16[128,2048]{1,0:T(8,128)(2,1)S(1)} %get-tuple-element.33.refs_4_.refs_8_), channel_id=1, source_target_pairs={{0,1},{1,0},{2,3},{3,2},{4,5},{5,4},{6,7},{7,6},{8,9},{9,8},{10,11... | collective-permute-start | bytes 1572872 | tf_op jit(solution)/shard_map/ppermute | solution.py:62
  36.4 16.9 %collective-permute-start.10 = (bf16[128,2048]{1,0:T(8,128)(2,1)S(1)}, bf16[128,2048]{1,0:T(8,128)(2,1)}, u32[]{:S(2)}, u32[]{:S(2)}) collective-permute-start(bf16[128,2048]{1,0:T(8,128)(2,1)S(1)} %get-tuple-element.29.refs_3_.refs_2_), channel_id=1, source_target_pairs={{0,2},{1,3},{2,0},{3,1},{4,6},{5,7},{6,4},{7,5},{8,10},{9,11},{10,... | collective-permute-start | bytes 1572872 | tf_op jit(solution)/shard_map/ppermute | solution.py:62
  36.5 16.8 %collective-permute-start.11 = (bf16[128,2048]{1,0:T(8,128)(2,1)S(1)}, bf16[128,2048]{1,0:T(8,128)(2,1)S(1)}, u32[]{:S(2)}, u32[]{:S(2)}) collective-permute-start(bf16[128,2048]{1,0:T(8,128)(2,1)S(1)} %get-tuple-element.29.refs_3_.refs_2_), channel_id=1, source_target_pairs={{0,4},{1,5},{2,6},{3,7},{4,8},{5,9},{6,10},{7,11},{8,12},{9,13},{1... | collective-permute-start | bytes 1572872 | tf_op jit(solution)/shard_map/ppermute | solution.py:62
  39.0 2.2 %copy-start.6 = (bf16[1,2048,1024]{2,1,0:T(8,128)(2,1)S(1)}, bf16[1,2048,1024]{2,1,0:T(8,128)(2,1)}, u32[]{:S(2)}) copy-start(bf16[1,2048,1024]{2,1,0:T(8,128)(2,1)} %param.18) | copy-start | bytes 12582916
  41.2 2.2 %copy-start.7 = (bf16[1,1024,2048]{2,1,0:T(8,128)(2,1)S(1)}, bf16[1,1024,2048]{2,1,0:T(8,128)(2,1)}, u32[]{:S(2)}) copy-start(bf16[1,1024,2048]{2,1,0:T(8,128)(2,1)} %param.19) | copy-start | bytes 12582916
  43.4 15.3 %copy-start.14 = (f32[1,2048]{1,0:T(1,128)S(1)}, f32[1,2048]{1,0:T(1,128)}, u32[]{:S(2)}) copy-start(f32[1,2048]{1,0:T(1,128)} %refs_4_.1) | copy-start | bytes 24580
  43.4 15.4 %copy-start.16 = (s32[1,4]{1,0:T(1,128)S(1)}, s32[1,4]{1,0:T(1,128)}, u32[]{:S(2)}) copy-start(s32[1,4]{1,0:T(1,128)} %param.23) | copy-start | bytes 52
  45.8 0.8 copy-start.10
  46.6 32.0 %copy-start.17 = (s32[1,4]{1,0:T(1,128)S(1)}, s32[1,4]{1,0:T(1,128)}, u32[]{:S(2)}) copy-start(s32[1,4]{1,0:T(1,128)} %param.22) | copy-start | bytes 52
  46.6 18.4 %all-to-all-start.1 = ((bf16[16,8,2048]{2,1,0:T(8,128)(2,1)}), bf16[16,8,2048]{2,1,0:T(8,128)(2,1)}, u32[]{:S(2)}, u32[]{:S(2)}) async-start(bf16[16,8,2048]{2,1,0:T(8,128)(2,1)} %bitcast.40), calls=%async_computation.1 | async-start | bytes 1048576 | tf_op jit(solution)/shard_map/all_to_all | solution.py:200
  53.3 19.9 %collective-permute-start.12 = (bf16[128,2048]{1,0:T(8,128)(2,1)S(1)}, bf16[128,2048]{1,0:T(8,128)(2,1)}, u32[]{:S(2)}, u32[]{:S(2)}) collective-permute-start(bf16[128,2048]{1,0:T(8,128)(2,1)S(1)} %get-tuple-element.36.refs_4_), channel_id=1, source_target_pairs={{0,4},{1,5},{2,6},{3,7},{4,8},{5,9},{6,10},{7,11},{8,12},{9,13},{1... | collective-permute-start | bytes 1572872 | tf_op jit(solution)/shard_map/ppermute | solution.py:62
  53.6 19.5 %collective-permute-start.13 = (bf16[128,2048]{1,0:T(8,128)(2,1)S(1)}, bf16[128,2048]{1,0:T(8,128)(2,1)}, u32[]{:S(2)}, u32[]{:S(2)}) collective-permute-start(bf16[128,2048]{1,0:T(8,128)(2,1)S(1)} %get-tuple-element.37.refs_3_), channel_id=1, source_target_pairs={{0,2},{1,3},{2,0},{3,1},{4,6},{5,7},{6,4},{7,5},{8,10},{9,11},{10,... | collective-permute-start | bytes 1572872 | tf_op jit(solution)/shard_map/ppermute | solution.py:62
  53.8 19.4 %collective-permute-start.14 = (bf16[128,2048]{1,0:T(8,128)(2,1)S(1)}, bf16[128,2048]{1,0:T(8,128)(2,1)}, u32[]{:S(2)}, u32[]{:S(2)}) collective-permute-start(bf16[128,2048]{1,0:T(8,128)(2,1)S(1)} %get-tuple-element.35.refs_5_.refs_9_), channel_id=1, source_target_pairs={{0,1},{1,0},{2,3},{3,2},{4,5},{5,4},{6,7},{7,6},{8,9},{9,8},{10,11... | collective-permute-start | bytes 1572872 | tf_op jit(solution)/shard_map/ppermute | solution.py:62
  55.1 33.1 %collective-permute-start.6 = (bf16[256,2048]{1,0:T(8,128)(2,1)}, bf16[256,2048]{1,0:T(8,128)(2,1)}, u32[]{:S(2)}, u32[]{:S(2)}) collective-permute-start(bf16[256,2048]{1,0:T(8,128)(2,1)} %bitcast.37), channel_id=1, source_target_pairs={{0,16},{16,0},{1,17},{17,1},{2,18},{18,2},{3,19},{19,3},{4,20},{20... | collective-permute-start | bytes 3145736 | tf_op jit(solution)/shard_map/ppermute | solution.py:444
  58.7 20.5 %collective-permute-start.7 = (f32[2,2048]{1,0:T(2,128)S(1)}, f32[2,2048]{1,0:T(2,128)S(1)}, u32[]{:S(2)}, u32[]{:S(2)}) collective-permute-start(f32[2,2048]{1,0:T(2,128)S(1)} %fusion), channel_id=1, source_target_pairs={{0,16},{16,0},{1,17},{17,1},{2,18},{18,2},{3,19},{19,3},{4,20},{20... | collective-permute-start | bytes 49160 | tf_op jit(solution)/shard_map/ppermute | solution.py:230
  73.1 26.4 %collective-permute-start.15 = (bf16[128,2048]{1,0:T(8,128)(2,1)S(1)}, bf16[128,2048]{1,0:T(8,128)(2,1)}, u32[]{:S(2)}, u32[]{:S(2)}) collective-permute-start(bf16[128,2048]{1,0:T(8,128)(2,1)S(1)} %get-tuple-element.38.refs_6_.refs_10_), channel_id=1, source_target_pairs={{0,1},{1,0},{2,3},{3,2},{4,5},{5,4},{6,7},{7,6},{8,9},{9,8},{10,11... | collective-permute-start | bytes 1572872 | tf_op jit(solution)/shard_map/ppermute | solution.py:62
  74.4 25.1 %collective-permute-start.16 = (bf16[128,2048]{1,0:T(8,128)(2,1)S(1)}, bf16[128,2048]{1,0:T(8,128)(2,1)}, u32[]{:S(2)}, u32[]{:S(2)}) collective-permute-start(bf16[128,2048]{1,0:T(8,128)(2,1)S(1)} %get-tuple-element.39.refs_13_.refs_17_), channel_id=1, source_target_pairs={{0,12},{1,13},{2,14},{3,15},{4,0},{5,1},{6,2},{7,3},{8,4},{9,5},{1... | collective-permute-start | bytes 1572872 | tf_op jit(solution)/shard_map/ppermute | solution.py:62
  77.9 21.6 %collective-permute-start.17 = (bf16[128,2048]{1,0:T(8,128)(2,1)}, bf16[128,2048]{1,0:T(8,128)(2,1)}, u32[]{:S(2)}, u32[]{:S(2)}) collective-permute-start(bf16[128,2048]{1,0:T(8,128)(2,1)} %get-tuple-element.40.refs_15_.refs_19_), channel_id=1, source_target_pairs={{0,2},{1,3},{2,0},{3,1},{4,6},{5,7},{6,4},{7,5},{8,10},{9,11},{10,... | collective-permute-start | bytes 1572872 | tf_op jit(solution)/shard_map/ppermute | solution.py:62
  79.2 9.3 %collective-permute-start.8 = (f32[16,2048]{1,0:T(8,128)S(1)}, f32[16,2048]{1,0:T(8,128)}, u32[]{:S(2)}, u32[]{:S(2)}) collective-permute-start(f32[16,2048]{1,0:T(8,128)S(1)} %rows.1.refs_3_.refs_2_), channel_id=1, source_target_pairs={{0,16},{16,0},{1,17},{17,1},{2,18},{18,2},{3,19},{19,3},{4,20},{20... | collective-permute-start | bytes 393224 | tf_op jit(solution)/shard_map/ppermute | solution.py:231
  88.5 1.2 %copy-start.9 = (bf16[1,256,2048]{2,1,0:T(8,128)(2,1)S(1)}, bf16[1,256,2048]{2,1,0:T(8,128)(2,1)}, u32[]{:S(2)}) copy-start(bf16[1,256,2048]{2,1,0:T(8,128)(2,1)} %param.14) | copy-start | bytes 3145732
  89.7 0.9 copy-start.11
  93.5 1.0 copy-start.1
  94.5 1.0 copy-start.3
  95.6 1.0 copy-start.5
  103.7 4.1 %collective-permute-start.18 = (bf16[176,2048]{1,0:T(8,128)(2,1)S(1)}, bf16[176,2048]{1,0:T(8,128)(2,1)S(1)}, u32[]{:S(2)}, u32[]{:S(2)}) collective-permute-start(bf16[176,2048]{1,0:T(8,128)(2,1)S(1)} %get-tuple-element.44), channel_id=1, source_target_pairs={{0,16},{1,17},{2,18},{3,19},{4,20},{5,21},{6,22},{7,23},{8,24},{9,... | collective-permute-start | bytes 2162696 | tf_op jit(solution)/shard_map/ppermute | solution.py:464

commit v9 on v8

--- a/solution.py
+++ b/solution.py
@@ -114,18 +114,31 @@
     pass
 
 
-def mlp_kernel(rows, w_in, w_out, pieces):
+def mlp_kernel(held, rows, w_in, w_out, pieces):
     inner = jnp.maximum(dot(rows[...], w_in[...]), 0.0).astype(jnp.bfloat16)
-    pieces[...] = dot(inner, w_out[...]).astype(jnp.bfloat16)
-
-
-def rows_kernel(experts, gate, parts, rows):
-    count = gate.shape[0]
-    summed = [None] * (count // PAD)
-    for i, e in enumerate(experts):
-        part = parts[i * PAD : (i + 1) * PAD].astype(jnp.float32)
-        summed[e] = part if summed[e] is None else summed[e] + part
-    rows[...] = gate[...] * jnp.concatenate(summed, axis=0)
+    piece = dot(inner, w_out[...])
+    middle = piece.shape[0] // 2
+    first = held[0] == 0
+    near = jnp.where(first, piece[:middle], piece[middle:])
+    far = jnp.where(first, piece[middle:], piece[:middle])
+    for low in range(0, middle, PAD):
+        both = jnp.concatenate([near[low : low + PAD], far[low : low + PAD]], axis=0)
+        pieces[2 * low : 2 * low + 2 * PAD] = both.astype(jnp.bfloat16)
+
+
+def sum_kernel(pieces, own, other):
+    total = pieces[: 2 * PAD].astype(jnp.float32)
+    for low in range(2 * PAD, pieces.shape[0], 2 * PAD):
+        total = total + pieces[low : low + 2 * PAD].astype(jnp.float32)
+    own[...] = total[:PAD]
+    other[...] = total[PAD:]
+
+
+def rows_kernel(held, gate, own, arrived, rows):
+    first = held[0] == 0
+    near = jnp.where(first, own[...], arrived[...])
+    far = jnp.where(first, arrived[...], own[...])
+    rows[...] = gate[...] * jnp.concatenate([near, far], axis=0)
 
 
 def mixed_rows(hidden, place, rows_ref):
@@ -195,9 +208,15 @@
     held = [device // SPLIT for device in range(devices)]
     blocks = (devices * PAD, width)
 
-    def exchanged(values):
-        parts = values.reshape(devices, PAD, width)
-        parts = lax.all_to_all(parts, "ep", split_axis=0, concat_axis=0, tiled=True)
+    depth = chips()[0]
+    half = (place_of(lax.axis_index("ep"))[0] // (depth // 2))[None]
+    halves = [list(range(low, low + SPLIT)) for low in range(0, devices, SPLIT)]
+
+    def exchanged(values, groups=None):
+        parts = values.reshape(len(groups[0]) if groups else devices, -1, width)
+        parts = lax.all_to_all(
+            parts, "ep", split_axis=0, concat_axis=0, tiled=True, axis_index_groups=groups
+        )
         return parts.reshape(values.shape)
 
     gate, send = local(
@@ -212,12 +231,17 @@
         [(blocks, jnp.bfloat16)],
         (exchanged(send), w_in, w_out),
         mark,
+        order=half,
+    )
+    own, other = local(
+        sum_kernel, "sum", [((PAD, width), jnp.float32)] * 2, (exchanged(pieces, halves),)
     )
     (rows,) = local(
-        functools.partial(rows_kernel, held),
+        rows_kernel,
         "rows",
-        [((experts * PAD, width), jnp.float32)],
-        (gate, exchanged(pieces)),
+        [((2 * PAD, width), jnp.float32)],
+        (gate, own, moved(other, dz=depth // 2)),
+        order=half,
     )
     return rows
 

time: 110 us -> 105 us (0.955)
  the two profiles are of different devices: /device:TPU:29 before, /device:TPU:1 now
where the time goes in v9:
time: 105 us; the launch traced here: 104 us
  waiting for transfers between devices  37.5 us (36%)
  starting transfers between devices  31.9 us (30%)
  local copies, waits for them, and re-layouts  17.3 us (16%)
  Pallas kernels  15.7 us (15%)
  other arithmetic  1.13 us (1%)
    ppermute x16, waiting for transfers between devices, moved(): return lax.ppermute(value, 'ep', pairs)  34.3 us
    ppermute x16, starting transfers between devices, moved(): return lax.ppermute(value, 'ep', pairs)  17.8 us
    pallas_call x12, Pallas kernels, local(): pl.pallas_call(run, out_shape=[jax.ShapeDtypeStruct(shape, dtype) for sha...  15.7 us
    unnamed x36, local copies, waits for them, and re-layouts  14.2 us
    all_to_all x2, starting transfers between devices, exchanged(): lax.all_to_all(parts, 'ep', split_axis=0, concat_axis=0, tiled=True, axis...  8.54 us
    ppermute x1, starting transfers between devices, body(): other_hidden = lax.ppermute(hidden[0], 'grp', [(0, 1), (1, 0)])  3.05 us
    ppermute x1, waiting for transfers between devices, body(): received = lax.ppermute(sent, 'grp', [(0, 1)])  2.77 us
  transfers between devices with their start and end apart: 22, of which 7 were waited for; matrix products, arithmetic and copies ran while one was open for 2% of the time, Pallas kernels for 10%

profile of v9, /device:TPU:1, one launch (start us, length us, event | category | flops | bytes accessed | tf_op | source)
XLA Modules:
  0.0 104.0 jit_solution(1630936090328755217)
XLA Ops:
  0.0 1.0 constant_dynamic-slice_fusion
  1.0 1.0 constant_dynamic-slice_fusion.2
  2.1 2.1 %collective-permute-start = (bf16[128,2048]{1,0:T(8,128)(2,1)S(1)}, bf16[128,2048]{1,0:T(8,128)(2,1)S(1)}, u32[]{:S(2)}, u32[]{:S(2)}) collective-permute-start(bf16[128,2048]{1,0:T(8,128)(2,1)S(1)} %pad_maximum_fusion.refs_3_.refs_7_), channel_id=1, source_target_pairs={{0,1},{1,0},{2,3},{3,2},{4,5},{5,4},{6,7},{7,6},{8,9},{9,8},{10,11... | collective-permute-start | bytes 1572872 | tf_op jit(solution)/shard_map/ppermute | solution.py:62
  4.2 1.3 %collective-permute-start.1 = (bf16[128,2048]{1,0:T(8,128)(2,1)S(1)}, bf16[128,2048]{1,0:T(8,128)(2,1)S(1)}, u32[]{:S(2)}, u32[]{:S(2)}) collective-permute-start(bf16[128,2048]{1,0:T(8,128)(2,1)S(1)} %pad_maximum_fusion.refs_3_.refs_7_), channel_id=1, source_target_pairs={{0,4},{1,5},{2,6},{3,7},{4,8},{5,9},{6,10},{7,11},{8,12},{9,13},{1... | collective-permute-start | bytes 1572872 | tf_op jit(solution)/shard_map/ppermute | solution.py:62
  5.5 1.2 %collective-permute-start.2 = (bf16[128,2048]{1,0:T(8,128)(2,1)S(1)}, bf16[128,2048]{1,0:T(8,128)(2,1)S(1)}, u32[]{:S(2)}, u32[]{:S(2)}) collective-permute-start(bf16[128,2048]{1,0:T(8,128)(2,1)S(1)} %pad_maximum_fusion.refs_3_.refs_7_), channel_id=1, source_target_pairs={{0,2},{1,3},{2,0},{3,1},{4,6},{5,7},{6,4},{7,5},{8,10},{9,11},{10,... | collective-permute-start | bytes 1572872 | tf_op jit(solution)/shard_map/ppermute | solution.py:62
  6.7 0.7 fusion.2
  7.4 1.2 %copy-done.8 = bf16[1,256,2048]{2,1,0:T(8,128)(2,1)S(1)} copy-done((bf16[1,256,2048]{2,1,0:T(8,128)(2,1)S(1)}, bf16[1,256,2048]{2,1,0:T(8,128)(2,1)}, u32[]{:S(2)}) %copy-start.8) | copy-done | bytes 1048600
  8.6 1.0 copy-done.12
  9.7 0.7 copy-done.15
  10.4 0.7 pack.1
  11.1 0.8 copy-done.13
  11.9 4.3 %all-to-all-start = ((bf16[16,8,2048]{2,1,0:T(8,128)(2,1)}), bf16[16,8,2048]{2,1,0:T(8,128)(2,1)}, u32[]{:S(2)}, u32[]{:S(2)}) async-start(bf16[16,8,2048]{2,1,0:T(8,128)(2,1)} %bitcast.43), calls=%async_computation | async-start | bytes 1048576 | tf_op jit(solution)/shard_map/all_to_all | solution.py:217
  16.2 2.4 %collective-permute-done.1.refs_1_ = bf16[128,2048]{1,0:T(8,128)(2,1)S(1)} collective-permute-done((bf16[128,2048]{1,0:T(8,128)(2,1)S(1)}, bf16[128,2048]{1,0:T(8,128)(2,1)S(1)}, u32[]{:S(2)}, u32[]{:S(2)}) %collective-permute-start.1) | collective-permute-done | bytes 524320 | tf_op jit(solution)/shard_map/ppermute | solution.py:62
  18.6 1.3 %collective-permute-start.3 = (bf16[128,2048]{1,0:T(8,128)(2,1)S(1)}, bf16[128,2048]{1,0:T(8,128)(2,1)S(1)}, u32[]{:S(2)}, u32[]{:S(2)}) collective-permute-start(bf16[128,2048]{1,0:T(8,128)(2,1)S(1)} %get-tuple-element.29.refs_1_), channel_id=1, source_target_pairs={{0,2},{1,3},{2,0},{3,1},{4,6},{5,7},{6,4},{7,5},{8,10},{9,11},{10,... | collective-permute-start | bytes 1572872 | tf_op jit(solution)/shard_map/ppermute | solution.py:62
  19.9 0.3 collective-permute-start.4
  20.4 15.4 %collective-permute-done.3.refs_0_.refs_10_.refs_14_ = bf16[128,2048]{1,0:T(8,128)(2,1)S(1)} collective-permute-done((bf16[128,2048]{1,0:T(8,128)(2,1)S(1)}, bf16[128,2048]{1,0:T(8,128)(2,1)S(1)}, u32[]{:S(2)}, u32[]{:S(2)}) %collective-permute-start.3) | collective-permute-done | bytes 524320 | tf_op jit(solution)/shard_map/ppermute | solution.py:62
  35.8 2.7 %collective-permute-done.4.refs_2_ = bf16[128,2048]{1,0:T(8,128)(2,1)S(1)} collective-permute-done((bf16[128,2048]{1,0:T(8,128)(2,1)S(1)}, bf16[128,2048]{1,0:T(8,128)(2,1)S(1)}, u32[]{:S(2)}, u32[]{:S(2)}) %collective-permute-start.4) | collective-permute-done | bytes 524320 | tf_op jit(solution)/shard_map/ppermute | solution.py:62
  38.5 1.2 %collective-permute-start.10 = (bf16[128,2048]{1,0:T(8,128)(2,1)S(1)}, bf16[128,2048]{1,0:T(8,128)(2,1)S(1)}, u32[]{:S(2)}, u32[]{:S(2)}) collective-permute-start(bf16[128,2048]{1,0:T(8,128)(2,1)S(1)} %get-tuple-element.37.refs_4_.refs_8_), channel_id=1, source_target_pairs={{0,1},{1,0},{2,3},{3,2},{4,5},{5,4},{6,7},{7,6},{8,9},{9,8},{10,11... | collective-permute-start | bytes 1572872 | tf_op jit(solution)/shard_map/ppermute | solution.py:62
  39.6 1.2 %collective-permute-start.11 = (bf16[128,2048]{1,0:T(8,128)(2,1)S(1)}, bf16[128,2048]{1,0:T(8,128)(2,1)}, u32[]{:S(2)}, u32[]{:S(2)}) collective-permute-start(bf16[128,2048]{1,0:T(8,128)(2,1)S(1)} %get-tuple-element.31.refs_4_.refs_2_), channel_id=1, source_target_pairs={{0,2},{1,3},{2,0},{3,1},{4,6},{5,7},{6,4},{7,5},{8,10},{9,11},{10,... | collective-permute-start | bytes 1572872 | tf_op jit(solution)/shard_map/ppermute | solution.py:62
  40.9 1.5 %collective-permute-start.12 = (bf16[128,2048]{1,0:T(8,128)(2,1)S(1)}, bf16[128,2048]{1,0:T(8,128)(2,1)S(1)}, u32[]{:S(2)}, u32[]{:S(2)}) collective-permute-start(bf16[128,2048]{1,0:T(8,128)(2,1)S(1)} %get-tuple-element.31.refs_4_.refs_2_), channel_id=1, source_target_pairs={{0,4},{1,5},{2,6},{3,7},{4,8},{5,9},{6,10},{7,11},{8,12},{9,13},{1... | collective-permute-start | bytes 1572872 | tf_op jit(solution)/shard_map/ppermute | solution.py:62
  42.3 2.2 %copy-done.6 = bf16[1,2048,1024]{2,1,0:T(8,128)(2,1)S(1)} copy-done((bf16[1,2048,1024]{2,1,0:T(8,128)(2,1)S(1)}, bf16[1,2048,1024]{2,1,0:T(8,128)(2,1)}, u32[]{:S(2)}) %copy-start.6) | copy-done | bytes 4194328
  44.5 2.2 %copy-done.7 = bf16[1,1024,2048]{2,1,0:T(8,128)(2,1)S(1)} copy-done((bf16[1,1024,2048]{2,1,0:T(8,128)(2,1)S(1)}, bf16[1,1024,2048]{2,1,0:T(8,128)(2,1)}, u32[]{:S(2)}) %copy-start.7) | copy-done | bytes 4194328
  46.7 2.4 %mlp.1 = bf16[128,2048]{1,0:T(8,128)(2,1)S(1)} custom-call(s32[1]{0:T(128)} %bitcast.3.refs_0_, bf16[128,2048]{1,0:T(8,128)(2,1)} %bitcast.8.refs_1_, bf16[2048,1024]{1,0:T(8,128)(2,1)S(1)} %bitcast.36, bf16[1024,2048]{1,0:T(8,128)(2,1)S(1)} %bitcast.37, bf16[128,2048]{1,0:T(8,128)(2,1)S(1)} %get-tuple-element.31.refs_4_.refs_2_), custom_call_target="tpu_custom_call" | custom-call | tf_op jit(solution)/shard_map/mlp/pallas_call | solution.py:83
  49.1 0.8 copy-done.10
  49.9 4.3 %all-to-all-start.1 = ((bf16[8,16,2048]{2,1,0:T(8,128)(2,1)}), bf16[8,16,2048]{2,1,0:T(8,128)(2,1)}, u32[]{:S(2)}, u32[]{:S(2)}) async-start(bf16[8,16,2048]{2,1,0:T(8,128)(2,1)} %bitcast.41), calls=%async_computation.1 | async-start | bytes 1048576 | tf_op jit(solution)/shard_map/all_to_all | solution.py:217
  54.2 2.2 %collective-permute-start.13 = (bf16[128,2048]{1,0:T(8,128)(2,1)S(1)}, bf16[128,2048]{1,0:T(8,128)(2,1)}, u32[]{:S(2)}, u32[]{:S(2)}) collective-permute-start(bf16[128,2048]{1,0:T(8,128)(2,1)S(1)} %get-tuple-element.40.refs_4_), channel_id=1, source_target_pairs={{0,4},{1,5},{2,6},{3,7},{4,8},{5,9},{6,10},{7,11},{8,12},{9,13},{1... | collective-permute-start | bytes 1572872 | tf_op jit(solution)/shard_map/ppermute | solution.py:62
  56.4 0.5 collective-permute-start.14
  56.9 1.2 %collective-permute-start.15 = (bf16[128,2048]{1,0:T(8,128)(2,1)S(1)}, bf16[128,2048]{1,0:T(8,128)(2,1)}, u32[]{:S(2)}, u32[]{:S(2)}) collective-permute-start(bf16[128,2048]{1,0:T(8,128)(2,1)S(1)} %get-tuple-element.39.refs_5_.refs_9_), channel_id=1, source_target_pairs={{0,1},{1,0},{2,3},{3,2},{4,5},{5,4},{6,7},{7,6},{8,9},{9,8},{10,11... | collective-permute-start | bytes 1572872 | tf_op jit(solution)/shard_map/ppermute | solution.py:62
  58.1 3.0 %collective-permute-start.7 = (bf16[256,2048]{1,0:T(8,128)(2,1)}, bf16[256,2048]{1,0:T(8,128)(2,1)}, u32[]{:S(2)}, u32[]{:S(2)}) collective-permute-start(bf16[256,2048]{1,0:T(8,128)(2,1)} %bitcast.38), channel_id=1, source_target_pairs={{0,16},{16,0},{1,17},{17,1},{2,18},{18,2},{3,19},{19,3},{4,20},{20... | collective-permute-start | bytes 3145736 | tf_op jit(solution)/shard_map/ppermute | solution.py:468
  61.3 1.1 %sum.1 = (f32[8,2048]{1,0:T(8,128)S(1)}, f32[8,2048]{1,0:T(8,128)S(1)}) custom-call(bf16[128,2048]{1,0:T(8,128)(2,1)} %bitcast.12.refs_0_), custom_call_target="tpu_custom_call" | custom-call | tf_op jit(solution)/shard_map/sum/pallas_call | solution.py:83
  62.4 1.6 %collective-permute-start.6 = (f32[8,2048]{1,0:T(8,128)S(1)}, f32[8,2048]{1,0:T(8,128)S(1)}, u32[]{:S(2)}, u32[]{:S(2)}) collective-permute-start(f32[8,2048]{1,0:T(8,128)S(1)} %get-tuple-element.33), channel_id=1, source_target_pairs={{0,8},{1,9},{2,10},{3,11},{4,12},{5,13},{6,14},{7,15},{8,0},{9,1},... | collective-permute-start | bytes 196616 | tf_op jit(solution)/shard_map/ppermute | solution.py:62
  64.1 13.8 %collective-permute-done.6.refs_3_ = f32[8,2048]{1,0:T(8,128)S(1)} collective-permute-done((f32[8,2048]{1,0:T(8,128)S(1)}, f32[8,2048]{1,0:T(8,128)S(1)}, u32[]{:S(2)}, u32[]{:S(2)}) %collective-permute-start.6) | collective-permute-done | bytes 65568 | tf_op jit(solution)/shard_map/ppermute | solution.py:62
  77.9 0.7 collective-permute-start.8
  78.7 1.2 %collective-permute-start.16 = (bf16[128,2048]{1,0:T(8,128)(2,1)S(1)}, bf16[128,2048]{1,0:T(8,128)(2,1)}, u32[]{:S(2)}, u32[]{:S(2)}) collective-permute-start(bf16[128,2048]{1,0:T(8,128)(2,1)S(1)} %get-tuple-element.42.refs_6_.refs_10_), channel_id=1, source_target_pairs={{0,1},{1,0},{2,3},{3,2},{4,5},{5,4},{6,7},{7,6},{8,9},{9,8},{10,11... | collective-permute-start | bytes 1572872 | tf_op jit(solution)/shard_map/ppermute | solution.py:62
  79.9 0.8 collective-permute-start.18
  81.4 0.6 collective-permute-start.9
  82.0 0.8 copy.35.refs_6_
  83.2 1.2 %copy-done.9 = bf16[1,256,2048]{2,1,0:T(8,128)(2,1)S(1)} copy-done((bf16[1,256,2048]{2,1,0:T(8,128)(2,1)S(1)}, bf16[1,256,2048]{2,1,0:T(8,128)(2,1)}, u32[]{:S(2)}) %copy-start.9) | copy-done | bytes 1048600
  84.4 0.9 copy-done.11
  85.3 2.9 %norm.1 = (bf16[256,2048]{1,0:T(8,128)(2,1)S(1)}, bf16[176,2048]{1,0:T(8,128)(2,1)S(1)}, f32[256,2048]{1,0:T(8,128)S(1)}) custom-call(s32[1]{0:T(128)} %bitcast.refs_0_, bf16[256,2048]{1,0:T(8,128)(2,1)S(1)} %bitcast.40, f32[256,1]{1,0:T(8,128)S(1)} %copy.34.refs_2_, f32[16,2048]{1,0:T(8,128)S(1)} %rows.1.refs_3_.refs_2_, f32[1,2048]{1,0:T(1,128)S(1)} %copy-done.14, ...), custom_call_target="tpu_custom_call" | custom-call | tf_op jit(solution)/shard_map/norm/pallas_call | solution.py:83
  88.2 1.0 copy-done.1
  89.2 1.0 copy-done.3
  90.3 1.0 copy-done.5
  91.3 2.9 %project.1 = (f32[256,1024]{1,0:T(8,128)S(1)}, f32[176,512]{1,0:T(8,128)S(1)}) custom-call(s32[16]{0:T(128)S(1)} %stack.67.refs_0_, bf16[256,2048]{1,0:T(8,128)(2,1)S(1)} %get-tuple-element.34.refs_1_.refs_3_, bf16[176,2048]{1,0:T(8,128)(2,1)S(1)} %get-tuple-element.36.refs_2_.refs_4_, bf16[128,2048]{1,0:T(8,128)(2,1)S(1)} %copy-done.3, ...), custom_call_target="tpu_custom_call" | custom-call | tf_op jit(solution)/shard_map/project/pallas_call | solution.py:83
  94.2 4.2 %attend.1 = (f32[176,2048]{1,0:T(8,128)S(1)}, bf16[176,2048]{1,0:T(8,128)(2,1)S(1)}) custom-call(s32[16]{0:T(128)S(1)} %stack.67.refs_0_, s32[176,1]{1,0:T(8,128)S(1)} %copy.36.refs_1_, s32[1,256]{1,0:T(1,128)S(1)} %bitcast.47, bf16[256,2048]{1,0:T(8,128)(2,1)S(1)} %get-tuple-element.34.refs_1_.refs_3_, ...), custom_call_target="tpu_custom_call" | custom-call | tf_op jit(solution)/shard_map/attend/pallas_call | solution.py:83
  98.4 1.3 %collective-permute-start.19 = (bf16[176,2048]{1,0:T(8,128)(2,1)S(1)}, bf16[176,2048]{1,0:T(8,128)(2,1)S(1)}, u32[]{:S(2)}, u32[]{:S(2)}) collective-permute-start(bf16[176,2048]{1,0:T(8,128)(2,1)S(1)} %get-tuple-element.48), channel_id=1, source_target_pairs={{0,16},{1,17},{2,18},{3,19},{4,20},{5,21},{6,22},{7,23},{8,24},{9,... | collective-permute-start | bytes 2162696 | tf_op jit(solution)/shard_map/ppermute | solution.py:488
  99.7 2.8 %collective-permute-done.19.refs_4_ = bf16[176,2048]{1,0:T(8,128)(2,1)S(1)} collective-permute-done((bf16[176,2048]{1,0:T(8,128)(2,1)S(1)}, bf16[176,2048]{1,0:T(8,128)(2,1)S(1)}, u32[]{:S(2)}, u32[]{:S(2)}) %collective-permute-start.19) | collective-permute-done | bytes 720928 | tf_op jit(solution)/shard_map/ppermute | solution.py:488
  102.5 1.5 %finish.1 = bf16[256,2048]{1,0:T(8,128)(2,1)} custom-call(s32[1]{0:T(128)} %bitcast.refs_0_, bf16[256,2048]{1,0:T(8,128)(2,1)S(1)} %get-tuple-element.34.refs_1_.refs_3_, f32[256,2048]{1,0:T(8,128)S(1)} %get-tuple-element.35.refs_2_, f32[176,2048]{1,0:T(8,128)S(1)} %get-tuple-element.47.refs_3_, bf16[176,2048]{1,0:T(8,128)(2,1)S(1)} %collective-permute-done.19.refs_4_, ...), custom_call_target="tpu_custom_call" | custom-call | tf_op jit(solution)/shard_map/finish/pallas_call | solution.py:83
  (62 shorter events, 1.7 us)
Async XLA Ops:
  2.0 16.5 %copy-start.2 = (bf16[128,2048]{1,0:T(8,128)(2,1)}, bf16[128,2048]{1,0:T(8,128)(2,1)S(1)}, u32[]{:S(2)}) copy-start(bf16[128,2048]{1,0:T(8,128)(2,1)S(1)} %pad_maximum_fusion.refs_3_.refs_7_) | copy-start | bytes 1572868
  2.1 14.1 %collective-permute-start = (bf16[128,2048]{1,0:T(8,128)(2,1)S(1)}, bf16[128,2048]{1,0:T(8,128)(2,1)S(1)}, u32[]{:S(2)}, u32[]{:S(2)}) collective-permute-start(bf16[128,2048]{1,0:T(8,128)(2,1)S(1)} %pad_maximum_fusion.refs_3_.refs_7_), channel_id=1, source_target_pairs={{0,1},{1,0},{2,3},{3,2},{4,5},{5,4},{6,7},{7,6},{8,9},{9,8},{10,11... | collective-permute-start | bytes 1572872 | tf_op jit(solution)/shard_map/ppermute | solution.py:62
  4.2 14.4 %collective-permute-start.1 = (bf16[128,2048]{1,0:T(8,128)(2,1)S(1)}, bf16[128,2048]{1,0:T(8,128)(2,1)S(1)}, u32[]{:S(2)}, u32[]{:S(2)}) collective-permute-start(bf16[128,2048]{1,0:T(8,128)(2,1)S(1)} %pad_maximum_fusion.refs_3_.refs_7_), channel_id=1, source_target_pairs={{0,4},{1,5},{2,6},{3,7},{4,8},{5,9},{6,10},{7,11},{8,12},{9,13},{1... | collective-permute-start | bytes 1572872 | tf_op jit(solution)/shard_map/ppermute | solution.py:62
  5.5 13.1 %collective-permute-start.2 = (bf16[128,2048]{1,0:T(8,128)(2,1)S(1)}, bf16[128,2048]{1,0:T(8,128)(2,1)S(1)}, u32[]{:S(2)}, u32[]{:S(2)}) collective-permute-start(bf16[128,2048]{1,0:T(8,128)(2,1)S(1)} %pad_maximum_fusion.refs_3_.refs_7_), channel_id=1, source_target_pairs={{0,2},{1,3},{2,0},{3,1},{4,6},{5,7},{6,4},{7,5},{8,10},{9,11},{10,... | collective-permute-start | bytes 1572872 | tf_op jit(solution)/shard_map/ppermute | solution.py:62
  7.4 1.2 %copy-start.8 = (bf16[1,256,2048]{2,1,0:T(8,128)(2,1)S(1)}, bf16[1,256,2048]{2,1,0:T(8,128)(2,1)}, u32[]{:S(2)}) copy-start(bf16[1,256,2048]{2,1,0:T(8,128)(2,1)} %param.14) | copy-start | bytes 3145732
  8.6 1.0 %copy-start.12 = (bf16[1,2048,128]{2,1,0:T(8,128)(2,1)S(1)}, bf16[1,2048,128]{2,1,0:T(8,128)(2,1)}, u32[]{:S(2)}) copy-start(bf16[1,2048,128]{2,1,0:T(8,128)(2,1)} %param.17) | copy-start | bytes 1572868
  9.7 0.7 copy-start.15
  11.1 0.8 copy-start.13
  11.9 30.5 %all-to-all-start = ((bf16[16,8,2048]{2,1,0:T(8,128)(2,1)}), bf16[16,8,2048]{2,1,0:T(8,128)(2,1)}, u32[]{:S(2)}, u32[]{:S(2)}) async-start(bf16[16,8,2048]{2,1,0:T(8,128)(2,1)} %bitcast.43), calls=%async_computation | async-start | bytes 1048576 | tf_op jit(solution)/shard_map/all_to_all | solution.py:217
  18.6 21.1 %copy-start = (bf16[128,2048]{1,0:T(8,128)(2,1)}, bf16[128,2048]{1,0:T(8,128)(2,1)S(1)}, u32[]{:S(2)}) copy-start(bf16[128,2048]{1,0:T(8,128)(2,1)S(1)} %get-tuple-element.30.refs_9_.refs_13_) | copy-start | bytes 1572868
  18.6 17.2 %collective-permute-start.3 = (bf16[128,2048]{1,0:T(8,128)(2,1)S(1)}, bf16[128,2048]{1,0:T(8,128)(2,1)S(1)}, u32[]{:S(2)}, u32[]{:S(2)}) collective-permute-start(bf16[128,2048]{1,0:T(8,128)(2,1)S(1)} %get-tuple-element.29.refs_1_), channel_id=1, source_target_pairs={{0,2},{1,3},{2,0},{3,1},{4,6},{5,7},{6,4},{7,5},{8,10},{9,11},{10,... | collective-permute-start | bytes 1572872 | tf_op jit(solution)/shard_map/ppermute | solution.py:62
  19.9 18.6 %collective-permute-start.4 = (bf16[128,2048]{1,0:T(8,128)(2,1)S(1)}, bf16[128,2048]{1,0:T(8,128)(2,1)S(1)}, u32[]{:S(2)}, u32[]{:S(2)}) collective-permute-start(bf16[128,2048]{1,0:T(8,128)(2,1)S(1)} %get-tuple-element.29.refs_1_), channel_id=1, source_target_pairs={{0,4},{1,5},{2,6},{3,7},{4,8},{5,9},{6,10},{7,11},{8,12},{9,13},{1... | collective-permute-start | bytes 1572872 | tf_op jit(solution)/shard_map/ppermute | solution.py:62
  20.2 18.3 %collective-permute-start.5 = (bf16[128,2048]{1,0:T(8,128)(2,1)S(1)}, bf16[128,2048]{1,0:T(8,128)(2,1)S(1)}, u32[]{:S(2)}, u32[]{:S(2)}) collective-permute-start(bf16[128,2048]{1,0:T(8,128)(2,1)S(1)} %get-tuple-element.30.refs_9_.refs_13_), channel_id=1, source_target_pairs={{0,1},{1,0},{2,3},{3,2},{4,5},{5,4},{6,7},{7,6},{8,9},{9,8},{10,11... | collective-permute-start | bytes 1572872 | tf_op jit(solution)/shard_map/ppermute | solution.py:62
  35.8 5.1 %copy-start.4 = (bf16[128,2048]{1,0:T(8,128)(2,1)}, bf16[128,2048]{1,0:T(8,128)(2,1)S(1)}, u32[]{:S(2)}) copy-start(bf16[128,2048]{1,0:T(8,128)(2,1)S(1)} %collective-permute-done.3.refs_0_.refs_10_.refs_14_) | copy-start | bytes 1572868
  38.5 15.7 %collective-permute-start.10 = (bf16[128,2048]{1,0:T(8,128)(2,1)S(1)}, bf16[128,2048]{1,0:T(8,128)(2,1)S(1)}, u32[]{:S(2)}, u32[]{:S(2)}) collective-permute-start(bf16[128,2048]{1,0:T(8,128)(2,1)S(1)} %get-tuple-element.37.refs_4_.refs_8_), channel_id=1, source_target_pairs={{0,1},{1,0},{2,3},{3,2},{4,5},{5,4},{6,7},{7,6},{8,9},{9,8},{10,11... | collective-permute-start | bytes 1572872 | tf_op jit(solution)/shard_map/ppermute | solution.py:62
  39.6 14.6 %collective-permute-start.11 = (bf16[128,2048]{1,0:T(8,128)(2,1)S(1)}, bf16[128,2048]{1,0:T(8,128)(2,1)}, u32[]{:S(2)}, u32[]{:S(2)}) collective-permute-start(bf16[128,2048]{1,0:T(8,128)(2,1)S(1)} %get-tuple-element.31.refs_4_.refs_2_), channel_id=1, source_target_pairs={{0,2},{1,3},{2,0},{3,1},{4,6},{5,7},{6,4},{7,5},{8,10},{9,11},{10,... | collective-permute-start | bytes 1572872 | tf_op jit(solution)/shard_map/ppermute | solution.py:62
  40.9 13.4 %collective-permute-start.12 = (bf16[128,2048]{1,0:T(8,128)(2,1)S(1)}, bf16[128,2048]{1,0:T(8,128)(2,1)S(1)}, u32[]{:S(2)}, u32[]{:S(2)}) collective-permute-start(bf16[128,2048]{1,0:T(8,128)(2,1)S(1)} %get-tuple-element.31.refs_4_.refs_2_), channel_id=1, source_target_pairs={{0,4},{1,5},{2,6},{3,7},{4,8},{5,9},{6,10},{7,11},{8,12},{9,13},{1... | collective-permute-start | bytes 1572872 | tf_op jit(solution)/shard_map/ppermute | solution.py:62
  42.3 2.2 %copy-start.6 = (bf16[1,2048,1024]{2,1,0:T(8,128)(2,1)S(1)}, bf16[1,2048,1024]{2,1,0:T(8,128)(2,1)}, u32[]{:S(2)}) copy-start(bf16[1,2048,1024]{2,1,0:T(8,128)(2,1)} %param.18) | copy-start | bytes 12582916
  44.5 2.2 %copy-start.7 = (bf16[1,1024,2048]{2,1,0:T(8,128)(2,1)S(1)}, bf16[1,1024,2048]{2,1,0:T(8,128)(2,1)}, u32[]{:S(2)}) copy-start(bf16[1,1024,2048]{2,1,0:T(8,128)(2,1)} %param.19) | copy-start | bytes 12582916
  46.7 14.4 %copy-start.14 = (f32[1,2048]{1,0:T(1,128)S(1)}, f32[1,2048]{1,0:T(1,128)}, u32[]{:S(2)}) copy-start(f32[1,2048]{1,0:T(1,128)} %refs_4_.1) | copy-start | bytes 24580
  49.1 0.8 copy-start.10
  49.9 14.1 %copy-start.16 = (s32[1,4]{1,0:T(1,128)S(1)}, s32[1,4]{1,0:T(1,128)}, u32[]{:S(2)}) copy-start(s32[1,4]{1,0:T(1,128)} %param.23) | copy-start | bytes 52
  49.9 30.8 %copy-start.17 = (s32[1,4]{1,0:T(1,128)S(1)}, s32[1,4]{1,0:T(1,128)}, u32[]{:S(2)}) copy-start(s32[1,4]{1,0:T(1,128)} %param.22) | copy-start | bytes 52
  49.9 11.4 %all-to-all-start.1 = ((bf16[8,16,2048]{2,1,0:T(8,128)(2,1)}), bf16[8,16,2048]{2,1,0:T(8,128)(2,1)}, u32[]{:S(2)}, u32[]{:S(2)}) async-start(bf16[8,16,2048]{2,1,0:T(8,128)(2,1)} %bitcast.41), calls=%async_computation.1 | async-start | bytes 1048576 | tf_op jit(solution)/shard_map/all_to_all | solution.py:217
  54.2 24.4 %collective-permute-start.13 = (bf16[128,2048]{1,0:T(8,128)(2,1)S(1)}, bf16[128,2048]{1,0:T(8,128)(2,1)}, u32[]{:S(2)}, u32[]{:S(2)}) collective-permute-start(bf16[128,2048]{1,0:T(8,128)(2,1)S(1)} %get-tuple-element.40.refs_4_), channel_id=1, source_target_pairs={{0,4},{1,5},{2,6},{3,7},{4,8},{5,9},{6,10},{7,11},{8,12},{9,13},{1... | collective-permute-start | bytes 1572872 | tf_op jit(solution)/shard_map/ppermute | solution.py:62
  56.4 22.2 %collective-permute-start.14 = (bf16[128,2048]{1,0:T(8,128)(2,1)S(1)}, bf16[128,2048]{1,0:T(8,128)(2,1)}, u32[]{:S(2)}, u32[]{:S(2)}) collective-permute-start(bf16[128,2048]{1,0:T(8,128)(2,1)S(1)} %get-tuple-element.41.refs_3_), channel_id=1, source_target_pairs={{0,2},{1,3},{2,0},{3,1},{4,6},{5,7},{6,4},{7,5},{8,10},{9,11},{10,... | collective-permute-start | bytes 1572872 | tf_op jit(solution)/shard_map/ppermute | solution.py:62
  56.9 21.8 %collective-permute-start.15 = (bf16[128,2048]{1,0:T(8,128)(2,1)S(1)}, bf16[128,2048]{1,0:T(8,128)(2,1)}, u32[]{:S(2)}, u32[]{:S(2)}) collective-permute-start(bf16[128,2048]{1,0:T(8,128)(2,1)S(1)} %get-tuple-element.39.refs_5_.refs_9_), channel_id=1, source_target_pairs={{0,1},{1,0},{2,3},{3,2},{4,5},{5,4},{6,7},{7,6},{8,9},{9,8},{10,11... | collective-permute-start | bytes 1572872 | tf_op jit(solution)/shard_map/ppermute | solution.py:62
  58.1 24.8 %collective-permute-start.7 = (bf16[256,2048]{1,0:T(8,128)(2,1)}, bf16[256,2048]{1,0:T(8,128)(2,1)}, u32[]{:S(2)}, u32[]{:S(2)}) collective-permute-start(bf16[256,2048]{1,0:T(8,128)(2,1)} %bitcast.38), channel_id=1, source_target_pairs={{0,16},{16,0},{1,17},{17,1},{2,18},{18,2},{3,19},{19,3},{4,20},{20... | collective-permute-start | bytes 3145736 | tf_op jit(solution)/shard_map/ppermute | solution.py:468
  62.4 15.5 %collective-permute-start.6 = (f32[8,2048]{1,0:T(8,128)S(1)}, f32[8,2048]{1,0:T(8,128)S(1)}, u32[]{:S(2)}, u32[]{:S(2)}) collective-permute-start(f32[8,2048]{1,0:T(8,128)S(1)} %get-tuple-element.33), channel_id=1, source_target_pairs={{0,8},{1,9},{2,10},{3,11},{4,12},{5,13},{6,14},{7,15},{8,0},{9,1},... | collective-permute-start | bytes 196616 | tf_op jit(solution)/shard_map/ppermute | solution.py:62
  77.9 3.5 %collective-permute-start.8 = (f32[2,2048]{1,0:T(2,128)S(1)}, f32[2,2048]{1,0:T(2,128)S(1)}, u32[]{:S(2)}, u32[]{:S(2)}) collective-permute-start(f32[2,2048]{1,0:T(2,128)S(1)} %fusion), channel_id=1, source_target_pairs={{0,16},{16,0},{1,17},{17,1},{2,18},{18,2},{3,19},{19,3},{4,20},{20... | collective-permute-start | bytes 49160 | tf_op jit(solution)/shard_map/ppermute | solution.py:254
  78.7 15.5 %collective-permute-start.16 = (bf16[128,2048]{1,0:T(8,128)(2,1)S(1)}, bf16[128,2048]{1,0:T(8,128)(2,1)}, u32[]{:S(2)}, u32[]{:S(2)}) collective-permute-start(bf16[128,2048]{1,0:T(8,128)(2,1)S(1)} %get-tuple-element.42.refs_6_.refs_10_), channel_id=1, source_target_pairs={{0,1},{1,0},{2,3},{3,2},{4,5},{5,4},{6,7},{7,6},{8,9},{9,8},{10,11... | collective-permute-start | bytes 1572872 | tf_op jit(solution)/shard_map/ppermute | solution.py:62
  79.9 14.3 %collective-permute-start.17 = (bf16[128,2048]{1,0:T(8,128)(2,1)S(1)}, bf16[128,2048]{1,0:T(8,128)(2,1)}, u32[]{:S(2)}, u32[]{:S(2)}) collective-permute-start(bf16[128,2048]{1,0:T(8,128)(2,1)S(1)} %get-tuple-element.43.refs_13_.refs_17_), channel_id=1, source_target_pairs={{0,12},{1,13},{2,14},{3,15},{4,0},{5,1},{6,2},{7,3},{8,4},{9,5},{1... | collective-permute-start | bytes 1572872 | tf_op jit(solution)/shard_map/ppermute | solution.py:62
  79.9 14.3 %collective-permute-start.18 = (bf16[128,2048]{1,0:T(8,128)(2,1)}, bf16[128,2048]{1,0:T(8,128)(2,1)}, u32[]{:S(2)}, u32[]{:S(2)}) collective-permute-start(bf16[128,2048]{1,0:T(8,128)(2,1)} %get-tuple-element.44.refs_15_.refs_19_), channel_id=1, source_target_pairs={{0,2},{1,3},{2,0},{3,1},{4,6},{5,7},{6,4},{7,5},{8,10},{9,11},{10,... | collective-permute-start | bytes 1572872 | tf_op jit(solution)/shard_map/ppermute | solution.py:62
  81.4 1.7 %collective-permute-start.9 = (f32[16,2048]{1,0:T(8,128)S(1)}, f32[16,2048]{1,0:T(8,128)}, u32[]{:S(2)}, u32[]{:S(2)}) collective-permute-start(f32[16,2048]{1,0:T(8,128)S(1)} %rows.1.refs_3_.refs_2_), channel_id=1, source_target_pairs={{0,16},{16,0},{1,17},{17,1},{2,18},{18,2},{3,19},{19,3},{4,20},{20... | collective-permute-start | bytes 393224 | tf_op jit(solution)/shard_map/ppermute | solution.py:255
  83.2 1.2 %copy-start.9 = (bf16[1,256,2048]{2,1,0:T(8,128)(2,1)S(1)}, bf16[1,256,2048]{2,1,0:T(8,128)(2,1)}, u32[]{:S(2)}) copy-start(bf16[1,256,2048]{2,1,0:T(8,128)(2,1)} %param.14) | copy-start | bytes 3145732
  84.4 0.9 copy-start.11
  88.2 1.0 %copy-start.1 = (bf16[128,2048]{1,0:T(8,128)(2,1)S(1)}, bf16[128,2048]{1,0:T(8,128)(2,1)}, u32[]{:S(2)}) copy-start(bf16[128,2048]{1,0:T(8,128)(2,1)} %copy-done) | copy-start | bytes 1572868
  89.2 1.0 %copy-start.3 = (bf16[128,2048]{1,0:T(8,128)(2,1)S(1)}, bf16[128,2048]{1,0:T(8,128)(2,1)}, u32[]{:S(2)}) copy-start(bf16[128,2048]{1,0:T(8,128)(2,1)} %copy-done.2) | copy-start | bytes 1572868
  90.2 1.0 %copy-start.5 = (bf16[128,2048]{1,0:T(8,128)(2,1)S(1)}, bf16[128,2048]{1,0:T(8,128)(2,1)}, u32[]{:S(2)}) copy-start(bf16[128,2048]{1,0:T(8,128)(2,1)} %copy-done.4) | copy-start | bytes 1572868
  98.4 4.1 %collective-permute-start.19 = (bf16[176,2048]{1,0:T(8,128)(2,1)S(1)}, bf16[176,2048]{1,0:T(8,128)(2,1)S(1)}, u32[]{:S(2)}, u32[]{:S(2)}) collective-permute-start(bf16[176,2048]{1,0:T(8,128)(2,1)S(1)} %get-tuple-element.48), channel_id=1, source_target_pairs={{0,16},{1,17},{2,18},{3,19},{4,20},{5,21},{6,22},{7,23},{8,24},{9,... | collective-permute-start | bytes 2162696 | tf_op jit(solution)/shard_map/ppermute | solution.py:488

commit v10 on v9

--- a/solution.py
+++ b/solution.py
@@ -282,13 +282,13 @@
         return local(gate_kernel, "gate", [], (), there, blocks)
 
     z1, x0, y0 = moved(part, dz=1), moved(part, dx=1), moved(part, dy=1)
-    z1, y0 = once([x0], z1, y0)
-    z2, far0, y1 = moved(z1, dz=1), moved(y0, dx=1), moved(z1, dy=1)
-    z1, z2, far0 = once([y1], z1, z2, far0)
-    second = [z2]
-    z3, x1, y2 = moved(z2, dz=1), moved(z1, dx=1), moved(z2, dy=1)
-    z2, z3, far0 = once([x1, y2], z2, z3, far0)
-    far1, x2, y3 = moved(far0, dz=1), moved(z2, dx=1), moved(z3, dy=1)
+    (y0,) = once([x0, z1], y0)
+    z2, y1, far0 = moved(z1, dz=1), moved(z1, dy=1), moved(y0, dx=1)
+    z1, far0 = once([y1, z2], z1, far0)
+    second = [z1]
+    z3, y2, x1 = moved(z2, dz=1), moved(z2, dy=1), moved(z1, dx=1)
+    z2, far0 = once([x1, y2, z3], z2, far0)
+    y3, x2, far1 = moved(z3, dy=1), moved(z2, dx=1), moved(far0, dz=1)
     return [part, z1, z2, z3, x0, x1, y0, y1, y2, y3, far0, far1, x2], second
 
 

time: 105 us -> 106 us (level)
    unnamed x36 -> x38, local copies, waits for them, and re-layouts: 14.2 us -> 14.4 us
where the time goes in v10:
time: 106 us; the launch traced here: 105 us
  waiting for transfers between devices  37.1 us (35%)
  starting transfers between devices  32.2 us (30%)
  local copies, waits for them, and re-layouts  17.6 us (17%)
  Pallas kernels  16.2 us (15%)
  other arithmetic  1.13 us (1%)
    ppermute x16, waiting for transfers between devices, moved(): return lax.ppermute(value, 'ep', pairs)  33.8 us
    ppermute x16, starting transfers between devices, moved(): return lax.ppermute(value, 'ep', pairs)  18.1 us
    pallas_call x12, Pallas kernels, local(): pl.pallas_call(run, out_shape=[jax.ShapeDtypeStruct(shape, dtype) for sha...  16.2 us
    unnamed x38, local copies, waits for them, and re-layouts  14.4 us
    all_to_all x2, starting transfers between devices, exchanged(): lax.all_to_all(parts, 'ep', split_axis=0, concat_axis=0, tiled=True, axis...  8.54 us
    ppermute x1, starting transfers between devices, body(): other_hidden = lax.ppermute(hidden[0], 'grp', [(0, 1), (1, 0)])  2.99 us
    ppermute x1, waiting for transfers between devices, body(): received = lax.ppermute(sent, 'grp', [(0, 1)])  2.77 us
  transfers between devices with their start and end apart: 22, of which 7 were waited for; matrix products, arithmetic and copies ran while one was open for 2% of the time, Pallas kernels for 10%

profile of v10, /device:TPU:1, one launch (start us, length us, event | category | flops | bytes accessed | tf_op | source)
XLA Modules:
  0.0 104.7 jit_solution(16988751222653290956)
XLA Ops:
  0.0 1.0 constant_dynamic-slice_fusion
  1.0 1.0 constant_dynamic-slice_fusion.2
  2.1 2.2 %collective-permute-start = (bf16[128,2048]{1,0:T(8,128)(2,1)S(1)}, bf16[128,2048]{1,0:T(8,128)(2,1)S(1)}, u32[]{:S(2)}, u32[]{:S(2)}) collective-permute-start(bf16[128,2048]{1,0:T(8,128)(2,1)S(1)} %pad_maximum_fusion.refs_3_.refs_7_), channel_id=1, source_target_pairs={{0,4},{1,5},{2,6},{3,7},{4,8},{5,9},{6,10},{7,11},{8,12},{9,13},{1... | collective-permute-start | bytes 1572872 | tf_op jit(solution)/shard_map/ppermute | solution.py:62
  4.2 1.2 %collective-permute-start.3 = (bf16[128,2048]{1,0:T(8,128)(2,1)S(1)}, bf16[128,2048]{1,0:T(8,128)(2,1)S(1)}, u32[]{:S(2)}, u32[]{:S(2)}) collective-permute-start(bf16[128,2048]{1,0:T(8,128)(2,1)S(1)} %pad_maximum_fusion.refs_3_.refs_7_), channel_id=1, source_target_pairs={{0,1},{1,0},{2,3},{3,2},{4,5},{5,4},{6,7},{7,6},{8,9},{9,8},{10,11... | collective-permute-start | bytes 1572872 | tf_op jit(solution)/shard_map/ppermute | solution.py:62
  5.4 1.2 %collective-permute-start.4 = (bf16[128,2048]{1,0:T(8,128)(2,1)S(1)}, bf16[128,2048]{1,0:T(8,128)(2,1)S(1)}, u32[]{:S(2)}, u32[]{:S(2)}) collective-permute-start(bf16[128,2048]{1,0:T(8,128)(2,1)S(1)} %pad_maximum_fusion.refs_3_.refs_7_), channel_id=1, source_target_pairs={{0,2},{1,3},{2,0},{3,1},{4,6},{5,7},{6,4},{7,5},{8,10},{9,11},{10,... | collective-permute-start | bytes 1572872 | tf_op jit(solution)/shard_map/ppermute | solution.py:62
  6.7 0.7 fusion.2
  7.4 1.2 %copy-done.10 = bf16[1,256,2048]{2,1,0:T(8,128)(2,1)S(1)} copy-done((bf16[1,256,2048]{2,1,0:T(8,128)(2,1)S(1)}, bf16[1,256,2048]{2,1,0:T(8,128)(2,1)}, u32[]{:S(2)}) %copy-start.10) | copy-done | bytes 1048600
  8.6 1.0 copy-done.14
  9.7 0.7 copy-done.16
  10.4 1.3 %pack.1 = (f32[16,1]{1,0:T(8,128)S(1)}, bf16[128,2048]{1,0:T(8,128)(2,1)}) custom-call(s32[1,256]{1,0:T(1,128)S(1)} %bitcast.43, s32[1,256]{1,0:T(1,128)S(1)} %bitcast.45, bf16[256,2048]{1,0:T(8,128)(2,1)S(1)} %bitcast.39, f32[1,2048]{1,0:T(1,128)S(1)} %copy-done.16, bf16[2048,128]{1,0:T(8,128)(2,1)S(1)} %bitcast.42), custom_call_target="tpu_custom_call" | custom-call | tf_op jit(solution)/shard_map/pack/pallas_call | solution.py:83
  11.6 4.3 %all-to-all-start = ((bf16[16,8,2048]{2,1,0:T(8,128)(2,1)}), bf16[16,8,2048]{2,1,0:T(8,128)(2,1)}, u32[]{:S(2)}, u32[]{:S(2)}) async-start(bf16[16,8,2048]{2,1,0:T(8,128)(2,1)} %bitcast.7), calls=%async_computation | async-start | bytes 1048576 | tf_op jit(solution)/shard_map/all_to_all | solution.py:217
  15.9 2.0 %collective-permute-done.refs_1_.refs_2_ = bf16[128,2048]{1,0:T(8,128)(2,1)S(1)} collective-permute-done((bf16[128,2048]{1,0:T(8,128)(2,1)S(1)}, bf16[128,2048]{1,0:T(8,128)(2,1)S(1)}, u32[]{:S(2)}, u32[]{:S(2)}) %collective-permute-start) | collective-permute-done | bytes 524320 | tf_op jit(solution)/shard_map/ppermute | solution.py:62
  17.9 1.0 collective-permute-start.1
  19.0 1.3 %collective-permute-start.5 = (bf16[128,2048]{1,0:T(8,128)(2,1)S(1)}, bf16[128,2048]{1,0:T(8,128)(2,1)S(1)}, u32[]{:S(2)}, u32[]{:S(2)}) collective-permute-start(bf16[128,2048]{1,0:T(8,128)(2,1)S(1)} %gate.4.refs_9_.refs_13_), channel_id=1, source_target_pairs={{0,1},{1,0},{2,3},{3,2},{4,5},{5,4},{6,7},{7,6},{8,9},{9,8},{10,11... | collective-permute-start | bytes 1572872 | tf_op jit(solution)/shard_map/ppermute | solution.py:62
  20.2 15.2 %collective-permute-done.1.refs_0_.refs_10_.refs_14_ = bf16[128,2048]{1,0:T(8,128)(2,1)S(1)} collective-permute-done((bf16[128,2048]{1,0:T(8,128)(2,1)S(1)}, bf16[128,2048]{1,0:T(8,128)(2,1)S(1)}, u32[]{:S(2)}, u32[]{:S(2)}) %collective-permute-start.1) | collective-permute-done | bytes 524320 | tf_op jit(solution)/shard_map/ppermute | solution.py:62
  35.5 2.7 %collective-permute-done.2.refs_1_.refs_3_ = bf16[128,2048]{1,0:T(8,128)(2,1)S(1)} collective-permute-done((bf16[128,2048]{1,0:T(8,128)(2,1)S(1)}, bf16[128,2048]{1,0:T(8,128)(2,1)S(1)}, u32[]{:S(2)}, u32[]{:S(2)}) %collective-permute-start.2) | collective-permute-done | bytes 524320 | tf_op jit(solution)/shard_map/ppermute | solution.py:62
  38.2 1.2 %collective-permute-start.10 = (bf16[128,2048]{1,0:T(8,128)(2,1)S(1)}, bf16[128,2048]{1,0:T(8,128)(2,1)S(1)}, u32[]{:S(2)}, u32[]{:S(2)}) collective-permute-start(bf16[128,2048]{1,0:T(8,128)(2,1)S(1)} %get-tuple-element.25.refs_4_.refs_8_), channel_id=1, source_target_pairs={{0,1},{1,0},{2,3},{3,2},{4,5},{5,4},{6,7},{7,6},{8,9},{9,8},{10,11... | collective-permute-start | bytes 1572872 | tf_op jit(solution)/shard_map/ppermute | solution.py:62
  39.4 1.2 %collective-permute-start.11 = (bf16[128,2048]{1,0:T(8,128)(2,1)S(1)}, bf16[128,2048]{1,0:T(8,128)(2,1)S(1)}, u32[]{:S(2)}, u32[]{:S(2)}) collective-permute-start(bf16[128,2048]{1,0:T(8,128)(2,1)S(1)} %collective-permute-done.2.refs_1_.refs_3_), channel_id=1, source_target_pairs={{0,2},{1,3},{2,0},{3,1},{4,6},{5,7},{6,4},{7,5},{8,10},{9,11},{10,... | collective-permute-start | bytes 1572872 | tf_op jit(solution)/shard_map/ppermute | solution.py:62
  40.6 1.5 %collective-permute-start.12 = (bf16[128,2048]{1,0:T(8,128)(2,1)S(1)}, bf16[128,2048]{1,0:T(8,128)(2,1)S(1)}, u32[]{:S(2)}, u32[]{:S(2)}) collective-permute-start(bf16[128,2048]{1,0:T(8,128)(2,1)S(1)} %collective-permute-done.2.refs_1_.refs_3_), channel_id=1, source_target_pairs={{0,4},{1,5},{2,6},{3,7},{4,8},{5,9},{6,10},{7,11},{8,12},{9,13},{1... | collective-permute-start | bytes 1572872 | tf_op jit(solution)/shard_map/ppermute | solution.py:62
  42.1 2.2 %copy-done.8 = bf16[1,2048,1024]{2,1,0:T(8,128)(2,1)S(1)} copy-done((bf16[1,2048,1024]{2,1,0:T(8,128)(2,1)S(1)}, bf16[1,2048,1024]{2,1,0:T(8,128)(2,1)}, u32[]{:S(2)}) %copy-start.8) | copy-done | bytes 4194328
  44.3 2.2 %copy-done.9 = bf16[1,1024,2048]{2,1,0:T(8,128)(2,1)S(1)} copy-done((bf16[1,1024,2048]{2,1,0:T(8,128)(2,1)S(1)}, bf16[1,1024,2048]{2,1,0:T(8,128)(2,1)}, u32[]{:S(2)}) %copy-start.9) | copy-done | bytes 4194328
  46.5 2.4 %mlp.1 = bf16[128,2048]{1,0:T(8,128)(2,1)S(1)} custom-call(s32[1]{0:T(128)} %bitcast.3.refs_0_, bf16[128,2048]{1,0:T(8,128)(2,1)} %bitcast.8.refs_1_, bf16[2048,1024]{1,0:T(8,128)(2,1)S(1)} %bitcast.36, bf16[1024,2048]{1,0:T(8,128)(2,1)S(1)} %bitcast.37, bf16[128,2048]{1,0:T(8,128)(2,1)S(1)} %get-tuple-element.25.refs_4_.refs_8_), custom_call_target="tpu_custom_call" | custom-call | tf_op jit(solution)/shard_map/mlp/pallas_call | solution.py:83
  48.9 0.8 copy-done.12
  49.7 4.3 %all-to-all-start.1 = ((bf16[8,16,2048]{2,1,0:T(8,128)(2,1)}), bf16[8,16,2048]{2,1,0:T(8,128)(2,1)}, u32[]{:S(2)}, u32[]{:S(2)}) async-start(bf16[8,16,2048]{2,1,0:T(8,128)(2,1)} %bitcast.41), calls=%async_computation.1 | async-start | bytes 1048576 | tf_op jit(solution)/shard_map/all_to_all | solution.py:217
  54.0 2.2 %collective-permute-start.13 = (bf16[128,2048]{1,0:T(8,128)(2,1)S(1)}, bf16[128,2048]{1,0:T(8,128)(2,1)}, u32[]{:S(2)}, u32[]{:S(2)}) collective-permute-start(bf16[128,2048]{1,0:T(8,128)(2,1)S(1)} %get-tuple-element.33.refs_4_), channel_id=1, source_target_pairs={{0,4},{1,5},{2,6},{3,7},{4,8},{5,9},{6,10},{7,11},{8,12},{9,13},{1... | collective-permute-start | bytes 1572872 | tf_op jit(solution)/shard_map/ppermute | solution.py:62
  56.2 0.4 collective-permute-start.14
  56.6 1.2 %collective-permute-start.15 = (bf16[128,2048]{1,0:T(8,128)(2,1)S(1)}, bf16[128,2048]{1,0:T(8,128)(2,1)}, u32[]{:S(2)}, u32[]{:S(2)}) collective-permute-start(bf16[128,2048]{1,0:T(8,128)(2,1)S(1)} %get-tuple-element.32.refs_5_.refs_9_), channel_id=1, source_target_pairs={{0,1},{1,0},{2,3},{3,2},{4,5},{5,4},{6,7},{7,6},{8,9},{9,8},{10,11... | collective-permute-start | bytes 1572872 | tf_op jit(solution)/shard_map/ppermute | solution.py:62
  57.8 3.0 %collective-permute-start.7 = (bf16[256,2048]{1,0:T(8,128)(2,1)}, bf16[256,2048]{1,0:T(8,128)(2,1)}, u32[]{:S(2)}, u32[]{:S(2)}) collective-permute-start(bf16[256,2048]{1,0:T(8,128)(2,1)} %bitcast.38), channel_id=1, source_target_pairs={{0,16},{16,0},{1,17},{17,1},{2,18},{18,2},{3,19},{19,3},{4,20},{20... | collective-permute-start | bytes 3145736 | tf_op jit(solution)/shard_map/ppermute | solution.py:468
  61.0 1.1 %sum.1 = (f32[8,2048]{1,0:T(8,128)S(1)}, f32[8,2048]{1,0:T(8,128)S(1)}) custom-call(bf16[128,2048]{1,0:T(8,128)(2,1)} %bitcast.12.refs_0_), custom_call_target="tpu_custom_call" | custom-call | tf_op jit(solution)/shard_map/sum/pallas_call | solution.py:83
  62.2 1.6 %collective-permute-start.6 = (f32[8,2048]{1,0:T(8,128)S(1)}, f32[8,2048]{1,0:T(8,128)S(1)}, u32[]{:S(2)}, u32[]{:S(2)}) collective-permute-start(f32[8,2048]{1,0:T(8,128)S(1)} %get-tuple-element.27), channel_id=1, source_target_pairs={{0,8},{1,9},{2,10},{3,11},{4,12},{5,13},{6,14},{7,15},{8,0},{9,1},... | collective-permute-start | bytes 196616 | tf_op jit(solution)/shard_map/ppermute | solution.py:62
  63.8 13.8 %collective-permute-done.6.refs_3_ = f32[8,2048]{1,0:T(8,128)S(1)} collective-permute-done((f32[8,2048]{1,0:T(8,128)S(1)}, f32[8,2048]{1,0:T(8,128)S(1)}, u32[]{:S(2)}, u32[]{:S(2)}) %collective-permute-start.6) | collective-permute-done | bytes 65568 | tf_op jit(solution)/shard_map/ppermute | solution.py:62
  77.6 0.7 collective-permute-start.8
  78.4 1.1 %collective-permute-start.16 = (bf16[128,2048]{1,0:T(8,128)(2,1)S(1)}, bf16[128,2048]{1,0:T(8,128)(2,1)}, u32[]{:S(2)}, u32[]{:S(2)}) collective-permute-start(bf16[128,2048]{1,0:T(8,128)(2,1)S(1)} %get-tuple-element.34.refs_6_.refs_10_), channel_id=1, source_target_pairs={{0,1},{1,0},{2,3},{3,2},{4,5},{5,4},{6,7},{7,6},{8,9},{9,8},{10,11... | collective-permute-start | bytes 1572872 | tf_op jit(solution)/shard_map/ppermute | solution.py:62
  79.5 0.9 collective-permute-start.18
  81.2 0.6 collective-permute-start.9
  81.8 0.8 copy.32.refs_6_
  82.9 1.2 %copy-done.11 = bf16[1,256,2048]{2,1,0:T(8,128)(2,1)S(1)} copy-done((bf16[1,256,2048]{2,1,0:T(8,128)(2,1)S(1)}, bf16[1,256,2048]{2,1,0:T(8,128)(2,1)}, u32[]{:S(2)}) %copy-start.11) | copy-done | bytes 1048600
  84.1 0.9 copy-done.13
  85.0 2.9 %norm.1 = (bf16[256,2048]{1,0:T(8,128)(2,1)S(1)}, bf16[176,2048]{1,0:T(8,128)(2,1)S(1)}, f32[256,2048]{1,0:T(8,128)S(1)}) custom-call(s32[1]{0:T(128)} %bitcast.refs_0_, bf16[256,2048]{1,0:T(8,128)(2,1)S(1)} %bitcast.40, f32[256,1]{1,0:T(8,128)S(1)} %copy.31.refs_2_, f32[16,2048]{1,0:T(8,128)S(1)} %rows.1.refs_3_.refs_2_, f32[1,2048]{1,0:T(1,128)S(1)} %copy-done.15, ...), custom_call_target="tpu_custom_call" | custom-call | tf_op jit(solution)/shard_map/norm/pallas_call | solution.py:83
  87.9 1.0 copy-done.1
  89.0 1.0 copy-done.3
  90.0 1.0 copy-done.5
  91.0 1.0 copy-done.7
  92.1 2.8 %project.1 = (f32[256,1024]{1,0:T(8,128)S(1)}, f32[176,512]{1,0:T(8,128)S(1)}) custom-call(s32[16]{0:T(128)S(1)} %stack.67.refs_0_, bf16[256,2048]{1,0:T(8,128)(2,1)S(1)} %get-tuple-element.28.refs_1_.refs_3_, bf16[176,2048]{1,0:T(8,128)(2,1)S(1)} %get-tuple-element.30.refs_2_.refs_4_, bf16[128,2048]{1,0:T(8,128)(2,1)S(1)} %copy-done.1, ...), custom_call_target="tpu_custom_call" | custom-call | tf_op jit(solution)/shard_map/project/pallas_call | solution.py:83
  94.9 4.2 %attend.1 = (f32[176,2048]{1,0:T(8,128)S(1)}, bf16[176,2048]{1,0:T(8,128)(2,1)S(1)}) custom-call(s32[16]{0:T(128)S(1)} %stack.67.refs_0_, s32[176,1]{1,0:T(8,128)S(1)} %copy.33.refs_1_, s32[1,256]{1,0:T(1,128)S(1)} %bitcast.46, bf16[256,2048]{1,0:T(8,128)(2,1)S(1)} %get-tuple-element.28.refs_1_.refs_3_, ...), custom_call_target="tpu_custom_call" | custom-call | tf_op jit(solution)/shard_map/attend/pallas_call | solution.py:83
  99.1 1.3 %collective-permute-start.19 = (bf16[176,2048]{1,0:T(8,128)(2,1)S(1)}, bf16[176,2048]{1,0:T(8,128)(2,1)S(1)}, u32[]{:S(2)}, u32[]{:S(2)}) collective-permute-start(bf16[176,2048]{1,0:T(8,128)(2,1)S(1)} %get-tuple-element.40), channel_id=1, source_target_pairs={{0,16},{1,17},{2,18},{3,19},{4,20},{5,21},{6,22},{7,23},{8,24},{9,... | collective-permute-start | bytes 2162696 | tf_op jit(solution)/shard_map/ppermute | solution.py:488
  100.4 2.8 %collective-permute-done.19.refs_4_ = bf16[176,2048]{1,0:T(8,128)(2,1)S(1)} collective-permute-done((bf16[176,2048]{1,0:T(8,128)(2,1)S(1)}, bf16[176,2048]{1,0:T(8,128)(2,1)S(1)}, u32[]{:S(2)}, u32[]{:S(2)}) %collective-permute-start.19) | collective-permute-done | bytes 720928 | tf_op jit(solution)/shard_map/ppermute | solution.py:488
  103.2 1.5 %finish.1 = bf16[256,2048]{1,0:T(8,128)(2,1)} custom-call(s32[1]{0:T(128)} %bitcast.refs_0_, bf16[256,2048]{1,0:T(8,128)(2,1)S(1)} %get-tuple-element.28.refs_1_.refs_3_, f32[256,2048]{1,0:T(8,128)S(1)} %get-tuple-element.29.refs_2_, f32[176,2048]{1,0:T(8,128)S(1)} %get-tuple-element.39.refs_3_, bf16[176,2048]{1,0:T(8,128)(2,1)S(1)} %collective-permute-done.19.refs_4_, ...), custom_call_target="tpu_custom_call" | custom-call | tf_op jit(solution)/shard_map/finish/pallas_call | solution.py:83
  (64 shorter events, 1.5 us)
Async XLA Ops:
  2.0 16.9 %copy-start = (bf16[128,2048]{1,0:T(8,128)(2,1)}, bf16[128,2048]{1,0:T(8,128)(2,1)S(1)}, u32[]{:S(2)}) copy-start(bf16[128,2048]{1,0:T(8,128)(2,1)S(1)} %pad_maximum_fusion.refs_3_.refs_7_) | copy-start | bytes 1572868
  2.1 15.9 %collective-permute-start = (bf16[128,2048]{1,0:T(8,128)(2,1)S(1)}, bf16[128,2048]{1,0:T(8,128)(2,1)S(1)}, u32[]{:S(2)}, u32[]{:S(2)}) collective-permute-start(bf16[128,2048]{1,0:T(8,128)(2,1)S(1)} %pad_maximum_fusion.refs_3_.refs_7_), channel_id=1, source_target_pairs={{0,4},{1,5},{2,6},{3,7},{4,8},{5,9},{6,10},{7,11},{8,12},{9,13},{1... | collective-permute-start | bytes 1572872 | tf_op jit(solution)/shard_map/ppermute | solution.py:62
  4.2 14.7 %collective-permute-start.3 = (bf16[128,2048]{1,0:T(8,128)(2,1)S(1)}, bf16[128,2048]{1,0:T(8,128)(2,1)S(1)}, u32[]{:S(2)}, u32[]{:S(2)}) collective-permute-start(bf16[128,2048]{1,0:T(8,128)(2,1)S(1)} %pad_maximum_fusion.refs_3_.refs_7_), channel_id=1, source_target_pairs={{0,1},{1,0},{2,3},{3,2},{4,5},{5,4},{6,7},{7,6},{8,9},{9,8},{10,11... | collective-permute-start | bytes 1572872 | tf_op jit(solution)/shard_map/ppermute | solution.py:62
  5.4 13.5 %collective-permute-start.4 = (bf16[128,2048]{1,0:T(8,128)(2,1)S(1)}, bf16[128,2048]{1,0:T(8,128)(2,1)S(1)}, u32[]{:S(2)}, u32[]{:S(2)}) collective-permute-start(bf16[128,2048]{1,0:T(8,128)(2,1)S(1)} %pad_maximum_fusion.refs_3_.refs_7_), channel_id=1, source_target_pairs={{0,2},{1,3},{2,0},{3,1},{4,6},{5,7},{6,4},{7,5},{8,10},{9,11},{10,... | collective-permute-start | bytes 1572872 | tf_op jit(solution)/shard_map/ppermute | solution.py:62
  7.4 1.2 %copy-start.10 = (bf16[1,256,2048]{2,1,0:T(8,128)(2,1)S(1)}, bf16[1,256,2048]{2,1,0:T(8,128)(2,1)}, u32[]{:S(2)}) copy-start(bf16[1,256,2048]{2,1,0:T(8,128)(2,1)} %param.14) | copy-start | bytes 3145732
  8.6 1.0 copy-start.14
  9.7 0.7 copy-start.16
  11.6 30.5 %all-to-all-start = ((bf16[16,8,2048]{2,1,0:T(8,128)(2,1)}), bf16[16,8,2048]{2,1,0:T(8,128)(2,1)}, u32[]{:S(2)}, u32[]{:S(2)}) async-start(bf16[16,8,2048]{2,1,0:T(8,128)(2,1)} %bitcast.7), calls=%async_computation | async-start | bytes 1048576 | tf_op jit(solution)/shard_map/all_to_all | solution.py:217
  17.9 17.6 %collective-permute-start.1 = (bf16[128,2048]{1,0:T(8,128)(2,1)S(1)}, bf16[128,2048]{1,0:T(8,128)(2,1)S(1)}, u32[]{:S(2)}, u32[]{:S(2)}) collective-permute-start(bf16[128,2048]{1,0:T(8,128)(2,1)S(1)} %collective-permute-done.refs_1_.refs_2_), channel_id=1, source_target_pairs={{0,2},{1,3},{2,0},{3,1},{4,6},{5,7},{6,4},{7,5},{8,10},{9,11},{10,... | collective-permute-start | bytes 1572872 | tf_op jit(solution)/shard_map/ppermute | solution.py:62
  18.9 19.3 %collective-permute-start.2 = (bf16[128,2048]{1,0:T(8,128)(2,1)S(1)}, bf16[128,2048]{1,0:T(8,128)(2,1)S(1)}, u32[]{:S(2)}, u32[]{:S(2)}) collective-permute-start(bf16[128,2048]{1,0:T(8,128)(2,1)S(1)} %collective-permute-done.refs_1_.refs_2_), channel_id=1, source_target_pairs={{0,4},{1,5},{2,6},{3,7},{4,8},{5,9},{6,10},{7,11},{8,12},{9,13},{1... | collective-permute-start | bytes 1572872 | tf_op jit(solution)/shard_map/ppermute | solution.py:62
  18.9 20.5 %copy-start.2 = (bf16[128,2048]{1,0:T(8,128)(2,1)}, bf16[128,2048]{1,0:T(8,128)(2,1)S(1)}, u32[]{:S(2)}) copy-start(bf16[128,2048]{1,0:T(8,128)(2,1)S(1)} %collective-permute-done.3.refs_0_.refs_7_.refs_11_) | copy-start | bytes 1572868
  18.9 19.3 %copy-start.6 = (bf16[128,2048]{1,0:T(8,128)(2,1)}, bf16[128,2048]{1,0:T(8,128)(2,1)S(1)}, u32[]{:S(2)}) copy-start(bf16[128,2048]{1,0:T(8,128)(2,1)S(1)} %gate.4.refs_9_.refs_13_) | copy-start | bytes 1572868
  19.0 19.3 %collective-permute-start.5 = (bf16[128,2048]{1,0:T(8,128)(2,1)S(1)}, bf16[128,2048]{1,0:T(8,128)(2,1)S(1)}, u32[]{:S(2)}, u32[]{:S(2)}) collective-permute-start(bf16[128,2048]{1,0:T(8,128)(2,1)S(1)} %gate.4.refs_9_.refs_13_), channel_id=1, source_target_pairs={{0,1},{1,0},{2,3},{3,2},{4,5},{5,4},{6,7},{7,6},{8,9},{9,8},{10,11... | collective-permute-start | bytes 1572872 | tf_op jit(solution)/shard_map/ppermute | solution.py:62
  35.5 5.2 %copy-start.4 = (bf16[128,2048]{1,0:T(8,128)(2,1)}, bf16[128,2048]{1,0:T(8,128)(2,1)S(1)}, u32[]{:S(2)}) copy-start(bf16[128,2048]{1,0:T(8,128)(2,1)S(1)} %collective-permute-done.1.refs_0_.refs_10_.refs_14_) | copy-start | bytes 1572868
  38.2 15.8 %collective-permute-start.10 = (bf16[128,2048]{1,0:T(8,128)(2,1)S(1)}, bf16[128,2048]{1,0:T(8,128)(2,1)S(1)}, u32[]{:S(2)}, u32[]{:S(2)}) collective-permute-start(bf16[128,2048]{1,0:T(8,128)(2,1)S(1)} %get-tuple-element.25.refs_4_.refs_8_), channel_id=1, source_target_pairs={{0,1},{1,0},{2,3},{3,2},{4,5},{5,4},{6,7},{7,6},{8,9},{9,8},{10,11... | collective-permute-start | bytes 1572872 | tf_op jit(solution)/shard_map/ppermute | solution.py:62
  39.4 14.6 %collective-permute-start.11 = (bf16[128,2048]{1,0:T(8,128)(2,1)S(1)}, bf16[128,2048]{1,0:T(8,128)(2,1)S(1)}, u32[]{:S(2)}, u32[]{:S(2)}) collective-permute-start(bf16[128,2048]{1,0:T(8,128)(2,1)S(1)} %collective-permute-done.2.refs_1_.refs_3_), channel_id=1, source_target_pairs={{0,2},{1,3},{2,0},{3,1},{4,6},{5,7},{6,4},{7,5},{8,10},{9,11},{10,... | collective-permute-start | bytes 1572872 | tf_op jit(solution)/shard_map/ppermute | solution.py:62
  40.6 13.4 %collective-permute-start.12 = (bf16[128,2048]{1,0:T(8,128)(2,1)S(1)}, bf16[128,2048]{1,0:T(8,128)(2,1)S(1)}, u32[]{:S(2)}, u32[]{:S(2)}) collective-permute-start(bf16[128,2048]{1,0:T(8,128)(2,1)S(1)} %collective-permute-done.2.refs_1_.refs_3_), channel_id=1, source_target_pairs={{0,4},{1,5},{2,6},{3,7},{4,8},{5,9},{6,10},{7,11},{8,12},{9,13},{1... | collective-permute-start | bytes 1572872 | tf_op jit(solution)/shard_map/ppermute | solution.py:62
  42.1 2.2 %copy-start.8 = (bf16[1,2048,1024]{2,1,0:T(8,128)(2,1)S(1)}, bf16[1,2048,1024]{2,1,0:T(8,128)(2,1)}, u32[]{:S(2)}) copy-start(bf16[1,2048,1024]{2,1,0:T(8,128)(2,1)} %param.18) | copy-start | bytes 12582916
  44.3 2.2 %copy-start.9 = (bf16[1,1024,2048]{2,1,0:T(8,128)(2,1)S(1)}, bf16[1,1024,2048]{2,1,0:T(8,128)(2,1)}, u32[]{:S(2)}) copy-start(bf16[1,1024,2048]{2,1,0:T(8,128)(2,1)} %param.19) | copy-start | bytes 12582916
  46.5 14.3 %copy-start.15 = (f32[1,2048]{1,0:T(1,128)S(1)}, f32[1,2048]{1,0:T(1,128)}, u32[]{:S(2)}) copy-start(f32[1,2048]{1,0:T(1,128)} %refs_4_.1) | copy-start | bytes 24580
  48.9 0.8 copy-start.12
  49.7 14.1 %copy-start.17 = (s32[1,4]{1,0:T(1,128)S(1)}, s32[1,4]{1,0:T(1,128)}, u32[]{:S(2)}) copy-start(s32[1,4]{1,0:T(1,128)} %param.23) | copy-start | bytes 52
  49.7 30.8 %copy-start.18 = (s32[1,4]{1,0:T(1,128)S(1)}, s32[1,4]{1,0:T(1,128)}, u32[]{:S(2)}) copy-start(s32[1,4]{1,0:T(1,128)} %param.22) | copy-start | bytes 52
  49.7 11.4 %all-to-all-start.1 = ((bf16[8,16,2048]{2,1,0:T(8,128)(2,1)}), bf16[8,16,2048]{2,1,0:T(8,128)(2,1)}, u32[]{:S(2)}, u32[]{:S(2)}) async-start(bf16[8,16,2048]{2,1,0:T(8,128)(2,1)} %bitcast.41), calls=%async_computation.1 | async-start | bytes 1048576 | tf_op jit(solution)/shard_map/all_to_all | solution.py:217
  54.0 24.4 %collective-permute-start.13 = (bf16[128,2048]{1,0:T(8,128)(2,1)S(1)}, bf16[128,2048]{1,0:T(8,128)(2,1)}, u32[]{:S(2)}, u32[]{:S(2)}) collective-permute-start(bf16[128,2048]{1,0:T(8,128)(2,1)S(1)} %get-tuple-element.33.refs_4_), channel_id=1, source_target_pairs={{0,4},{1,5},{2,6},{3,7},{4,8},{5,9},{6,10},{7,11},{8,12},{9,13},{1... | collective-permute-start | bytes 1572872 | tf_op jit(solution)/shard_map/ppermute | solution.py:62
  56.2 22.2 %collective-permute-start.14 = (bf16[128,2048]{1,0:T(8,128)(2,1)S(1)}, bf16[128,2048]{1,0:T(8,128)(2,1)}, u32[]{:S(2)}, u32[]{:S(2)}) collective-permute-start(bf16[128,2048]{1,0:T(8,128)(2,1)S(1)} %collective-permute-done.12.refs_2_.refs_3_), channel_id=1, source_target_pairs={{0,2},{1,3},{2,0},{3,1},{4,6},{5,7},{6,4},{7,5},{8,10},{9,11},{10,... | collective-permute-start | bytes 1572872 | tf_op jit(solution)/shard_map/ppermute | solution.py:62
  56.6 21.8 %collective-permute-start.15 = (bf16[128,2048]{1,0:T(8,128)(2,1)S(1)}, bf16[128,2048]{1,0:T(8,128)(2,1)}, u32[]{:S(2)}, u32[]{:S(2)}) collective-permute-start(bf16[128,2048]{1,0:T(8,128)(2,1)S(1)} %get-tuple-element.32.refs_5_.refs_9_), channel_id=1, source_target_pairs={{0,1},{1,0},{2,3},{3,2},{4,5},{5,4},{6,7},{7,6},{8,9},{9,8},{10,11... | collective-permute-start | bytes 1572872 | tf_op jit(solution)/shard_map/ppermute | solution.py:62
  57.8 24.8 %collective-permute-start.7 = (bf16[256,2048]{1,0:T(8,128)(2,1)}, bf16[256,2048]{1,0:T(8,128)(2,1)}, u32[]{:S(2)}, u32[]{:S(2)}) collective-permute-start(bf16[256,2048]{1,0:T(8,128)(2,1)} %bitcast.38), channel_id=1, source_target_pairs={{0,16},{16,0},{1,17},{17,1},{2,18},{18,2},{3,19},{19,3},{4,20},{20... | collective-permute-start | bytes 3145736 | tf_op jit(solution)/shard_map/ppermute | solution.py:468
  62.2 15.5 %collective-permute-start.6 = (f32[8,2048]{1,0:T(8,128)S(1)}, f32[8,2048]{1,0:T(8,128)S(1)}, u32[]{:S(2)}, u32[]{:S(2)}) collective-permute-start(f32[8,2048]{1,0:T(8,128)S(1)} %get-tuple-element.27), channel_id=1, source_target_pairs={{0,8},{1,9},{2,10},{3,11},{4,12},{5,13},{6,14},{7,15},{8,0},{9,1},... | collective-permute-start | bytes 196616 | tf_op jit(solution)/shard_map/ppermute | solution.py:62
  77.6 3.5 %collective-permute-start.8 = (f32[2,2048]{1,0:T(2,128)S(1)}, f32[2,2048]{1,0:T(2,128)S(1)}, u32[]{:S(2)}, u32[]{:S(2)}) collective-permute-start(f32[2,2048]{1,0:T(2,128)S(1)} %fusion), channel_id=1, source_target_pairs={{0,16},{16,0},{1,17},{17,1},{2,18},{18,2},{3,19},{19,3},{4,20},{20... | collective-permute-start | bytes 49160 | tf_op jit(solution)/shard_map/ppermute | solution.py:254
  78.4 16.5 %collective-permute-start.16 = (bf16[128,2048]{1,0:T(8,128)(2,1)S(1)}, bf16[128,2048]{1,0:T(8,128)(2,1)}, u32[]{:S(2)}, u32[]{:S(2)}) collective-permute-start(bf16[128,2048]{1,0:T(8,128)(2,1)S(1)} %get-tuple-element.34.refs_6_.refs_10_), channel_id=1, source_target_pairs={{0,1},{1,0},{2,3},{3,2},{4,5},{5,4},{6,7},{7,6},{8,9},{9,8},{10,11... | collective-permute-start | bytes 1572872 | tf_op jit(solution)/shard_map/ppermute | solution.py:62
  79.5 15.4 %collective-permute-start.17 = (bf16[128,2048]{1,0:T(8,128)(2,1)S(1)}, bf16[128,2048]{1,0:T(8,128)(2,1)}, u32[]{:S(2)}, u32[]{:S(2)}) collective-permute-start(bf16[128,2048]{1,0:T(8,128)(2,1)S(1)} %get-tuple-element.35.refs_13_.refs_17_), channel_id=1, source_target_pairs={{0,12},{1,13},{2,14},{3,15},{4,0},{5,1},{6,2},{7,3},{8,4},{9,5},{1... | collective-permute-start | bytes 1572872 | tf_op jit(solution)/shard_map/ppermute | solution.py:62
  79.5 15.4 %collective-permute-start.18 = (bf16[128,2048]{1,0:T(8,128)(2,1)}, bf16[128,2048]{1,0:T(8,128)(2,1)}, u32[]{:S(2)}, u32[]{:S(2)}) collective-permute-start(bf16[128,2048]{1,0:T(8,128)(2,1)} %get-tuple-element.36.refs_15_.refs_19_), channel_id=1, source_target_pairs={{0,2},{1,3},{2,0},{3,1},{4,6},{5,7},{6,4},{7,5},{8,10},{9,11},{10,... | collective-permute-start | bytes 1572872 | tf_op jit(solution)/shard_map/ppermute | solution.py:62
  81.2 1.7 %collective-permute-start.9 = (f32[16,2048]{1,0:T(8,128)S(1)}, f32[16,2048]{1,0:T(8,128)}, u32[]{:S(2)}, u32[]{:S(2)}) collective-permute-start(f32[16,2048]{1,0:T(8,128)S(1)} %rows.1.refs_3_.refs_2_), channel_id=1, source_target_pairs={{0,16},{16,0},{1,17},{17,1},{2,18},{18,2},{3,19},{19,3},{4,20},{20... | collective-permute-start | bytes 393224 | tf_op jit(solution)/shard_map/ppermute | solution.py:255
  82.9 1.2 %copy-start.11 = (bf16[1,256,2048]{2,1,0:T(8,128)(2,1)S(1)}, bf16[1,256,2048]{2,1,0:T(8,128)(2,1)}, u32[]{:S(2)}) copy-start(bf16[1,256,2048]{2,1,0:T(8,128)(2,1)} %param.14) | copy-start | bytes 3145732
  84.1 0.9 copy-start.13
  87.9 1.0 copy-start.1
  89.0 1.0 copy-start.3
  90.0 1.0 copy-start.5
  91.0 1.0 copy-start.7
  99.1 4.1 %collective-permute-start.19 = (bf16[176,2048]{1,0:T(8,128)(2,1)S(1)}, bf16[176,2048]{1,0:T(8,128)(2,1)S(1)}, u32[]{:S(2)}, u32[]{:S(2)}) collective-permute-start(bf16[176,2048]{1,0:T(8,128)(2,1)S(1)} %get-tuple-element.40), channel_id=1, source_target_pairs={{0,16},{1,17},{2,18},{3,19},{4,20},{5,21},{6,22},{7,23},{8,24},{9,... | collective-permute-start | bytes 2162696 | tf_op jit(solution)/shard_map/ppermute | solution.py:488

commit v11 on v10

--- a/solution.py
+++ b/solution.py
@@ -93,15 +93,15 @@
     )(*scalars, *vmem, *far, *after, *onward)
 
 
-def pack_kernel(experts, place, both, hidden, gain, router, gate, send):
+def pack_kernel(held, place, both, hidden, gain, router, gate, own, other):
     count = gate.shape[0]
     slot = lax.broadcasted_iota(jnp.int32, (count, hidden.shape[0]), 0)
     table = slot == place[...]
     rows = dot(table.astype(jnp.bfloat16), hidden[...])
     normed = normalize(rows, gain[...])
-    send[...] = jnp.concatenate(
-        [normed[e * PAD : (e + 1) * PAD] for e in experts], axis=0
-    ).astype(jnp.bfloat16)
+    near, far = halves(held, normed)
+    own[...] = near.astype(jnp.bfloat16)
+    other[...] = far.astype(jnp.bfloat16)
     logits = dot(normed.astype(jnp.bfloat16), router[...])
     mine = lax.broadcasted_iota(jnp.int32, (count, 1), 0) // PAD
     others = jnp.sum(jnp.where(table, both[...], 0), axis=1, keepdims=True) - mine
@@ -110,20 +110,25 @@
     gate[...] = 1.0 / (1.0 + jnp.exp(-jnp.sum(lead, axis=1, keepdims=True)))
 
 
+def halves(held, rows):
+    first = held[0] == 0
+    return jnp.where(first, rows[:PAD], rows[PAD:]), jnp.where(first, rows[PAD:], rows[:PAD])
+
+
+def copies_kernel(own, arrived, out):
+    rows = jnp.concatenate([ref[...].astype(jnp.float32) for ref in (own, arrived)], axis=0)
+    rows = rows.astype(jnp.bfloat16)
+    for low in range(0, out.shape[0], 2 * PAD):
+        out[low : low + 2 * PAD] = rows
+
+
 def gate_kernel():
     pass
 
 
-def mlp_kernel(held, rows, w_in, w_out, pieces):
+def mlp_kernel(rows, w_in, w_out, pieces):
     inner = jnp.maximum(dot(rows[...], w_in[...]), 0.0).astype(jnp.bfloat16)
-    piece = dot(inner, w_out[...])
-    middle = piece.shape[0] // 2
-    first = held[0] == 0
-    near = jnp.where(first, piece[:middle], piece[middle:])
-    far = jnp.where(first, piece[middle:], piece[:middle])
-    for low in range(0, middle, PAD):
-        both = jnp.concatenate([near[low : low + PAD], far[low : low + PAD]], axis=0)
-        pieces[2 * low : 2 * low + 2 * PAD] = both.astype(jnp.bfloat16)
+    pieces[...] = dot(inner, w_out[...]).astype(jnp.bfloat16)
 
 
 def sum_kernel(pieces, own, other):
@@ -202,39 +207,40 @@
 
 def expert_layer(mark, hidden, norm_gain, router, w_in, w_out, routes, slots):
     devices = lax.axis_size("ep")
-    experts = devices // SPLIT
     width = hidden.shape[1]
-    place = places(routes, slots)
-    held = [device // SPLIT for device in range(devices)]
-    blocks = (devices * PAD, width)
-
     depth = chips()[0]
     half = (place_of(lax.axis_index("ep"))[0] // (depth // 2))[None]
-    halves = [list(range(low, low + SPLIT)) for low in range(0, devices, SPLIT)]
-
-    def exchanged(values, groups=None):
-        parts = values.reshape(len(groups[0]) if groups else devices, -1, width)
+    groups = [list(range(low, low + SPLIT)) for low in range(0, devices, SPLIT)]
+    small, wide = (PAD, width), (2 * PAD * SPLIT, width)
+
+    def exchanged(values):
+        parts = values.reshape(SPLIT, 2 * PAD, width)
         parts = lax.all_to_all(
             parts, "ep", split_axis=0, concat_axis=0, tiled=True, axis_index_groups=groups
         )
         return parts.reshape(values.shape)
 
-    gate, send = local(
-        functools.partial(pack_kernel, held),
+    gate, own, other = local(
+        pack_kernel,
         "pack",
-        [((experts * PAD, 1), jnp.float32), (blocks, jnp.bfloat16)],
-        (place[None, :], jnp.sum(routes, axis=1)[None, :], hidden, norm_gain[None, :], router),
+        [((2 * PAD, 1), jnp.float32), (small, jnp.bfloat16), (small, jnp.bfloat16)],
+        (
+            places(routes, slots)[None, :],
+            jnp.sum(routes, axis=1)[None, :],
+            hidden,
+            norm_gain[None, :],
+            router,
+        ),
+        order=half,
+    )
+    (send,) = local(
+        copies_kernel, "copies", [(wide, jnp.bfloat16)], (own, moved(other, dz=depth // 2))
     )
     (pieces,) = local(
-        mlp_kernel,
-        "mlp",
-        [(blocks, jnp.bfloat16)],
-        (exchanged(send), w_in, w_out),
-        mark,
-        order=half,
+        mlp_kernel, "mlp", [(wide, jnp.bfloat16)], (exchanged(send), w_in, w_out), mark
     )
     own, other = local(
-        sum_kernel, "sum", [((PAD, width), jnp.float32)] * 2, (exchanged(pieces, halves),)
+        sum_kernel, "sum", [((PAD, width), jnp.float32)] * 2, (exchanged(pieces),)
     )
     (rows,) = local(
         rows_kernel,

time: 106 us -> 110 us (1.038)
  waiting for transfers between devices: 37.1 us -> 40 us
  starting transfers between devices: 32.2 us -> 33.5 us
    ppermute x16 -> x17, waiting for transfers between devices: 33.8 us -> 36.7 us  [moved(): return lax.ppermute(value, 'ep', pairs)]
    ppermute x16 -> x17, starting transfers between devices: 18.1 us -> 20.1 us  [moved(): return lax.ppermute(value, 'ep', pairs)]
    pallas_call x12 -> x13, Pallas kernels: 16.2 us -> 16.4 us  [local(): pl.pallas_call(run, out_shape=[jax.ShapeDtypeStruct(shape, dtype) for sha...]
  transfers between devices with their start and end apart: 22 -> 23, of which waited for: 7 -> 8; matrix products, arithmetic and copies ran while one was open for 2% -> 2% of each run, Pallas kernels for 10% -> 10%
where the time goes in v11:
time: 110 us; the launch traced here: 109 us
  waiting for transfers between devices  40 us (36%)
  starting transfers between devices  33.5 us (30%)
  local copies, waits for them, and re-layouts  17.6 us (16%)
  Pallas kernels  16.4 us (15%)
  other arithmetic  1.13 us (1%)
    ppermute x17, waiting for transfers between devices, moved(): return lax.ppermute(value, 'ep', pairs)  36.7 us
    ppermute x17, starting transfers between devices, moved(): return lax.ppermute(value, 'ep', pairs)  20.1 us
    pallas_call x13, Pallas kernels, local(): pl.pallas_call(run, out_shape=[jax.ShapeDtypeStruct(shape, dtype) for sha...  16.4 us
    unnamed x38, local copies, waits for them, and re-layouts  14.4 us
    all_to_all x2, starting transfers between devices, exchanged(): lax.all_to_all(parts, 'ep', split_axis=0, concat_axis=0, tiled=True, axis...  8.41 us
    ppermute x1, waiting for transfers between devices, body(): received = lax.ppermute(sent, 'grp', [(0, 1)])  2.77 us
    ppermute x1, starting transfers between devices, body(): other_hidden = lax.ppermute(hidden[0], 'grp', [(0, 1), (1, 0)])  2.61 us
  transfers between devices with their start and end apart: 23, of which 8 were waited for; matrix products, arithmetic and copies ran while one was open for 2% of the time, Pallas kernels for 10%

profile of v11, /device:TPU:1, one launch (start us, length us, event | category | flops | bytes accessed | tf_op | source)
XLA Modules:
  0.0 109.1 jit_solution(8223307434234711195)
XLA Ops:
  0.0 1.0 constant_dynamic-slice_fusion
  1.0 1.0 constant_dynamic-slice_fusion.2
  2.1 2.2 %collective-permute-start.1 = (bf16[128,2048]{1,0:T(8,128)(2,1)S(1)}, bf16[128,2048]{1,0:T(8,128)(2,1)S(1)}, u32[]{:S(2)}, u32[]{:S(2)}) collective-permute-start(bf16[128,2048]{1,0:T(8,128)(2,1)S(1)} %pad_maximum_fusion.refs_3_.refs_7_), channel_id=1, source_target_pairs={{0,4},{1,5},{2,6},{3,7},{4,8},{5,9},{6,10},{7,11},{8,12},{9,13},{1... | collective-permute-start | bytes 1572872 | tf_op jit(solution)/shard_map/ppermute | solution.py:62
  4.2 1.2 %collective-permute-start.4 = (bf16[128,2048]{1,0:T(8,128)(2,1)S(1)}, bf16[128,2048]{1,0:T(8,128)(2,1)S(1)}, u32[]{:S(2)}, u32[]{:S(2)}) collective-permute-start(bf16[128,2048]{1,0:T(8,128)(2,1)S(1)} %pad_maximum_fusion.refs_3_.refs_7_), channel_id=1, source_target_pairs={{0,1},{1,0},{2,3},{3,2},{4,5},{5,4},{6,7},{7,6},{8,9},{9,8},{10,11... | collective-permute-start | bytes 1572872 | tf_op jit(solution)/shard_map/ppermute | solution.py:62
  5.4 1.2 %collective-permute-start.5 = (bf16[128,2048]{1,0:T(8,128)(2,1)S(1)}, bf16[128,2048]{1,0:T(8,128)(2,1)S(1)}, u32[]{:S(2)}, u32[]{:S(2)}) collective-permute-start(bf16[128,2048]{1,0:T(8,128)(2,1)S(1)} %pad_maximum_fusion.refs_3_.refs_7_), channel_id=1, source_target_pairs={{0,2},{1,3},{2,0},{3,1},{4,6},{5,7},{6,4},{7,5},{8,10},{9,11},{10,... | collective-permute-start | bytes 1572872 | tf_op jit(solution)/shard_map/ppermute | solution.py:62
  6.7 0.7 fusion.2
  7.4 1.2 %copy-done.10 = bf16[1,256,2048]{2,1,0:T(8,128)(2,1)S(1)} copy-done((bf16[1,256,2048]{2,1,0:T(8,128)(2,1)S(1)}, bf16[1,256,2048]{2,1,0:T(8,128)(2,1)}, u32[]{:S(2)}) %copy-start.10) | copy-done | bytes 1048600
  8.6 1.0 copy-done.13
  9.7 0.7 copy-done.16
  10.4 0.7 pack.1
  11.0 2.3 %collective-permute-start = (bf16[8,2048]{1,0:T(8,128)(2,1)S(1)}, bf16[8,2048]{1,0:T(8,128)(2,1)S(1)}, u32[]{:S(2)}, u32[]{:S(2)}) collective-permute-start(bf16[8,2048]{1,0:T(8,128)(2,1)S(1)} %get-tuple-element.26), channel_id=1, source_target_pairs={{0,8},{1,9},{2,10},{3,11},{4,12},{5,13},{6,14},{7,15},{8,0},{9,1},... | collective-permute-start | bytes 98312 | tf_op jit(solution)/shard_map/ppermute | solution.py:62
  13.4 6.7 %collective-permute-done.refs_1_ = bf16[8,2048]{1,0:T(8,128)(2,1)S(1)} collective-permute-done((bf16[8,2048]{1,0:T(8,128)(2,1)S(1)}, bf16[8,2048]{1,0:T(8,128)(2,1)S(1)}, u32[]{:S(2)}, u32[]{:S(2)}) %collective-permute-start) | collective-permute-done | bytes 32800 | tf_op jit(solution)/shard_map/ppermute | solution.py:62
  20.0 0.8 copies.1
  20.9 4.1 %all-to-all-start = ((bf16[8,16,2048]{2,1,0:T(8,128)(2,1)}), bf16[8,16,2048]{2,1,0:T(8,128)(2,1)}, u32[]{:S(2)}, u32[]{:S(2)}) async-start(bf16[8,16,2048]{2,1,0:T(8,128)(2,1)} %bitcast.7), calls=%async_computation | async-start | bytes 1048576 | tf_op jit(solution)/shard_map/all_to_all | solution.py:218
  25.0 1.3 %collective-permute-start.2 = (bf16[128,2048]{1,0:T(8,128)(2,1)S(1)}, bf16[128,2048]{1,0:T(8,128)(2,1)S(1)}, u32[]{:S(2)}, u32[]{:S(2)}) collective-permute-start(bf16[128,2048]{1,0:T(8,128)(2,1)S(1)} %collective-permute-done.1.refs_1_.refs_2_), channel_id=1, source_target_pairs={{0,2},{1,3},{2,0},{3,1},{4,6},{5,7},{6,4},{7,5},{8,10},{9,11},{10,... | collective-permute-start | bytes 1572872 | tf_op jit(solution)/shard_map/ppermute | solution.py:62
  26.4 1.2 %collective-permute-start.3 = (bf16[128,2048]{1,0:T(8,128)(2,1)S(1)}, bf16[128,2048]{1,0:T(8,128)(2,1)S(1)}, u32[]{:S(2)}, u32[]{:S(2)}) collective-permute-start(bf16[128,2048]{1,0:T(8,128)(2,1)S(1)} %collective-permute-done.1.refs_1_.refs_2_), channel_id=1, source_target_pairs={{0,4},{1,5},{2,6},{3,7},{4,8},{5,9},{6,10},{7,11},{8,12},{9,13},{1... | collective-permute-start | bytes 1572872 | tf_op jit(solution)/shard_map/ppermute | solution.py:62
  27.6 1.3 %collective-permute-start.6 = (bf16[128,2048]{1,0:T(8,128)(2,1)S(1)}, bf16[128,2048]{1,0:T(8,128)(2,1)S(1)}, u32[]{:S(2)}, u32[]{:S(2)}) collective-permute-start(bf16[128,2048]{1,0:T(8,128)(2,1)S(1)} %gate.4.refs_9_.refs_13_), channel_id=1, source_target_pairs={{0,1},{1,0},{2,3},{3,2},{4,5},{5,4},{6,7},{7,6},{8,9},{9,8},{10,11... | collective-permute-start | bytes 1572872 | tf_op jit(solution)/shard_map/ppermute | solution.py:62
  28.9 14.6 %collective-permute-done.2.refs_0_.refs_10_.refs_14_ = bf16[128,2048]{1,0:T(8,128)(2,1)S(1)} collective-permute-done((bf16[128,2048]{1,0:T(8,128)(2,1)S(1)}, bf16[128,2048]{1,0:T(8,128)(2,1)S(1)}, u32[]{:S(2)}, u32[]{:S(2)}) %collective-permute-start.2) | collective-permute-done | bytes 524320 | tf_op jit(solution)/shard_map/ppermute | solution.py:62
  43.6 2.2 %collective-permute-start.11 = (bf16[128,2048]{1,0:T(8,128)(2,1)S(1)}, bf16[128,2048]{1,0:T(8,128)(2,1)S(1)}, u32[]{:S(2)}, u32[]{:S(2)}) collective-permute-start(bf16[128,2048]{1,0:T(8,128)(2,1)S(1)} %get-tuple-element.27.refs_3_.refs_4_.refs_8_), channel_id=1, source_target_pairs={{0,1},{1,0},{2,3},{3,2},{4,5},{5,4},{6,7},{7,6},{8,9},{9,8},{10,11... | collective-permute-start | bytes 1572872 | tf_op jit(solution)/shard_map/ppermute | solution.py:62
  45.9 1.3 %collective-permute-start.13 = (bf16[128,2048]{1,0:T(8,128)(2,1)S(1)}, bf16[128,2048]{1,0:T(8,128)(2,1)S(1)}, u32[]{:S(2)}, u32[]{:S(2)}) collective-permute-start(bf16[128,2048]{1,0:T(8,128)(2,1)S(1)} %collective-permute-done.3.refs_1_.refs_3_), channel_id=1, source_target_pairs={{0,4},{1,5},{2,6},{3,7},{4,8},{5,9},{6,10},{7,11},{8,12},{9,13},{1... | collective-permute-start | bytes 1572872 | tf_op jit(solution)/shard_map/ppermute | solution.py:62
  47.2 2.2 %copy-done.8 = bf16[1,2048,1024]{2,1,0:T(8,128)(2,1)S(1)} copy-done((bf16[1,2048,1024]{2,1,0:T(8,128)(2,1)S(1)}, bf16[1,2048,1024]{2,1,0:T(8,128)(2,1)}, u32[]{:S(2)}) %copy-start.8) | copy-done | bytes 4194328
  49.4 2.2 %copy-done.9 = bf16[1,1024,2048]{2,1,0:T(8,128)(2,1)S(1)} copy-done((bf16[1,1024,2048]{2,1,0:T(8,128)(2,1)S(1)}, bf16[1,1024,2048]{2,1,0:T(8,128)(2,1)}, u32[]{:S(2)}) %copy-start.9) | copy-done | bytes 4194328
  51.6 2.4 %mlp.1 = bf16[128,2048]{1,0:T(8,128)(2,1)S(1)} custom-call(bf16[128,2048]{1,0:T(8,128)(2,1)} %bitcast.8.refs_0_, bf16[2048,1024]{1,0:T(8,128)(2,1)S(1)} %bitcast.36, bf16[1024,2048]{1,0:T(8,128)(2,1)S(1)} %bitcast.37, bf16[128,2048]{1,0:T(8,128)(2,1)S(1)} %get-tuple-element.27.refs_3_.refs_4_.refs_8_), custom_call_target="tpu_custom_call" | custom-call | tf_op jit(solution)/shard_map/mlp/pallas_call | solution.py:83
  54.0 0.8 copy-done.12
  54.8 4.3 %all-to-all-start.1 = ((bf16[8,16,2048]{2,1,0:T(8,128)(2,1)}), bf16[8,16,2048]{2,1,0:T(8,128)(2,1)}, u32[]{:S(2)}, u32[]{:S(2)}) async-start(bf16[8,16,2048]{2,1,0:T(8,128)(2,1)} %bitcast.41), calls=%async_computation.1 | async-start | bytes 1048576 | tf_op jit(solution)/shard_map/all_to_all | solution.py:218
  59.1 1.0 collective-permute-done.13.refs_2_.refs_3_
  60.5 1.2 %collective-permute-start.15 = (bf16[128,2048]{1,0:T(8,128)(2,1)S(1)}, bf16[128,2048]{1,0:T(8,128)(2,1)}, u32[]{:S(2)}, u32[]{:S(2)}) collective-permute-start(bf16[128,2048]{1,0:T(8,128)(2,1)S(1)} %collective-permute-done.13.refs_2_.refs_3_), channel_id=1, source_target_pairs={{0,2},{1,3},{2,0},{3,1},{4,6},{5,7},{6,4},{7,5},{8,10},{9,11},{10,... | collective-permute-start | bytes 1572872 | tf_op jit(solution)/shard_map/ppermute | solution.py:62
  61.7 1.2 %collective-permute-start.16 = (bf16[128,2048]{1,0:T(8,128)(2,1)S(1)}, bf16[128,2048]{1,0:T(8,128)(2,1)}, u32[]{:S(2)}, u32[]{:S(2)}) collective-permute-start(bf16[128,2048]{1,0:T(8,128)(2,1)S(1)} %get-tuple-element.34.refs_5_.refs_9_), channel_id=1, source_target_pairs={{0,1},{1,0},{2,3},{3,2},{4,5},{5,4},{6,7},{7,6},{8,9},{9,8},{10,11... | collective-permute-start | bytes 1572872 | tf_op jit(solution)/shard_map/ppermute | solution.py:62
  62.9 2.6 %collective-permute-start.8 = (bf16[256,2048]{1,0:T(8,128)(2,1)}, bf16[256,2048]{1,0:T(8,128)(2,1)}, u32[]{:S(2)}, u32[]{:S(2)}) collective-permute-start(bf16[256,2048]{1,0:T(8,128)(2,1)} %bitcast.38), channel_id=1, source_target_pairs={{0,16},{16,0},{1,17},{17,1},{2,18},{18,2},{3,19},{19,3},{4,20},{20... | collective-permute-start | bytes 3145736 | tf_op jit(solution)/shard_map/ppermute | solution.py:474
  65.8 1.1 %sum.1 = (f32[8,2048]{1,0:T(8,128)S(1)}, f32[8,2048]{1,0:T(8,128)S(1)}) custom-call(bf16[128,2048]{1,0:T(8,128)(2,1)} %bitcast.12.refs_0_), custom_call_target="tpu_custom_call" | custom-call | tf_op jit(solution)/shard_map/sum/pallas_call | solution.py:83
  66.9 0.7 collective-permute-start.7
  67.6 14.3 %collective-permute-done.7.refs_3_ = f32[8,2048]{1,0:T(8,128)S(1)} collective-permute-done((f32[8,2048]{1,0:T(8,128)S(1)}, f32[8,2048]{1,0:T(8,128)S(1)}, u32[]{:S(2)}, u32[]{:S(2)}) %collective-permute-start.7) | collective-permute-done | bytes 65568 | tf_op jit(solution)/shard_map/ppermute | solution.py:62
  82.5 1.0 collective-permute-start.17
  83.6 1.2 %collective-permute-start.19 = (bf16[128,2048]{1,0:T(8,128)(2,1)}, bf16[128,2048]{1,0:T(8,128)(2,1)}, u32[]{:S(2)}, u32[]{:S(2)}) collective-permute-start(bf16[128,2048]{1,0:T(8,128)(2,1)} %get-tuple-element.38.refs_15_.refs_19_), channel_id=1, source_target_pairs={{0,2},{1,3},{2,0},{3,1},{4,6},{5,7},{6,4},{7,5},{8,10},{9,11},{10,... | collective-permute-start | bytes 1572872 | tf_op jit(solution)/shard_map/ppermute | solution.py:62
  85.5 0.6 collective-permute-start.10
  86.2 0.8 copy.32.refs_6_
  87.3 1.2 %copy-done.11 = bf16[1,256,2048]{2,1,0:T(8,128)(2,1)S(1)} copy-done((bf16[1,256,2048]{2,1,0:T(8,128)(2,1)S(1)}, bf16[1,256,2048]{2,1,0:T(8,128)(2,1)}, u32[]{:S(2)}) %copy-start.11) | copy-done | bytes 1048600
  88.5 0.9 copy-done.14
  89.4 2.9 %norm.1 = (bf16[256,2048]{1,0:T(8,128)(2,1)S(1)}, bf16[176,2048]{1,0:T(8,128)(2,1)S(1)}, f32[256,2048]{1,0:T(8,128)S(1)}) custom-call(s32[1]{0:T(128)} %bitcast.refs_0_, bf16[256,2048]{1,0:T(8,128)(2,1)S(1)} %bitcast.40, f32[256,1]{1,0:T(8,128)S(1)} %copy.31.refs_2_, f32[16,2048]{1,0:T(8,128)S(1)} %rows.1.refs_3_.refs_2_, f32[1,2048]{1,0:T(1,128)S(1)} %copy-done.15, ...), custom_call_target="tpu_custom_call" | custom-call | tf_op jit(solution)/shard_map/norm/pallas_call | solution.py:83
  92.3 1.0 copy-done.1
  93.3 1.0 copy-done.3
  94.4 1.0 copy-done.5
  95.4 1.0 copy-done.7
  96.5 2.8 %project.1 = (f32[256,1024]{1,0:T(8,128)S(1)}, f32[176,512]{1,0:T(8,128)S(1)}) custom-call(s32[16]{0:T(128)S(1)} %stack.67.refs_0_, bf16[256,2048]{1,0:T(8,128)(2,1)S(1)} %get-tuple-element.30.refs_1_.refs_3_, bf16[176,2048]{1,0:T(8,128)(2,1)S(1)} %get-tuple-element.32.refs_2_.refs_4_, bf16[128,2048]{1,0:T(8,128)(2,1)S(1)} %copy-done.1, ...), custom_call_target="tpu_custom_call" | custom-call | tf_op jit(solution)/shard_map/project/pallas_call | solution.py:83
  99.3 4.2 %attend.1 = (f32[176,2048]{1,0:T(8,128)S(1)}, bf16[176,2048]{1,0:T(8,128)(2,1)S(1)}) custom-call(s32[16]{0:T(128)S(1)} %stack.67.refs_0_, s32[176,1]{1,0:T(8,128)S(1)} %copy.33.refs_1_, s32[1,256]{1,0:T(1,128)S(1)} %bitcast.46, bf16[256,2048]{1,0:T(8,128)(2,1)S(1)} %get-tuple-element.30.refs_1_.refs_3_, ...), custom_call_target="tpu_custom_call" | custom-call | tf_op jit(solution)/shard_map/attend/pallas_call | solution.py:83
  103.5 1.3 %collective-permute-start.20 = (bf16[176,2048]{1,0:T(8,128)(2,1)S(1)}, bf16[176,2048]{1,0:T(8,128)(2,1)S(1)}, u32[]{:S(2)}, u32[]{:S(2)}) collective-permute-start(bf16[176,2048]{1,0:T(8,128)(2,1)S(1)} %get-tuple-element.42), channel_id=1, source_target_pairs={{0,16},{1,17},{2,18},{3,19},{4,20},{5,21},{6,22},{7,23},{8,24},{9,... | collective-permute-start | bytes 2162696 | tf_op jit(solution)/shard_map/ppermute | solution.py:494
  104.8 2.8 %collective-permute-done.20.refs_4_ = bf16[176,2048]{1,0:T(8,128)(2,1)S(1)} collective-permute-done((bf16[176,2048]{1,0:T(8,128)(2,1)S(1)}, bf16[176,2048]{1,0:T(8,128)(2,1)S(1)}, u32[]{:S(2)}, u32[]{:S(2)}) %collective-permute-start.20) | collective-permute-done | bytes 720928 | tf_op jit(solution)/shard_map/ppermute | solution.py:494
  107.6 1.5 %finish.1 = bf16[256,2048]{1,0:T(8,128)(2,1)} custom-call(s32[1]{0:T(128)} %bitcast.refs_0_, bf16[256,2048]{1,0:T(8,128)(2,1)S(1)} %get-tuple-element.30.refs_1_.refs_3_, f32[256,2048]{1,0:T(8,128)S(1)} %get-tuple-element.31.refs_2_, f32[176,2048]{1,0:T(8,128)S(1)} %get-tuple-element.41.refs_3_, bf16[176,2048]{1,0:T(8,128)(2,1)S(1)} %collective-permute-done.20.refs_4_, ...), custom_call_target="tpu_custom_call" | custom-call | tf_op jit(solution)/shard_map/finish/pallas_call | solution.py:83
  (67 shorter events, 2.6 us)
Async XLA Ops:
  2.0 25.5 %copy-start = (bf16[128,2048]{1,0:T(8,128)(2,1)}, bf16[128,2048]{1,0:T(8,128)(2,1)S(1)}, u32[]{:S(2)}) copy-start(bf16[128,2048]{1,0:T(8,128)(2,1)S(1)} %pad_maximum_fusion.refs_3_.refs_7_) | copy-start | bytes 1572868
  2.1 23.0 %collective-permute-start.1 = (bf16[128,2048]{1,0:T(8,128)(2,1)S(1)}, bf16[128,2048]{1,0:T(8,128)(2,1)S(1)}, u32[]{:S(2)}, u32[]{:S(2)}) collective-permute-start(bf16[128,2048]{1,0:T(8,128)(2,1)S(1)} %pad_maximum_fusion.refs_3_.refs_7_), channel_id=1, source_target_pairs={{0,4},{1,5},{2,6},{3,7},{4,8},{5,9},{6,10},{7,11},{8,12},{9,13},{1... | collective-permute-start | bytes 1572872 | tf_op jit(solution)/shard_map/ppermute | solution.py:62
  4.2 23.3 %collective-permute-start.4 = (bf16[128,2048]{1,0:T(8,128)(2,1)S(1)}, bf16[128,2048]{1,0:T(8,128)(2,1)S(1)}, u32[]{:S(2)}, u32[]{:S(2)}) collective-permute-start(bf16[128,2048]{1,0:T(8,128)(2,1)S(1)} %pad_maximum_fusion.refs_3_.refs_7_), channel_id=1, source_target_pairs={{0,1},{1,0},{2,3},{3,2},{4,5},{5,4},{6,7},{7,6},{8,9},{9,8},{10,11... | collective-permute-start | bytes 1572872 | tf_op jit(solution)/shard_map/ppermute | solution.py:62
  5.4 22.1 %collective-permute-start.5 = (bf16[128,2048]{1,0:T(8,128)(2,1)S(1)}, bf16[128,2048]{1,0:T(8,128)(2,1)S(1)}, u32[]{:S(2)}, u32[]{:S(2)}) collective-permute-start(bf16[128,2048]{1,0:T(8,128)(2,1)S(1)} %pad_maximum_fusion.refs_3_.refs_7_), channel_id=1, source_target_pairs={{0,2},{1,3},{2,0},{3,1},{4,6},{5,7},{6,4},{7,5},{8,10},{9,11},{10,... | collective-permute-start | bytes 1572872 | tf_op jit(solution)/shard_map/ppermute | solution.py:62
  7.4 1.2 %copy-start.10 = (bf16[1,256,2048]{2,1,0:T(8,128)(2,1)S(1)}, bf16[1,256,2048]{2,1,0:T(8,128)(2,1)}, u32[]{:S(2)}) copy-start(bf16[1,256,2048]{2,1,0:T(8,128)(2,1)} %param.14) | copy-start | bytes 3145732
  8.6 1.0 copy-start.13
  9.7 0.7 copy-start.16
  11.0 9.0 %collective-permute-start = (bf16[8,2048]{1,0:T(8,128)(2,1)S(1)}, bf16[8,2048]{1,0:T(8,128)(2,1)S(1)}, u32[]{:S(2)}, u32[]{:S(2)}) collective-permute-start(bf16[8,2048]{1,0:T(8,128)(2,1)S(1)} %get-tuple-element.26), channel_id=1, source_target_pairs={{0,8},{1,9},{2,10},{3,11},{4,12},{5,13},{6,14},{7,15},{8,0},{9,1},... | collective-permute-start | bytes 98312 | tf_op jit(solution)/shard_map/ppermute | solution.py:62
  20.9 26.3 %all-to-all-start = ((bf16[8,16,2048]{2,1,0:T(8,128)(2,1)}), bf16[8,16,2048]{2,1,0:T(8,128)(2,1)}, u32[]{:S(2)}, u32[]{:S(2)}) async-start(bf16[8,16,2048]{2,1,0:T(8,128)(2,1)} %bitcast.7), calls=%async_computation | async-start | bytes 1048576 | tf_op jit(solution)/shard_map/all_to_all | solution.py:218
  25.0 18.5 %collective-permute-start.2 = (bf16[128,2048]{1,0:T(8,128)(2,1)S(1)}, bf16[128,2048]{1,0:T(8,128)(2,1)S(1)}, u32[]{:S(2)}, u32[]{:S(2)}) collective-permute-start(bf16[128,2048]{1,0:T(8,128)(2,1)S(1)} %collective-permute-done.1.refs_1_.refs_2_), channel_id=1, source_target_pairs={{0,2},{1,3},{2,0},{3,1},{4,6},{5,7},{6,4},{7,5},{8,10},{9,11},{10,... | collective-permute-start | bytes 1572872 | tf_op jit(solution)/shard_map/ppermute | solution.py:62
  26.4 17.1 %collective-permute-start.3 = (bf16[128,2048]{1,0:T(8,128)(2,1)S(1)}, bf16[128,2048]{1,0:T(8,128)(2,1)S(1)}, u32[]{:S(2)}, u32[]{:S(2)}) collective-permute-start(bf16[128,2048]{1,0:T(8,128)(2,1)S(1)} %collective-permute-done.1.refs_1_.refs_2_), channel_id=1, source_target_pairs={{0,4},{1,5},{2,6},{3,7},{4,8},{5,9},{6,10},{7,11},{8,12},{9,13},{1... | collective-permute-start | bytes 1572872 | tf_op jit(solution)/shard_map/ppermute | solution.py:62
  27.6 18.2 %copy-start.2 = (bf16[128,2048]{1,0:T(8,128)(2,1)}, bf16[128,2048]{1,0:T(8,128)(2,1)S(1)}, u32[]{:S(2)}) copy-start(bf16[128,2048]{1,0:T(8,128)(2,1)S(1)} %collective-permute-done.4.refs_0_.refs_7_.refs_11_) | copy-start | bytes 1572868
  27.6 16.0 %copy-start.6 = (bf16[128,2048]{1,0:T(8,128)(2,1)}, bf16[128,2048]{1,0:T(8,128)(2,1)S(1)}, u32[]{:S(2)}) copy-start(bf16[128,2048]{1,0:T(8,128)(2,1)S(1)} %gate.4.refs_9_.refs_13_) | copy-start | bytes 1572868
  27.6 15.9 %collective-permute-start.6 = (bf16[128,2048]{1,0:T(8,128)(2,1)S(1)}, bf16[128,2048]{1,0:T(8,128)(2,1)S(1)}, u32[]{:S(2)}, u32[]{:S(2)}) collective-permute-start(bf16[128,2048]{1,0:T(8,128)(2,1)S(1)} %gate.4.refs_9_.refs_13_), channel_id=1, source_target_pairs={{0,1},{1,0},{2,3},{3,2},{4,5},{5,4},{6,7},{7,6},{8,9},{9,8},{10,11... | collective-permute-start | bytes 1572872 | tf_op jit(solution)/shard_map/ppermute | solution.py:62
  43.5 2.4 %copy-start.4 = (bf16[128,2048]{1,0:T(8,128)(2,1)}, bf16[128,2048]{1,0:T(8,128)(2,1)S(1)}, u32[]{:S(2)}) copy-start(bf16[128,2048]{1,0:T(8,128)(2,1)S(1)} %collective-permute-done.2.refs_0_.refs_10_.refs_14_) | copy-start | bytes 1572868
  43.6 15.5 %collective-permute-start.11 = (bf16[128,2048]{1,0:T(8,128)(2,1)S(1)}, bf16[128,2048]{1,0:T(8,128)(2,1)S(1)}, u32[]{:S(2)}, u32[]{:S(2)}) collective-permute-start(bf16[128,2048]{1,0:T(8,128)(2,1)S(1)} %get-tuple-element.27.refs_3_.refs_4_.refs_8_), channel_id=1, source_target_pairs={{0,1},{1,0},{2,3},{3,2},{4,5},{5,4},{6,7},{7,6},{8,9},{9,8},{10,11... | collective-permute-start | bytes 1572872 | tf_op jit(solution)/shard_map/ppermute | solution.py:62
  45.8 13.3 %collective-permute-start.12 = (bf16[128,2048]{1,0:T(8,128)(2,1)S(1)}, bf16[128,2048]{1,0:T(8,128)(2,1)S(1)}, u32[]{:S(2)}, u32[]{:S(2)}) collective-permute-start(bf16[128,2048]{1,0:T(8,128)(2,1)S(1)} %collective-permute-done.3.refs_1_.refs_3_), channel_id=1, source_target_pairs={{0,2},{1,3},{2,0},{3,1},{4,6},{5,7},{6,4},{7,5},{8,10},{9,11},{10,... | collective-permute-start | bytes 1572872 | tf_op jit(solution)/shard_map/ppermute | solution.py:62
  45.9 14.2 %collective-permute-start.13 = (bf16[128,2048]{1,0:T(8,128)(2,1)S(1)}, bf16[128,2048]{1,0:T(8,128)(2,1)S(1)}, u32[]{:S(2)}, u32[]{:S(2)}) collective-permute-start(bf16[128,2048]{1,0:T(8,128)(2,1)S(1)} %collective-permute-done.3.refs_1_.refs_3_), channel_id=1, source_target_pairs={{0,4},{1,5},{2,6},{3,7},{4,8},{5,9},{6,10},{7,11},{8,12},{9,13},{1... | collective-permute-start | bytes 1572872 | tf_op jit(solution)/shard_map/ppermute | solution.py:62
  47.2 2.2 %copy-start.8 = (bf16[1,2048,1024]{2,1,0:T(8,128)(2,1)S(1)}, bf16[1,2048,1024]{2,1,0:T(8,128)(2,1)}, u32[]{:S(2)}) copy-start(bf16[1,2048,1024]{2,1,0:T(8,128)(2,1)} %param.18) | copy-start | bytes 12582916
  49.4 2.2 %copy-start.9 = (bf16[1,1024,2048]{2,1,0:T(8,128)(2,1)S(1)}, bf16[1,1024,2048]{2,1,0:T(8,128)(2,1)}, u32[]{:S(2)}) copy-start(bf16[1,1024,2048]{2,1,0:T(8,128)(2,1)} %param.19) | copy-start | bytes 12582916
  51.6 13.9 %copy-start.15 = (f32[1,2048]{1,0:T(1,128)S(1)}, f32[1,2048]{1,0:T(1,128)}, u32[]{:S(2)}) copy-start(f32[1,2048]{1,0:T(1,128)} %refs_4_.3) | copy-start | bytes 24580
  54.0 0.8 copy-start.12
  54.8 12.8 %copy-start.17 = (s32[1,4]{1,0:T(1,128)S(1)}, s32[1,4]{1,0:T(1,128)}, u32[]{:S(2)}) copy-start(s32[1,4]{1,0:T(1,128)} %param.23) | copy-start | bytes 52
  54.8 30.1 %copy-start.18 = (s32[1,4]{1,0:T(1,128)S(1)}, s32[1,4]{1,0:T(1,128)}, u32[]{:S(2)}) copy-start(s32[1,4]{1,0:T(1,128)} %param.22) | copy-start | bytes 52
  54.8 11.0 %all-to-all-start.1 = ((bf16[8,16,2048]{2,1,0:T(8,128)(2,1)}), bf16[8,16,2048]{2,1,0:T(8,128)(2,1)}, u32[]{:S(2)}, u32[]{:S(2)}) async-start(bf16[8,16,2048]{2,1,0:T(8,128)(2,1)} %bitcast.41), calls=%async_computation.1 | async-start | bytes 1048576 | tf_op jit(solution)/shard_map/all_to_all | solution.py:218
  60.1 22.4 %collective-permute-start.14 = (bf16[128,2048]{1,0:T(8,128)(2,1)S(1)}, bf16[128,2048]{1,0:T(8,128)(2,1)}, u32[]{:S(2)}, u32[]{:S(2)}) collective-permute-start(bf16[128,2048]{1,0:T(8,128)(2,1)S(1)} %get-tuple-element.35.refs_4_), channel_id=1, source_target_pairs={{0,4},{1,5},{2,6},{3,7},{4,8},{5,9},{6,10},{7,11},{8,12},{9,13},{1... | collective-permute-start | bytes 1572872 | tf_op jit(solution)/shard_map/ppermute | solution.py:62
  60.5 22.0 %collective-permute-start.15 = (bf16[128,2048]{1,0:T(8,128)(2,1)S(1)}, bf16[128,2048]{1,0:T(8,128)(2,1)}, u32[]{:S(2)}, u32[]{:S(2)}) collective-permute-start(bf16[128,2048]{1,0:T(8,128)(2,1)S(1)} %collective-permute-done.13.refs_2_.refs_3_), channel_id=1, source_target_pairs={{0,2},{1,3},{2,0},{3,1},{4,6},{5,7},{6,4},{7,5},{8,10},{9,11},{10,... | collective-permute-start | bytes 1572872 | tf_op jit(solution)/shard_map/ppermute | solution.py:62
  61.7 20.8 %collective-permute-start.16 = (bf16[128,2048]{1,0:T(8,128)(2,1)S(1)}, bf16[128,2048]{1,0:T(8,128)(2,1)}, u32[]{:S(2)}, u32[]{:S(2)}) collective-permute-start(bf16[128,2048]{1,0:T(8,128)(2,1)S(1)} %get-tuple-element.34.refs_5_.refs_9_), channel_id=1, source_target_pairs={{0,1},{1,0},{2,3},{3,2},{4,5},{5,4},{6,7},{7,6},{8,9},{9,8},{10,11... | collective-permute-start | bytes 1572872 | tf_op jit(solution)/shard_map/ppermute | solution.py:62
  62.9 24.1 %collective-permute-start.8 = (bf16[256,2048]{1,0:T(8,128)(2,1)}, bf16[256,2048]{1,0:T(8,128)(2,1)}, u32[]{:S(2)}, u32[]{:S(2)}) collective-permute-start(bf16[256,2048]{1,0:T(8,128)(2,1)} %bitcast.38), channel_id=1, source_target_pairs={{0,16},{16,0},{1,17},{17,1},{2,18},{18,2},{3,19},{19,3},{4,20},{20... | collective-permute-start | bytes 3145736 | tf_op jit(solution)/shard_map/ppermute | solution.py:474
  66.9 15.0 %collective-permute-start.7 = (f32[8,2048]{1,0:T(8,128)S(1)}, f32[8,2048]{1,0:T(8,128)S(1)}, u32[]{:S(2)}, u32[]{:S(2)}) collective-permute-start(f32[8,2048]{1,0:T(8,128)S(1)} %get-tuple-element.29), channel_id=1, source_target_pairs={{0,8},{1,9},{2,10},{3,11},{4,12},{5,13},{6,14},{7,15},{8,0},{9,1},... | collective-permute-start | bytes 196616 | tf_op jit(solution)/shard_map/ppermute | solution.py:62
  81.9 3.6 %collective-permute-start.9 = (f32[2,2048]{1,0:T(2,128)S(1)}, f32[2,2048]{1,0:T(2,128)S(1)}, u32[]{:S(2)}, u32[]{:S(2)}) collective-permute-start(f32[2,2048]{1,0:T(2,128)S(1)} %fusion), channel_id=1, source_target_pairs={{0,16},{16,0},{1,17},{17,1},{2,18},{18,2},{3,19},{19,3},{4,20},{20... | collective-permute-start | bytes 49160 | tf_op jit(solution)/shard_map/ppermute | solution.py:260
  82.5 16.7 %collective-permute-start.17 = (bf16[128,2048]{1,0:T(8,128)(2,1)S(1)}, bf16[128,2048]{1,0:T(8,128)(2,1)}, u32[]{:S(2)}, u32[]{:S(2)}) collective-permute-start(bf16[128,2048]{1,0:T(8,128)(2,1)S(1)} %get-tuple-element.36.refs_6_.refs_10_), channel_id=1, source_target_pairs={{0,1},{1,0},{2,3},{3,2},{4,5},{5,4},{6,7},{7,6},{8,9},{9,8},{10,11... | collective-permute-start | bytes 1572872 | tf_op jit(solution)/shard_map/ppermute | solution.py:62
  83.6 15.7 %collective-permute-start.18 = (bf16[128,2048]{1,0:T(8,128)(2,1)S(1)}, bf16[128,2048]{1,0:T(8,128)(2,1)}, u32[]{:S(2)}, u32[]{:S(2)}) collective-permute-start(bf16[128,2048]{1,0:T(8,128)(2,1)S(1)} %get-tuple-element.37.refs_13_.refs_17_), channel_id=1, source_target_pairs={{0,12},{1,13},{2,14},{3,15},{4,0},{5,1},{6,2},{7,3},{8,4},{9,5},{1... | collective-permute-start | bytes 1572872 | tf_op jit(solution)/shard_map/ppermute | solution.py:62
  83.6 15.7 %collective-permute-start.19 = (bf16[128,2048]{1,0:T(8,128)(2,1)}, bf16[128,2048]{1,0:T(8,128)(2,1)}, u32[]{:S(2)}, u32[]{:S(2)}) collective-permute-start(bf16[128,2048]{1,0:T(8,128)(2,1)} %get-tuple-element.38.refs_15_.refs_19_), channel_id=1, source_target_pairs={{0,2},{1,3},{2,0},{3,1},{4,6},{5,7},{6,4},{7,5},{8,10},{9,11},{10,... | collective-permute-start | bytes 1572872 | tf_op jit(solution)/shard_map/ppermute | solution.py:62
  85.5 1.8 %collective-permute-start.10 = (f32[16,2048]{1,0:T(8,128)S(1)}, f32[16,2048]{1,0:T(8,128)}, u32[]{:S(2)}, u32[]{:S(2)}) collective-permute-start(f32[16,2048]{1,0:T(8,128)S(1)} %rows.1.refs_3_.refs_2_), channel_id=1, source_target_pairs={{0,16},{16,0},{1,17},{17,1},{2,18},{18,2},{3,19},{19,3},{4,20},{20... | collective-permute-start | bytes 393224 | tf_op jit(solution)/shard_map/ppermute | solution.py:261
  87.3 1.2 %copy-start.11 = (bf16[1,256,2048]{2,1,0:T(8,128)(2,1)S(1)}, bf16[1,256,2048]{2,1,0:T(8,128)(2,1)}, u32[]{:S(2)}) copy-start(bf16[1,256,2048]{2,1,0:T(8,128)(2,1)} %param.14) | copy-start | bytes 3145732
  88.5 0.9 copy-start.14
  92.3 1.0 copy-start.1
  93.3 1.0 copy-start.3
  94.4 1.0 copy-start.5
  95.4 1.0 copy-start.7
  103.5 4.1 %collective-permute-start.20 = (bf16[176,2048]{1,0:T(8,128)(2,1)S(1)}, bf16[176,2048]{1,0:T(8,128)(2,1)S(1)}, u32[]{:S(2)}, u32[]{:S(2)}) collective-permute-start(bf16[176,2048]{1,0:T(8,128)(2,1)S(1)} %get-tuple-element.42), channel_id=1, source_target_pairs={{0,16},{1,17},{2,18},{3,19},{4,20},{5,21},{6,22},{7,23},{8,24},{9,... | collective-permute-start | bytes 2162696 | tf_op jit(solution)/shard_map/ppermute | solution.py:494
